TPU v7x, 32 devices: a whole 2x2x4 slice. The times are simulated.
32 devices in a mesh: groups: 2 (over y), space: 4 (over z), inst: 2 (over x), row: 2 (over core).
Axes of the slice: x: 2, y: 2, z: 4, core: 2. Of those that a mesh axis runs over, the one named last changes fastest.
Arguments:
- solution: bfloat16 [2, 4, 320, 8192], P('row', 'inst', None, ('groups', 'space')), parts along dimension 3, may hold values from -6 to 6
- forcing: bfloat16 [2, 4, 320, 8192], P('row', 'inst', None, ('groups', 'space')), parts along dimension 3, may hold values from -6 to 6
- metric_scale: float32 [2, 8192], P('row', ('groups', 'space')), parts along dimension 1, may hold values from 0.5 to 2
- frequency: float32 [1], replicated, may hold values from 0.1 to 0.4
- adjacency: int32 [2, 6, 8192], P('row', None, ('groups', 'space')), parts along dimension 2, may hold values from 0 to 1151, as said below
- partner: int32 [2, 4, 512], P('row', 'inst', ('groups', 'space')), parts along dimension 2, may hold values from 0 to 255, as said below
- volume_matrix: bfloat16 [320, 320], replicated, may hold values from -0.3125 to 0.3125
- trace_matrix: bfloat16 [480, 320], replicated, may hold values from -0.3125 to 0.3125
- lift_matrix: bfloat16 [320, 480], replicated, may hold values from -0.25 to 0.25
- block_inverse: bfloat16 [320, 320], replicated, may hold values from -0.3125 to 0.3125
Outputs:
- updated: bfloat16 [2, 4, 320, 8192], P('row', 'inst', None, ('groups', 'space')), parts along dimension 3
There are 2 independent parts, one for each index of `groups`. A program takes and returns all parts, laid end to end along the dimension named above; an argument that names none is the same for every part. Nothing has to cross between parts.
Inputs may be any that keep to these rules, and one draw needn't show every extreme that they name: The element beside e across face f is (e - e % 1024 - 64 + adjacency[s, f, e]) mod 4096 of the same section, never e itself; the relation is mutual (the element beside e across f has e beside it across face f xor 1); faces 0 to 3 stay within e's block of 1024 elements, and faces 4 and 5 leave it only from the first or the last 64 elements of a block. partner[0, n] is a permutation of the 256 interface rows and partner[1, n] its inverse; for every instance, exactly 16 of the rows k with the same k // 64 map to each block of 64 rows.
All inputs are finite; a program needn't handle non-finite values.
Results may differ from a plain program's by a relative error of at most 0.0054.
Values may be sent and summed in bfloat16 or wider, within the bound.
No kernel may reach another device: no remote copies, remote signals or barrier semaphores. Data moves between devices by JAX's collectives and lax.ppermute only.
A program may use at most 64 MiB of HBM per device.

v0:
```python
import jax
import jax.numpy as jnp
from jax import lax
from jax.sharding import PartitionSpec as P

LAYER = 64


OPPOSITE = (1, 0, 3, 2, 5, 4)


def with_halo(block, sides, width):
    for axis, dim in sides:
        count = lax.axis_size(axis)
        forward = [(i, i + 1) for i in range(count - 1)]
        forward.append((count - 1, 0))
        backward = [(target, source) for source, target in forward]
        low = lax.ppermute(
            lax.slice_in_dim(block, block.shape[dim] - width, None, axis=dim), axis, forward
        )
        high = lax.ppermute(lax.slice_in_dim(block, 0, width, axis=dim), axis, backward)
        block = jnp.concatenate([low, block, high], axis=dim)
    return block


def swapped(block, axis, stride):
    count = lax.axis_size(axis)
    route = []
    for low in range(count):
        high = low | 1 << stride
        if high != low and high < count:
            route += [(low, high), (high, low)]
    return lax.ppermute(block, axis, route)


def spectral_table(instances, frequency):
    positions = jnp.arange(instances, dtype=jnp.int32)
    distance = (positions[:, None] - positions[None, :]).astype(jnp.float32)
    parity = 1.0 - 2.0 * jnp.mod(positions[:, None] + positions[None, :], 2).astype(jnp.float32)
    angles = jnp.pi * distance / instances
    sine_values = jnp.where(distance == 0.0, 1.0, jnp.sin(angles))
    cotangent = jnp.where(distance == 0.0, 0.0, jnp.cos(angles) / sine_values)
    return frequency * 0.5 * parity * cotangent


def rank_within(groups, orders):
    same_group = groups[:, None] == groups[None, :]
    before = orders[None, :] < orders[:, None]
    return jnp.sum(jnp.logical_and(same_group, before).astype(jnp.int32), axis=1)


def scatter_rows(row_values, slot_ids, columns_total):

    def place(values_block, pick_index):
        empty = jnp.zeros((values_block.shape[0], columns_total), values_block.dtype)
        return empty.at[:, pick_index].set(values_block)

    return jax.vmap(place)(row_values, slot_ids)


def body(
    solution,
    forcing,
    metric_scale,
    frequency,
    adjacency,
    partner,
    volume_matrix,
    trace_matrix,
    lift_matrix,
    block_inverse,
):
    current = solution[0]
    forcing_local = forcing[0]
    scales = metric_scale[0]
    neighbours = adjacency[0]
    partner_rows = partner[0]
    local_inst = current.shape[0]
    trace_width = trace_matrix.shape[0] // 6
    iface_rows = partner_rows.shape[1]
    shards = lax.axis_size("space")
    section = lax.axis_index("row")
    capacity = iface_rows // shards
    all_inst = local_inst * lax.axis_size("inst")
    own_traces = jnp.einsum(
        "fd,nde->nfe", trace_matrix, current, preferred_element_type=jnp.float32
    ).astype(jnp.bfloat16)
    end_traces = own_traces[:, 4 * trace_width :, :]
    padded_ends = with_halo(end_traces, (("space", 2),), LAYER)
    out_face = 1 - section
    sending = lax.dynamic_slice_in_dim(own_traces, out_face * trace_width, trace_width, 1)[
        :, :, :iface_rows
    ]
    peer_device = partner_rows // iface_rows
    order_local = jnp.arange(iface_rows, dtype=jnp.int32)
    send_rank = jax.vmap(lambda group_ids: rank_within(group_ids, order_local))(peer_device)
    recv_rank = jax.vmap(rank_within)(peer_device, partner_rows)
    outgoing = scatter_rows(sending, peer_device * capacity + send_rank, shards * capacity)
    crossed = lax.all_to_all(outgoing, "space", split_axis=2, concat_axis=2, tiled=True)
    arrived = swapped(crossed, "row", 0)
    where_from = peer_device * capacity + recv_rank
    partner_traces = jax.vmap(
        lambda values_block, pick_index: jnp.take(values_block, pick_index, axis=1)
    )(arrived, where_from)
    blocks = []
    for face_number in range(4):
        facing = OPPOSITE[face_number]
        source_block = own_traces[:, facing * trace_width : (facing + 1) * trace_width, :]
        blocks.append(jnp.take(source_block, neighbours[face_number] - LAYER, axis=2))
    blocks.append(jnp.take(padded_ends[:, trace_width:, :], neighbours[4], axis=2))
    blocks.append(jnp.take(padded_ends[:, :trace_width, :], neighbours[5], axis=2))
    beside = jnp.concatenate(blocks, axis=1)
    beside = lax.dynamic_update_slice(beside, partner_traces, (0, out_face * trace_width, 0))
    coupled = jnp.einsum("df,nfe->nde", lift_matrix, beside, preferred_element_type=jnp.float32)
    volume = jnp.einsum("dk,nke->nde", volume_matrix, current, preferred_element_type=jnp.float32)
    weights_all = spectral_table(all_inst, frequency[0])
    mixed_rows = jnp.einsum(
        "nm,mde->nde",
        weights_all,
        lax.all_to_all(current, "inst", split_axis=2, concat_axis=0, tiled=True).astype(
            jnp.float32
        ),
        precision=lax.Precision.HIGHEST,
    ).astype(jnp.bfloat16)
    source_term = lax.all_to_all(mixed_rows, "inst", split_axis=0, concat_axis=2, tiled=True)
    residual = (
        forcing_local.astype(jnp.float32)
        - scales * (volume + coupled)
        - source_term.astype(jnp.float32)
    ).astype(jnp.bfloat16)
    update = jnp.einsum("dk,nke->nde", block_inverse, residual, preferred_element_type=jnp.float32)
    result = (current.astype(jnp.float32) + update / scales).astype(jnp.bfloat16)
    return result[None]


def solution(mesh):
    in_specs = (
        P("row", "inst", None, ("groups", "space")),
        P("row", "inst", None, ("groups", "space")),
        P("row", ("groups", "space")),
        P(),
        P("row", None, ("groups", "space")),
        P("row", "inst", ("groups", "space")),
        P(),
        P(),
        P(),
        P(),
    )
    out_specs = P("row", "inst", None, ("groups", "space"))
    return jax.shard_map(body, mesh=mesh, in_specs=in_specs, out_specs=out_specs, check_vma=False)
```

profile of v0, /device:TPU:0, one launch (start us, length us, event | category | flops | bytes accessed | tf_op | source)
XLA Modules:
  0.0 139.2 jit_solution(6239436131740232292)
XLA Ops:
  0.0 1.0 copy-done
  1.0 2.5 %convolution_convert_fusion = bf16[2,1024,480]{1,2,0:T(8,128)(2,1)S(1)} fusion(bf16[480,320]{0,1:T(8,128)(2,1)S(1)} %copy-done, bf16[1,2,320,1024]{3,2,1,0:T(8,128)(2,1)} %param.14), kind=kOutput, calls=%fused_computation.16 | convolution fusion | flops 630128640 | bytes 3584000 | tf_op jit(solution)/shard_map/fd,nde->nfe/dot_general | solution.py:85
  3.5 0.8 fusion.70
  4.4 3.0 %collective-permute-start = (bf16[2,160,64]{2,1,0:T(8,128)(2,1)}, bf16[2,160,64]{2,1,0:T(8,128)(2,1)S(1)}, u32[]{:S(2)}, u32[]{:S(2)}) collective-permute-start(bf16[2,160,64]{2,1,0:T(8,128)(2,1)} %get-tuple-element.12), channel_id=1, source_target_pairs={{0,4},{4,8},{8,12},{12,0},{1,5},{5,9},{9,13},{13,1},{2,6},{6,10},{... | collective-permute-start | bytes 122888 | tf_op jit(solution)/shard_map/ppermute | solution.py:18
  7.4 2.0 %collective-permute-start.1 = (bf16[2,160,64]{2,1,0:T(8,128)(2,1)}, bf16[2,160,64]{2,1,0:T(8,128)(2,1)S(1)}, u32[]{:S(2)}, u32[]{:S(2)}) collective-permute-start(bf16[2,160,64]{2,1,0:T(8,128)(2,1)} %get-tuple-element.11), channel_id=1, source_target_pairs={{4,0},{8,4},{12,8},{0,12},{5,1},{9,5},{13,9},{1,13},{6,2},{10,6},{... | collective-permute-start | bytes 122888 | tf_op jit(solution)/shard_map/ppermute | solution.py:21
  9.5 0.1 copy.47
  9.6 0.2 convert_reduce_fusion
  9.9 0.1 reshape.272
  10.0 7.1 %scatter_fusion = bf16[2,80,64]{1,2,0:T(8,128)(2,1)S(1)} fusion(bf16[2,80,64]{1,2,0:T(8,128)(2,1)S(1)} %broadcast_in_dim.50, s32[128]{0:T(128)S(1)} %reshape.272, bf16[128,80]{1,0:T(8,128)(2,1)S(1)} %bitcast.115), kind=kCustom, calls=%fused_computation.7 | custom fusion | bytes 62464 | tf_op jit(solution)/shard_map/vmap()/scatter | solution.py:56
  17.1 0.7 copy.48
  17.7 3.3 %all-to-all-start = ((bf16[2,80,64]{1,0,2:T(2,128)(2,1)}), bf16[2,80,64]{1,0,2:T(2,128)(2,1)S(1)}, u32[]{:S(2)}, u32[]{:S(2)}) async-start(bf16[2,80,64]{1,0,2:T(2,128)(2,1)} %copy.48), calls=%async_computation | async-start | bytes 65536 | tf_op jit(solution)/shard_map/all_to_all | solution.py:99
  21.1 0.9 fusion.71
  22.2 1.3 copy.40
  23.4 1.3 copy.41
  24.7 0.4 copy.43
  25.1 0.4 copy.42
  25.5 3.7 %gather_fusion.1 = bf16[1024,2,80]{2,1,0:T(2,128)(2,1)S(1)} fusion(bf16[2,80,1024]{1,0,2:T(2,128)(2,1)S(1)} %copy.40, s32[1024]{0:T(1024)S(1)} %fusion.20), kind=kCustom, calls=%fused_computation.clone | custom fusion | bytes 659456 | tf_op jit(solution)/shard_map/jit(_take)/gather | solution.py:109
  29.2 3.7 %gather_fusion.2 = bf16[1024,2,80]{2,1,0:T(2,128)(2,1)S(1)} fusion(bf16[2,80,1024]{1,0,2:T(2,128)(2,1)S(1)} %copy.41, s32[1024]{0:T(1024)S(1)} %fusion.21), kind=kCustom, calls=%fused_computation.2.clone | custom fusion | bytes 659456 | tf_op jit(solution)/shard_map/jit(_take)/gather | solution.py:109
  32.9 3.7 %gather_fusion.4 = bf16[1024,2,80]{2,1,0:T(2,128)(2,1)S(1)} fusion(bf16[2,80,1024]{1,0,2:T(2,128)(2,1)S(1)} %copy.43, s32[1024]{0:T(1024)S(1)} %fusion.23), kind=kCustom, calls=%fused_computation.4.clone | custom fusion | bytes 659456 | tf_op jit(solution)/shard_map/jit(_take)/gather | solution.py:109
  36.6 3.7 %gather_fusion.3 = bf16[1024,2,80]{2,1,0:T(2,128)(2,1)S(1)} fusion(bf16[2,80,1024]{1,0,2:T(2,128)(2,1)S(1)} %copy.42, s32[1024]{0:T(1024)S(1)} %fusion.22), kind=kCustom, calls=%fused_computation.3.clone | custom fusion | bytes 659456 | tf_op jit(solution)/shard_map/jit(_take)/gather | solution.py:109
  40.3 5.8 %fusion.8 = (bf16[2,80,1024]{1,0,2:T(2,128)(2,1)}, bf16[2,80,1024]{1,0,2:T(2,128)(2,1)}) fusion(bf16[1024,2,80]{2,1,0:T(2,128)(2,1)S(1)} %gather_fusion.1, pred[1024]{0:T(1024)(128)(4,1)S(1)} %compare_and_fusion.7, bf16[1024,2,80]{2,1,0:T(2,128)(2,1)S(1)} %gather_fusion.2, pred[1024]{0:T(1024)(128)(4,1)S(1)} %compare_and_fusion.6), kind=kLoop, calls=%fused_computation.27 | loop fusion | flops 327680 | bytes 1312768 | tf_op jit(solution)/shard_map/jit(_take)/select_n | solution.py:109
  46.2 5.8 %fusion.10 = (bf16[2,80,1024]{1,0,2:T(2,128)(2,1)}, bf16[2,80,1024]{1,0,2:T(2,128)(2,1)}) fusion(bf16[1024,2,80]{2,1,0:T(2,128)(2,1)S(1)} %gather_fusion.3, pred[1024]{0:T(1024)(128)(4,1)S(1)} %compare_and_fusion.5, bf16[1024,2,80]{2,1,0:T(2,128)(2,1)S(1)} %gather_fusion.4, pred[1024]{0:T(1024)(128)(4,1)S(1)} %compare_and_fusion.4), kind=kLoop, calls=%fused_computation.29 | loop fusion | flops 327680 | bytes 1312768 | tf_op jit(solution)/shard_map/jit(_take)/select_n | solution.py:109
  52.0 3.0 %copy.52 = bf16[2,320,1024]{1,0,2:T(2,128)(2,1)} copy(bf16[2,320,1024]{2,1,0:T(8,128)(2,1)S(1)} %bitcast.114) | data formatting | bytes 2621440 | tf_op jit(solution)/shard_map/squeeze | solution.py:73
  55.0 3.7 %all-to-all-start.1 = ((bf16[2,320,1024]{1,0,2:T(2,128)(2,1)}), bf16[2,320,1024]{1,0,2:T(2,128)(2,1)S(1)}, u32[]{:S(2)}, u32[]{:S(2)}) async-start(bf16[2,320,1024]{1,0,2:T(2,128)(2,1)} %copy.52), calls=%async_computation.1 | async-start | bytes 3145728 | tf_op jit(solution)/shard_map/all_to_all | solution.py:120
  58.7 1.1 slice.93
  59.9 0.1 reshape.266
  59.9 0.1 copy.46
  60.7 0.6 copy.49
  61.3 0.8 concatenate.6
  62.1 0.1 fusion.72
  62.2 0.7 copy.44
  62.9 1.3 copy.45
  64.2 7.2 %gather_fusion.5 = bf16[1024,2,80]{2,1,0:T(2,128)(2,1)} fusion(bf16[2,80,1152]{1,0,2:T(2,128)(2,1)S(1)} %copy.44, s32[1024]{0:T(1024)S(1)} %fusion.24), kind=kCustom, calls=%fused_computation.1.clone | custom fusion | bytes 659456 | tf_op jit(solution)/shard_map/jit(_take)/gather | solution.py:110
  71.3 8.2 %gather_fusion.6 = bf16[1024,2,80]{2,1,0:T(2,128)(2,1)} fusion(bf16[2,80,1152]{1,0,2:T(2,128)(2,1)} %copy.45, s32[1024]{0:T(1024)S(1)} %fusion.25), kind=kCustom, calls=%fused_computation.5.clone | custom fusion | bytes 659456 | tf_op jit(solution)/shard_map/jit(_take)/gather | solution.py:111
  79.6 2.5 %copy.53 = bf16[2,320,2,512]{3,0,2,1:T(2,128)(2,1)S(1)} copy(bf16[2,320,2,512]{1,0,3,2:T(2,128)(2,1)S(1)} %bitcast.109) | data formatting | bytes 2621440 | tf_op jit(solution)/shard_map/all_to_all | solution.py:120
  82.1 0.5 all_to_all.27
  82.6 2.3 %convolution_convert_fusion.1 = bf16[4,320,512]{2,0,1:T(4,128)(2,1)S(1)} fusion(bf16[4,320,512]{2,0,1:T(4,128)(2,1)S(1)} %all_to_all.27, f32[]{:T(128)} %bitcast.29), kind=kOutput, calls=%fused_computation.17 | convolution fusion | flops 32113024 | bytes 2621444 | tf_op jit(solution)/shard_map/nm,mde->nde/dot_general | solution.py:117
  84.9 1.3 copy.54
  86.2 4.8 %all-to-all-start.2 = ((bf16[4,320,512]{2,1,0:T(8,128)(2,1)}), bf16[4,320,512]{2,1,0:T(8,128)(2,1)}, u32[]{:S(2)}, u32[]{:S(2)}) async-start(bf16[4,320,512]{2,1,0:T(8,128)(2,1)} %copy.54), calls=%async_computation.2 | async-start | bytes 2621440 | tf_op jit(solution)/shard_map/all_to_all | solution.py:125
  91.1 5.9 %fusion.12 = (bf16[2,80,1024]{1,0,2:T(2,128)(2,1)}, bf16[2,80,1024]{1,0,2:T(2,128)(2,1)}) fusion(bf16[1024,2,80]{2,1,0:T(2,128)(2,1)S(1)} %copy-done.4, pred[1024]{0:T(1024)(128)(4,1)S(1)} %compare_and_fusion.3, bf16[1024,2,80]{2,1,0:T(2,128)(2,1)S(1)} %copy-done.5, pred[1024]{0:T(1024)(128)(4,1)S(1)} %compare_and_fusion.2), kind=kLoop, calls=%fused_computation.31 | loop fusion | flops 327680 | bytes 1312768 | tf_op jit(solution)/shard_map/jit(_take)/select_n | solution.py:110
  97.0 15.5 %concatenate.7 = bf16[2,480,1024]{1,0,2:T(2,128)(2,1)S(1)} concatenate(bf16[2,80,1024]{1,0,2:T(2,128)(2,1)S(1)} %copy-done.2, bf16[2,80,1024]{1,0,2:T(2,128)(2,1)S(1)} %copy-done.3, bf16[2,80,1024]{1,0,2:T(2,128)(2,1)} %get-tuple-element.27, bf16[2,80,1024]{1,0,2:T(2,128)(2,1)} %get-tuple-element.28, bf16[2,80,1024]{1,0,2:T(2,128)(2,1)} %get-tuple-element.29, ...), dimensions={1} | concatenate | bytes 3932160 | tf_op jit(solution)/shard_map/concatenate | solution.py:112
  112.5 1.1 gather_fusion
  113.6 0.1 fusion.19
  113.8 9.7 %dynamic_update_slice.3 = bf16[2,480,1024]{1,0,2:T(2,128)(2,1)S(1)} dynamic-update-slice(bf16[2,480,1024]{1,0,2:T(2,128)(2,1)S(1)} %concatenate.7, bf16[2,80,64]{1,0,2:T(2,128)(2,1)S(1)} %fusion.19, s32[]{:T(128)} %constant.54.clone.1, s32[]{:T(128)S(6)} %select_n.92, s32[]{:T(128)} %constant.54.clone.1) | dynamic-update-slice | bytes 40964 | tf_op jit(solution)/shard_map/dynamic_update_slice | solution.py:113
  123.4 3.4 %fusion.3 = f32[2,1024,320]{1,2,0:T(8,128)} fusion(bf16[2,480,1024]{1,0,2:T(2,128)(2,1)S(1)} %dynamic_update_slice.3, bf16[320,480]{1,0:T(8,128)(2,1)} %param.22), kind=kOutput, calls=%fused_computation.14 | convolution fusion | flops 629145600 | bytes 4894720 | tf_op jit(solution)/shard_map/df,nfe->nde/dot_general | solution.py:114
  126.8 2.7 %copy.60 = f32[2,2,320,512]{3,0,2,1:T(2,128)S(1)} copy(bf16[2,2,320,512]{3,2,1,0:T(8,128)(2,1)} %bitcast.39) | data formatting | bytes 3932160 | tf_op jit(solution)/shard_map/convert_element_type | solution.py:129
  129.5 3.3 %reshape.216 = f32[2,320,1024]{2,1,0:T(8,128)} reshape(f32[2,320,2,512]{3,2,1,0:T(2,128)S(1)} %bitcast.108) | data formatting | bytes 5242880 | tf_op jit(solution)/shard_map/convert_element_type | solution.py:129
  132.9 6.3 %fusion.5 = bf16[1,2,320,1024]{3,2,1,0:T(8,128)(2,1)} fusion(f32[2,320,1024]{2,1,0:T(8,128)} %reshape.216, f32[2,1024,320]{1,2,0:T(8,128)} %fusion.3, bf16[1,2,320,1024]{3,2,1,0:T(8,128)(2,1)} %param.15, f32[1024]{0:T(1024)S(1)} %bitcast.130, bf16[320,320]{1,0:T(8,128)(2,1)S(1)} %copy-done.9, bf16[320,320]{1,0:T(8,128)(2,1)S(1)} %copy-done.10, ...), kind=kOutput, calls=%fused_computation.18 | convolution fusion | flops 845414400 | bytes 9588736 | tf_op jit(solution)/shard_map/dk,nke->nde/dot_general | solution.py:131
  (51 shorter events, 0.3 us)
Async XLA Ops:
  0.0 1.0 copy-start
  0.0 9.6 %copy-start.7 = (s32[1,2,64]{2,1,0:T(2,128)S(1)}, s32[1,2,64]{2,1,0:T(2,128)}, u32[]{:S(2)}) copy-start(s32[1,2,64]{2,1,0:T(2,128)} %param.19) | copy-start | bytes 1540
  3.5 18.5 %copy-start.1 = (bf16[2,1024,480]{1,2,0:T(8,128)(2,1)}, bf16[2,1024,480]{1,2,0:T(8,128)(2,1)S(1)}, u32[]{:S(2)}) copy-start(bf16[2,1024,480]{1,2,0:T(8,128)(2,1)S(1)} %convolution_convert_fusion) | copy-start | bytes 5898244
  3.5 17.5 %copy-start.8 = (s32[1,6,1024]{2,0,1:T(1,128)S(1)}, s32[1,6,1024]{2,0,1:T(1,128)}, u32[]{:S(2)}) copy-start(s32[1,6,1024]{2,0,1:T(1,128)} %param.18) | copy-start | bytes 73732
  4.4 56.9 %collective-permute-start = (bf16[2,160,64]{2,1,0:T(8,128)(2,1)}, bf16[2,160,64]{2,1,0:T(8,128)(2,1)S(1)}, u32[]{:S(2)}, u32[]{:S(2)}) collective-permute-start(bf16[2,160,64]{2,1,0:T(8,128)(2,1)} %get-tuple-element.12), channel_id=1, source_target_pairs={{0,4},{4,8},{8,12},{12,0},{1,5},{5,9},{9,13},{13,1},{2,6},{6,10},{... | collective-permute-start | bytes 122888 | tf_op jit(solution)/shard_map/ppermute | solution.py:18
  7.4 53.9 %collective-permute-start.1 = (bf16[2,160,64]{2,1,0:T(8,128)(2,1)}, bf16[2,160,64]{2,1,0:T(8,128)(2,1)S(1)}, u32[]{:S(2)}, u32[]{:S(2)}) collective-permute-start(bf16[2,160,64]{2,1,0:T(8,128)(2,1)} %get-tuple-element.11), channel_id=1, source_target_pairs={{4,0},{8,4},{12,8},{0,12},{5,1},{9,5},{13,9},{1,13},{6,2},{10,6},{... | collective-permute-start | bytes 122888 | tf_op jit(solution)/shard_map/ppermute | solution.py:21
  17.7 37.3 %all-to-all-start = ((bf16[2,80,64]{1,0,2:T(2,128)(2,1)}), bf16[2,80,64]{1,0,2:T(2,128)(2,1)S(1)}, u32[]{:S(2)}, u32[]{:S(2)}) async-start(bf16[2,80,64]{1,0,2:T(2,128)(2,1)} %copy.48), calls=%async_computation | async-start | bytes 65536 | tf_op jit(solution)/shard_map/all_to_all | solution.py:99
  46.2 5.9 %copy-start.6 = (bf16[1,2,320,1024]{3,2,1,0:T(8,128)(2,1)S(1)}, bf16[1,2,320,1024]{3,2,1,0:T(8,128)(2,1)}, u32[]{:S(2)}) copy-start(bf16[1,2,320,1024]{3,2,1,0:T(8,128)(2,1)} %param.14) | copy-start | bytes 3932164
  55.0 24.5 %all-to-all-start.1 = ((bf16[2,320,1024]{1,0,2:T(2,128)(2,1)}), bf16[2,320,1024]{1,0,2:T(2,128)(2,1)S(1)}, u32[]{:S(2)}, u32[]{:S(2)}) async-start(bf16[2,320,1024]{1,0,2:T(2,128)(2,1)} %copy.52), calls=%async_computation.1 | async-start | bytes 3145728 | tf_op jit(solution)/shard_map/all_to_all | solution.py:120
  61.3 51.1 %collective-permute-start.2 = (bf16[2,80,64]{1,2,0:T(8,128)(2,1)}, bf16[2,80,64]{1,2,0:T(8,128)(2,1)S(1)}, u32[]{:S(2)}, u32[]{:S(2)}) collective-permute-start(bf16[2,80,64]{1,2,0:T(8,128)(2,1)} %copy.49), channel_id=1, source_target_pairs={{0,1},{1,0},{2,3},{3,2},{4,5},{5,4},{6,7},{7,6},{8,9},{9,8},{10,11... | collective-permute-start | bytes 61448 | tf_op jit(solution)/shard_map/ppermute | solution.py:33
  86.2 4.9 %copy-start.4 = (bf16[1024,2,80]{2,1,0:T(2,128)(2,1)S(1)}, bf16[1024,2,80]{2,1,0:T(2,128)(2,1)}, u32[]{:S(2)}) copy-start(bf16[1024,2,80]{2,1,0:T(2,128)(2,1)} %gather_fusion.5) | copy-start | bytes 983044
  86.2 4.9 %copy-start.5 = (bf16[1024,2,80]{2,1,0:T(2,128)(2,1)S(1)}, bf16[1024,2,80]{2,1,0:T(2,128)(2,1)}, u32[]{:S(2)}) copy-start(bf16[1024,2,80]{2,1,0:T(2,128)(2,1)} %gather_fusion.6) | copy-start | bytes 983044
  86.2 10.7 %copy-start.2 = (bf16[2,80,1024]{1,0,2:T(2,128)(2,1)S(1)}, bf16[2,80,1024]{1,0,2:T(2,128)(2,1)}, u32[]{:S(2)}) copy-start(bf16[2,80,1024]{1,0,2:T(2,128)(2,1)} %get-tuple-element.25) | copy-start | bytes 983044
  86.2 10.7 %copy-start.3 = (bf16[2,80,1024]{1,0,2:T(2,128)(2,1)S(1)}, bf16[2,80,1024]{1,0,2:T(2,128)(2,1)}, u32[]{:S(2)}) copy-start(bf16[2,80,1024]{1,0,2:T(2,128)(2,1)} %get-tuple-element.26) | copy-start | bytes 983044
  86.2 40.6 %all-to-all-start.2 = ((bf16[4,320,512]{2,1,0:T(8,128)(2,1)}), bf16[4,320,512]{2,1,0:T(8,128)(2,1)}, u32[]{:S(2)}, u32[]{:S(2)}) async-start(bf16[4,320,512]{2,1,0:T(8,128)(2,1)} %copy.54), calls=%async_computation.2 | async-start | bytes 2621440 | tf_op jit(solution)/shard_map/all_to_all | solution.py:125
  129.5 3.4 %copy-start.9 = (bf16[320,320]{1,0:T(8,128)(2,1)S(1)}, bf16[320,320]{1,0:T(8,128)(2,1)}, u32[]{:S(2)}) copy-start(bf16[320,320]{1,0:T(8,128)(2,1)} %param.23) | copy-start | bytes 614404
  129.5 3.4 %copy-start.10 = (bf16[320,320]{1,0:T(8,128)(2,1)S(1)}, bf16[320,320]{1,0:T(8,128)(2,1)}, u32[]{:S(2)}) copy-start(bf16[320,320]{1,0:T(8,128)(2,1)} %param.20) | copy-start | bytes 614404
  129.5 3.4 %copy-start.11 = (f32[1,1024]{1,0:T(1,128)S(1)}, f32[1,1024]{1,0:T(1,128)}, u32[]{:S(2)}) copy-start(f32[1,1024]{1,0:T(1,128)} %param.16) | copy-start | bytes 12292
where the time goes:
time: 141 us; the launch traced here: 139 us
  local copies, waits for them, and re-layouts  88.6 us (63%)
  other arithmetic  18.1 us (13%)
  starting transfers between devices  16.8 us (12%)
  matrix products  14.6 us (10%)
    concatenate x1, local copies, waits for them, and re-layouts, body(): beside = jnp.concatenate(blocks, axis=1)  15.5 us
    gather x4, local copies, waits for them, and re-layouts, body(): jnp.take(source_block, neighbours[face_number] - LAYER, axis=2)  14.7 us
    select_n x2, other arithmetic, body(): jnp.take(source_block, neighbours[face_number] - LAYER, axis=2)  11.7 us
    dynamic_update_slice x1, local copies, waits for them, and re-layouts, body(): lax.dynamic_update_slice(beside, partner_traces, (0, out_face * trace_wid...  9.67 us
    gather x1, local copies, waits for them, and re-layouts, body(): jnp.take(padded_ends[:, :trace_width, :], neighbours[5], axis=2)  8.22 us
    scatter x3, local copies, waits for them, and re-layouts, place(): return empty.at[:, pick_index].set(values_block)  7.81 us
    gather x1, local copies, waits for them, and re-layouts, body(): jnp.take(padded_ends[:, trace_width:, :], neighbours[4], axis=2)  7.18 us
    dot_general x1, matrix products, body(): jnp.einsum('dk,nke->nde', block_inverse, residual, preferred_element_type...  6.35 us
  transfers between devices with their start and end apart: 6, of which 0 were waited for; matrix products, arithmetic and copies ran while one was open for 75% of the time, Pallas kernels for 0%

commit v1 on v0

v1 whole, which is shorter than its diff:
```python
import functools

import jax
import jax.numpy as jnp
import numpy as np
from jax import lax
from jax.experimental import pallas as pl
from jax.experimental.pallas import tpu as pltpu
from jax.sharding import PartitionSpec as P

LAYER = 64
OPPOSITE = (1, 0, 3, 2, 5, 4)
LANES = 128
VMEM_LIMIT = 40 * 1024 * 1024


def spectral_table(instances):
    positions = np.arange(instances)
    distance = positions[:, None] - positions[None, :]
    parity = np.where(distance % 2 == 0, 1.0, -1.0)
    angles = np.pi * distance / instances
    sines = np.where(distance == 0, 1.0, np.sin(angles))
    cotangent = np.where(distance == 0, 0.0, np.cos(angles) / sines)
    return (0.5 * parity * cotangent).astype(np.float32)


def one_hot(picked, rows):
    numbers = lax.broadcasted_iota(jnp.int32, (rows, picked.shape[1]), 0)
    return jnp.where(numbers == picked, 1.0, 0.0).astype(jnp.bfloat16)


def dot(left, right):
    return jnp.dot(left, right, preferred_element_type=jnp.float32)


def ends_kernel(place_ref, first_ref, last_ref, trace_ref, up_ref, down_ref, cross_ref):
    width = trace_ref.shape[0] // 6
    section = place_ref[0]
    for n in range(first_ref.shape[0]):
        first = dot(trace_ref[...], first_ref[n]).astype(jnp.bfloat16)
        last = dot(trace_ref[4 * width :, :], last_ref[n]).astype(jnp.bfloat16)
        down_ref[n] = first[4 * width :, :LAYER]
        up_ref[n] = last[:, last.shape[1] - LAYER :]
        rows = cross_ref.shape[2]
        cross_ref[n] = jnp.where(section == 0, first[width : 2 * width, :rows], first[:width, :rows])


def couple_kernel(shards, place_ref, freq_ref, table_ref, adj_ref, partner_ref, all_ref, tile_ref, forcing_ref,
                  scale_ref, trace_ref, lift_ref, volume_ref, low_ref, high_ref, *rest):
    pieces, (out_ref, traces) = rest[:shards], rest[shards:]
    step = pl.program_id(0)
    steps = pl.num_programs(0)
    count, dof, total = all_ref.shape
    width = trace_ref.shape[0] // 6
    tile = tile_ref.shape[2]
    section, inst, space = place_ref[0], place_ref[1], place_ref[2]

    @pl.when(step == 0)
    def _():
        for n in range(count):
            for c in range(total // tile):
                cols = slice(c * tile, (c + 1) * tile)
                made = dot(trace_ref[...], all_ref[n, :, cols]).astype(jnp.bfloat16)
                for f in range(6):
                    traces[f, n * width : (n + 1) * width, cols] = made[f * width : (f + 1) * width]

    column = lax.broadcasted_iota(jnp.int32, (1, tile), 1)
    at_edge = jnp.logical_or(step == 0, step == steps - 1)

    def gathered(edge):
        found = []
        for f in range(6):
            adj = adj_ref[f : f + 1, :]
            values = dot(traces[OPPOSITE[f]], one_hot(adj - LAYER, total))
            if edge and f >= 4:
                part = slice((5 - f) * width, (6 - f) * width)
                below = jnp.concatenate([low_ref[n, part, :] for n in range(count)], axis=0)
                above = jnp.concatenate([high_ref[n, part, :] for n in range(count)], axis=0)
                values += dot(below, one_hot(adj, LAYER))
                values += dot(above, one_hot(adj - (LAYER + total), LAYER))
            values = values.astype(jnp.bfloat16)
            if edge and f < 2:
                rows = partner_ref.shape[1]
                use = jnp.logical_and(step == 0, section == 1 - f)
                crossed = []
                for n in range(count):
                    wanted = partner_ref[n : n + 1, :]
                    arrived = jnp.zeros((width, rows), jnp.float32)
                    for d in range(shards):
                        source = lax.rem(space - d + shards, shards)
                        arrived += dot(pieces[d][n], one_hot(wanted - source * rows, rows))
                    crossed.append(arrived)
                crossed = jnp.concatenate(crossed, axis=0).astype(jnp.bfloat16)
                crossed = jnp.concatenate(
                    [crossed, jnp.zeros((count * width, tile - rows), jnp.bfloat16)], axis=1)
                take = jnp.logical_and(column < rows, use)
                values = jnp.where(take, crossed, values)
            found.append(values)
        return found

    def finish(edge):
        found = gathered(edge)
        frequency = freq_ref[0]
        scale = scale_ref[...]
        for n in range(count):
            beside = jnp.concatenate([v[n * width : (n + 1) * width] for v in found], axis=0)
            inner = dot(lift_ref[...], beside) + dot(volume_ref[...], tile_ref[n])
            value = forcing_ref[n].astype(jnp.float32) - scale * inner
            for m in range(count):
                weight = table_ref[inst * count + n, inst * count + m] * frequency
                value -= weight * tile_ref[m].astype(jnp.float32)
            out_ref[n] = value

    @pl.when(at_edge)
    def _():
        finish(True)

    @pl.when(jnp.logical_not(at_edge))
    def _():
        finish(False)


def update_kernel(peers, place_ref, freq_ref, table_ref, partial_ref, current_ref, scale_ref, inverse_ref, *rest):
    others, out_ref = rest[: peers - 1], rest[peers - 1]
    count = current_ref.shape[0]
    inst = place_ref[1]
    frequency = freq_ref[0]
    inverse_scale = 1.0 / scale_ref[...]
    for n in range(count):
        value = partial_ref[n]
        for d in range(1, peers):
            owner = lax.rem(inst - d + peers, peers)
            for m in range(count):
                weight = table_ref[inst * count + n, owner * count + m] * frequency
                value -= weight * others[d - 1][m].astype(jnp.float32)
        update = dot(inverse_ref[...], value.astype(jnp.bfloat16))
        out_ref[n] = (current_ref[n].astype(jnp.float32) + update * inverse_scale).astype(jnp.bfloat16)


def whole(array):
    return pl.BlockSpec(array.shape, lambda j: (0,) * array.ndim)


def body(solution, forcing, metric_scale, frequency, adjacency, partner, volume_matrix, trace_matrix, lift_matrix,
         block_inverse):
    current = solution[0]
    forcing_local = forcing[0]
    neighbours = adjacency[0]
    partner_rows = partner[0]
    count, dof, total = current.shape
    width = trace_matrix.shape[0] // 6
    iface_rows = partner_rows.shape[1]
    shards = lax.axis_size("space")
    peers = lax.axis_size("inst")
    section = lax.axis_index("row")
    place = jnp.stack([section, lax.axis_index("inst"), lax.axis_index("space")]).astype(jnp.int32)
    table = jnp.asarray(spectral_table(count * peers))
    smem = pl.BlockSpec(memory_space=pltpu.SMEM)
    bf16 = jnp.bfloat16

    with jax.named_scope("instances"):
        others = [lax.ppermute(current, "inst", [(i, (i + d) % peers) for i in range(peers)])
                  for d in range(1, peers)]

    with jax.named_scope("ends"):
        up, down, cross = pl.pallas_call(
            ends_kernel,
            grid=(1,),
            out_shape=(jax.ShapeDtypeStruct((count, 2 * width, LAYER), bf16),
                       jax.ShapeDtypeStruct((count, 2 * width, LAYER), bf16),
                       jax.ShapeDtypeStruct((count, width, iface_rows), bf16)),
            in_specs=[smem,
                      pl.BlockSpec((count, dof, LANES), lambda j: (0, 0, 0)),
                      pl.BlockSpec((count, dof, LANES), lambda j: (0, 0, total // LANES - 1)),
                      whole(trace_matrix)],
            out_specs=(pl.BlockSpec((count, 2 * width, LAYER), lambda j: (0, 0, 0)),
                       pl.BlockSpec((count, 2 * width, LAYER), lambda j: (0, 0, 0)),
                       pl.BlockSpec((count, width, iface_rows), lambda j: (0, 0, 0))),
            compiler_params=pltpu.CompilerParams(vmem_limit_bytes=VMEM_LIMIT),
            cost_estimate=pl.CostEstimate(flops=8 * width * dof * LANES * 2 * count,
                                          bytes_accessed=1_000_000, transcendentals=0),
            name="ends",
        )(place, current, current, trace_matrix)

    with jax.named_scope("halo"):
        low = lax.ppermute(up, "space", [(i, (i + 1) % shards) for i in range(shards)])
        high = lax.ppermute(down, "space", [(i, (i - 1) % shards) for i in range(shards)])
    with jax.named_scope("interface"):
        pieces = [lax.ppermute(cross, ("space", "row"),
                               [(i * 2 + r, (i + d) % shards * 2 + 1 - r) for i in range(shards) for r in range(2)])
                  for d in range(shards)]

    tile = 256
    steps = total // tile
    by_tile = lambda *lead: pl.BlockSpec(lead + (tile,), lambda j: (0,) * len(lead) + (j,))
    with jax.named_scope("couple"):
        partial = pl.pallas_call(
            functools.partial(couple_kernel, shards),
            grid=(steps,),
            out_shape=jax.ShapeDtypeStruct((count, dof, total), jnp.float32),
            in_specs=[smem, smem, smem, by_tile(6), whole(partner_rows), whole(current), by_tile(count, dof),
                      by_tile(count, dof), by_tile(1), whole(trace_matrix), whole(lift_matrix),
                      whole(volume_matrix), whole(low), whole(high)] + [whole(p) for p in pieces],
            out_specs=by_tile(count, dof),
            scratch_shapes=[pltpu.VMEM((6, count * width, total), bf16)],
            compiler_params=pltpu.CompilerParams(vmem_limit_bytes=VMEM_LIMIT),
            cost_estimate=pl.CostEstimate(
                flops=2 * count * total * (6 * width * dof * 2 + dof * dof + 6 * width * total),
                bytes_accessed=count * dof * total * 10, transcendentals=0),
            name="couple",
        )(place, frequency, table, neighbours, partner_rows, current, current, forcing_local, metric_scale,
          trace_matrix, lift_matrix, volume_matrix, low, high, *pieces)

    with jax.named_scope("update"):
        result = pl.pallas_call(
            functools.partial(update_kernel, peers),
            grid=(steps,),
            out_shape=jax.ShapeDtypeStruct((count, dof, total), bf16),
            in_specs=[smem, smem, smem, by_tile(count, dof), by_tile(count, dof), by_tile(1), whole(block_inverse)]
            + [by_tile(count, dof)] * (peers - 1),
            out_specs=by_tile(count, dof),
            compiler_params=pltpu.CompilerParams(vmem_limit_bytes=VMEM_LIMIT),
            cost_estimate=pl.CostEstimate(flops=2 * count * total * dof * dof,
                                          bytes_accessed=count * dof * total * 10, transcendentals=0),
            name="update",
        )(place, frequency, table, partial, current, metric_scale, block_inverse, *others)
    return result[None]


def solution(mesh):
    in_specs = (
        P("row", "inst", None, ("groups", "space")),
        P("row", "inst", None, ("groups", "space")),
        P("row", ("groups", "space")),
        P(),
        P("row", None, ("groups", "space")),
        P("row", "inst", ("groups", "space")),
        P(),
        P(),
        P(),
        P(),
    )
    out_specs = P("row", "inst", None, ("groups", "space"))
    return jax.shard_map(body, mesh=mesh, in_specs=in_specs, out_specs=out_specs, check_vma=False)
```

time: 141 us -> 35.7 us (0.25); the launches traced: 139 us -> 35.5 us
  local copies, waits for them, and re-layouts: 88.6 us -> 2.58 us
  other arithmetic: 18.1 us -> 0.08 us
  matrix products: 14.6 us -> 0 us
  Pallas kernels: 0 us -> 12 us
  waiting for transfers between devices: 0.02 us -> 7.74 us
  starting transfers between devices: 16.8 us -> 12.4 us
    gather x8 -> x0, local copies, waits for them, and re-layouts: 31.3 us -> none  [the longest x4 14.7 us: body(): jnp.take(source_block, neighbours[face_number] - LAYER, axis=2)]
    select_n x5 -> x0, other arithmetic: 17.7 us -> none  [the longest x2 11.7 us: body(): jnp.take(source_block, neighbours[face_number] - LAYER, axis=2)]
    concatenate x2 -> x0, local copies, waits for them, and re-layouts: 16.3 us -> none  [the longest x1 15.5 us: body(): beside = jnp.concatenate(blocks, axis=1)]
    dot_general x4 -> x0, matrix products: 14.6 us -> none  [the longest x1 6.35 us: body(): jnp.einsum('dk,nke->nde', block_inverse, residual, preferred_element_type...]
    pallas_call x0 -> x3, Pallas kernels: none -> 12 us  [the longest x1 7.34 us: body(): pl.pallas_call(functools.partial(couple_kernel, shards), grid=(steps,), o...]
    all_to_all x3 -> x0, starting transfers between devices: 11.8 us -> none  [the longest x1 4.83 us: body(): lax.all_to_all(mixed_rows, 'inst', split_axis=0, concat_axis=2, tiled=True)]
    dynamic_update_slice x1 -> x0, local copies, waits for them, and re-layouts: 9.67 us -> none  [body(): lax.dynamic_update_slice(beside, partner_traces, (0, out_face * trace_wid...]
    slice x12 -> x0, local copies, waits for them, and re-layouts: 8.43 us -> none  [the longest x5 4.31 us: body(): own_traces[:, facing * trace_width:(facing + 1) * trace_width, :]]
  transfers between devices with their start and end apart: 6 -> 7, of which waited for: 0 -> 3; matrix products, arithmetic and copies ran while one was open for 75% -> 4% of each run, Pallas kernels for 0% -> 24%
where the time goes in v1:
time: 35.7 us; the launch traced here: 35.5 us
  starting transfers between devices  12.4 us (35%)
  Pallas kernels  12 us (34%)
  waiting for transfers between devices  7.74 us (22%)
  local copies, waits for them, and re-layouts  2.58 us (7%)
  between operations  0.79 us (2%)
    pallas_call x1, Pallas kernels, body(): pl.pallas_call(functools.partial(couple_kernel, shards), grid=(steps,), o...  7.34 us
    ppermute x4, starting transfers between devices, body(): lax.ppermute(cross, ('space', 'row'), [(i * 2 + r, (i + d) % shards * 2 +...  5.62 us
    ppermute x1, waiting for transfers between devices, body(): lax.ppermute(current, 'inst', [(i, (i + d) % peers) for i in range(peers)])  5.56 us
    pallas_call x1, Pallas kernels, body(): pl.pallas_call(functools.partial(update_kernel, peers), grid=(steps,), ou...  3.6 us
    ppermute x1, starting transfers between devices, body(): lax.ppermute(current, 'inst', [(i, (i + d) % peers) for i in range(peers)])  2.94 us
    unnamed x20, local copies, waits for them, and re-layouts  2.58 us
    ppermute x1, starting transfers between devices, body(): lax.ppermute(down, 'space', [(i, (i - 1) % shards) for i in range(shards)])  2.26 us
    ppermute x4, waiting for transfers between devices, body(): lax.ppermute(cross, ('space', 'row'), [(i * 2 + r, (i + d) % shards * 2 +...  2.17 us
  transfers between devices with their start and end apart: 7, of which 3 were waited for; matrix products, arithmetic and copies ran while one was open for 4% of the time, Pallas kernels for 24%

profile of v1, /device:TPU:0, one launch (start us, length us, event | category | flops | bytes accessed | tf_op | source)
XLA Modules:
  0.0 35.5 jit_solution(14378925272605240037)
XLA Ops:
  0.0 2.9 %collective-permute-start.6 = (bf16[2,320,1024]{2,1,0:T(8,128)(2,1)}, bf16[2,320,1024]{2,1,0:T(8,128)(2,1)S(1)}, u32[]{:S(2)}, u32[]{:S(2)}) collective-permute-start(bf16[2,320,1024]{2,1,0:T(8,128)(2,1)} %bitcast.10), channel_id=1, source_target_pairs={{0,2},{2,0},{1,3},{3,1},{4,6},{6,4},{5,7},{7,5},{8,10},{10,8},{9,1... | collective-permute-start | bytes 3932168 | tf_op jit(solution)/shard_map/instances/ppermute | solution.py:162
  2.9 1.2 %copy.13.trace_ref = bf16[480,320]{1,0:T(8,128)(2,1)S(1)} copy(bf16[480,320]{0,1:T(8,128)(2,1)} %param.18) | data formatting | bytes 614400 | tf_op args[7]
  4.2 0.1 pad_add_fusion.place_ref
  4.2 0.0 copy-start
  4.2 1.3 %copy-done = bf16[1,2,320,1024]{3,2,1,0:T(8,128)(2,1)S(1)} copy-done((bf16[1,2,320,1024]{3,2,1,0:T(8,128)(2,1)S(1)}, bf16[1,2,320,1024]{3,2,1,0:T(8,128)(2,1)}, u32[]{:S(2)}) %copy-start) | copy-done | bytes 1310744
  5.6 0.0 copy-start.8
  5.6 0.0 copy-start.2
  5.6 0.0 copy-start.3
  5.6 0.0 copy-start.4
  5.6 0.0 copy-start.5
  5.6 0.0 copy-start.6
  5.6 0.0 copy-start.7
  5.6 1.0 %ends.1 = (bf16[2,160,64]{2,1,0:T(8,128)(2,1)S(1)}, bf16[2,160,64]{2,1,0:T(8,128)(2,1)S(1)}, bf16[2,80,64]{2,1,0:T(8,128)(2,1)S(1)}) custom-call(s32[3]{0:T(128)S(1)} %pad_add_fusion.place_ref, bf16[2,320,1024]{2,1,0:T(8,128)(2,1)S(1)} %bitcast.11, bf16[2,320,1024]{2,1,0:T(8,128)(2,1)S(1)} %bitcast.12, bf16[480,320]{1,0:T(8,128)(2,1)S(1)} %copy.13.trace_ref), custom_call_target="tpu_custom_call" | custom-call | flops 104857600 | bytes 1000000 | tf_op jit(solution)/shard_map/ends/ends/pallas_call | solution.py:166
  6.6 2.8 %collective-permute-start.5 = (bf16[2,80,64]{2,1,0:T(8,128)(2,1)S(1)}, bf16[2,80,64]{2,1,0:T(8,128)(2,1)S(1)}, u32[]{:S(2)}, u32[]{:S(2)}) collective-permute-start(bf16[2,80,64]{2,1,0:T(8,128)(2,1)S(1)} %get-tuple-element.10), channel_id=1, source_target_pairs={{0,13},{1,12},{4,1},{5,0},{8,5},{9,4},{12,9},{13,8},{2,15},{3,14},... | collective-permute-start | bytes 61448 | tf_op jit(solution)/shard_map/interface/ppermute | solution.py:189
  9.4 0.0 collective-permute-start.4
  9.4 1.6 %collective-permute-start = (bf16[2,160,64]{2,1,0:T(8,128)(2,1)S(1)}, bf16[2,160,64]{2,1,0:T(8,128)(2,1)S(1)}, u32[]{:S(2)}, u32[]{:S(2)}) collective-permute-start(bf16[2,160,64]{2,1,0:T(8,128)(2,1)S(1)} %get-tuple-element.8), channel_id=1, source_target_pairs={{0,4},{4,8},{8,12},{12,0},{1,5},{5,9},{9,13},{13,1},{2,6},{6,10},{... | collective-permute-start | bytes 122888 | tf_op jit(solution)/shard_map/halo/ppermute | solution.py:186
  11.0 2.3 %collective-permute-start.1 = (bf16[2,160,64]{2,1,0:T(8,128)(2,1)S(1)}, bf16[2,160,64]{2,1,0:T(8,128)(2,1)S(1)}, u32[]{:S(2)}, u32[]{:S(2)}) collective-permute-start(bf16[2,160,64]{2,1,0:T(8,128)(2,1)S(1)} %get-tuple-element.9), channel_id=1, source_target_pairs={{0,12},{4,0},{8,4},{12,8},{1,13},{5,1},{9,5},{13,9},{2,14},{6,2},{... | collective-permute-start | bytes 122888 | tf_op jit(solution)/shard_map/halo/ppermute | solution.py:187
  13.3 0.0 collective-permute-done.5.rest_3_
  13.3 0.0 collective-permute-start.3
  13.3 0.6 %collective-permute-done.4.rest_2_ = bf16[2,80,64]{2,1,0:T(8,128)(2,1)S(1)} collective-permute-done((bf16[2,80,64]{2,1,0:T(8,128)(2,1)S(1)}, bf16[2,80,64]{2,1,0:T(8,128)(2,1)S(1)}, u32[]{:S(2)}, u32[]{:S(2)}) %collective-permute-start.4) | collective-permute-done | bytes 20512 | tf_op jit(solution)/shard_map/interface/ppermute | solution.py:189
  13.9 2.8 %collective-permute-start.2 = (bf16[2,80,64]{2,1,0:T(8,128)(2,1)S(1)}, bf16[2,80,64]{2,1,0:T(8,128)(2,1)S(1)}, u32[]{:S(2)}, u32[]{:S(2)}) collective-permute-start(bf16[2,80,64]{2,1,0:T(8,128)(2,1)S(1)} %get-tuple-element.10), channel_id=1, source_target_pairs={{0,1},{1,0},{4,5},{5,4},{8,9},{9,8},{12,13},{13,12},{2,3},{3,2},{6... | collective-permute-start | bytes 61448 | tf_op jit(solution)/shard_map/interface/ppermute | solution.py:189
  17.4 0.0 copy-done.8
  17.4 1.5 %collective-permute-done.3.rest_1_ = bf16[2,80,64]{2,1,0:T(8,128)(2,1)S(1)} collective-permute-done((bf16[2,80,64]{2,1,0:T(8,128)(2,1)S(1)}, bf16[2,80,64]{2,1,0:T(8,128)(2,1)S(1)}, u32[]{:S(2)}, u32[]{:S(2)}) %collective-permute-start.3) | collective-permute-done | bytes 20512 | tf_op jit(solution)/shard_map/interface/ppermute | solution.py:189
  18.9 0.0 collective-permute-done.2.rest_0_
  18.9 0.0 collective-permute-done.low_ref
  18.9 0.0 collective-permute-done.1.high_ref
  18.9 0.0 copy-done.2
  19.0 0.0 copy-done.3
  19.0 0.0 copy-done.4
  19.0 0.0 copy-done.5
  19.0 0.0 copy-done.6
  19.0 0.0 copy-done.7
  19.0 0.0 copy-start.1
  19.0 7.3 %couple.1.partial_ref = f32[2,320,1024]{2,1,0:T(8,128)S(1)} custom-call(s32[3]{0:T(128)S(1)} %pad_add_fusion.place_ref, f32[1]{0:T(128)S(6)} %copy.17.freq_ref, f32[4,4]{1,0:T(4,128)S(1)} %copy-done.3, s32[6,1024]{1,0:T(8,128)S(1)} %bitcast.16, s32[2,64]{1,0:T(2,128)S(1)} %bitcast.18, bf16[2,320,1024]{2,1,0:T(8,128)(2,1)S(1)} %bitcast.13, ...), custom_call_target="tpu_custom_call" | custom-call | flops 3690987520 | bytes 6553600 | tf_op jit(solution)/shard_map/couple/couple/pallas_call | solution.py:197
  26.4 5.6 %collective-permute-done.6.rest_0_ = bf16[2,320,1024]{2,1,0:T(8,128)(2,1)S(1)} collective-permute-done((bf16[2,320,1024]{2,1,0:T(8,128)(2,1)}, bf16[2,320,1024]{2,1,0:T(8,128)(2,1)S(1)}, u32[]{:S(2)}, u32[]{:S(2)}) %collective-permute-start.6) | collective-permute-done | bytes 1310752 | tf_op jit(solution)/shard_map/instances/ppermute | solution.py:162
  31.9 0.0 copy-done.1
  31.9 3.6 %update.1 = bf16[2,320,1024]{2,1,0:T(8,128)(2,1)} custom-call(s32[3]{0:T(128)S(1)} %pad_add_fusion.place_ref, f32[1]{0:T(128)S(6)} %copy.17.freq_ref, f32[4,4]{1,0:T(4,128)S(1)} %copy-done.3, f32[2,320,1024]{2,1,0:T(8,128)S(1)} %couple.1.partial_ref, bf16[2,320,1024]{2,1,0:T(8,128)(2,1)S(1)} %bitcast.15, f32[1,1024]{1,0:T(1,128)S(1)} %copy-done.2, ...), custom_call_target="tpu_custom_call" | custom-call | flops 419430400 | bytes 6553600 | tf_op jit(solution)/shard_map/update/update/pallas_call | solution.py:215
  (1 shorter events, 0.0 us)
Async XLA Ops:
  0.0 31.9 %collective-permute-start.6 = (bf16[2,320,1024]{2,1,0:T(8,128)(2,1)}, bf16[2,320,1024]{2,1,0:T(8,128)(2,1)S(1)}, u32[]{:S(2)}, u32[]{:S(2)}) collective-permute-start(bf16[2,320,1024]{2,1,0:T(8,128)(2,1)} %bitcast.10), channel_id=1, source_target_pairs={{0,2},{2,0},{1,3},{3,1},{4,6},{6,4},{5,7},{7,5},{8,10},{10,8},{9,1... | collective-permute-start | bytes 3932168 | tf_op jit(solution)/shard_map/instances/ppermute | solution.py:162
  4.2 1.3 %copy-start = (bf16[1,2,320,1024]{3,2,1,0:T(8,128)(2,1)S(1)}, bf16[1,2,320,1024]{3,2,1,0:T(8,128)(2,1)}, u32[]{:S(2)}) copy-start(bf16[1,2,320,1024]{3,2,1,0:T(8,128)(2,1)} %param.11) | copy-start | bytes 3932164
  5.6 11.8 %copy-start.8 = (s32[1,6,1024]{2,0,1:T(1,128)S(1)}, s32[1,6,1024]{2,0,1:T(1,128)}, u32[]{:S(2)}) copy-start(s32[1,6,1024]{2,0,1:T(1,128)} %param.15) | copy-start | bytes 73732
  5.6 13.4 %copy-start.2 = (f32[1,1024]{1,0:T(1,128)S(1)}, f32[1,1024]{1,0:T(1,128)}, u32[]{:S(2)}) copy-start(f32[1,1024]{1,0:T(1,128)} %scale_ref.3) | copy-start | bytes 12292
  5.6 13.4 %copy-start.3 = (f32[4,4]{1,0:T(4,128)S(1)}, f32[4,4]{1,0:T(4,128)}, u32[]{:S(2)}) copy-start(f32[4,4]{1,0:T(4,128)} %constant.13.clone.table_ref) | copy-start | bytes 196
  5.6 13.4 %copy-start.4 = (bf16[1,2,320,1024]{3,2,1,0:T(8,128)(2,1)S(1)}, bf16[1,2,320,1024]{3,2,1,0:T(8,128)(2,1)}, u32[]{:S(2)}) copy-start(bf16[1,2,320,1024]{3,2,1,0:T(8,128)(2,1)} %param.12) | copy-start | bytes 3932164
  5.6 13.4 %copy-start.5 = (bf16[320,480]{1,0:T(8,128)(2,1)S(1)}, bf16[320,480]{1,0:T(8,128)(2,1)}, u32[]{:S(2)}) copy-start(bf16[320,480]{1,0:T(8,128)(2,1)} %lift_ref.1) | copy-start | bytes 921604
  5.6 13.4 %copy-start.6 = (bf16[320,320]{1,0:T(8,128)(2,1)S(1)}, bf16[320,320]{1,0:T(8,128)(2,1)}, u32[]{:S(2)}) copy-start(bf16[320,320]{1,0:T(8,128)(2,1)} %volume_ref.1) | copy-start | bytes 614404
  5.6 13.4 %copy-start.7 = (s32[1,2,64]{2,1,0:T(2,128)S(1)}, s32[1,2,64]{2,1,0:T(2,128)}, u32[]{:S(2)}) copy-start(s32[1,2,64]{2,1,0:T(2,128)} %param.16) | copy-start | bytes 1540
  6.6 6.6 %collective-permute-start.5 = (bf16[2,80,64]{2,1,0:T(8,128)(2,1)S(1)}, bf16[2,80,64]{2,1,0:T(8,128)(2,1)S(1)}, u32[]{:S(2)}, u32[]{:S(2)}) collective-permute-start(bf16[2,80,64]{2,1,0:T(8,128)(2,1)S(1)} %get-tuple-element.10), channel_id=1, source_target_pairs={{0,13},{1,12},{4,1},{5,0},{8,5},{9,4},{12,9},{13,8},{2,15},{3,14},... | collective-permute-start | bytes 61448 | tf_op jit(solution)/shard_map/interface/ppermute | solution.py:189
  9.4 4.5 %collective-permute-start.4 = (bf16[2,80,64]{2,1,0:T(8,128)(2,1)S(1)}, bf16[2,80,64]{2,1,0:T(8,128)(2,1)S(1)}, u32[]{:S(2)}, u32[]{:S(2)}) collective-permute-start(bf16[2,80,64]{2,1,0:T(8,128)(2,1)S(1)} %get-tuple-element.10), channel_id=1, source_target_pairs={{0,9},{1,8},{4,13},{5,12},{8,1},{9,0},{12,5},{13,4},{2,11},{3,10},... | collective-permute-start | bytes 61448 | tf_op jit(solution)/shard_map/interface/ppermute | solution.py:189
  9.4 9.5 %collective-permute-start = (bf16[2,160,64]{2,1,0:T(8,128)(2,1)S(1)}, bf16[2,160,64]{2,1,0:T(8,128)(2,1)S(1)}, u32[]{:S(2)}, u32[]{:S(2)}) collective-permute-start(bf16[2,160,64]{2,1,0:T(8,128)(2,1)S(1)} %get-tuple-element.8), channel_id=1, source_target_pairs={{0,4},{4,8},{8,12},{12,0},{1,5},{5,9},{9,13},{13,1},{2,6},{6,10},{... | collective-permute-start | bytes 122888 | tf_op jit(solution)/shard_map/halo/ppermute | solution.py:186
  11.0 7.9 %collective-permute-start.1 = (bf16[2,160,64]{2,1,0:T(8,128)(2,1)S(1)}, bf16[2,160,64]{2,1,0:T(8,128)(2,1)S(1)}, u32[]{:S(2)}, u32[]{:S(2)}) collective-permute-start(bf16[2,160,64]{2,1,0:T(8,128)(2,1)S(1)} %get-tuple-element.9), channel_id=1, source_target_pairs={{0,12},{4,0},{8,4},{12,8},{1,13},{5,1},{9,5},{13,9},{2,14},{6,2},{... | collective-permute-start | bytes 122888 | tf_op jit(solution)/shard_map/halo/ppermute | solution.py:187
  13.3 5.7 %collective-permute-start.3 = (bf16[2,80,64]{2,1,0:T(8,128)(2,1)S(1)}, bf16[2,80,64]{2,1,0:T(8,128)(2,1)S(1)}, u32[]{:S(2)}, u32[]{:S(2)}) collective-permute-start(bf16[2,80,64]{2,1,0:T(8,128)(2,1)S(1)} %get-tuple-element.10), channel_id=1, source_target_pairs={{0,5},{1,4},{4,9},{5,8},{8,13},{9,12},{12,1},{13,0},{2,7},{3,6},{6... | collective-permute-start | bytes 61448 | tf_op jit(solution)/shard_map/interface/ppermute | solution.py:189
  13.9 5.0 %collective-permute-start.2 = (bf16[2,80,64]{2,1,0:T(8,128)(2,1)S(1)}, bf16[2,80,64]{2,1,0:T(8,128)(2,1)S(1)}, u32[]{:S(2)}, u32[]{:S(2)}) collective-permute-start(bf16[2,80,64]{2,1,0:T(8,128)(2,1)S(1)} %get-tuple-element.10), channel_id=1, source_target_pairs={{0,1},{1,0},{4,5},{5,4},{8,9},{9,8},{12,13},{13,12},{2,3},{3,2},{6... | collective-permute-start | bytes 61448 | tf_op jit(solution)/shard_map/interface/ppermute | solution.py:189
  19.0 12.9 %copy-start.1 = (bf16[320,320]{1,0:T(8,128)(2,1)S(1)}, bf16[320,320]{1,0:T(8,128)(2,1)}, u32[]{:S(2)}) copy-start(bf16[320,320]{1,0:T(8,128)(2,1)} %inverse_ref.1) | copy-start | bytes 614404

commit v2 on v1

--- a/solution.py
+++ b/solution.py
@@ -46,7 +46,7 @@
 
 
 def couple_kernel(shards, place_ref, freq_ref, table_ref, adj_ref, partner_ref, all_ref, tile_ref, forcing_ref,
-                  scale_ref, trace_ref, lift_ref, volume_ref, low_ref, high_ref, *rest):
+                  scale_ref, trace_ref, lift_ref, volume_ref, inverse_ref, low_ref, high_ref, *rest):
     pieces, (out_ref, traces) = rest[:shards], rest[shards:]
     step = pl.program_id(0)
     steps = pl.num_programs(0)
@@ -102,6 +102,7 @@
         found = gathered(edge)
         frequency = freq_ref[0]
         scale = scale_ref[...]
+        inverse_scale = 1.0 / scale
         for n in range(count):
             beside = jnp.concatenate([v[n * width : (n + 1) * width] for v in found], axis=0)
             inner = dot(lift_ref[...], beside) + dot(volume_ref[...], tile_ref[n])
@@ -109,7 +110,8 @@
             for m in range(count):
                 weight = table_ref[inst * count + n, inst * count + m] * frequency
                 value -= weight * tile_ref[m].astype(jnp.float32)
-            out_ref[n] = value
+            update = dot(inverse_ref[...], value.astype(jnp.bfloat16))
+            out_ref[n] = tile_ref[n].astype(jnp.float32) + update * inverse_scale
 
     @pl.when(at_edge)
     def _():
@@ -120,21 +122,25 @@
         finish(False)
 
 
-def update_kernel(peers, place_ref, freq_ref, table_ref, partial_ref, current_ref, scale_ref, inverse_ref, *rest):
-    others, out_ref = rest[: peers - 1], rest[peers - 1]
-    count = current_ref.shape[0]
+def update_kernel(peers, first, place_ref, freq_ref, table_ref, ready_ref, scale_ref, inverse_ref, *rest):
+    others, out_ref = rest[: peers - 1], rest[-1]
+    count = ready_ref.shape[0]
+    tile = out_ref.shape[2]
+    step = pl.program_id(0)
+    here = pl.ds(pl.multiple_of(step * tile, tile), tile)
+    there = pl.ds(pl.multiple_of(first + step * tile, tile), tile)
     inst = place_ref[1]
-    frequency = freq_ref[0]
-    inverse_scale = 1.0 / scale_ref[...]
+    factor = freq_ref[0] / scale_ref[:, there]
+    values = [ready_ref[n, :, there] for n in range(count)]
+    for d in range(1, peers):
+        owner = lax.rem(inst - d + peers, peers)
+        for m in range(count):
+            moved = dot(inverse_ref[...], others[d - 1][m, :, here])
+            for n in range(count):
+                weight = table_ref[inst * count + n, owner * count + m]
+                values[n] -= (weight * factor) * moved
     for n in range(count):
-        value = partial_ref[n]
-        for d in range(1, peers):
-            owner = lax.rem(inst - d + peers, peers)
-            for m in range(count):
-                weight = table_ref[inst * count + n, owner * count + m] * frequency
-                value -= weight * others[d - 1][m].astype(jnp.float32)
-        update = dot(inverse_ref[...], value.astype(jnp.bfloat16))
-        out_ref[n] = (current_ref[n].astype(jnp.float32) + update * inverse_scale).astype(jnp.bfloat16)
+        out_ref[n] = values[n].astype(jnp.bfloat16)
 
 
 def whole(array):
@@ -159,8 +165,9 @@
     bf16 = jnp.bfloat16
 
     with jax.named_scope("instances"):
-        others = [lax.ppermute(current, "inst", [(i, (i + d) % peers) for i in range(peers)])
-                  for d in range(1, peers)]
+        bounds = [(0, total)]
+        arriving = [[lax.ppermute(current[:, :, first:last], "inst", [(i, (i + d) % peers) for i in range(peers)])
+                     for d in range(1, peers)] for first, last in bounds]
 
     with jax.named_scope("ends"):
         up, down, cross = pl.pallas_call(
@@ -194,13 +201,13 @@
     steps = total // tile
     by_tile = lambda *lead: pl.BlockSpec(lead + (tile,), lambda j: (0,) * len(lead) + (j,))
     with jax.named_scope("couple"):
-        partial = pl.pallas_call(
+        ready = pl.pallas_call(
             functools.partial(couple_kernel, shards),
             grid=(steps,),
             out_shape=jax.ShapeDtypeStruct((count, dof, total), jnp.float32),
             in_specs=[smem, smem, smem, by_tile(6), whole(partner_rows), whole(current), by_tile(count, dof),
                       by_tile(count, dof), by_tile(1), whole(trace_matrix), whole(lift_matrix),
-                      whole(volume_matrix), whole(low), whole(high)] + [whole(p) for p in pieces],
+                      whole(volume_matrix), whole(block_inverse), whole(low), whole(high)] + [whole(p) for p in pieces],
             out_specs=by_tile(count, dof),
             scratch_shapes=[pltpu.VMEM((6, count * width, total), bf16)],
             compiler_params=pltpu.CompilerParams(vmem_limit_bytes=VMEM_LIMIT),
@@ -209,21 +216,25 @@
                 bytes_accessed=count * dof * total * 10, transcendentals=0),
             name="couple",
         )(place, frequency, table, neighbours, partner_rows, current, current, forcing_local, metric_scale,
-          trace_matrix, lift_matrix, volume_matrix, low, high, *pieces)
-
+          trace_matrix, lift_matrix, volume_matrix, block_inverse, low, high, *pieces)
+
+    vmem = pl.BlockSpec(memory_space=pltpu.VMEM)
     with jax.named_scope("update"):
-        result = pl.pallas_call(
-            functools.partial(update_kernel, peers),
-            grid=(steps,),
-            out_shape=jax.ShapeDtypeStruct((count, dof, total), bf16),
-            in_specs=[smem, smem, smem, by_tile(count, dof), by_tile(count, dof), by_tile(1), whole(block_inverse)]
-            + [by_tile(count, dof)] * (peers - 1),
-            out_specs=by_tile(count, dof),
-            compiler_params=pltpu.CompilerParams(vmem_limit_bytes=VMEM_LIMIT),
-            cost_estimate=pl.CostEstimate(flops=2 * count * total * dof * dof,
-                                          bytes_accessed=count * dof * total * 10, transcendentals=0),
-            name="update",
-        )(place, frequency, table, partial, current, metric_scale, block_inverse, *others)
+        result = None
+        for (first, last), others in zip(bounds, arriving):
+            more = [] if result is None else [result]
+            result = pl.pallas_call(
+                functools.partial(update_kernel, peers, first),
+                grid=((last - first) // tile,),
+                out_shape=jax.ShapeDtypeStruct((count, dof, total), bf16),
+                in_specs=[smem, smem, smem] + [vmem] * (2 + peers) + [pl.BlockSpec(memory_space=pl.ANY)] * len(more),
+                out_specs=pl.BlockSpec((count, dof, tile), lambda j, at=first // tile: (0, 0, at + j)),
+                input_output_aliases={5 + peers: 0} if more else {},
+                compiler_params=pltpu.CompilerParams(vmem_limit_bytes=VMEM_LIMIT),
+                cost_estimate=pl.CostEstimate(flops=2 * count * (last - first) * dof * dof * (peers - 1),
+                                              bytes_accessed=count * dof * (last - first) * 8, transcendentals=0),
+                name="update",
+            )(place, frequency, table, ready, metric_scale, block_inverse, *others, *more)
     return result[None]
 
 

time: 35.7 us -> 35.3 us (0.989)
  waiting for transfers between devices: 7.74 us -> 4.67 us
  Pallas kernels: 12 us -> 14.6 us
    pallas_call x1, Pallas kernels: 7.34 us -> 10.4 us  [body(): pl.pallas_call(functools.partial(couple_kernel, shards), grid=(steps,), o...]
    ppermute x1, waiting for transfers between devices: 5.56 us -> 2.5 us  [body(): lax.ppermute(current[:, :, first:last], 'inst', [(i, (i + d) % peers) for...]
    pallas_call x1, Pallas kernels: 3.6 us -> 3.14 us  [body(): pl.pallas_call(functools.partial(update_kernel, peers, first), grid=((las...]
  transfers between devices with their start and end apart: 7 -> 7, of which waited for: 3 -> 3; matrix products, arithmetic and copies ran while one was open for 4% -> 4% of each run, Pallas kernels for 24% -> 33%
where the time goes in v2:
time: 35.3 us; the launch traced here: 35.1 us
  Pallas kernels  14.6 us (41%)
  starting transfers between devices  12.4 us (35%)
  waiting for transfers between devices  4.67 us (13%)
  local copies, waits for them, and re-layouts  2.58 us (7%)
  between operations  0.79 us (2%)
    pallas_call x1, Pallas kernels, body(): pl.pallas_call(functools.partial(couple_kernel, shards), grid=(steps,), o...  10.4 us
    ppermute x4, starting transfers between devices, body(): lax.ppermute(cross, ('space', 'row'), [(i * 2 + r, (i + d) % shards * 2 +...  5.62 us
    pallas_call x1, Pallas kernels, body(): pl.pallas_call(functools.partial(update_kernel, peers, first), grid=((las...  3.14 us
    ppermute x1, starting transfers between devices, body(): lax.ppermute(current[:, :, first:last], 'inst', [(i, (i + d) % peers) for...  2.94 us
    unnamed x20, local copies, waits for them, and re-layouts  2.58 us
    ppermute x1, waiting for transfers between devices, body(): lax.ppermute(current[:, :, first:last], 'inst', [(i, (i + d) % peers) for...  2.5 us
    ppermute x1, starting transfers between devices, body(): lax.ppermute(down, 'space', [(i, (i - 1) % shards) for i in range(shards)])  2.25 us
    ppermute x4, waiting for transfers between devices, body(): lax.ppermute(cross, ('space', 'row'), [(i * 2 + r, (i + d) % shards * 2 +...  2.17 us
  transfers between devices with their start and end apart: 7, of which 3 were waited for; matrix products, arithmetic and copies ran while one was open for 4% of the time, Pallas kernels for 33%

profile of v2, /device:TPU:0, one launch (start us, length us, event | category | flops | bytes accessed | tf_op | source)
XLA Modules:
  0.0 35.1 jit_solution(4772397058138792119)
XLA Ops:
  0.0 2.9 %collective-permute-start.6 = (bf16[2,320,1024]{2,1,0:T(8,128)(2,1)}, bf16[2,320,1024]{2,1,0:T(8,128)(2,1)S(1)}, u32[]{:S(2)}, u32[]{:S(2)}) collective-permute-start(bf16[2,320,1024]{2,1,0:T(8,128)(2,1)} %bitcast.10), channel_id=1, source_target_pairs={{0,2},{2,0},{1,3},{3,1},{4,6},{6,4},{5,7},{7,5},{8,10},{10,8},{9,1... | collective-permute-start | bytes 3932168 | tf_op jit(solution)/shard_map/instances/ppermute | solution.py:169
  2.9 1.2 %copy.13.trace_ref = bf16[480,320]{1,0:T(8,128)(2,1)S(1)} copy(bf16[480,320]{0,1:T(8,128)(2,1)} %param.18) | data formatting | bytes 614400 | tf_op args[7]
  4.2 0.1 pad_add_fusion.place_ref
  4.2 0.0 copy-start
  4.2 1.3 %copy-done = bf16[1,2,320,1024]{3,2,1,0:T(8,128)(2,1)S(1)} copy-done((bf16[1,2,320,1024]{3,2,1,0:T(8,128)(2,1)S(1)}, bf16[1,2,320,1024]{3,2,1,0:T(8,128)(2,1)}, u32[]{:S(2)}) %copy-start) | copy-done | bytes 1310744
  5.6 0.0 copy-start.8
  5.6 0.0 copy-start.1
  5.6 0.0 copy-start.2
  5.6 0.0 copy-start.3
  5.6 0.0 copy-start.4
  5.6 0.0 copy-start.5
  5.6 0.0 copy-start.6
  5.6 0.0 copy-start.7
  5.6 1.0 %ends.1 = (bf16[2,160,64]{2,1,0:T(8,128)(2,1)S(1)}, bf16[2,160,64]{2,1,0:T(8,128)(2,1)S(1)}, bf16[2,80,64]{2,1,0:T(8,128)(2,1)S(1)}) custom-call(s32[3]{0:T(128)S(1)} %pad_add_fusion.place_ref, bf16[2,320,1024]{2,1,0:T(8,128)(2,1)S(1)} %bitcast.11, bf16[2,320,1024]{2,1,0:T(8,128)(2,1)S(1)} %bitcast.12, bf16[480,320]{1,0:T(8,128)(2,1)S(1)} %copy.13.trace_ref), custom_call_target="tpu_custom_call" | custom-call | flops 104857600 | bytes 1000000 | tf_op jit(solution)/shard_map/ends/ends/pallas_call | solution.py:173
  6.6 2.8 %collective-permute-start.5 = (bf16[2,80,64]{2,1,0:T(8,128)(2,1)S(1)}, bf16[2,80,64]{2,1,0:T(8,128)(2,1)S(1)}, u32[]{:S(2)}, u32[]{:S(2)}) collective-permute-start(bf16[2,80,64]{2,1,0:T(8,128)(2,1)S(1)} %get-tuple-element.10), channel_id=1, source_target_pairs={{0,13},{1,12},{4,1},{5,0},{8,5},{9,4},{12,9},{13,8},{2,15},{3,14},... | collective-permute-start | bytes 61448 | tf_op jit(solution)/shard_map/interface/ppermute | solution.py:196
  9.5 0.0 collective-permute-start.4
  9.5 1.6 %collective-permute-start = (bf16[2,160,64]{2,1,0:T(8,128)(2,1)S(1)}, bf16[2,160,64]{2,1,0:T(8,128)(2,1)S(1)}, u32[]{:S(2)}, u32[]{:S(2)}) collective-permute-start(bf16[2,160,64]{2,1,0:T(8,128)(2,1)S(1)} %get-tuple-element.8), channel_id=1, source_target_pairs={{0,4},{4,8},{8,12},{12,0},{1,5},{5,9},{9,13},{13,1},{2,6},{6,10},{... | collective-permute-start | bytes 122888 | tf_op jit(solution)/shard_map/halo/ppermute | solution.py:193
  11.0 2.2 %collective-permute-start.1 = (bf16[2,160,64]{2,1,0:T(8,128)(2,1)S(1)}, bf16[2,160,64]{2,1,0:T(8,128)(2,1)S(1)}, u32[]{:S(2)}, u32[]{:S(2)}) collective-permute-start(bf16[2,160,64]{2,1,0:T(8,128)(2,1)S(1)} %get-tuple-element.9), channel_id=1, source_target_pairs={{0,12},{4,0},{8,4},{12,8},{1,13},{5,1},{9,5},{13,9},{2,14},{6,2},{... | collective-permute-start | bytes 122888 | tf_op jit(solution)/shard_map/halo/ppermute | solution.py:194
  13.3 0.0 collective-permute-done.5.rest_3_
  13.3 0.0 collective-permute-start.3
  13.3 0.6 %collective-permute-done.4.rest_2_ = bf16[2,80,64]{2,1,0:T(8,128)(2,1)S(1)} collective-permute-done((bf16[2,80,64]{2,1,0:T(8,128)(2,1)S(1)}, bf16[2,80,64]{2,1,0:T(8,128)(2,1)S(1)}, u32[]{:S(2)}, u32[]{:S(2)}) %collective-permute-start.4) | collective-permute-done | bytes 20512 | tf_op jit(solution)/shard_map/interface/ppermute | solution.py:196
  13.9 2.8 %collective-permute-start.2 = (bf16[2,80,64]{2,1,0:T(8,128)(2,1)S(1)}, bf16[2,80,64]{2,1,0:T(8,128)(2,1)S(1)}, u32[]{:S(2)}, u32[]{:S(2)}) collective-permute-start(bf16[2,80,64]{2,1,0:T(8,128)(2,1)S(1)} %get-tuple-element.10), channel_id=1, source_target_pairs={{0,1},{1,0},{4,5},{5,4},{8,9},{9,8},{12,13},{13,12},{2,3},{3,2},{6... | collective-permute-start | bytes 61448 | tf_op jit(solution)/shard_map/interface/ppermute | solution.py:196
  17.4 0.0 copy-done.8
  17.4 1.5 %collective-permute-done.3.rest_1_ = bf16[2,80,64]{2,1,0:T(8,128)(2,1)S(1)} collective-permute-done((bf16[2,80,64]{2,1,0:T(8,128)(2,1)S(1)}, bf16[2,80,64]{2,1,0:T(8,128)(2,1)S(1)}, u32[]{:S(2)}, u32[]{:S(2)}) %collective-permute-start.3) | collective-permute-done | bytes 20512 | tf_op jit(solution)/shard_map/interface/ppermute | solution.py:196
  18.9 0.0 collective-permute-done.2.rest_0_
  18.9 0.0 collective-permute-done.low_ref
  18.9 0.0 collective-permute-done.1.high_ref
  18.9 0.0 copy-done.1
  18.9 0.0 copy-done.2
  19.0 0.0 copy-done.3
  19.0 0.0 copy-done.4
  19.0 0.0 copy-done.5
  19.0 0.0 copy-done.6
  19.0 0.0 copy-done.7
  19.0 10.4 %couple.1.ready_ref = f32[2,320,1024]{2,1,0:T(8,128)S(1)} custom-call(s32[3]{0:T(128)S(1)} %pad_add_fusion.place_ref, f32[1]{0:T(128)S(6)} %copy.17.freq_ref, f32[4,4]{1,0:T(4,128)S(1)} %copy-done.3, s32[6,1024]{1,0:T(8,128)S(1)} %bitcast.15, s32[2,64]{1,0:T(2,128)S(1)} %bitcast.17, bf16[2,320,1024]{2,1,0:T(8,128)(2,1)S(1)} %bitcast.13, ...), custom_call_target="tpu_custom_call" | custom-call | flops 3690987520 | bytes 6553600 | tf_op jit(solution)/shard_map/couple/couple/pallas_call | solution.py:204
  29.4 2.5 %collective-permute-done.6.rest_0_ = bf16[2,320,1024]{2,1,0:T(8,128)(2,1)S(1)} collective-permute-done((bf16[2,320,1024]{2,1,0:T(8,128)(2,1)}, bf16[2,320,1024]{2,1,0:T(8,128)(2,1)S(1)}, u32[]{:S(2)}, u32[]{:S(2)}) %collective-permute-start.6) | collective-permute-done | bytes 1310752 | tf_op jit(solution)/shard_map/instances/ppermute | solution.py:169
  31.9 3.1 %update.1 = bf16[2,320,1024]{2,1,0:T(8,128)(2,1)} custom-call(s32[3]{0:T(128)S(1)} %pad_add_fusion.place_ref, f32[1]{0:T(128)S(6)} %copy.17.freq_ref, f32[4,4]{1,0:T(4,128)S(1)} %copy-done.3, f32[2,320,1024]{2,1,0:T(8,128)S(1)} %couple.1.ready_ref, f32[1,1024]{1,0:T(1,128)S(1)} %copy-done.2, bf16[320,320]{1,0:T(8,128)(2,1)S(1)} %copy-done.1, ...), custom_call_target="tpu_custom_call" | custom-call | flops 419430400 | bytes 5242880 | tf_op jit(solution)/shard_map/update/update/pallas_call | solution.py:226
  (1 shorter events, 0.0 us)
Async XLA Ops:
  0.0 31.9 %collective-permute-start.6 = (bf16[2,320,1024]{2,1,0:T(8,128)(2,1)}, bf16[2,320,1024]{2,1,0:T(8,128)(2,1)S(1)}, u32[]{:S(2)}, u32[]{:S(2)}) collective-permute-start(bf16[2,320,1024]{2,1,0:T(8,128)(2,1)} %bitcast.10), channel_id=1, source_target_pairs={{0,2},{2,0},{1,3},{3,1},{4,6},{6,4},{5,7},{7,5},{8,10},{10,8},{9,1... | collective-permute-start | bytes 3932168 | tf_op jit(solution)/shard_map/instances/ppermute | solution.py:169
  4.2 1.3 %copy-start = (bf16[1,2,320,1024]{3,2,1,0:T(8,128)(2,1)S(1)}, bf16[1,2,320,1024]{3,2,1,0:T(8,128)(2,1)}, u32[]{:S(2)}) copy-start(bf16[1,2,320,1024]{3,2,1,0:T(8,128)(2,1)} %param.11) | copy-start | bytes 3932164
  5.6 11.8 %copy-start.8 = (s32[1,6,1024]{2,0,1:T(1,128)S(1)}, s32[1,6,1024]{2,0,1:T(1,128)}, u32[]{:S(2)}) copy-start(s32[1,6,1024]{2,0,1:T(1,128)} %param.15) | copy-start | bytes 73732
  5.6 13.4 %copy-start.1 = (bf16[320,320]{1,0:T(8,128)(2,1)S(1)}, bf16[320,320]{1,0:T(8,128)(2,1)}, u32[]{:S(2)}) copy-start(bf16[320,320]{1,0:T(8,128)(2,1)} %inverse_ref.3) | copy-start | bytes 614404
  5.6 13.4 %copy-start.2 = (f32[1,1024]{1,0:T(1,128)S(1)}, f32[1,1024]{1,0:T(1,128)}, u32[]{:S(2)}) copy-start(f32[1,1024]{1,0:T(1,128)} %scale_ref.3) | copy-start | bytes 12292
  5.6 13.4 %copy-start.3 = (f32[4,4]{1,0:T(4,128)S(1)}, f32[4,4]{1,0:T(4,128)}, u32[]{:S(2)}) copy-start(f32[4,4]{1,0:T(4,128)} %constant.13.clone.table_ref) | copy-start | bytes 196
  5.6 13.4 %copy-start.4 = (bf16[1,2,320,1024]{3,2,1,0:T(8,128)(2,1)S(1)}, bf16[1,2,320,1024]{3,2,1,0:T(8,128)(2,1)}, u32[]{:S(2)}) copy-start(bf16[1,2,320,1024]{3,2,1,0:T(8,128)(2,1)} %param.12) | copy-start | bytes 3932164
  5.6 13.4 %copy-start.5 = (bf16[320,480]{1,0:T(8,128)(2,1)S(1)}, bf16[320,480]{1,0:T(8,128)(2,1)}, u32[]{:S(2)}) copy-start(bf16[320,480]{1,0:T(8,128)(2,1)} %lift_ref.1) | copy-start | bytes 921604
  5.6 13.4 %copy-start.6 = (bf16[320,320]{1,0:T(8,128)(2,1)S(1)}, bf16[320,320]{1,0:T(8,128)(2,1)}, u32[]{:S(2)}) copy-start(bf16[320,320]{1,0:T(8,128)(2,1)} %volume_ref.1) | copy-start | bytes 614404
  5.6 13.4 %copy-start.7 = (s32[1,2,64]{2,1,0:T(2,128)S(1)}, s32[1,2,64]{2,1,0:T(2,128)}, u32[]{:S(2)}) copy-start(s32[1,2,64]{2,1,0:T(2,128)} %param.16) | copy-start | bytes 1540
  6.6 6.6 %collective-permute-start.5 = (bf16[2,80,64]{2,1,0:T(8,128)(2,1)S(1)}, bf16[2,80,64]{2,1,0:T(8,128)(2,1)S(1)}, u32[]{:S(2)}, u32[]{:S(2)}) collective-permute-start(bf16[2,80,64]{2,1,0:T(8,128)(2,1)S(1)} %get-tuple-element.10), channel_id=1, source_target_pairs={{0,13},{1,12},{4,1},{5,0},{8,5},{9,4},{12,9},{13,8},{2,15},{3,14},... | collective-permute-start | bytes 61448 | tf_op jit(solution)/shard_map/interface/ppermute | solution.py:196
  9.5 4.5 %collective-permute-start.4 = (bf16[2,80,64]{2,1,0:T(8,128)(2,1)S(1)}, bf16[2,80,64]{2,1,0:T(8,128)(2,1)S(1)}, u32[]{:S(2)}, u32[]{:S(2)}) collective-permute-start(bf16[2,80,64]{2,1,0:T(8,128)(2,1)S(1)} %get-tuple-element.10), channel_id=1, source_target_pairs={{0,9},{1,8},{4,13},{5,12},{8,1},{9,0},{12,5},{13,4},{2,11},{3,10},... | collective-permute-start | bytes 61448 | tf_op jit(solution)/shard_map/interface/ppermute | solution.py:196
  9.5 9.5 %collective-permute-start = (bf16[2,160,64]{2,1,0:T(8,128)(2,1)S(1)}, bf16[2,160,64]{2,1,0:T(8,128)(2,1)S(1)}, u32[]{:S(2)}, u32[]{:S(2)}) collective-permute-start(bf16[2,160,64]{2,1,0:T(8,128)(2,1)S(1)} %get-tuple-element.8), channel_id=1, source_target_pairs={{0,4},{4,8},{8,12},{12,0},{1,5},{5,9},{9,13},{13,1},{2,6},{6,10},{... | collective-permute-start | bytes 122888 | tf_op jit(solution)/shard_map/halo/ppermute | solution.py:193
  11.0 7.9 %collective-permute-start.1 = (bf16[2,160,64]{2,1,0:T(8,128)(2,1)S(1)}, bf16[2,160,64]{2,1,0:T(8,128)(2,1)S(1)}, u32[]{:S(2)}, u32[]{:S(2)}) collective-permute-start(bf16[2,160,64]{2,1,0:T(8,128)(2,1)S(1)} %get-tuple-element.9), channel_id=1, source_target_pairs={{0,12},{4,0},{8,4},{12,8},{1,13},{5,1},{9,5},{13,9},{2,14},{6,2},{... | collective-permute-start | bytes 122888 | tf_op jit(solution)/shard_map/halo/ppermute | solution.py:194
  13.3 5.6 %collective-permute-start.3 = (bf16[2,80,64]{2,1,0:T(8,128)(2,1)S(1)}, bf16[2,80,64]{2,1,0:T(8,128)(2,1)S(1)}, u32[]{:S(2)}, u32[]{:S(2)}) collective-permute-start(bf16[2,80,64]{2,1,0:T(8,128)(2,1)S(1)} %get-tuple-element.10), channel_id=1, source_target_pairs={{0,5},{1,4},{4,9},{5,8},{8,13},{9,12},{12,1},{13,0},{2,7},{3,6},{6... | collective-permute-start | bytes 61448 | tf_op jit(solution)/shard_map/interface/ppermute | solution.py:196
  13.9 5.0 %collective-permute-start.2 = (bf16[2,80,64]{2,1,0:T(8,128)(2,1)S(1)}, bf16[2,80,64]{2,1,0:T(8,128)(2,1)S(1)}, u32[]{:S(2)}, u32[]{:S(2)}) collective-permute-start(bf16[2,80,64]{2,1,0:T(8,128)(2,1)S(1)} %get-tuple-element.10), channel_id=1, source_target_pairs={{0,1},{1,0},{4,5},{5,4},{8,9},{9,8},{12,13},{13,12},{2,3},{3,2},{6... | collective-permute-start | bytes 61448 | tf_op jit(solution)/shard_map/interface/ppermute | solution.py:196

commit v3 on v2

--- a/solution.py
+++ b/solution.py
@@ -165,7 +165,8 @@
     bf16 = jnp.bfloat16
 
     with jax.named_scope("instances"):
-        bounds = [(0, total)]
+        tile = 256
+        bounds = [(0, tile), (tile, total - tile), (total - tile, total)]
         arriving = [[lax.ppermute(current[:, :, first:last], "inst", [(i, (i + d) % peers) for i in range(peers)])
                      for d in range(1, peers)] for first, last in bounds]
 
@@ -197,7 +198,6 @@
                                [(i * 2 + r, (i + d) % shards * 2 + 1 - r) for i in range(shards) for r in range(2)])
                   for d in range(shards)]
 
-    tile = 256
     steps = total // tile
     by_tile = lambda *lead: pl.BlockSpec(lead + (tile,), lambda j: (0,) * len(lead) + (j,))
     with jax.named_scope("couple"):

time: 35.3 us -> 36 us (1.020)
  waiting for transfers between devices: 4.67 us -> 1.39 us
  Pallas kernels: 14.6 us -> 16.7 us
  starting transfers between devices: 12.4 us -> 14.3 us
    ppermute x1 -> x3, waiting for transfers between devices: 2.5 us -> 0.01 us  [body(): lax.ppermute(current[:, :, first:last], 'inst', [(i, (i + d) % peers) for...]
    ppermute x1 -> x3, starting transfers between devices: 2.94 us -> 5.12 us  [body(): lax.ppermute(current[:, :, first:last], 'inst', [(i, (i + d) % peers) for...]
    pallas_call x1 -> x3, Pallas kernels: 3.14 us -> 5.33 us  [body(): pl.pallas_call(functools.partial(update_kernel, peers, first), grid=((las...]
    ppermute x4, waiting for transfers between devices: 2.17 us -> 0.29 us  [body(): lax.ppermute(cross, ('space', 'row'), [(i * 2 + r, (i + d) % shards * 2 +...]
    unnamed x20, local copies, waits for them, and re-layouts: 2.58 us -> 1.28 us
    slice x0 -> x2, local copies, waits for them, and re-layouts: none -> 1.28 us  [body(): current[:, :, first:last]]
    ppermute x4, starting transfers between devices: 5.62 us -> 4.49 us  [body(): lax.ppermute(cross, ('space', 'row'), [(i * 2 + r, (i + d) % shards * 2 +...]
    ppermute x1, waiting for transfers between devices: 0.01 us -> 0.93 us  [body(): lax.ppermute(down, 'space', [(i, (i - 1) % shards) for i in range(shards)])]
  transfers between devices with their start and end apart: 7 -> 9, of which waited for: 3 -> 3; matrix products, arithmetic and copies ran while one was open for 4% -> 4% of each run, Pallas kernels for 33% -> 42%
where the time goes in v3:
time: 36 us; the launch traced here: 35.8 us
  Pallas kernels  16.7 us (46%)
  starting transfers between devices  14.3 us (40%)
  local copies, waits for them, and re-layouts  2.56 us (7%)
  waiting for transfers between devices  1.39 us (4%)
  between operations  0.83 us (2%)
    pallas_call x1, Pallas kernels, body(): pl.pallas_call(functools.partial(couple_kernel, shards), grid=(steps,), o...  10.4 us
    pallas_call x3, Pallas kernels, body(): pl.pallas_call(functools.partial(update_kernel, peers, first), grid=((las...  5.33 us
    ppermute x3, starting transfers between devices, body(): lax.ppermute(current[:, :, first:last], 'inst', [(i, (i + d) % peers) for...  5.12 us
    ppermute x4, starting transfers between devices, body(): lax.ppermute(cross, ('space', 'row'), [(i * 2 + r, (i + d) % shards * 2 +...  4.49 us
    ppermute x1, starting transfers between devices, body(): lax.ppermute(up, 'space', [(i, (i + 1) % shards) for i in range(shards)])  2.47 us
    ppermute x1, starting transfers between devices, body(): lax.ppermute(down, 'space', [(i, (i - 1) % shards) for i in range(shards)])  2.17 us
    unnamed x20, local copies, waits for them, and re-layouts  1.28 us
    slice x2, local copies, waits for them, and re-layouts, body(): current[:, :, first:last]  1.28 us
  transfers between devices with their start and end apart: 9, of which 3 were waited for; matrix products, arithmetic and copies ran while one was open for 4% of the time, Pallas kernels for 42%

profile of v3, /device:TPU:0, one launch (start us, length us, event | category | flops | bytes accessed | tf_op | source)
XLA Modules:
  0.0 35.8 jit_solution(12066295594953541308)
XLA Ops:
  0.0 0.0 copy-start
  0.0 1.2 %slice.13 = bf16[2,320,512]{2,1,0:T(8,128)(2,1)S(1)} slice(bf16[2,320,1024]{2,1,0:T(8,128)(2,1)} %bitcast.10), slice={[0:2], [0:320], [256:768]} | slice | bytes 1310720 | tf_op jit(solution)/shard_map/instances/slice | solution.py:170
  1.2 3.0 %collective-permute-start.7 = (bf16[2,320,512]{2,1,0:T(8,128)(2,1)S(1)}, bf16[2,320,512]{2,1,0:T(8,128)(2,1)S(1)}, u32[]{:S(2)}, u32[]{:S(2)}) collective-permute-start(bf16[2,320,512]{2,1,0:T(8,128)(2,1)S(1)} %slice.13), channel_id=1, source_target_pairs={{0,2},{2,0},{1,3},{3,1},{4,6},{6,4},{5,7},{7,5},{8,10},{10,8},{9,1... | collective-permute-start | bytes 1966088 | tf_op jit(solution)/shard_map/instances/ppermute | solution.py:170
  4.2 0.1 pad_add_fusion.place_ref
  4.3 1.2 %copy.15.trace_ref = bf16[480,320]{1,0:T(8,128)(2,1)S(1)} copy(bf16[480,320]{0,1:T(8,128)(2,1)} %param.18) | data formatting | bytes 614400 | tf_op args[7]
  5.5 0.0 copy-done
  5.6 0.0 copy-start.4
  5.6 1.0 %ends.1 = (bf16[2,160,64]{2,1,0:T(8,128)(2,1)S(1)}, bf16[2,160,64]{2,1,0:T(8,128)(2,1)S(1)}, bf16[2,80,64]{2,1,0:T(8,128)(2,1)S(1)}) custom-call(s32[3]{0:T(128)S(1)} %pad_add_fusion.place_ref, bf16[2,320,1024]{2,1,0:T(8,128)(2,1)S(1)} %bitcast.11, bf16[2,320,1024]{2,1,0:T(8,128)(2,1)S(1)} %bitcast.12, bf16[480,320]{1,0:T(8,128)(2,1)S(1)} %copy.15.trace_ref), custom_call_target="tpu_custom_call" | custom-call | flops 104857600 | bytes 1000000 | tf_op jit(solution)/shard_map/ends/ends/pallas_call | solution.py:174
  6.6 0.0 copy-start.8
  6.6 0.0 copy-start.1
  6.6 0.0 copy-start.2
  6.6 0.0 copy-start.3
  6.6 0.0 copy-start.5
  6.7 0.0 copy-start.6
  6.7 0.0 copy-start.7
  6.7 2.8 %collective-permute-start.5 = (bf16[2,80,64]{2,1,0:T(8,128)(2,1)S(1)}, bf16[2,80,64]{2,1,0:T(8,128)(2,1)S(1)}, u32[]{:S(2)}, u32[]{:S(2)}) collective-permute-start(bf16[2,80,64]{2,1,0:T(8,128)(2,1)S(1)} %get-tuple-element.10), channel_id=1, source_target_pairs={{0,13},{1,12},{4,1},{5,0},{8,5},{9,4},{12,9},{13,8},{2,15},{3,14},... | collective-permute-start | bytes 61448 | tf_op jit(solution)/shard_map/interface/ppermute | solution.py:197
  9.5 0.0 collective-permute-start.4
  9.5 1.2 %collective-permute-start.3 = (bf16[2,80,64]{2,1,0:T(8,128)(2,1)S(1)}, bf16[2,80,64]{2,1,0:T(8,128)(2,1)S(1)}, u32[]{:S(2)}, u32[]{:S(2)}) collective-permute-start(bf16[2,80,64]{2,1,0:T(8,128)(2,1)S(1)} %get-tuple-element.10), channel_id=1, source_target_pairs={{0,5},{1,4},{4,9},{5,8},{8,13},{9,12},{12,1},{13,0},{2,7},{3,6},{6... | collective-permute-start | bytes 61448 | tf_op jit(solution)/shard_map/interface/ppermute | solution.py:197
  10.7 0.5 %collective-permute-start.2 = (bf16[2,80,64]{2,1,0:T(8,128)(2,1)S(1)}, bf16[2,80,64]{2,1,0:T(8,128)(2,1)S(1)}, u32[]{:S(2)}, u32[]{:S(2)}) collective-permute-start(bf16[2,80,64]{2,1,0:T(8,128)(2,1)S(1)} %get-tuple-element.10), channel_id=1, source_target_pairs={{0,1},{1,0},{4,5},{5,4},{8,9},{9,8},{12,13},{13,12},{2,3},{3,2},{6... | collective-permute-start | bytes 61448 | tf_op jit(solution)/shard_map/interface/ppermute | solution.py:197
  11.2 0.0 collective-permute-done.5.rest_3_
  11.2 2.5 %collective-permute-start = (bf16[2,160,64]{2,1,0:T(8,128)(2,1)S(1)}, bf16[2,160,64]{2,1,0:T(8,128)(2,1)S(1)}, u32[]{:S(2)}, u32[]{:S(2)}) collective-permute-start(bf16[2,160,64]{2,1,0:T(8,128)(2,1)S(1)} %get-tuple-element.8), channel_id=1, source_target_pairs={{0,4},{4,8},{8,12},{12,0},{1,5},{5,9},{9,13},{13,1},{2,6},{6,10},{... | collective-permute-start | bytes 122888 | tf_op jit(solution)/shard_map/halo/ppermute | solution.py:194
  13.7 0.3 collective-permute-done.4.rest_2_
  13.9 2.2 %collective-permute-start.1 = (bf16[2,160,64]{2,1,0:T(8,128)(2,1)S(1)}, bf16[2,160,64]{2,1,0:T(8,128)(2,1)S(1)}, u32[]{:S(2)}, u32[]{:S(2)}) collective-permute-start(bf16[2,160,64]{2,1,0:T(8,128)(2,1)S(1)} %get-tuple-element.9), channel_id=1, source_target_pairs={{0,12},{4,0},{8,4},{12,8},{1,13},{5,1},{9,5},{13,9},{2,14},{6,2},{... | collective-permute-start | bytes 122888 | tf_op jit(solution)/shard_map/halo/ppermute | solution.py:195
  16.8 0.0 copy-done.8
  16.8 0.0 collective-permute-done.3.rest_1_
  16.8 0.6 %collective-permute-start.8 = (bf16[2,320,256]{2,1,0:T(8,128)(2,1)S(1)}, bf16[2,320,256]{2,1,0:T(8,128)(2,1)S(1)}, u32[]{:S(2)}, u32[]{:S(2)}) collective-permute-start(bf16[2,320,256]{2,1,0:T(8,128)(2,1)S(1)} %get-tuple-element.11), channel_id=1, source_target_pairs={{0,2},{2,0},{1,3},{3,1},{4,6},{6,4},{5,7},{7,5},{8,10},{10,8},{9,1... | collective-permute-start | bytes 983048 | tf_op jit(solution)/shard_map/instances/ppermute | solution.py:170
  17.4 0.0 collective-permute-done.2.rest_0_
  17.4 1.5 %collective-permute-start.6 = (bf16[2,320,256]{2,1,0:T(8,128)(2,1)S(1)}, bf16[2,320,256]{2,1,0:T(8,128)(2,1)S(1)}, u32[]{:S(2)}, u32[]{:S(2)}) collective-permute-start(bf16[2,320,256]{2,1,0:T(8,128)(2,1)S(1)} %get-tuple-element.12), channel_id=1, source_target_pairs={{0,2},{2,0},{1,3},{3,1},{4,6},{6,4},{5,7},{7,5},{8,10},{10,8},{9,1... | collective-permute-start | bytes 983048 | tf_op jit(solution)/shard_map/instances/ppermute | solution.py:170
  19.0 0.2 collective-permute-done.low_ref
  19.1 0.9 %collective-permute-done.1.high_ref = bf16[2,160,64]{2,1,0:T(8,128)(2,1)S(1)} collective-permute-done((bf16[2,160,64]{2,1,0:T(8,128)(2,1)S(1)}, bf16[2,160,64]{2,1,0:T(8,128)(2,1)S(1)}, u32[]{:S(2)}, u32[]{:S(2)}) %collective-permute-start.1) | collective-permute-done | bytes 40992 | tf_op jit(solution)/shard_map/halo/ppermute | solution.py:195
  20.0 0.0 copy-done.4
  20.0 0.0 copy-done.1
  20.0 0.0 copy-done.2
  20.1 0.0 copy-done.3
  20.1 0.0 copy-done.5
  20.1 0.0 copy-done.6
  20.1 0.0 copy-done.7
  20.1 10.4 %couple.1.ready_ref = f32[2,320,1024]{2,1,0:T(8,128)S(1)} custom-call(s32[3]{0:T(128)S(1)} %pad_add_fusion.place_ref, f32[1]{0:T(128)S(6)} %copy.21.freq_ref, f32[4,4]{1,0:T(4,128)S(1)} %copy-done.3, s32[6,1024]{1,0:T(8,128)S(1)} %bitcast.16, s32[2,64]{1,0:T(2,128)S(1)} %bitcast.18, bf16[2,320,1024]{2,1,0:T(8,128)(2,1)S(1)} %bitcast.14, ...), custom_call_target="tpu_custom_call" | custom-call | flops 3690987520 | bytes 6553600 | tf_op jit(solution)/shard_map/couple/couple/pallas_call | solution.py:204
  30.5 0.0 collective-permute-done.8.rest_0_
  30.5 1.6 %update.3.rest_1_ = bf16[2,320,1024]{2,1,0:T(8,128)(2,1)} custom-call(s32[3]{0:T(128)S(1)} %pad_add_fusion.place_ref, f32[1]{0:T(128)S(6)} %copy.21.freq_ref, f32[4,4]{1,0:T(4,128)S(1)} %copy-done.3, f32[2,320,1024]{2,1,0:T(8,128)S(1)} %couple.1.ready_ref, f32[1,1024]{1,0:T(1,128)S(1)} %copy-done.2, bf16[320,320]{1,0:T(8,128)(2,1)S(1)} %copy-done.1, ...), custom_call_target="tpu_custom_call" | custom-call | flops 104857600 | bytes 1310720 | tf_op jit(solution)/shard_map/update/update/pallas_call | solution.py:226
  32.2 0.0 collective-permute-done.7.rest_0_
  32.2 2.0 %update.4.rest_1_ = bf16[2,320,1024]{2,1,0:T(8,128)(2,1)} custom-call(s32[3]{0:T(128)S(1)} %pad_add_fusion.place_ref, f32[1]{0:T(128)S(6)} %copy.21.freq_ref, f32[4,4]{1,0:T(4,128)S(1)} %copy-done.3, f32[2,320,1024]{2,1,0:T(8,128)S(1)} %couple.1.ready_ref, f32[1,1024]{1,0:T(1,128)S(1)} %copy-done.2, ...), custom_call_target="tpu_custom_call", output_to_operand_aliasing={{}: (7, {})} | custom-call | flops 209715200 | bytes 2621440 | tf_op jit(solution)/shard_map/update/update/pallas_call | solution.py:226
  34.2 0.0 collective-permute-done.6.rest_0_
  34.2 1.6 %update.5 = bf16[2,320,1024]{2,1,0:T(8,128)(2,1)} custom-call(s32[3]{0:T(128)S(1)} %pad_add_fusion.place_ref, f32[1]{0:T(128)S(6)} %copy.21.freq_ref, f32[4,4]{1,0:T(4,128)S(1)} %copy-done.3, f32[2,320,1024]{2,1,0:T(8,128)S(1)} %couple.1.ready_ref, f32[1,1024]{1,0:T(1,128)S(1)} %copy-done.2, ...), custom_call_target="tpu_custom_call", output_to_operand_aliasing={{}: (7, {})} | custom-call | flops 104857600 | bytes 1310720 | tf_op jit(solution)/shard_map/update/update/pallas_call | solution.py:226
  (2 shorter events, 0.1 us)
Async XLA Ops:
  0.0 5.5 %copy-start = (bf16[1,2,320,1024]{3,2,1,0:T(8,128)(2,1)S(1)}, bf16[1,2,320,1024]{3,2,1,0:T(8,128)(2,1)}, u32[]{:S(2)}) copy-start(bf16[1,2,320,1024]{3,2,1,0:T(8,128)(2,1)} %param.11) | copy-start | bytes 3932164
  1.2 30.9 %collective-permute-start.7 = (bf16[2,320,512]{2,1,0:T(8,128)(2,1)S(1)}, bf16[2,320,512]{2,1,0:T(8,128)(2,1)S(1)}, u32[]{:S(2)}, u32[]{:S(2)}) collective-permute-start(bf16[2,320,512]{2,1,0:T(8,128)(2,1)S(1)} %slice.13), channel_id=1, source_target_pairs={{0,2},{2,0},{1,3},{3,1},{4,6},{6,4},{5,7},{7,5},{8,10},{10,8},{9,1... | collective-permute-start | bytes 1966088 | tf_op jit(solution)/shard_map/instances/ppermute | solution.py:170
  5.6 14.5 %copy-start.4 = (bf16[1,2,320,1024]{3,2,1,0:T(8,128)(2,1)S(1)}, bf16[1,2,320,1024]{3,2,1,0:T(8,128)(2,1)}, u32[]{:S(2)}) copy-start(bf16[1,2,320,1024]{3,2,1,0:T(8,128)(2,1)} %param.12) | copy-start | bytes 3932164
  6.6 10.2 %copy-start.8 = (s32[1,6,1024]{2,0,1:T(1,128)S(1)}, s32[1,6,1024]{2,0,1:T(1,128)}, u32[]{:S(2)}) copy-start(s32[1,6,1024]{2,0,1:T(1,128)} %param.15) | copy-start | bytes 73732
  6.6 13.4 %copy-start.1 = (bf16[320,320]{1,0:T(8,128)(2,1)S(1)}, bf16[320,320]{1,0:T(8,128)(2,1)}, u32[]{:S(2)}) copy-start(bf16[320,320]{1,0:T(8,128)(2,1)} %inverse_ref.7) | copy-start | bytes 614404
  6.6 13.4 %copy-start.2 = (f32[1,1024]{1,0:T(1,128)S(1)}, f32[1,1024]{1,0:T(1,128)}, u32[]{:S(2)}) copy-start(f32[1,1024]{1,0:T(1,128)} %scale_ref.7) | copy-start | bytes 12292
  6.6 13.4 %copy-start.3 = (f32[4,4]{1,0:T(4,128)S(1)}, f32[4,4]{1,0:T(4,128)}, u32[]{:S(2)}) copy-start(f32[4,4]{1,0:T(4,128)} %constant.13.clone.table_ref) | copy-start | bytes 196
  6.6 13.4 %copy-start.5 = (bf16[320,480]{1,0:T(8,128)(2,1)S(1)}, bf16[320,480]{1,0:T(8,128)(2,1)}, u32[]{:S(2)}) copy-start(bf16[320,480]{1,0:T(8,128)(2,1)} %lift_ref.1) | copy-start | bytes 921604
  6.7 13.4 %copy-start.6 = (bf16[320,320]{1,0:T(8,128)(2,1)S(1)}, bf16[320,320]{1,0:T(8,128)(2,1)}, u32[]{:S(2)}) copy-start(bf16[320,320]{1,0:T(8,128)(2,1)} %volume_ref.1) | copy-start | bytes 614404
  6.7 13.4 %copy-start.7 = (s32[1,2,64]{2,1,0:T(2,128)S(1)}, s32[1,2,64]{2,1,0:T(2,128)}, u32[]{:S(2)}) copy-start(s32[1,2,64]{2,1,0:T(2,128)} %param.16) | copy-start | bytes 1540
  6.7 4.5 %collective-permute-start.5 = (bf16[2,80,64]{2,1,0:T(8,128)(2,1)S(1)}, bf16[2,80,64]{2,1,0:T(8,128)(2,1)S(1)}, u32[]{:S(2)}, u32[]{:S(2)}) collective-permute-start(bf16[2,80,64]{2,1,0:T(8,128)(2,1)S(1)} %get-tuple-element.10), channel_id=1, source_target_pairs={{0,13},{1,12},{4,1},{5,0},{8,5},{9,4},{12,9},{13,8},{2,15},{3,14},... | collective-permute-start | bytes 61448 | tf_op jit(solution)/shard_map/interface/ppermute | solution.py:197
  9.5 4.4 %collective-permute-start.4 = (bf16[2,80,64]{2,1,0:T(8,128)(2,1)S(1)}, bf16[2,80,64]{2,1,0:T(8,128)(2,1)S(1)}, u32[]{:S(2)}, u32[]{:S(2)}) collective-permute-start(bf16[2,80,64]{2,1,0:T(8,128)(2,1)S(1)} %get-tuple-element.10), channel_id=1, source_target_pairs={{0,9},{1,8},{4,13},{5,12},{8,1},{9,0},{12,5},{13,4},{2,11},{3,10},... | collective-permute-start | bytes 61448 | tf_op jit(solution)/shard_map/interface/ppermute | solution.py:197
  9.5 7.3 %collective-permute-start.3 = (bf16[2,80,64]{2,1,0:T(8,128)(2,1)S(1)}, bf16[2,80,64]{2,1,0:T(8,128)(2,1)S(1)}, u32[]{:S(2)}, u32[]{:S(2)}) collective-permute-start(bf16[2,80,64]{2,1,0:T(8,128)(2,1)S(1)} %get-tuple-element.10), channel_id=1, source_target_pairs={{0,5},{1,4},{4,9},{5,8},{8,13},{9,12},{12,1},{13,0},{2,7},{3,6},{6... | collective-permute-start | bytes 61448 | tf_op jit(solution)/shard_map/interface/ppermute | solution.py:197
  10.7 6.7 %collective-permute-start.2 = (bf16[2,80,64]{2,1,0:T(8,128)(2,1)S(1)}, bf16[2,80,64]{2,1,0:T(8,128)(2,1)S(1)}, u32[]{:S(2)}, u32[]{:S(2)}) collective-permute-start(bf16[2,80,64]{2,1,0:T(8,128)(2,1)S(1)} %get-tuple-element.10), channel_id=1, source_target_pairs={{0,1},{1,0},{4,5},{5,4},{8,9},{9,8},{12,13},{13,12},{2,3},{3,2},{6... | collective-permute-start | bytes 61448 | tf_op jit(solution)/shard_map/interface/ppermute | solution.py:197
  11.2 7.9 %collective-permute-start = (bf16[2,160,64]{2,1,0:T(8,128)(2,1)S(1)}, bf16[2,160,64]{2,1,0:T(8,128)(2,1)S(1)}, u32[]{:S(2)}, u32[]{:S(2)}) collective-permute-start(bf16[2,160,64]{2,1,0:T(8,128)(2,1)S(1)} %get-tuple-element.8), channel_id=1, source_target_pairs={{0,4},{4,8},{8,12},{12,0},{1,5},{5,9},{9,13},{13,1},{2,6},{6,10},{... | collective-permute-start | bytes 122888 | tf_op jit(solution)/shard_map/halo/ppermute | solution.py:194
  13.9 6.1 %collective-permute-start.1 = (bf16[2,160,64]{2,1,0:T(8,128)(2,1)S(1)}, bf16[2,160,64]{2,1,0:T(8,128)(2,1)S(1)}, u32[]{:S(2)}, u32[]{:S(2)}) collective-permute-start(bf16[2,160,64]{2,1,0:T(8,128)(2,1)S(1)} %get-tuple-element.9), channel_id=1, source_target_pairs={{0,12},{4,0},{8,4},{12,8},{1,13},{5,1},{9,5},{13,9},{2,14},{6,2},{... | collective-permute-start | bytes 122888 | tf_op jit(solution)/shard_map/halo/ppermute | solution.py:195
  16.8 13.7 %collective-permute-start.8 = (bf16[2,320,256]{2,1,0:T(8,128)(2,1)S(1)}, bf16[2,320,256]{2,1,0:T(8,128)(2,1)S(1)}, u32[]{:S(2)}, u32[]{:S(2)}) collective-permute-start(bf16[2,320,256]{2,1,0:T(8,128)(2,1)S(1)} %get-tuple-element.11), channel_id=1, source_target_pairs={{0,2},{2,0},{1,3},{3,1},{4,6},{6,4},{5,7},{7,5},{8,10},{10,8},{9,1... | collective-permute-start | bytes 983048 | tf_op jit(solution)/shard_map/instances/ppermute | solution.py:170
  17.4 16.8 %collective-permute-start.6 = (bf16[2,320,256]{2,1,0:T(8,128)(2,1)S(1)}, bf16[2,320,256]{2,1,0:T(8,128)(2,1)S(1)}, u32[]{:S(2)}, u32[]{:S(2)}) collective-permute-start(bf16[2,320,256]{2,1,0:T(8,128)(2,1)S(1)} %get-tuple-element.12), channel_id=1, source_target_pairs={{0,2},{2,0},{1,3},{3,1},{4,6},{6,4},{5,7},{7,5},{8,10},{10,8},{9,1... | collective-permute-start | bytes 983048 | tf_op jit(solution)/shard_map/instances/ppermute | solution.py:170

commit v4 on v1

--- a/solution.py
+++ b/solution.py
@@ -45,9 +45,9 @@
         cross_ref[n] = jnp.where(section == 0, first[width : 2 * width, :rows], first[:width, :rows])
 
 
-def couple_kernel(shards, place_ref, freq_ref, table_ref, adj_ref, partner_ref, all_ref, tile_ref, forcing_ref,
-                  scale_ref, trace_ref, lift_ref, volume_ref, low_ref, high_ref, *rest):
-    pieces, (out_ref, traces) = rest[:shards], rest[shards:]
+def couple_kernel(shards, peers, place_ref, freq_ref, table_ref, adj_ref, partner_ref, all_ref, tile_ref, forcing_ref,
+                  scale_ref, trace_ref, lift_ref, volume_ref, inverse_ref, low_ref, high_ref, *rest):
+    pieces, (out_ref, factor_ref, traces) = rest[:shards], rest[shards:]
     step = pl.program_id(0)
     steps = pl.num_programs(0)
     count, dof, total = all_ref.shape
@@ -102,6 +102,14 @@
         found = gathered(edge)
         frequency = freq_ref[0]
         scale = scale_ref[...]
+        inverse_scale = 1.0 / scale
+        for n in range(count):
+            for d in range(1, peers):
+                owner = lax.rem(inst - d + peers, peers)
+                for m in range(count):
+                    weight = table_ref[inst * count + n, owner * count + m] * frequency
+                    at = (n * (peers - 1) + d - 1) * count + m
+                    factor_ref[at : at + 1, :] = weight * inverse_scale
         for n in range(count):
             beside = jnp.concatenate([v[n * width : (n + 1) * width] for v in found], axis=0)
             inner = dot(lift_ref[...], beside) + dot(volume_ref[...], tile_ref[n])
@@ -109,7 +117,8 @@
             for m in range(count):
                 weight = table_ref[inst * count + n, inst * count + m] * frequency
                 value -= weight * tile_ref[m].astype(jnp.float32)
-            out_ref[n] = value
+            update = dot(inverse_ref[...], value.astype(jnp.bfloat16))
+            out_ref[n] = tile_ref[n].astype(jnp.float32) + update * inverse_scale
 
     @pl.when(at_edge)
     def _():
@@ -120,21 +129,24 @@
         finish(False)
 
 
-def update_kernel(peers, place_ref, freq_ref, table_ref, partial_ref, current_ref, scale_ref, inverse_ref, *rest):
-    others, out_ref = rest[: peers - 1], rest[peers - 1]
-    count = current_ref.shape[0]
-    inst = place_ref[1]
-    frequency = freq_ref[0]
-    inverse_scale = 1.0 / scale_ref[...]
-    for n in range(count):
-        value = partial_ref[n]
-        for d in range(1, peers):
-            owner = lax.rem(inst - d + peers, peers)
-            for m in range(count):
-                weight = table_ref[inst * count + n, owner * count + m] * frequency
-                value -= weight * others[d - 1][m].astype(jnp.float32)
-        update = dot(inverse_ref[...], value.astype(jnp.bfloat16))
-        out_ref[n] = (current_ref[n].astype(jnp.float32) + update * inverse_scale).astype(jnp.bfloat16)
+def update_kernel(tile, ready_ref, factor_ref, inverse_ref, *rest):
+    others, (out_ref, made, sems) = rest[:-3], rest[-3:]
+    count, dof, total = ready_ref.shape
+    copies = []
+    for t in range(total // tile):
+        cols = slice(t * tile, (t + 1) * tile)
+        moved = [dot(inverse_ref[...], other[m, :, cols]) for other in others for m in range(count)]
+        for n in range(count):
+            value = ready_ref[n, :, cols]
+            for k, part in enumerate(moved):
+                at = n * len(moved) + k
+                value -= factor_ref[at : at + 1, cols] * part
+            made[t, n] = value.astype(jnp.bfloat16)
+        copy = pltpu.make_async_copy(made.at[t], out_ref.at[:, :, cols], sems.at[t])
+        copy.start()
+        copies.append(copy)
+    for copy in copies:
+        copy.wait()
 
 
 def whole(array):
@@ -194,14 +206,15 @@
     steps = total // tile
     by_tile = lambda *lead: pl.BlockSpec(lead + (tile,), lambda j: (0,) * len(lead) + (j,))
     with jax.named_scope("couple"):
-        partial = pl.pallas_call(
-            functools.partial(couple_kernel, shards),
+        ready, factors = pl.pallas_call(
+            functools.partial(couple_kernel, shards, peers),
             grid=(steps,),
-            out_shape=jax.ShapeDtypeStruct((count, dof, total), jnp.float32),
+            out_shape=(jax.ShapeDtypeStruct((count, dof, total), jnp.float32),
+                       jax.ShapeDtypeStruct((count * count * (peers - 1), total), jnp.float32)),
             in_specs=[smem, smem, smem, by_tile(6), whole(partner_rows), whole(current), by_tile(count, dof),
                       by_tile(count, dof), by_tile(1), whole(trace_matrix), whole(lift_matrix),
-                      whole(volume_matrix), whole(low), whole(high)] + [whole(p) for p in pieces],
-            out_specs=by_tile(count, dof),
+                      whole(volume_matrix), whole(block_inverse), whole(low), whole(high)] + [whole(p) for p in pieces],
+            out_specs=(by_tile(count, dof), by_tile(count * count * (peers - 1))),
             scratch_shapes=[pltpu.VMEM((6, count * width, total), bf16)],
             compiler_params=pltpu.CompilerParams(vmem_limit_bytes=VMEM_LIMIT),
             cost_estimate=pl.CostEstimate(
@@ -209,21 +222,21 @@
                 bytes_accessed=count * dof * total * 10, transcendentals=0),
             name="couple",
         )(place, frequency, table, neighbours, partner_rows, current, current, forcing_local, metric_scale,
-          trace_matrix, lift_matrix, volume_matrix, low, high, *pieces)
-
+          trace_matrix, lift_matrix, volume_matrix, block_inverse, low, high, *pieces)
+
+    vmem = pl.BlockSpec(memory_space=pltpu.VMEM)
     with jax.named_scope("update"):
         result = pl.pallas_call(
-            functools.partial(update_kernel, peers),
-            grid=(steps,),
+            functools.partial(update_kernel, tile),
             out_shape=jax.ShapeDtypeStruct((count, dof, total), bf16),
-            in_specs=[smem, smem, smem, by_tile(count, dof), by_tile(count, dof), by_tile(1), whole(block_inverse)]
-            + [by_tile(count, dof)] * (peers - 1),
-            out_specs=by_tile(count, dof),
+            in_specs=[vmem] * (2 + peers),
+            out_specs=pl.BlockSpec(memory_space=pl.ANY),
+            scratch_shapes=[pltpu.VMEM((steps, count, dof, tile), bf16), pltpu.SemaphoreType.DMA((steps,))],
             compiler_params=pltpu.CompilerParams(vmem_limit_bytes=VMEM_LIMIT),
-            cost_estimate=pl.CostEstimate(flops=2 * count * total * dof * dof,
-                                          bytes_accessed=count * dof * total * 10, transcendentals=0),
+            cost_estimate=pl.CostEstimate(flops=2 * count * total * dof * dof * (peers - 1),
+                                          bytes_accessed=count * dof * total * 8, transcendentals=0),
             name="update",
-        )(place, frequency, table, partial, current, metric_scale, block_inverse, *others)
+        )(ready, factors, block_inverse, *others)
     return result[None]
 
 

time: 35.7 us -> 33.8 us (0.947)
  waiting for transfers between devices: 7.74 us -> 4.67 us
  Pallas kernels: 12 us -> 13.1 us
    ppermute x1, waiting for transfers between devices: 5.56 us -> 2.5 us  [body(): lax.ppermute(current, 'inst', [(i, (i + d) % peers) for i in range(peers)])]
    pallas_call x2, Pallas kernels: 10.9 us -> 12 us  [the longest x1 10.4 us: body(): pl.pallas_call(functools.partial(couple_kernel, shards, peers), grid=(ste...]
  transfers between devices with their start and end apart: 7 -> 7, of which waited for: 3 -> 3; matrix products, arithmetic and copies ran while one was open for 4% -> 4% of each run, Pallas kernels for 24% -> 34%
where the time goes in v4:
time: 33.8 us; the launch traced here: 33.6 us
  Pallas kernels  13.1 us (39%)
  starting transfers between devices  12.4 us (37%)
  waiting for transfers between devices  4.67 us (14%)
  local copies, waits for them, and re-layouts  2.58 us (8%)
  between operations  0.79 us (2%)
    pallas_call x1, Pallas kernels, body(): pl.pallas_call(functools.partial(couple_kernel, shards, peers), grid=(ste...  10.4 us
    ppermute x4, starting transfers between devices, body(): lax.ppermute(cross, ('space', 'row'), [(i * 2 + r, (i + d) % shards * 2 +...  5.62 us
    ppermute x1, starting transfers between devices, body(): lax.ppermute(current, 'inst', [(i, (i + d) % peers) for i in range(peers)])  2.94 us
    unnamed x20, local copies, waits for them, and re-layouts  2.58 us
    ppermute x1, waiting for transfers between devices, body(): lax.ppermute(current, 'inst', [(i, (i + d) % peers) for i in range(peers)])  2.5 us
    ppermute x1, starting transfers between devices, body(): lax.ppermute(down, 'space', [(i, (i - 1) % shards) for i in range(shards)])  2.25 us
    ppermute x4, waiting for transfers between devices, body(): lax.ppermute(cross, ('space', 'row'), [(i * 2 + r, (i + d) % shards * 2 +...  2.16 us
    pallas_call x1, Pallas kernels, body(): pl.pallas_call(functools.partial(update_kernel, tile), out_shape=jax.Shap...  1.64 us
  transfers between devices with their start and end apart: 7, of which 3 were waited for; matrix products, arithmetic and copies ran while one was open for 4% of the time, Pallas kernels for 34%

profile of v4, /device:TPU:0, one launch (start us, length us, event | category | flops | bytes accessed | tf_op | source)
XLA Modules:
  0.0 33.6 jit_solution(220306783451654093)
XLA Ops:
  0.0 2.9 %collective-permute-start.6 = (bf16[2,320,1024]{2,1,0:T(8,128)(2,1)}, bf16[2,320,1024]{2,1,0:T(8,128)(2,1)S(1)}, u32[]{:S(2)}, u32[]{:S(2)}) collective-permute-start(bf16[2,320,1024]{2,1,0:T(8,128)(2,1)} %bitcast.10), channel_id=1, source_target_pairs={{0,2},{2,0},{1,3},{3,1},{4,6},{6,4},{5,7},{7,5},{8,10},{10,8},{9,1... | collective-permute-start | bytes 3932168 | tf_op jit(solution)/shard_map/instances/ppermute | solution.py:174
  2.9 1.2 %copy.13.trace_ref = bf16[480,320]{1,0:T(8,128)(2,1)S(1)} copy(bf16[480,320]{0,1:T(8,128)(2,1)} %param.18) | data formatting | bytes 614400 | tf_op args[7]
  4.2 0.1 pad_add_fusion.place_ref
  4.2 0.0 copy-start
  4.2 1.3 %copy-done = bf16[1,2,320,1024]{3,2,1,0:T(8,128)(2,1)S(1)} copy-done((bf16[1,2,320,1024]{3,2,1,0:T(8,128)(2,1)S(1)}, bf16[1,2,320,1024]{3,2,1,0:T(8,128)(2,1)}, u32[]{:S(2)}) %copy-start) | copy-done | bytes 1310744
  5.6 0.0 copy-start.8
  5.6 0.0 copy-start.1
  5.6 0.0 copy-start.2
  5.6 0.0 copy-start.3
  5.6 0.0 copy-start.4
  5.6 0.0 copy-start.5
  5.6 0.0 copy-start.6
  5.6 0.0 copy-start.7
  5.6 1.0 %ends.1 = (bf16[2,160,64]{2,1,0:T(8,128)(2,1)S(1)}, bf16[2,160,64]{2,1,0:T(8,128)(2,1)S(1)}, bf16[2,80,64]{2,1,0:T(8,128)(2,1)S(1)}) custom-call(s32[3]{0:T(128)S(1)} %pad_add_fusion.place_ref, bf16[2,320,1024]{2,1,0:T(8,128)(2,1)S(1)} %bitcast.11, bf16[2,320,1024]{2,1,0:T(8,128)(2,1)S(1)} %bitcast.12, bf16[480,320]{1,0:T(8,128)(2,1)S(1)} %copy.13.trace_ref), custom_call_target="tpu_custom_call" | custom-call | flops 104857600 | bytes 1000000 | tf_op jit(solution)/shard_map/ends/ends/pallas_call | solution.py:178
  6.6 2.8 %collective-permute-start.5 = (bf16[2,80,64]{2,1,0:T(8,128)(2,1)S(1)}, bf16[2,80,64]{2,1,0:T(8,128)(2,1)S(1)}, u32[]{:S(2)}, u32[]{:S(2)}) collective-permute-start(bf16[2,80,64]{2,1,0:T(8,128)(2,1)S(1)} %get-tuple-element.12), channel_id=1, source_target_pairs={{0,13},{1,12},{4,1},{5,0},{8,5},{9,4},{12,9},{13,8},{2,15},{3,14},... | collective-permute-start | bytes 61448 | tf_op jit(solution)/shard_map/interface/ppermute | solution.py:201
  9.5 0.0 collective-permute-start.4
  9.5 1.6 %collective-permute-start = (bf16[2,160,64]{2,1,0:T(8,128)(2,1)S(1)}, bf16[2,160,64]{2,1,0:T(8,128)(2,1)S(1)}, u32[]{:S(2)}, u32[]{:S(2)}) collective-permute-start(bf16[2,160,64]{2,1,0:T(8,128)(2,1)S(1)} %get-tuple-element.10), channel_id=1, source_target_pairs={{0,4},{4,8},{8,12},{12,0},{1,5},{5,9},{9,13},{13,1},{2,6},{6,10},{... | collective-permute-start | bytes 122888 | tf_op jit(solution)/shard_map/halo/ppermute | solution.py:198
  11.0 2.2 %collective-permute-start.1 = (bf16[2,160,64]{2,1,0:T(8,128)(2,1)S(1)}, bf16[2,160,64]{2,1,0:T(8,128)(2,1)S(1)}, u32[]{:S(2)}, u32[]{:S(2)}) collective-permute-start(bf16[2,160,64]{2,1,0:T(8,128)(2,1)S(1)} %get-tuple-element.11), channel_id=1, source_target_pairs={{0,12},{4,0},{8,4},{12,8},{1,13},{5,1},{9,5},{13,9},{2,14},{6,2},{... | collective-permute-start | bytes 122888 | tf_op jit(solution)/shard_map/halo/ppermute | solution.py:199
  13.3 0.0 collective-permute-done.5.rest_3_
  13.3 0.0 collective-permute-start.3
  13.3 0.6 %collective-permute-done.4.rest_2_ = bf16[2,80,64]{2,1,0:T(8,128)(2,1)S(1)} collective-permute-done((bf16[2,80,64]{2,1,0:T(8,128)(2,1)S(1)}, bf16[2,80,64]{2,1,0:T(8,128)(2,1)S(1)}, u32[]{:S(2)}, u32[]{:S(2)}) %collective-permute-start.4) | collective-permute-done | bytes 20512 | tf_op jit(solution)/shard_map/interface/ppermute | solution.py:201
  13.9 2.8 %collective-permute-start.2 = (bf16[2,80,64]{2,1,0:T(8,128)(2,1)S(1)}, bf16[2,80,64]{2,1,0:T(8,128)(2,1)S(1)}, u32[]{:S(2)}, u32[]{:S(2)}) collective-permute-start(bf16[2,80,64]{2,1,0:T(8,128)(2,1)S(1)} %get-tuple-element.12), channel_id=1, source_target_pairs={{0,1},{1,0},{4,5},{5,4},{8,9},{9,8},{12,13},{13,12},{2,3},{3,2},{6... | collective-permute-start | bytes 61448 | tf_op jit(solution)/shard_map/interface/ppermute | solution.py:201
  17.4 0.0 copy-done.8
  17.4 1.5 %collective-permute-done.3.rest_1_ = bf16[2,80,64]{2,1,0:T(8,128)(2,1)S(1)} collective-permute-done((bf16[2,80,64]{2,1,0:T(8,128)(2,1)S(1)}, bf16[2,80,64]{2,1,0:T(8,128)(2,1)S(1)}, u32[]{:S(2)}, u32[]{:S(2)}) %collective-permute-start.3) | collective-permute-done | bytes 20512 | tf_op jit(solution)/shard_map/interface/ppermute | solution.py:201
  18.9 0.0 collective-permute-done.2.rest_0_
  18.9 0.0 collective-permute-done.low_ref
  18.9 0.0 collective-permute-done.1.high_ref
  18.9 0.0 copy-done.1
  18.9 0.0 copy-done.2
  19.0 0.0 copy-done.3
  19.0 0.0 copy-done.4
  19.0 0.0 copy-done.5
  19.0 0.0 copy-done.6
  19.0 0.0 copy-done.7
  19.0 10.4 %couple.1 = (f32[2,320,1024]{2,1,0:T(8,128)S(1)}, f32[4,1024]{1,0:T(4,128)S(1)}) custom-call(s32[3]{0:T(128)S(1)} %pad_add_fusion.place_ref, f32[1]{0:T(128)S(6)} %copy.17.freq_ref, f32[4,4]{1,0:T(4,128)S(1)} %copy-done.7, s32[6,1024]{1,0:T(8,128)S(1)} %bitcast.15, s32[2,64]{1,0:T(2,128)S(1)} %bitcast.17, bf16[2,320,1024]{2,1,0:T(8,128)(2,1)S(1)} %bitcast.13, ...), custom_call_target="tpu_custom_call" | custom-call | flops 3690987520 | bytes 6553600 | tf_op jit(solution)/shard_map/couple/couple/pallas_call | solution.py:209
  29.4 2.5 %collective-permute-done.6.rest_0_ = bf16[2,320,1024]{2,1,0:T(8,128)(2,1)S(1)} collective-permute-done((bf16[2,320,1024]{2,1,0:T(8,128)(2,1)}, bf16[2,320,1024]{2,1,0:T(8,128)(2,1)S(1)}, u32[]{:S(2)}, u32[]{:S(2)}) %collective-permute-start.6) | collective-permute-done | bytes 1310752 | tf_op jit(solution)/shard_map/instances/ppermute | solution.py:174
  31.9 1.6 %update.1 = bf16[2,320,1024]{2,1,0:T(8,128)(2,1)} custom-call(f32[2,320,1024]{2,1,0:T(8,128)S(1)} %get-tuple-element.13.ready_ref, f32[4,1024]{1,0:T(4,128)S(1)} %get-tuple-element.14.factor_ref, bf16[320,320]{1,0:T(8,128)(2,1)S(1)} %copy-done.1, bf16[2,320,1024]{2,1,0:T(8,128)(2,1)S(1)} %collective-permute-done.6.rest_0_), custom_call_target="tpu_custom_call" | custom-call | flops 419430400 | bytes 5242880 | tf_op jit(solution)/shard_map/update/update/pallas_call | solution.py:229
  (1 shorter events, 0.0 us)
Async XLA Ops:
  0.0 31.9 %collective-permute-start.6 = (bf16[2,320,1024]{2,1,0:T(8,128)(2,1)}, bf16[2,320,1024]{2,1,0:T(8,128)(2,1)S(1)}, u32[]{:S(2)}, u32[]{:S(2)}) collective-permute-start(bf16[2,320,1024]{2,1,0:T(8,128)(2,1)} %bitcast.10), channel_id=1, source_target_pairs={{0,2},{2,0},{1,3},{3,1},{4,6},{6,4},{5,7},{7,5},{8,10},{10,8},{9,1... | collective-permute-start | bytes 3932168 | tf_op jit(solution)/shard_map/instances/ppermute | solution.py:174
  4.2 1.3 %copy-start = (bf16[1,2,320,1024]{3,2,1,0:T(8,128)(2,1)S(1)}, bf16[1,2,320,1024]{3,2,1,0:T(8,128)(2,1)}, u32[]{:S(2)}) copy-start(bf16[1,2,320,1024]{3,2,1,0:T(8,128)(2,1)} %param.11) | copy-start | bytes 3932164
  5.6 11.8 %copy-start.8 = (s32[1,6,1024]{2,0,1:T(1,128)S(1)}, s32[1,6,1024]{2,0,1:T(1,128)}, u32[]{:S(2)}) copy-start(s32[1,6,1024]{2,0,1:T(1,128)} %param.15) | copy-start | bytes 73732
  5.6 13.4 %copy-start.1 = (bf16[320,320]{1,0:T(8,128)(2,1)S(1)}, bf16[320,320]{1,0:T(8,128)(2,1)}, u32[]{:S(2)}) copy-start(bf16[320,320]{1,0:T(8,128)(2,1)} %inverse_ref.3) | copy-start | bytes 614404
  5.6 13.4 %copy-start.2 = (bf16[1,2,320,1024]{3,2,1,0:T(8,128)(2,1)S(1)}, bf16[1,2,320,1024]{3,2,1,0:T(8,128)(2,1)}, u32[]{:S(2)}) copy-start(bf16[1,2,320,1024]{3,2,1,0:T(8,128)(2,1)} %param.12) | copy-start | bytes 3932164
  5.6 13.4 %copy-start.3 = (bf16[320,480]{1,0:T(8,128)(2,1)S(1)}, bf16[320,480]{1,0:T(8,128)(2,1)}, u32[]{:S(2)}) copy-start(bf16[320,480]{1,0:T(8,128)(2,1)} %lift_ref.1) | copy-start | bytes 921604
  5.6 13.4 %copy-start.4 = (bf16[320,320]{1,0:T(8,128)(2,1)S(1)}, bf16[320,320]{1,0:T(8,128)(2,1)}, u32[]{:S(2)}) copy-start(bf16[320,320]{1,0:T(8,128)(2,1)} %volume_ref.1) | copy-start | bytes 614404
  5.6 13.4 %copy-start.5 = (f32[1,1024]{1,0:T(1,128)S(1)}, f32[1,1024]{1,0:T(1,128)}, u32[]{:S(2)}) copy-start(f32[1,1024]{1,0:T(1,128)} %scale_ref.1) | copy-start | bytes 12292
  5.6 13.4 %copy-start.6 = (s32[1,2,64]{2,1,0:T(2,128)S(1)}, s32[1,2,64]{2,1,0:T(2,128)}, u32[]{:S(2)}) copy-start(s32[1,2,64]{2,1,0:T(2,128)} %param.16) | copy-start | bytes 1540
  5.6 13.4 %copy-start.7 = (f32[4,4]{1,0:T(4,128)S(1)}, f32[4,4]{1,0:T(4,128)}, u32[]{:S(2)}) copy-start(f32[4,4]{1,0:T(4,128)} %constant.13.clone.table_ref) | copy-start | bytes 196
  6.6 6.6 %collective-permute-start.5 = (bf16[2,80,64]{2,1,0:T(8,128)(2,1)S(1)}, bf16[2,80,64]{2,1,0:T(8,128)(2,1)S(1)}, u32[]{:S(2)}, u32[]{:S(2)}) collective-permute-start(bf16[2,80,64]{2,1,0:T(8,128)(2,1)S(1)} %get-tuple-element.12), channel_id=1, source_target_pairs={{0,13},{1,12},{4,1},{5,0},{8,5},{9,4},{12,9},{13,8},{2,15},{3,14},... | collective-permute-start | bytes 61448 | tf_op jit(solution)/shard_map/interface/ppermute | solution.py:201
  9.5 4.5 %collective-permute-start.4 = (bf16[2,80,64]{2,1,0:T(8,128)(2,1)S(1)}, bf16[2,80,64]{2,1,0:T(8,128)(2,1)S(1)}, u32[]{:S(2)}, u32[]{:S(2)}) collective-permute-start(bf16[2,80,64]{2,1,0:T(8,128)(2,1)S(1)} %get-tuple-element.12), channel_id=1, source_target_pairs={{0,9},{1,8},{4,13},{5,12},{8,1},{9,0},{12,5},{13,4},{2,11},{3,10},... | collective-permute-start | bytes 61448 | tf_op jit(solution)/shard_map/interface/ppermute | solution.py:201
  9.5 9.5 %collective-permute-start = (bf16[2,160,64]{2,1,0:T(8,128)(2,1)S(1)}, bf16[2,160,64]{2,1,0:T(8,128)(2,1)S(1)}, u32[]{:S(2)}, u32[]{:S(2)}) collective-permute-start(bf16[2,160,64]{2,1,0:T(8,128)(2,1)S(1)} %get-tuple-element.10), channel_id=1, source_target_pairs={{0,4},{4,8},{8,12},{12,0},{1,5},{5,9},{9,13},{13,1},{2,6},{6,10},{... | collective-permute-start | bytes 122888 | tf_op jit(solution)/shard_map/halo/ppermute | solution.py:198
  11.0 7.9 %collective-permute-start.1 = (bf16[2,160,64]{2,1,0:T(8,128)(2,1)S(1)}, bf16[2,160,64]{2,1,0:T(8,128)(2,1)S(1)}, u32[]{:S(2)}, u32[]{:S(2)}) collective-permute-start(bf16[2,160,64]{2,1,0:T(8,128)(2,1)S(1)} %get-tuple-element.11), channel_id=1, source_target_pairs={{0,12},{4,0},{8,4},{12,8},{1,13},{5,1},{9,5},{13,9},{2,14},{6,2},{... | collective-permute-start | bytes 122888 | tf_op jit(solution)/shard_map/halo/ppermute | solution.py:199
  13.3 5.6 %collective-permute-start.3 = (bf16[2,80,64]{2,1,0:T(8,128)(2,1)S(1)}, bf16[2,80,64]{2,1,0:T(8,128)(2,1)S(1)}, u32[]{:S(2)}, u32[]{:S(2)}) collective-permute-start(bf16[2,80,64]{2,1,0:T(8,128)(2,1)S(1)} %get-tuple-element.12), channel_id=1, source_target_pairs={{0,5},{1,4},{4,9},{5,8},{8,13},{9,12},{12,1},{13,0},{2,7},{3,6},{6... | collective-permute-start | bytes 61448 | tf_op jit(solution)/shard_map/interface/ppermute | solution.py:201
  13.9 5.0 %collective-permute-start.2 = (bf16[2,80,64]{2,1,0:T(8,128)(2,1)S(1)}, bf16[2,80,64]{2,1,0:T(8,128)(2,1)S(1)}, u32[]{:S(2)}, u32[]{:S(2)}) collective-permute-start(bf16[2,80,64]{2,1,0:T(8,128)(2,1)S(1)} %get-tuple-element.12), channel_id=1, source_target_pairs={{0,1},{1,0},{4,5},{5,4},{8,9},{9,8},{12,13},{13,12},{2,3},{3,2},{6... | collective-permute-start | bytes 61448 | tf_op jit(solution)/shard_map/interface/ppermute | solution.py:201

commit v5 on v4

--- a/solution.py
+++ b/solution.py
@@ -129,13 +129,24 @@
         finish(False)
 
 
-def update_kernel(tile, ready_ref, factor_ref, inverse_ref, *rest):
-    others, (out_ref, made, sems) = rest[:-3], rest[-3:]
+def update_kernel(tile, place_ref, ready_ref, factor_ref, inverse_ref, all_ref, out_ref, taken, made, in_sems, sems):
     count, dof, total = ready_ref.shape
+    peers = all_ref.shape[0]
+    steps = total // tile
+    loads = []
+    for t in range(steps):
+        cols = slice(t * tile, (t + 1) * tile)
+        for d in range(1, peers):
+            owner = lax.rem(place_ref[1] - d + peers, peers)
+            load = pltpu.make_async_copy(all_ref.at[owner, :, :, cols], taken.at[t, d - 1], in_sems.at[t, d - 1])
+            load.start()
+            loads.append(load)
     copies = []
-    for t in range(total // tile):
+    for t in range(steps):
         cols = slice(t * tile, (t + 1) * tile)
-        moved = [dot(inverse_ref[...], other[m, :, cols]) for other in others for m in range(count)]
+        for load in loads[t * (peers - 1) : (t + 1) * (peers - 1)]:
+            load.wait()
+        moved = [dot(inverse_ref[...], taken[t, d, m]) for d in range(peers - 1) for m in range(count)]
         for n in range(count):
             value = ready_ref[n, :, cols]
             for k, part in enumerate(moved):
@@ -171,8 +182,7 @@
     bf16 = jnp.bfloat16
 
     with jax.named_scope("instances"):
-        others = [lax.ppermute(current, "inst", [(i, (i + d) % peers) for i in range(peers)])
-                  for d in range(1, peers)]
+        gathered = lax.all_gather(current, "inst")
 
     with jax.named_scope("ends"):
         up, down, cross = pl.pallas_call(
@@ -229,14 +239,16 @@
         result = pl.pallas_call(
             functools.partial(update_kernel, tile),
             out_shape=jax.ShapeDtypeStruct((count, dof, total), bf16),
-            in_specs=[vmem] * (2 + peers),
+            in_specs=[smem, vmem, vmem, vmem, pl.BlockSpec(memory_space=pl.ANY)],
             out_specs=pl.BlockSpec(memory_space=pl.ANY),
-            scratch_shapes=[pltpu.VMEM((steps, count, dof, tile), bf16), pltpu.SemaphoreType.DMA((steps,))],
+            scratch_shapes=[pltpu.VMEM((steps, peers - 1, count, dof, tile), bf16),
+                            pltpu.VMEM((steps, count, dof, tile), bf16),
+                            pltpu.SemaphoreType.DMA((steps, peers - 1)), pltpu.SemaphoreType.DMA((steps,))],
             compiler_params=pltpu.CompilerParams(vmem_limit_bytes=VMEM_LIMIT),
             cost_estimate=pl.CostEstimate(flops=2 * count * total * dof * dof * (peers - 1),
                                           bytes_accessed=count * dof * total * 8, transcendentals=0),
             name="update",
-        )(ready, factors, block_inverse, *others)
+        )(place, ready, factors, block_inverse, gathered)
     return result[None]
 
 

time: 33.8 us -> 64.2 us (1.90)
  waiting for transfers between devices: 4.67 us -> 19.9 us
  between operations: 0.79 us -> 14.2 us
  local copies, waits for them, and re-layouts: 2.58 us -> 6.28 us
  starting transfers between devices: 12.4 us -> 9.08 us
  Pallas kernels: 13.1 us -> 14.3 us
    all_gather x0 -> x1, waiting for transfers between devices: none -> 14.4 us  [body(): gathered = lax.all_gather(current, 'inst')]
    unnamed x20 -> x26, local copies, waits for them, and re-layouts: 2.58 us -> 6.28 us
    ppermute x1 -> x0, starting transfers between devices: 2.94 us -> none  [body(): lax.ppermute(current, 'inst', [(i, (i + d) % peers) for i in range(peers)])]
    ppermute x4, waiting for transfers between devices: 2.16 us -> 4.83 us  [body(): lax.ppermute(cross, ('space', 'row'), [(i * 2 + r, (i + d) % shards * 2 +...]
    ppermute x1 -> x0, waiting for transfers between devices: 2.5 us -> none  [body(): lax.ppermute(current, 'inst', [(i, (i + d) % peers) for i in range(peers)])]
    ppermute x1, starting transfers between devices: 1.57 us -> 0.01 us  [body(): lax.ppermute(up, 'space', [(i, (i + 1) % shards) for i in range(shards)])]
    ppermute x1, starting transfers between devices: 2.25 us -> 3.82 us  [body(): lax.ppermute(down, 'space', [(i, (i - 1) % shards) for i in range(shards)])]
    pallas_call x1, Pallas kernels: 1.64 us -> 2.95 us  [body(): pl.pallas_call(functools.partial(update_kernel, tile), out_shape=jax.Shap...]
  transfers between devices with their start and end apart: 7 -> 7, of which waited for: 3 -> 3; matrix products, arithmetic and copies ran while one was open for 4% -> 2% of each run, Pallas kernels for 34% -> 18%
where the time goes in v5:
time: 64.2 us; the launch traced here: 64 us
  waiting for transfers between devices  19.9 us (31%)
  Pallas kernels  14.3 us (22%)
  between operations  14.2 us (22%)
  starting transfers between devices  9.08 us (14%)
  local copies, waits for them, and re-layouts  6.28 us (10%)
    all_gather x1, waiting for transfers between devices, body(): gathered = lax.all_gather(current, 'inst')  14.4 us
    pallas_call x1, Pallas kernels, body(): pl.pallas_call(functools.partial(couple_kernel, shards, peers), grid=(ste...  10.4 us
    unnamed x26, local copies, waits for them, and re-layouts  6.28 us
    ppermute x4, starting transfers between devices, body(): lax.ppermute(cross, ('space', 'row'), [(i * 2 + r, (i + d) % shards * 2 +...  5.26 us
    ppermute x4, waiting for transfers between devices, body(): lax.ppermute(cross, ('space', 'row'), [(i * 2 + r, (i + d) % shards * 2 +...  4.83 us
    ppermute x1, starting transfers between devices, body(): lax.ppermute(down, 'space', [(i, (i - 1) % shards) for i in range(shards)])  3.82 us
    pallas_call x1, Pallas kernels, body(): pl.pallas_call(functools.partial(update_kernel, tile), out_shape=jax.Shap...  2.95 us
  transfers between devices with their start and end apart: 7, of which 3 were waited for; matrix products, arithmetic and copies ran while one was open for 2% of the time, Pallas kernels for 18%

profile of v5, /device:TPU:0, one launch (start us, length us, event | category | flops | bytes accessed | tf_op | source)
XLA Modules:
  0.0 64.0 jit_solution(9871059366056518902)
XLA Ops:
  6.5 0.0 copy-start
  6.5 0.0 all-gather.2.cloned.1.call-start
  6.5 0.7 %all-gather.2.cloned.1.call-update = ((bf16[1,2,320,1024]{3,2,1,0:T(8,128)(2,1)}), bf16[2,2,320,1024]{3,2,1,0:T(8,128)(2,1)}) async-update(((), (), s32[]{:S(2)}) %all-gather.2.cloned.1.call-start, bf16[1,2,320,1024]{3,2,1,0:T(8,128)(2,1)} %param.11) | async-update | bytes 5242904
  7.3 1.2 %copy.15.trace_ref = bf16[480,320]{1,0:T(8,128)(2,1)S(1)} copy(bf16[480,320]{0,1:T(8,128)(2,1)} %param.18) | data formatting | bytes 614400 | tf_op args[7]
  8.5 0.1 pad_add_fusion.place_ref
  8.6 0.0 copy-done
  8.6 0.0 copy-start.11
  8.6 0.0 copy-start.4
  8.6 0.0 copy-start.5
  8.6 0.0 copy-start.6
  8.6 0.0 copy-start.7
  8.6 0.0 copy-start.8
  8.6 0.0 copy-start.9
  8.6 0.0 copy-start.10
  8.6 1.0 %ends.1 = (bf16[2,160,64]{2,1,0:T(8,128)(2,1)S(1)}, bf16[2,160,64]{2,1,0:T(8,128)(2,1)S(1)}, bf16[2,80,64]{2,1,0:T(8,128)(2,1)S(1)}) custom-call(s32[3]{0:T(128)S(1)} %pad_add_fusion.place_ref, bf16[2,320,1024]{2,1,0:T(8,128)(2,1)S(1)} %bitcast.10, bf16[2,320,1024]{2,1,0:T(8,128)(2,1)S(1)} %bitcast.11, bf16[480,320]{1,0:T(8,128)(2,1)S(1)} %copy.15.trace_ref), custom_call_target="tpu_custom_call" | custom-call | flops 104857600 | bytes 1000000 | tf_op jit(solution)/shard_map/ends/ends/pallas_call | solution.py:188
  9.7 4.5 %collective-permute-start.5 = (bf16[2,80,64]{2,1,0:T(8,128)(2,1)S(1)}, bf16[2,80,64]{2,1,0:T(8,128)(2,1)S(1)}, u32[]{:S(2)}, u32[]{:S(2)}) collective-permute-start(bf16[2,80,64]{2,1,0:T(8,128)(2,1)S(1)} %get-tuple-element.12), channel_id=1, source_target_pairs={{0,13},{1,12},{4,1},{5,0},{8,5},{9,4},{12,9},{13,8},{2,15},{3,14},... | collective-permute-start | bytes 61448 | tf_op jit(solution)/shard_map/interface/ppermute | solution.py:211
  14.2 0.0 collective-permute-start
  14.2 3.8 %collective-permute-start.1 = (bf16[2,160,64]{2,1,0:T(8,128)(2,1)S(1)}, bf16[2,160,64]{2,1,0:T(8,128)(2,1)S(1)}, u32[]{:S(2)}, u32[]{:S(2)}) collective-permute-start(bf16[2,160,64]{2,1,0:T(8,128)(2,1)S(1)} %get-tuple-element.11), channel_id=1, source_target_pairs={{0,12},{4,0},{8,4},{12,8},{1,13},{5,1},{9,5},{13,9},{2,14},{6,2},{... | collective-permute-start | bytes 122888 | tf_op jit(solution)/shard_map/halo/ppermute | solution.py:209
  18.0 0.0 collective-permute-start.4
  18.0 0.3 collective-permute-start.3
  18.3 0.0 collective-permute-done.5.rest_3_
  18.3 0.4 collective-permute-start.2
  19.4 0.0 copy-done.11
  19.4 3.0 %collective-permute-done.4.rest_2_ = bf16[2,80,64]{2,1,0:T(8,128)(2,1)S(1)} collective-permute-done((bf16[2,80,64]{2,1,0:T(8,128)(2,1)S(1)}, bf16[2,80,64]{2,1,0:T(8,128)(2,1)S(1)}, u32[]{:S(2)}, u32[]{:S(2)}) %collective-permute-start.4) | collective-permute-done | bytes 20512 | tf_op jit(solution)/shard_map/interface/ppermute | solution.py:211
  22.5 1.8 %collective-permute-done.3.rest_1_ = bf16[2,80,64]{2,1,0:T(8,128)(2,1)S(1)} collective-permute-done((bf16[2,80,64]{2,1,0:T(8,128)(2,1)S(1)}, bf16[2,80,64]{2,1,0:T(8,128)(2,1)S(1)}, u32[]{:S(2)}, u32[]{:S(2)}) %collective-permute-start.3) | collective-permute-done | bytes 20512 | tf_op jit(solution)/shard_map/interface/ppermute | solution.py:211
  24.3 0.0 collective-permute-done.2.rest_0_
  24.3 0.0 collective-permute-done.low_ref
  24.3 0.0 collective-permute-done.1.high_ref
  24.3 0.0 copy-done.4
  24.3 0.0 copy-done.5
  24.3 0.0 copy-done.6
  24.3 0.0 copy-done.7
  24.3 0.0 copy-done.8
  24.3 0.0 copy-done.9
  24.3 0.0 copy-done.10
  24.3 10.4 %couple.1 = (f32[2,320,1024]{2,1,0:T(8,128)S(1)}, f32[4,1024]{1,0:T(4,128)S(1)}) custom-call(s32[3]{0:T(128)S(1)} %pad_add_fusion.place_ref, f32[1]{0:T(128)S(6)} %copy.19.freq_ref, f32[4,4]{1,0:T(4,128)S(1)} %copy-done.10, s32[6,1024]{1,0:T(8,128)S(1)} %bitcast.14, s32[2,64]{1,0:T(2,128)S(1)} %bitcast.16, bf16[2,320,1024]{2,1,0:T(8,128)(2,1)S(1)} %bitcast.12, ...), custom_call_target="tpu_custom_call" | custom-call | flops 3690987520 | bytes 6553600 | tf_op jit(solution)/shard_map/couple/couple/pallas_call | solution.py:219
  34.7 0.0 copy-start.2
  34.7 1.5 %copy-done.2 = f32[2,320,1024]{2,1,0:T(8,128)} copy-done((f32[2,320,1024]{2,1,0:T(8,128)}, f32[2,320,1024]{2,1,0:T(8,128)S(1)}, u32[]{:S(2)}) %copy-start.2) | copy-done | bytes 2621464
  36.3 14.4 %all-gather.2.cloned.1.call-done.all_ref = bf16[2,2,320,1024]{3,2,1,0:T(8,128)(2,1)} async-done(((bf16[1,2,320,1024]{3,2,1,0:T(8,128)(2,1)}), bf16[2,2,320,1024]{3,2,1,0:T(8,128)(2,1)}) %all-gather.2.cloned.1.call-update) | async-done | bytes 2621456 | tf_op jit(solution)/shard_map/instances/all_gather | solution.py:185
  50.7 0.0 copy-start.1
  50.7 1.7 %copy-done.1 = bf16[2,2,320,1024]{3,2,1,0:T(8,128)(2,1)S(1)} copy-done((bf16[2,2,320,1024]{3,2,1,0:T(8,128)(2,1)S(1)}, bf16[2,2,320,1024]{3,2,1,0:T(8,128)(2,1)}, u32[]{:S(2)}) %copy-start.1) | copy-done | bytes 2621464
  52.4 0.0 copy-start.3
  52.4 1.7 %copy-done.3 = f32[2,320,1024]{2,1,0:T(8,128)S(1)} copy-done((f32[2,320,1024]{2,1,0:T(8,128)S(1)}, f32[2,320,1024]{2,1,0:T(8,128)}, u32[]{:S(2)}) %copy-start.3) | copy-done | bytes 2621464
  54.2 3.0 %update.1 = bf16[2,320,1024]{2,1,0:T(8,128)(2,1)} custom-call(s32[3]{0:T(128)S(1)} %pad_add_fusion.place_ref, f32[2,320,1024]{2,1,0:T(8,128)S(1)} %copy-done.3, f32[4,1024]{1,0:T(4,128)S(1)} %get-tuple-element.14.factor_ref, bf16[320,320]{1,0:T(8,128)(2,1)S(1)} %copy-done.4, bf16[2,2,320,1024]{3,2,1,0:T(8,128)(2,1)S(1)} %copy-done.1), custom_call_target="tpu_custom_call" | custom-call | flops 419430400 | bytes 5242880 | tf_op jit(solution)/shard_map/update/update/pallas_call | solution.py:239
  (1 shorter events, 0.0 us)
Async XLA Ops:
  6.5 2.0 %copy-start = (bf16[1,2,320,1024]{3,2,1,0:T(8,128)(2,1)S(1)}, bf16[1,2,320,1024]{3,2,1,0:T(8,128)(2,1)}, u32[]{:S(2)}) copy-start(bf16[1,2,320,1024]{3,2,1,0:T(8,128)(2,1)} %param.11) | copy-start | bytes 3932164
  6.5 44.1 %all-gather.2.cloned.1.call-start = ((), (), s32[]{:S(2)}) async-start(), calls=%async_computation | async-start | bytes 3932160 | tf_op jit(solution)/shard_map/instances/all_gather | solution.py:185
  8.6 10.8 %copy-start.11 = (s32[1,6,1024]{2,0,1:T(1,128)S(1)}, s32[1,6,1024]{2,0,1:T(1,128)}, u32[]{:S(2)}) copy-start(s32[1,6,1024]{2,0,1:T(1,128)} %param.15) | copy-start | bytes 73732
  8.6 15.7 %copy-start.4 = (bf16[320,320]{1,0:T(8,128)(2,1)S(1)}, bf16[320,320]{1,0:T(8,128)(2,1)}, u32[]{:S(2)}) copy-start(bf16[320,320]{1,0:T(8,128)(2,1)} %inverse_ref.3) | copy-start | bytes 614404
  8.6 15.7 %copy-start.5 = (bf16[1,2,320,1024]{3,2,1,0:T(8,128)(2,1)S(1)}, bf16[1,2,320,1024]{3,2,1,0:T(8,128)(2,1)}, u32[]{:S(2)}) copy-start(bf16[1,2,320,1024]{3,2,1,0:T(8,128)(2,1)} %param.12) | copy-start | bytes 3932164
  8.6 15.7 %copy-start.6 = (bf16[320,480]{1,0:T(8,128)(2,1)S(1)}, bf16[320,480]{1,0:T(8,128)(2,1)}, u32[]{:S(2)}) copy-start(bf16[320,480]{1,0:T(8,128)(2,1)} %lift_ref.1) | copy-start | bytes 921604
  8.6 15.7 %copy-start.7 = (bf16[320,320]{1,0:T(8,128)(2,1)S(1)}, bf16[320,320]{1,0:T(8,128)(2,1)}, u32[]{:S(2)}) copy-start(bf16[320,320]{1,0:T(8,128)(2,1)} %volume_ref.1) | copy-start | bytes 614404
  8.6 15.7 %copy-start.8 = (f32[1,1024]{1,0:T(1,128)S(1)}, f32[1,1024]{1,0:T(1,128)}, u32[]{:S(2)}) copy-start(f32[1,1024]{1,0:T(1,128)} %scale_ref.1) | copy-start | bytes 12292
  8.6 15.7 %copy-start.9 = (s32[1,2,64]{2,1,0:T(2,128)S(1)}, s32[1,2,64]{2,1,0:T(2,128)}, u32[]{:S(2)}) copy-start(s32[1,2,64]{2,1,0:T(2,128)} %param.16) | copy-start | bytes 1540
  8.6 15.7 %copy-start.10 = (f32[4,4]{1,0:T(4,128)S(1)}, f32[4,4]{1,0:T(4,128)}, u32[]{:S(2)}) copy-start(f32[4,4]{1,0:T(4,128)} %constant.13.clone.table_ref) | copy-start | bytes 196
  9.7 8.7 %collective-permute-start.5 = (bf16[2,80,64]{2,1,0:T(8,128)(2,1)S(1)}, bf16[2,80,64]{2,1,0:T(8,128)(2,1)S(1)}, u32[]{:S(2)}, u32[]{:S(2)}) collective-permute-start(bf16[2,80,64]{2,1,0:T(8,128)(2,1)S(1)} %get-tuple-element.12), channel_id=1, source_target_pairs={{0,13},{1,12},{4,1},{5,0},{8,5},{9,4},{12,9},{13,8},{2,15},{3,14},... | collective-permute-start | bytes 61448 | tf_op jit(solution)/shard_map/interface/ppermute | solution.py:211
  14.2 10.1 %collective-permute-start = (bf16[2,160,64]{2,1,0:T(8,128)(2,1)S(1)}, bf16[2,160,64]{2,1,0:T(8,128)(2,1)S(1)}, u32[]{:S(2)}, u32[]{:S(2)}) collective-permute-start(bf16[2,160,64]{2,1,0:T(8,128)(2,1)S(1)} %get-tuple-element.10), channel_id=1, source_target_pairs={{0,4},{4,8},{8,12},{12,0},{1,5},{5,9},{9,13},{13,1},{2,6},{6,10},{... | collective-permute-start | bytes 122888 | tf_op jit(solution)/shard_map/halo/ppermute | solution.py:208
  14.2 10.1 %collective-permute-start.1 = (bf16[2,160,64]{2,1,0:T(8,128)(2,1)S(1)}, bf16[2,160,64]{2,1,0:T(8,128)(2,1)S(1)}, u32[]{:S(2)}, u32[]{:S(2)}) collective-permute-start(bf16[2,160,64]{2,1,0:T(8,128)(2,1)S(1)} %get-tuple-element.11), channel_id=1, source_target_pairs={{0,12},{4,0},{8,4},{12,8},{1,13},{5,1},{9,5},{13,9},{2,14},{6,2},{... | collective-permute-start | bytes 122888 | tf_op jit(solution)/shard_map/halo/ppermute | solution.py:209
  18.0 4.4 %collective-permute-start.4 = (bf16[2,80,64]{2,1,0:T(8,128)(2,1)S(1)}, bf16[2,80,64]{2,1,0:T(8,128)(2,1)S(1)}, u32[]{:S(2)}, u32[]{:S(2)}) collective-permute-start(bf16[2,80,64]{2,1,0:T(8,128)(2,1)S(1)} %get-tuple-element.12), channel_id=1, source_target_pairs={{0,9},{1,8},{4,13},{5,12},{8,1},{9,0},{12,5},{13,4},{2,11},{3,10},... | collective-permute-start | bytes 61448 | tf_op jit(solution)/shard_map/interface/ppermute | solution.py:211
  18.0 6.2 %collective-permute-start.3 = (bf16[2,80,64]{2,1,0:T(8,128)(2,1)S(1)}, bf16[2,80,64]{2,1,0:T(8,128)(2,1)S(1)}, u32[]{:S(2)}, u32[]{:S(2)}) collective-permute-start(bf16[2,80,64]{2,1,0:T(8,128)(2,1)S(1)} %get-tuple-element.12), channel_id=1, source_target_pairs={{0,5},{1,4},{4,9},{5,8},{8,13},{9,12},{12,1},{13,0},{2,7},{3,6},{6... | collective-permute-start | bytes 61448 | tf_op jit(solution)/shard_map/interface/ppermute | solution.py:211
  18.3 5.9 %collective-permute-start.2 = (bf16[2,80,64]{2,1,0:T(8,128)(2,1)S(1)}, bf16[2,80,64]{2,1,0:T(8,128)(2,1)S(1)}, u32[]{:S(2)}, u32[]{:S(2)}) collective-permute-start(bf16[2,80,64]{2,1,0:T(8,128)(2,1)S(1)} %get-tuple-element.12), channel_id=1, source_target_pairs={{0,1},{1,0},{4,5},{5,4},{8,9},{9,8},{12,13},{13,12},{2,3},{3,2},{6... | collective-permute-start | bytes 61448 | tf_op jit(solution)/shard_map/interface/ppermute | solution.py:211
  34.7 1.5 %copy-start.2 = (f32[2,320,1024]{2,1,0:T(8,128)}, f32[2,320,1024]{2,1,0:T(8,128)S(1)}, u32[]{:S(2)}) copy-start(f32[2,320,1024]{2,1,0:T(8,128)S(1)} %get-tuple-element.13.ready_ref) | copy-start | bytes 7864324
  50.7 1.7 %copy-start.1 = (bf16[2,2,320,1024]{3,2,1,0:T(8,128)(2,1)S(1)}, bf16[2,2,320,1024]{3,2,1,0:T(8,128)(2,1)}, u32[]{:S(2)}) copy-start(bf16[2,2,320,1024]{3,2,1,0:T(8,128)(2,1)} %all-gather.2.cloned.1.call-done.all_ref) | copy-start | bytes 7864324
  52.4 1.7 %copy-start.3 = (f32[2,320,1024]{2,1,0:T(8,128)S(1)}, f32[2,320,1024]{2,1,0:T(8,128)}, u32[]{:S(2)}) copy-start(f32[2,320,1024]{2,1,0:T(8,128)} %copy-done.2) | copy-start | bytes 7864324
Sparse Core Ops, SparseCore 0:
  8.9 41.7 all-gather.1

commit v6 on v4

--- a/solution.py
+++ b/solution.py
@@ -129,20 +129,22 @@
         finish(False)
 
 
-def update_kernel(tile, ready_ref, factor_ref, inverse_ref, *rest):
+def update_kernel(tile, parts, ready_ref, factor_ref, inverse_ref, *rest):
     others, (out_ref, made, sems) = rest[:-3], rest[-3:]
     count, dof, total = ready_ref.shape
     copies = []
-    for t in range(total // tile):
-        cols = slice(t * tile, (t + 1) * tile)
-        moved = [dot(inverse_ref[...], other[m, :, cols]) for other in others for m in range(count)]
-        for n in range(count):
-            value = ready_ref[n, :, cols]
-            for k, part in enumerate(moved):
-                at = n * len(moved) + k
-                value -= factor_ref[at : at + 1, cols] * part
-            made[t, n] = value.astype(jnp.bfloat16)
-        copy = pltpu.make_async_copy(made.at[t], out_ref.at[:, :, cols], sems.at[t])
+    for p in range(parts):
+        whole_part = slice(p * total // parts, (p + 1) * total // parts)
+        for start in range(whole_part.start, whole_part.stop, tile):
+            cols = slice(start, start + tile)
+            moved = [dot(inverse_ref[...], other[m, :, cols]) for other in others for m in range(count)]
+            for n in range(count):
+                value = ready_ref[n, :, cols]
+                for k, part in enumerate(moved):
+                    at = n * len(moved) + k
+                    value -= factor_ref[at : at + 1, cols] * part
+                made[n, :, cols] = value.astype(jnp.bfloat16)
+        copy = pltpu.make_async_copy(made.at[:, :, whole_part], out_ref.at[:, :, whole_part], sems.at[p])
         copy.start()
         copies.append(copy)
     for copy in copies:
@@ -225,13 +227,14 @@
           trace_matrix, lift_matrix, volume_matrix, block_inverse, low, high, *pieces)
 
     vmem = pl.BlockSpec(memory_space=pltpu.VMEM)
+    parts = 2
     with jax.named_scope("update"):
         result = pl.pallas_call(
-            functools.partial(update_kernel, tile),
+            functools.partial(update_kernel, tile, parts),
             out_shape=jax.ShapeDtypeStruct((count, dof, total), bf16),
             in_specs=[vmem] * (2 + peers),
             out_specs=pl.BlockSpec(memory_space=pl.ANY),
-            scratch_shapes=[pltpu.VMEM((steps, count, dof, tile), bf16), pltpu.SemaphoreType.DMA((steps,))],
+            scratch_shapes=[pltpu.VMEM((count, dof, total), bf16), pltpu.SemaphoreType.DMA((parts,))],
             compiler_params=pltpu.CompilerParams(vmem_limit_bytes=VMEM_LIMIT),
             cost_estimate=pl.CostEstimate(flops=2 * count * total * dof * dof * (peers - 1),
                                           bytes_accessed=count * dof * total * 8, transcendentals=0),

time: 33.8 us -> 33.9 us (level)
  no operation moved by 1% of the time
where the time goes in v6:
time: 33.9 us; the launch traced here: 33.7 us
  Pallas kernels  13.2 us (39%)
  starting transfers between devices  12.4 us (37%)
  waiting for transfers between devices  4.67 us (14%)
  local copies, waits for them, and re-layouts  2.58 us (8%)
  between operations  0.79 us (2%)
    pallas_call x1, Pallas kernels, body(): pl.pallas_call(functools.partial(couple_kernel, shards, peers), grid=(ste...  10.4 us
    ppermute x4, starting transfers between devices, body(): lax.ppermute(cross, ('space', 'row'), [(i * 2 + r, (i + d) % shards * 2 +...  5.62 us
    ppermute x1, starting transfers between devices, body(): lax.ppermute(current, 'inst', [(i, (i + d) % peers) for i in range(peers)])  2.94 us
    unnamed x20, local copies, waits for them, and re-layouts  2.58 us
    ppermute x1, waiting for transfers between devices, body(): lax.ppermute(current, 'inst', [(i, (i + d) % peers) for i in range(peers)])  2.5 us
    ppermute x1, starting transfers between devices, body(): lax.ppermute(down, 'space', [(i, (i - 1) % shards) for i in range(shards)])  2.25 us
    ppermute x4, waiting for transfers between devices, body(): lax.ppermute(cross, ('space', 'row'), [(i * 2 + r, (i + d) % shards * 2 +...  2.16 us
    pallas_call x1, Pallas kernels, body(): pl.pallas_call(functools.partial(update_kernel, tile, parts), out_shape=j...  1.74 us
  transfers between devices with their start and end apart: 7, of which 3 were waited for; matrix products, arithmetic and copies ran while one was open for 4% of the time, Pallas kernels for 34%

profile of v6, /device:TPU:0, one launch (start us, length us, event | category | flops | bytes accessed | tf_op | source)
XLA Modules:
  0.0 33.7 jit_solution(13423210344972679446)
XLA Ops:
  0.0 2.9 %collective-permute-start.6 = (bf16[2,320,1024]{2,1,0:T(8,128)(2,1)}, bf16[2,320,1024]{2,1,0:T(8,128)(2,1)S(1)}, u32[]{:S(2)}, u32[]{:S(2)}) collective-permute-start(bf16[2,320,1024]{2,1,0:T(8,128)(2,1)} %bitcast.10), channel_id=1, source_target_pairs={{0,2},{2,0},{1,3},{3,1},{4,6},{6,4},{5,7},{7,5},{8,10},{10,8},{9,1... | collective-permute-start | bytes 3932168 | tf_op jit(solution)/shard_map/instances/ppermute | solution.py:176
  2.9 1.2 %copy.13.trace_ref = bf16[480,320]{1,0:T(8,128)(2,1)S(1)} copy(bf16[480,320]{0,1:T(8,128)(2,1)} %param.18) | data formatting | bytes 614400 | tf_op args[7]
  4.2 0.1 pad_add_fusion.place_ref
  4.2 0.0 copy-start
  4.2 1.3 %copy-done = bf16[1,2,320,1024]{3,2,1,0:T(8,128)(2,1)S(1)} copy-done((bf16[1,2,320,1024]{3,2,1,0:T(8,128)(2,1)S(1)}, bf16[1,2,320,1024]{3,2,1,0:T(8,128)(2,1)}, u32[]{:S(2)}) %copy-start) | copy-done | bytes 1310744
  5.6 0.0 copy-start.8
  5.6 0.0 copy-start.1
  5.6 0.0 copy-start.2
  5.6 0.0 copy-start.3
  5.6 0.0 copy-start.4
  5.6 0.0 copy-start.5
  5.6 0.0 copy-start.6
  5.6 0.0 copy-start.7
  5.6 1.0 %ends.1 = (bf16[2,160,64]{2,1,0:T(8,128)(2,1)S(1)}, bf16[2,160,64]{2,1,0:T(8,128)(2,1)S(1)}, bf16[2,80,64]{2,1,0:T(8,128)(2,1)S(1)}) custom-call(s32[3]{0:T(128)S(1)} %pad_add_fusion.place_ref, bf16[2,320,1024]{2,1,0:T(8,128)(2,1)S(1)} %bitcast.11, bf16[2,320,1024]{2,1,0:T(8,128)(2,1)S(1)} %bitcast.12, bf16[480,320]{1,0:T(8,128)(2,1)S(1)} %copy.13.trace_ref), custom_call_target="tpu_custom_call" | custom-call | flops 104857600 | bytes 1000000 | tf_op jit(solution)/shard_map/ends/ends/pallas_call | solution.py:180
  6.6 2.8 %collective-permute-start.5 = (bf16[2,80,64]{2,1,0:T(8,128)(2,1)S(1)}, bf16[2,80,64]{2,1,0:T(8,128)(2,1)S(1)}, u32[]{:S(2)}, u32[]{:S(2)}) collective-permute-start(bf16[2,80,64]{2,1,0:T(8,128)(2,1)S(1)} %get-tuple-element.12), channel_id=1, source_target_pairs={{0,13},{1,12},{4,1},{5,0},{8,5},{9,4},{12,9},{13,8},{2,15},{3,14},... | collective-permute-start | bytes 61448 | tf_op jit(solution)/shard_map/interface/ppermute | solution.py:203
  9.5 0.0 collective-permute-start.4
  9.5 1.6 %collective-permute-start = (bf16[2,160,64]{2,1,0:T(8,128)(2,1)S(1)}, bf16[2,160,64]{2,1,0:T(8,128)(2,1)S(1)}, u32[]{:S(2)}, u32[]{:S(2)}) collective-permute-start(bf16[2,160,64]{2,1,0:T(8,128)(2,1)S(1)} %get-tuple-element.10), channel_id=1, source_target_pairs={{0,4},{4,8},{8,12},{12,0},{1,5},{5,9},{9,13},{13,1},{2,6},{6,10},{... | collective-permute-start | bytes 122888 | tf_op jit(solution)/shard_map/halo/ppermute | solution.py:200
  11.0 2.2 %collective-permute-start.1 = (bf16[2,160,64]{2,1,0:T(8,128)(2,1)S(1)}, bf16[2,160,64]{2,1,0:T(8,128)(2,1)S(1)}, u32[]{:S(2)}, u32[]{:S(2)}) collective-permute-start(bf16[2,160,64]{2,1,0:T(8,128)(2,1)S(1)} %get-tuple-element.11), channel_id=1, source_target_pairs={{0,12},{4,0},{8,4},{12,8},{1,13},{5,1},{9,5},{13,9},{2,14},{6,2},{... | collective-permute-start | bytes 122888 | tf_op jit(solution)/shard_map/halo/ppermute | solution.py:201
  13.3 0.0 collective-permute-done.5.rest_3_
  13.3 0.0 collective-permute-start.3
  13.3 0.6 %collective-permute-done.4.rest_2_ = bf16[2,80,64]{2,1,0:T(8,128)(2,1)S(1)} collective-permute-done((bf16[2,80,64]{2,1,0:T(8,128)(2,1)S(1)}, bf16[2,80,64]{2,1,0:T(8,128)(2,1)S(1)}, u32[]{:S(2)}, u32[]{:S(2)}) %collective-permute-start.4) | collective-permute-done | bytes 20512 | tf_op jit(solution)/shard_map/interface/ppermute | solution.py:203
  13.9 2.8 %collective-permute-start.2 = (bf16[2,80,64]{2,1,0:T(8,128)(2,1)S(1)}, bf16[2,80,64]{2,1,0:T(8,128)(2,1)S(1)}, u32[]{:S(2)}, u32[]{:S(2)}) collective-permute-start(bf16[2,80,64]{2,1,0:T(8,128)(2,1)S(1)} %get-tuple-element.12), channel_id=1, source_target_pairs={{0,1},{1,0},{4,5},{5,4},{8,9},{9,8},{12,13},{13,12},{2,3},{3,2},{6... | collective-permute-start | bytes 61448 | tf_op jit(solution)/shard_map/interface/ppermute | solution.py:203
  17.4 0.0 copy-done.8
  17.4 1.5 %collective-permute-done.3.rest_1_ = bf16[2,80,64]{2,1,0:T(8,128)(2,1)S(1)} collective-permute-done((bf16[2,80,64]{2,1,0:T(8,128)(2,1)S(1)}, bf16[2,80,64]{2,1,0:T(8,128)(2,1)S(1)}, u32[]{:S(2)}, u32[]{:S(2)}) %collective-permute-start.3) | collective-permute-done | bytes 20512 | tf_op jit(solution)/shard_map/interface/ppermute | solution.py:203
  18.9 0.0 collective-permute-done.2.rest_0_
  18.9 0.0 collective-permute-done.low_ref
  18.9 0.0 collective-permute-done.1.high_ref
  18.9 0.0 copy-done.1
  18.9 0.0 copy-done.2
  19.0 0.0 copy-done.3
  19.0 0.0 copy-done.4
  19.0 0.0 copy-done.5
  19.0 0.0 copy-done.6
  19.0 0.0 copy-done.7
  19.0 10.4 %couple.1 = (f32[2,320,1024]{2,1,0:T(8,128)S(1)}, f32[4,1024]{1,0:T(4,128)S(1)}) custom-call(s32[3]{0:T(128)S(1)} %pad_add_fusion.place_ref, f32[1]{0:T(128)S(6)} %copy.17.freq_ref, f32[4,4]{1,0:T(4,128)S(1)} %copy-done.7, s32[6,1024]{1,0:T(8,128)S(1)} %bitcast.15, s32[2,64]{1,0:T(2,128)S(1)} %bitcast.17, bf16[2,320,1024]{2,1,0:T(8,128)(2,1)S(1)} %bitcast.13, ...), custom_call_target="tpu_custom_call" | custom-call | flops 3690987520 | bytes 6553600 | tf_op jit(solution)/shard_map/couple/couple/pallas_call | solution.py:211
  29.4 2.5 %collective-permute-done.6.rest_0_ = bf16[2,320,1024]{2,1,0:T(8,128)(2,1)S(1)} collective-permute-done((bf16[2,320,1024]{2,1,0:T(8,128)(2,1)}, bf16[2,320,1024]{2,1,0:T(8,128)(2,1)S(1)}, u32[]{:S(2)}, u32[]{:S(2)}) %collective-permute-start.6) | collective-permute-done | bytes 1310752 | tf_op jit(solution)/shard_map/instances/ppermute | solution.py:176
  31.9 1.7 %update.1 = bf16[2,320,1024]{2,1,0:T(8,128)(2,1)} custom-call(f32[2,320,1024]{2,1,0:T(8,128)S(1)} %get-tuple-element.13.ready_ref, f32[4,1024]{1,0:T(4,128)S(1)} %get-tuple-element.14.factor_ref, bf16[320,320]{1,0:T(8,128)(2,1)S(1)} %copy-done.1, bf16[2,320,1024]{2,1,0:T(8,128)(2,1)S(1)} %collective-permute-done.6.rest_0_), custom_call_target="tpu_custom_call" | custom-call | flops 419430400 | bytes 5242880 | tf_op jit(solution)/shard_map/update/update/pallas_call | solution.py:232
  (1 shorter events, 0.0 us)
Async XLA Ops:
  0.0 31.9 %collective-permute-start.6 = (bf16[2,320,1024]{2,1,0:T(8,128)(2,1)}, bf16[2,320,1024]{2,1,0:T(8,128)(2,1)S(1)}, u32[]{:S(2)}, u32[]{:S(2)}) collective-permute-start(bf16[2,320,1024]{2,1,0:T(8,128)(2,1)} %bitcast.10), channel_id=1, source_target_pairs={{0,2},{2,0},{1,3},{3,1},{4,6},{6,4},{5,7},{7,5},{8,10},{10,8},{9,1... | collective-permute-start | bytes 3932168 | tf_op jit(solution)/shard_map/instances/ppermute | solution.py:176
  4.2 1.3 %copy-start = (bf16[1,2,320,1024]{3,2,1,0:T(8,128)(2,1)S(1)}, bf16[1,2,320,1024]{3,2,1,0:T(8,128)(2,1)}, u32[]{:S(2)}) copy-start(bf16[1,2,320,1024]{3,2,1,0:T(8,128)(2,1)} %param.11) | copy-start | bytes 3932164
  5.6 11.8 %copy-start.8 = (s32[1,6,1024]{2,0,1:T(1,128)S(1)}, s32[1,6,1024]{2,0,1:T(1,128)}, u32[]{:S(2)}) copy-start(s32[1,6,1024]{2,0,1:T(1,128)} %param.15) | copy-start | bytes 73732
  5.6 13.4 %copy-start.1 = (bf16[320,320]{1,0:T(8,128)(2,1)S(1)}, bf16[320,320]{1,0:T(8,128)(2,1)}, u32[]{:S(2)}) copy-start(bf16[320,320]{1,0:T(8,128)(2,1)} %inverse_ref.3) | copy-start | bytes 614404
  5.6 13.4 %copy-start.2 = (bf16[1,2,320,1024]{3,2,1,0:T(8,128)(2,1)S(1)}, bf16[1,2,320,1024]{3,2,1,0:T(8,128)(2,1)}, u32[]{:S(2)}) copy-start(bf16[1,2,320,1024]{3,2,1,0:T(8,128)(2,1)} %param.12) | copy-start | bytes 3932164
  5.6 13.4 %copy-start.3 = (bf16[320,480]{1,0:T(8,128)(2,1)S(1)}, bf16[320,480]{1,0:T(8,128)(2,1)}, u32[]{:S(2)}) copy-start(bf16[320,480]{1,0:T(8,128)(2,1)} %lift_ref.1) | copy-start | bytes 921604
  5.6 13.4 %copy-start.4 = (bf16[320,320]{1,0:T(8,128)(2,1)S(1)}, bf16[320,320]{1,0:T(8,128)(2,1)}, u32[]{:S(2)}) copy-start(bf16[320,320]{1,0:T(8,128)(2,1)} %volume_ref.1) | copy-start | bytes 614404
  5.6 13.4 %copy-start.5 = (f32[1,1024]{1,0:T(1,128)S(1)}, f32[1,1024]{1,0:T(1,128)}, u32[]{:S(2)}) copy-start(f32[1,1024]{1,0:T(1,128)} %scale_ref.1) | copy-start | bytes 12292
  5.6 13.4 %copy-start.6 = (s32[1,2,64]{2,1,0:T(2,128)S(1)}, s32[1,2,64]{2,1,0:T(2,128)}, u32[]{:S(2)}) copy-start(s32[1,2,64]{2,1,0:T(2,128)} %param.16) | copy-start | bytes 1540
  5.6 13.4 %copy-start.7 = (f32[4,4]{1,0:T(4,128)S(1)}, f32[4,4]{1,0:T(4,128)}, u32[]{:S(2)}) copy-start(f32[4,4]{1,0:T(4,128)} %constant.13.clone.table_ref) | copy-start | bytes 196
  6.6 6.6 %collective-permute-start.5 = (bf16[2,80,64]{2,1,0:T(8,128)(2,1)S(1)}, bf16[2,80,64]{2,1,0:T(8,128)(2,1)S(1)}, u32[]{:S(2)}, u32[]{:S(2)}) collective-permute-start(bf16[2,80,64]{2,1,0:T(8,128)(2,1)S(1)} %get-tuple-element.12), channel_id=1, source_target_pairs={{0,13},{1,12},{4,1},{5,0},{8,5},{9,4},{12,9},{13,8},{2,15},{3,14},... | collective-permute-start | bytes 61448 | tf_op jit(solution)/shard_map/interface/ppermute | solution.py:203
  9.5 4.5 %collective-permute-start.4 = (bf16[2,80,64]{2,1,0:T(8,128)(2,1)S(1)}, bf16[2,80,64]{2,1,0:T(8,128)(2,1)S(1)}, u32[]{:S(2)}, u32[]{:S(2)}) collective-permute-start(bf16[2,80,64]{2,1,0:T(8,128)(2,1)S(1)} %get-tuple-element.12), channel_id=1, source_target_pairs={{0,9},{1,8},{4,13},{5,12},{8,1},{9,0},{12,5},{13,4},{2,11},{3,10},... | collective-permute-start | bytes 61448 | tf_op jit(solution)/shard_map/interface/ppermute | solution.py:203
  9.5 9.5 %collective-permute-start = (bf16[2,160,64]{2,1,0:T(8,128)(2,1)S(1)}, bf16[2,160,64]{2,1,0:T(8,128)(2,1)S(1)}, u32[]{:S(2)}, u32[]{:S(2)}) collective-permute-start(bf16[2,160,64]{2,1,0:T(8,128)(2,1)S(1)} %get-tuple-element.10), channel_id=1, source_target_pairs={{0,4},{4,8},{8,12},{12,0},{1,5},{5,9},{9,13},{13,1},{2,6},{6,10},{... | collective-permute-start | bytes 122888 | tf_op jit(solution)/shard_map/halo/ppermute | solution.py:200
  11.0 7.9 %collective-permute-start.1 = (bf16[2,160,64]{2,1,0:T(8,128)(2,1)S(1)}, bf16[2,160,64]{2,1,0:T(8,128)(2,1)S(1)}, u32[]{:S(2)}, u32[]{:S(2)}) collective-permute-start(bf16[2,160,64]{2,1,0:T(8,128)(2,1)S(1)} %get-tuple-element.11), channel_id=1, source_target_pairs={{0,12},{4,0},{8,4},{12,8},{1,13},{5,1},{9,5},{13,9},{2,14},{6,2},{... | collective-permute-start | bytes 122888 | tf_op jit(solution)/shard_map/halo/ppermute | solution.py:201
  13.3 5.6 %collective-permute-start.3 = (bf16[2,80,64]{2,1,0:T(8,128)(2,1)S(1)}, bf16[2,80,64]{2,1,0:T(8,128)(2,1)S(1)}, u32[]{:S(2)}, u32[]{:S(2)}) collective-permute-start(bf16[2,80,64]{2,1,0:T(8,128)(2,1)S(1)} %get-tuple-element.12), channel_id=1, source_target_pairs={{0,5},{1,4},{4,9},{5,8},{8,13},{9,12},{12,1},{13,0},{2,7},{3,6},{6... | collective-permute-start | bytes 61448 | tf_op jit(solution)/shard_map/interface/ppermute | solution.py:203
  13.9 5.0 %collective-permute-start.2 = (bf16[2,80,64]{2,1,0:T(8,128)(2,1)S(1)}, bf16[2,80,64]{2,1,0:T(8,128)(2,1)S(1)}, u32[]{:S(2)}, u32[]{:S(2)}) collective-permute-start(bf16[2,80,64]{2,1,0:T(8,128)(2,1)S(1)} %get-tuple-element.12), channel_id=1, source_target_pairs={{0,1},{1,0},{4,5},{5,4},{8,9},{9,8},{12,13},{13,12},{2,3},{3,2},{6... | collective-permute-start | bytes 61448 | tf_op jit(solution)/shard_map/interface/ppermute | solution.py:203

commit v7 on v4

--- a/solution.py
+++ b/solution.py
@@ -107,7 +107,8 @@
             for d in range(1, peers):
                 owner = lax.rem(inst - d + peers, peers)
                 for m in range(count):
-                    weight = table_ref[inst * count + n, owner * count + m] * frequency
+                    instance = lax.rem(inst + m, count) if paired(peers, count) else m
+                    weight = table_ref[inst * count + n, owner * count + instance] * frequency
                     at = (n * (peers - 1) + d - 1) * count + m
                     factor_ref[at : at + 1, :] = weight * inverse_scale
         for n in range(count):
@@ -129,7 +130,35 @@
         finish(False)
 
 
-def update_kernel(tile, ready_ref, factor_ref, inverse_ref, *rest):
+def fold_kernel(tile, place_ref, ready_ref, factor_ref, inverse_ref, other_ref, out_ref):
+    count, dof, total = ready_ref.shape
+    slot = 1 - place_ref[1]
+    for t in range(total // tile):
+        cols = slice(t * tile, (t + 1) * tile)
+        moved = dot(inverse_ref[...], other_ref[slot, :, cols])
+        for n in range(count):
+            at = n * count
+            out_ref[n, :, cols] = ready_ref[n, :, cols] - factor_ref[at : at + 1, cols] * moved
+
+
+def update_kernel(tile, place_ref, ready_ref, factor_ref, inverse_ref, other_ref, out_ref, made, sems):
+    count, dof, total = ready_ref.shape
+    slot = place_ref[1]
+    copies = []
+    for t in range(total // tile):
+        cols = slice(t * tile, (t + 1) * tile)
+        moved = dot(inverse_ref[...], other_ref[slot, :, cols])
+        for n in range(count):
+            at = n * count + 1
+            made[t, n] = (ready_ref[n, :, cols] - factor_ref[at : at + 1, cols] * moved).astype(jnp.bfloat16)
+        copy = pltpu.make_async_copy(made.at[t], out_ref.at[:, :, cols], sems.at[t])
+        copy.start()
+        copies.append(copy)
+    for copy in copies:
+        copy.wait()
+
+
+def ring_update_kernel(tile, ready_ref, factor_ref, inverse_ref, *rest):
     others, (out_ref, made, sems) = rest[:-3], rest[-3:]
     count, dof, total = ready_ref.shape
     copies = []
@@ -147,6 +176,10 @@
         copies.append(copy)
     for copy in copies:
         copy.wait()
+
+
+def paired(peers, count):
+    return peers == 2 and count == 2
 
 
 def whole(array):
@@ -171,8 +204,12 @@
     bf16 = jnp.bfloat16
 
     with jax.named_scope("instances"):
-        others = [lax.ppermute(current, "inst", [(i, (i + d) % peers) for i in range(peers)])
-                  for d in range(1, peers)]
+        if paired(peers, count):
+            others = [lax.all_to_all(current, "inst", split_axis=0, concat_axis=0, tiled=True, axis_index_groups=order)
+                      for order in ([[0, 1]], [[1, 0]])]
+        else:
+            others = [lax.ppermute(current, "inst", [(i, (i + d) % peers) for i in range(peers)])
+                      for d in range(1, peers)]
 
     with jax.named_scope("ends"):
         up, down, cross = pl.pallas_call(
@@ -225,18 +262,32 @@
           trace_matrix, lift_matrix, volume_matrix, block_inverse, low, high, *pieces)
 
     vmem = pl.BlockSpec(memory_space=pltpu.VMEM)
+    half = pl.CostEstimate(flops=count * total * dof * dof, bytes_accessed=count * dof * total * 4, transcendentals=0)
     with jax.named_scope("update"):
+        if paired(peers, count):
+            folded = pl.pallas_call(
+                functools.partial(fold_kernel, tile),
+                out_shape=jax.ShapeDtypeStruct((count, dof, total), jnp.float32),
+                in_specs=[smem] + [vmem] * 4,
+                out_specs=vmem,
+                input_output_aliases={1: 0},
+                compiler_params=pltpu.CompilerParams(vmem_limit_bytes=VMEM_LIMIT),
+                cost_estimate=half,
+                name="fold",
+            )(place, ready, factors, block_inverse, others[0])
+            kernel, operands = update_kernel, (place, folded, factors, block_inverse, others[1])
+        else:
+            kernel, operands = ring_update_kernel, (ready, factors, block_inverse, *others)
         result = pl.pallas_call(
-            functools.partial(update_kernel, tile),
+            functools.partial(kernel, tile),
             out_shape=jax.ShapeDtypeStruct((count, dof, total), bf16),
-            in_specs=[vmem] * (2 + peers),
+            in_specs=([smem] + [vmem] * 4) if paired(peers, count) else [vmem] * (2 + peers),
             out_specs=pl.BlockSpec(memory_space=pl.ANY),
             scratch_shapes=[pltpu.VMEM((steps, count, dof, tile), bf16), pltpu.SemaphoreType.DMA((steps,))],
             compiler_params=pltpu.CompilerParams(vmem_limit_bytes=VMEM_LIMIT),
-            cost_estimate=pl.CostEstimate(flops=2 * count * total * dof * dof * (peers - 1),
-                                          bytes_accessed=count * dof * total * 8, transcendentals=0),
+            cost_estimate=half,
             name="update",
-        )(ready, factors, block_inverse, *others)
+        )(*operands)
     return result[None]
 
 

time: 33.8 us -> 56.6 us (1.67)
  blocking collectives: 0 us -> 22.4 us
  waiting for transfers between devices: 4.67 us -> 3.07 us
  Pallas kernels: 13.1 us -> 14.7 us
  local copies, waits for them, and re-layouts: 2.58 us -> 3.54 us
  starting transfers between devices: 12.4 us -> 11.7 us
    all_to_all x0 -> x1, blocking collectives: none -> 22.4 us  [body(): lax.all_to_all(current, 'inst', split_axis=0, concat_axis=0, tiled=True,...]
    all_to_all x0 -> x1, starting transfers between devices: none -> 3.75 us  [body(): lax.all_to_all(current, 'inst', split_axis=0, concat_axis=0, tiled=True,...]
    ppermute x1 -> x0, starting transfers between devices: 2.94 us -> none  [body(): lax.ppermute(current, 'inst', [(i, (i + d) % peers) for i in range(peers)])]
    ppermute x1 -> x0, waiting for transfers between devices: 2.5 us -> none  [body(): lax.ppermute(current, 'inst', [(i, (i + d) % peers) for i in range(peers)])]
    ppermute x4, starting transfers between devices: 5.62 us -> 3.62 us  [body(): lax.ppermute(cross, ('space', 'row'), [(i * 2 + r, (i + d) % shards * 2 +...]
    pallas_call x1 -> x2, Pallas kernels: 1.64 us -> 3.33 us  [the longest x1 2 us: body(): pl.pallas_call(functools.partial(kernel, tile), out_shape=jax.ShapeDtypeS...]
    unnamed x20 -> x28, local copies, waits for them, and re-layouts: 2.58 us -> 3.54 us
    ppermute x4, waiting for transfers between devices: 2.16 us -> 3.07 us  [body(): lax.ppermute(cross, ('space', 'row'), [(i * 2 + r, (i + d) % shards * 2 +...]
  transfers between devices with their start and end apart: 7 -> 7, of which waited for: 3 -> 2; matrix products, arithmetic and copies ran while one was open for 4% -> 1% of each run, Pallas kernels for 34% -> 23%
where the time goes in v7:
time: 56.6 us; the launch traced here: 56.3 us
  blocking collectives  22.4 us (40%)
  Pallas kernels  14.7 us (26%)
  starting transfers between devices  11.7 us (21%)
  local copies, waits for them, and re-layouts  3.54 us (6%)
  waiting for transfers between devices  3.07 us (5%)
  between operations  0.85 us (2%)
    all_to_all x1, blocking collectives, body(): lax.all_to_all(current, 'inst', split_axis=0, concat_axis=0, tiled=True,...  22.4 us
    pallas_call x1, Pallas kernels, body(): pl.pallas_call(functools.partial(couple_kernel, shards, peers), grid=(ste...  10.4 us
    all_to_all x1, starting transfers between devices, body(): lax.all_to_all(current, 'inst', split_axis=0, concat_axis=0, tiled=True,...  3.75 us
    ppermute x4, starting transfers between devices, body(): lax.ppermute(cross, ('space', 'row'), [(i * 2 + r, (i + d) % shards * 2 +...  3.62 us
    unnamed x28, local copies, waits for them, and re-layouts  3.54 us
    ppermute x4, waiting for transfers between devices, body(): lax.ppermute(cross, ('space', 'row'), [(i * 2 + r, (i + d) % shards * 2 +...  3.07 us
    ppermute x1, starting transfers between devices, body(): lax.ppermute(up, 'space', [(i, (i + 1) % shards) for i in range(shards)])  2.17 us
    ppermute x1, starting transfers between devices, body(): lax.ppermute(down, 'space', [(i, (i - 1) % shards) for i in range(shards)])  2.11 us
  transfers between devices with their start and end apart: 7, of which 2 were waited for; matrix products, arithmetic and copies ran while one was open for 1% of the time, Pallas kernels for 23%

profile of v7, /device:TPU:0, one launch (start us, length us, event | category | flops | bytes accessed | tf_op | source)
XLA Modules:
  0.0 56.3 jit_solution(10010227241221152851)
XLA Ops:
  0.0 22.4 %all_to_all.10.other_ref = bf16[2,320,1024]{2,1,0:T(8,128)(2,1)} all-to-all(bf16[2,320,1024]{2,1,0:T(8,128)(2,1)} %bitcast.10), channel_id=1, replica_groups={{0,2},{1,3},{4,6},{5,7},{8,10},{9,11},{12,14},{13,15},{16,18},{17,19},{..., dimensions={0} | all-to-all | bytes 2621440 | tf_op jit(solution)/shard_map/instances/all_to_all | solution.py:208
  22.4 0.0 copy-start.11
  22.4 0.0 copy-start
  22.4 3.8 %all-to-all-start.1 = ((bf16[2,320,1024]{2,1,0:T(8,128)(2,1)}), bf16[2,320,1024]{2,1,0:T(8,128)(2,1)S(1)}, u32[]{:S(2)}, u32[]{:S(2)}) async-start(bf16[2,320,1024]{2,1,0:T(8,128)(2,1)} %bitcast.11), calls=%async_computation.1 | async-start | bytes 2621440 | tf_op jit(solution)/shard_map/instances/all_to_all | solution.py:208
  26.1 0.0 copy-done.11
  26.1 0.2 copy.14.trace_ref
  26.4 0.1 pad_add_fusion.place_ref
  26.5 0.0 copy-done
  26.5 0.0 copy-start.12
  26.5 0.0 copy-start.4
  26.5 0.0 copy-start.5
  26.5 0.0 copy-start.6
  26.5 0.0 copy-start.7
  26.5 0.0 copy-start.8
  26.5 0.0 copy-start.9
  26.5 0.0 copy-start.10
  26.6 1.0 %ends.1 = (bf16[2,160,64]{2,1,0:T(8,128)(2,1)S(1)}, bf16[2,160,64]{2,1,0:T(8,128)(2,1)S(1)}, bf16[2,80,64]{2,1,0:T(8,128)(2,1)S(1)}) custom-call(s32[3]{0:T(128)S(1)} %pad_add_fusion.place_ref, bf16[2,320,1024]{2,1,0:T(8,128)(2,1)S(1)} %bitcast.12, bf16[2,320,1024]{2,1,0:T(8,128)(2,1)S(1)} %bitcast.13, bf16[480,320]{1,0:T(8,128)(2,1)S(1)} %copy.14.trace_ref), custom_call_target="tpu_custom_call" | custom-call | flops 104857600 | bytes 1000000 | tf_op jit(solution)/shard_map/ends/ends/pallas_call | solution.py:215
  27.6 0.1 collective-permute-start.2
  27.7 2.2 %collective-permute-start = (bf16[2,160,64]{2,1,0:T(8,128)(2,1)S(1)}, bf16[2,160,64]{2,1,0:T(8,128)(2,1)S(1)}, u32[]{:S(2)}, u32[]{:S(2)}) collective-permute-start(bf16[2,160,64]{2,1,0:T(8,128)(2,1)S(1)} %get-tuple-element.10), channel_id=1, source_target_pairs={{0,4},{4,8},{8,12},{12,0},{1,5},{5,9},{9,13},{13,1},{2,6},{6,10},{... | collective-permute-start | bytes 122888 | tf_op jit(solution)/shard_map/halo/ppermute | solution.py:235
  29.8 2.1 %collective-permute-start.1 = (bf16[2,160,64]{2,1,0:T(8,128)(2,1)S(1)}, bf16[2,160,64]{2,1,0:T(8,128)(2,1)S(1)}, u32[]{:S(2)}, u32[]{:S(2)}) collective-permute-start(bf16[2,160,64]{2,1,0:T(8,128)(2,1)S(1)} %get-tuple-element.11), channel_id=1, source_target_pairs={{0,12},{4,0},{8,4},{12,8},{1,13},{5,1},{9,5},{13,9},{2,14},{6,2},{... | collective-permute-start | bytes 122888 | tf_op jit(solution)/shard_map/halo/ppermute | solution.py:236
  31.9 0.0 collective-permute-start.3
  31.9 2.2 %collective-permute-start.4 = (bf16[2,80,64]{2,1,0:T(8,128)(2,1)S(1)}, bf16[2,80,64]{2,1,0:T(8,128)(2,1)S(1)}, u32[]{:S(2)}, u32[]{:S(2)}) collective-permute-start(bf16[2,80,64]{2,1,0:T(8,128)(2,1)S(1)} %get-tuple-element.12), channel_id=1, source_target_pairs={{0,9},{1,8},{4,13},{5,12},{8,1},{9,0},{12,5},{13,4},{2,11},{3,10},... | collective-permute-start | bytes 61448 | tf_op jit(solution)/shard_map/interface/ppermute | solution.py:238
  34.2 0.0 collective-permute-done.2.rest_0_
  34.2 1.3 %collective-permute-start.5 = (bf16[2,80,64]{2,1,0:T(8,128)(2,1)S(1)}, bf16[2,80,64]{2,1,0:T(8,128)(2,1)S(1)}, u32[]{:S(2)}, u32[]{:S(2)}) collective-permute-start(bf16[2,80,64]{2,1,0:T(8,128)(2,1)S(1)} %get-tuple-element.12), channel_id=1, source_target_pairs={{0,13},{1,12},{4,1},{5,0},{8,5},{9,4},{12,9},{13,8},{2,15},{3,14},... | collective-permute-start | bytes 61448 | tf_op jit(solution)/shard_map/interface/ppermute | solution.py:238
  35.5 0.0 copy-done.12
  36.1 1.3 %collective-permute-done.3.rest_1_ = bf16[2,80,64]{2,1,0:T(8,128)(2,1)S(1)} collective-permute-done((bf16[2,80,64]{2,1,0:T(8,128)(2,1)S(1)}, bf16[2,80,64]{2,1,0:T(8,128)(2,1)S(1)}, u32[]{:S(2)}, u32[]{:S(2)}) %collective-permute-start.3) | collective-permute-done | bytes 20512 | tf_op jit(solution)/shard_map/interface/ppermute | solution.py:238
  37.5 1.7 %collective-permute-done.4.rest_2_ = bf16[2,80,64]{2,1,0:T(8,128)(2,1)S(1)} collective-permute-done((bf16[2,80,64]{2,1,0:T(8,128)(2,1)S(1)}, bf16[2,80,64]{2,1,0:T(8,128)(2,1)S(1)}, u32[]{:S(2)}, u32[]{:S(2)}) %collective-permute-start.4) | collective-permute-done | bytes 20512 | tf_op jit(solution)/shard_map/interface/ppermute | solution.py:238
  39.2 0.0 collective-permute-done.5.rest_3_
  39.2 0.0 collective-permute-done.low_ref
  39.2 0.0 collective-permute-done.1.high_ref
  39.2 0.0 copy-done.4
  39.2 0.0 copy-done.5
  39.2 0.0 copy-done.6
  39.3 0.0 copy-done.7
  39.3 0.0 copy-done.8
  39.3 0.0 copy-done.9
  39.3 0.0 copy-done.10
  39.3 0.0 copy-start.3
  39.3 10.4 %couple.1 = (f32[2,320,1024]{2,1,0:T(8,128)S(1)}, f32[4,1024]{1,0:T(4,128)S(1)}) custom-call(s32[3]{0:T(128)S(1)} %pad_add_fusion.place_ref, f32[1]{0:T(128)S(6)} %copy.19.freq_ref, f32[4,4]{1,0:T(4,128)S(1)} %copy-done.10, s32[6,1024]{1,0:T(8,128)S(1)} %bitcast.16, s32[2,64]{1,0:T(2,128)S(1)} %bitcast.18, bf16[2,320,1024]{2,1,0:T(8,128)(2,1)S(1)} %bitcast.14, ...), custom_call_target="tpu_custom_call" | custom-call | flops 3690987520 | bytes 6553600 | tf_op jit(solution)/shard_map/couple/couple/pallas_call | solution.py:246
  49.7 0.0 copy-done.3
  49.7 1.3 %fold.1.ready_ref = f32[2,320,1024]{2,1,0:T(8,128)S(1)} custom-call(s32[3]{0:T(128)S(1)} %pad_add_fusion.place_ref, f32[2,320,1024]{2,1,0:T(8,128)S(1)} %get-tuple-element.13.ready_ref, f32[4,1024]{1,0:T(4,128)S(1)} %get-tuple-element.14.factor_ref, bf16[320,320]{1,0:T(8,128)(2,1)S(1)} %copy-done.4, ...), custom_call_target="tpu_custom_call", output_to_operand_aliasing={{}: (1, {})} | custom-call | flops 209715200 | bytes 2621440 | tf_op jit(solution)/shard_map/update/fold/pallas_call | solution.py:268
  51.0 0.0 copy-start.1
  51.0 1.5 %copy-done.1 = f32[2,320,1024]{2,1,0:T(8,128)} copy-done((f32[2,320,1024]{2,1,0:T(8,128)}, f32[2,320,1024]{2,1,0:T(8,128)S(1)}, u32[]{:S(2)}) %copy-start.1) | copy-done | bytes 2621464
  52.5 0.0 all-to-all-done.1.other_ref
  52.5 0.0 copy-start.2
  52.5 1.7 %copy-done.2 = f32[2,320,1024]{2,1,0:T(8,128)S(1)} copy-done((f32[2,320,1024]{2,1,0:T(8,128)S(1)}, f32[2,320,1024]{2,1,0:T(8,128)}, u32[]{:S(2)}) %copy-start.2) | copy-done | bytes 2621464
  54.3 2.0 %update.1 = bf16[2,320,1024]{2,1,0:T(8,128)(2,1)} custom-call(s32[3]{0:T(128)S(1)} %pad_add_fusion.place_ref, f32[2,320,1024]{2,1,0:T(8,128)S(1)} %copy-done.2, f32[4,1024]{1,0:T(4,128)S(1)} %get-tuple-element.14.factor_ref, bf16[320,320]{1,0:T(8,128)(2,1)S(1)} %copy-done.4, bf16[2,320,1024]{2,1,0:T(8,128)(2,1)S(1)} %all-to-all-done.1.other_ref), custom_call_target="tpu_custom_call" | custom-call | flops 209715200 | bytes 2621440 | tf_op jit(solution)/shard_map/update/update/pallas_call | solution.py:281
  (1 shorter events, 0.0 us)
Async XLA Ops:
  22.4 3.8 %copy-start.11 = (bf16[480,320]{0,1:T(8,128)(2,1)S(1)}, bf16[480,320]{0,1:T(8,128)(2,1)}, u32[]{:S(2)}) copy-start(bf16[480,320]{0,1:T(8,128)(2,1)} %param.18) | copy-start | bytes 921604
  22.4 4.1 %copy-start = (bf16[1,2,320,1024]{3,2,1,0:T(8,128)(2,1)S(1)}, bf16[1,2,320,1024]{3,2,1,0:T(8,128)(2,1)}, u32[]{:S(2)}) copy-start(bf16[1,2,320,1024]{3,2,1,0:T(8,128)(2,1)} %param.11) | copy-start | bytes 3932164
  22.4 30.2 %all-to-all-start.1 = ((bf16[2,320,1024]{2,1,0:T(8,128)(2,1)}), bf16[2,320,1024]{2,1,0:T(8,128)(2,1)S(1)}, u32[]{:S(2)}, u32[]{:S(2)}) async-start(bf16[2,320,1024]{2,1,0:T(8,128)(2,1)} %bitcast.11), calls=%async_computation.1 | async-start | bytes 2621440 | tf_op jit(solution)/shard_map/instances/all_to_all | solution.py:208
  26.5 9.0 %copy-start.12 = (s32[1,6,1024]{2,0,1:T(1,128)S(1)}, s32[1,6,1024]{2,0,1:T(1,128)}, u32[]{:S(2)}) copy-start(s32[1,6,1024]{2,0,1:T(1,128)} %param.15) | copy-start | bytes 73732
  26.5 12.7 %copy-start.4 = (bf16[320,320]{1,0:T(8,128)(2,1)S(1)}, bf16[320,320]{1,0:T(8,128)(2,1)}, u32[]{:S(2)}) copy-start(bf16[320,320]{1,0:T(8,128)(2,1)} %inverse_ref.5) | copy-start | bytes 614404
  26.5 12.8 %copy-start.5 = (bf16[1,2,320,1024]{3,2,1,0:T(8,128)(2,1)S(1)}, bf16[1,2,320,1024]{3,2,1,0:T(8,128)(2,1)}, u32[]{:S(2)}) copy-start(bf16[1,2,320,1024]{3,2,1,0:T(8,128)(2,1)} %param.12) | copy-start | bytes 3932164
  26.5 12.8 %copy-start.6 = (bf16[320,480]{1,0:T(8,128)(2,1)S(1)}, bf16[320,480]{1,0:T(8,128)(2,1)}, u32[]{:S(2)}) copy-start(bf16[320,480]{1,0:T(8,128)(2,1)} %lift_ref.1) | copy-start | bytes 921604
  26.5 12.8 %copy-start.7 = (bf16[320,320]{1,0:T(8,128)(2,1)S(1)}, bf16[320,320]{1,0:T(8,128)(2,1)}, u32[]{:S(2)}) copy-start(bf16[320,320]{1,0:T(8,128)(2,1)} %volume_ref.1) | copy-start | bytes 614404
  26.5 12.8 %copy-start.8 = (f32[1,1024]{1,0:T(1,128)S(1)}, f32[1,1024]{1,0:T(1,128)}, u32[]{:S(2)}) copy-start(f32[1,1024]{1,0:T(1,128)} %scale_ref.1) | copy-start | bytes 12292
  26.5 12.7 %copy-start.9 = (s32[1,2,64]{2,1,0:T(2,128)S(1)}, s32[1,2,64]{2,1,0:T(2,128)}, u32[]{:S(2)}) copy-start(s32[1,2,64]{2,1,0:T(2,128)} %param.16) | copy-start | bytes 1540
  26.5 12.7 %copy-start.10 = (f32[4,4]{1,0:T(4,128)S(1)}, f32[4,4]{1,0:T(4,128)}, u32[]{:S(2)}) copy-start(f32[4,4]{1,0:T(4,128)} %constant.13.clone.table_ref) | copy-start | bytes 196
  27.6 6.6 %collective-permute-start.2 = (bf16[2,80,64]{2,1,0:T(8,128)(2,1)S(1)}, bf16[2,80,64]{2,1,0:T(8,128)(2,1)S(1)}, u32[]{:S(2)}, u32[]{:S(2)}) collective-permute-start(bf16[2,80,64]{2,1,0:T(8,128)(2,1)S(1)} %get-tuple-element.12), channel_id=1, source_target_pairs={{0,1},{1,0},{4,5},{5,4},{8,9},{9,8},{12,13},{13,12},{2,3},{3,2},{6... | collective-permute-start | bytes 61448 | tf_op jit(solution)/shard_map/interface/ppermute | solution.py:238
  27.7 11.6 %collective-permute-start = (bf16[2,160,64]{2,1,0:T(8,128)(2,1)S(1)}, bf16[2,160,64]{2,1,0:T(8,128)(2,1)S(1)}, u32[]{:S(2)}, u32[]{:S(2)}) collective-permute-start(bf16[2,160,64]{2,1,0:T(8,128)(2,1)S(1)} %get-tuple-element.10), channel_id=1, source_target_pairs={{0,4},{4,8},{8,12},{12,0},{1,5},{5,9},{9,13},{13,1},{2,6},{6,10},{... | collective-permute-start | bytes 122888 | tf_op jit(solution)/shard_map/halo/ppermute | solution.py:235
  29.8 9.4 %collective-permute-start.1 = (bf16[2,160,64]{2,1,0:T(8,128)(2,1)S(1)}, bf16[2,160,64]{2,1,0:T(8,128)(2,1)S(1)}, u32[]{:S(2)}, u32[]{:S(2)}) collective-permute-start(bf16[2,160,64]{2,1,0:T(8,128)(2,1)S(1)} %get-tuple-element.11), channel_id=1, source_target_pairs={{0,12},{4,0},{8,4},{12,8},{1,13},{5,1},{9,5},{13,9},{2,14},{6,2},{... | collective-permute-start | bytes 122888 | tf_op jit(solution)/shard_map/halo/ppermute | solution.py:236
  31.9 5.5 %collective-permute-start.3 = (bf16[2,80,64]{2,1,0:T(8,128)(2,1)S(1)}, bf16[2,80,64]{2,1,0:T(8,128)(2,1)S(1)}, u32[]{:S(2)}, u32[]{:S(2)}) collective-permute-start(bf16[2,80,64]{2,1,0:T(8,128)(2,1)S(1)} %get-tuple-element.12), channel_id=1, source_target_pairs={{0,5},{1,4},{4,9},{5,8},{8,13},{9,12},{12,1},{13,0},{2,7},{3,6},{6... | collective-permute-start | bytes 61448 | tf_op jit(solution)/shard_map/interface/ppermute | solution.py:238
  31.9 7.3 %collective-permute-start.4 = (bf16[2,80,64]{2,1,0:T(8,128)(2,1)S(1)}, bf16[2,80,64]{2,1,0:T(8,128)(2,1)S(1)}, u32[]{:S(2)}, u32[]{:S(2)}) collective-permute-start(bf16[2,80,64]{2,1,0:T(8,128)(2,1)S(1)} %get-tuple-element.12), channel_id=1, source_target_pairs={{0,9},{1,8},{4,13},{5,12},{8,1},{9,0},{12,5},{13,4},{2,11},{3,10},... | collective-permute-start | bytes 61448 | tf_op jit(solution)/shard_map/interface/ppermute | solution.py:238
  34.2 5.1 %collective-permute-start.5 = (bf16[2,80,64]{2,1,0:T(8,128)(2,1)S(1)}, bf16[2,80,64]{2,1,0:T(8,128)(2,1)S(1)}, u32[]{:S(2)}, u32[]{:S(2)}) collective-permute-start(bf16[2,80,64]{2,1,0:T(8,128)(2,1)S(1)} %get-tuple-element.12), channel_id=1, source_target_pairs={{0,13},{1,12},{4,1},{5,0},{8,5},{9,4},{12,9},{13,8},{2,15},{3,14},... | collective-permute-start | bytes 61448 | tf_op jit(solution)/shard_map/interface/ppermute | solution.py:238
  39.3 10.4 %copy-start.3 = (bf16[2,320,1024]{2,1,0:T(8,128)(2,1)S(1)}, bf16[2,320,1024]{2,1,0:T(8,128)(2,1)}, u32[]{:S(2)}) copy-start(bf16[2,320,1024]{2,1,0:T(8,128)(2,1)} %all_to_all.10.other_ref) | copy-start | bytes 3932164
  51.0 1.5 %copy-start.1 = (f32[2,320,1024]{2,1,0:T(8,128)}, f32[2,320,1024]{2,1,0:T(8,128)S(1)}, u32[]{:S(2)}) copy-start(f32[2,320,1024]{2,1,0:T(8,128)S(1)} %fold.1.ready_ref) | copy-start | bytes 7864324
  52.5 1.7 %copy-start.2 = (f32[2,320,1024]{2,1,0:T(8,128)S(1)}, f32[2,320,1024]{2,1,0:T(8,128)}, u32[]{:S(2)}) copy-start(f32[2,320,1024]{2,1,0:T(8,128)} %copy-done.1) | copy-start | bytes 7864324

commit v8 on v4

--- a/solution.py
+++ b/solution.py
@@ -129,22 +129,22 @@
         finish(False)
 
 
-def update_kernel(tile, ready_ref, factor_ref, inverse_ref, *rest):
+def update_kernel(cuts, ready_ref, factor_ref, inverse_ref, *rest):
     others, (out_ref, made, sems) = rest[:-3], rest[-3:]
-    count, dof, total = ready_ref.shape
+    count = ready_ref.shape[0]
     copies = []
-    for t in range(total // tile):
-        cols = slice(t * tile, (t + 1) * tile)
+    for t, (first, last) in enumerate(zip(cuts[:-1], cuts[1:])):
+        cols = slice(first, last)
         moved = [dot(inverse_ref[...], other[m, :, cols]) for other in others for m in range(count)]
         for n in range(count):
             value = ready_ref[n, :, cols]
             for k, part in enumerate(moved):
                 at = n * len(moved) + k
                 value -= factor_ref[at : at + 1, cols] * part
-            made[t, n] = value.astype(jnp.bfloat16)
-        copy = pltpu.make_async_copy(made.at[t], out_ref.at[:, :, cols], sems.at[t])
-        copy.start()
-        copies.append(copy)
+            made[n, :, cols] = value.astype(jnp.bfloat16)
+            copy = pltpu.make_async_copy(made.at[n, :, cols], out_ref.at[n, :, cols], sems.at[t, n])
+            copy.start()
+            copies.append(copy)
     for copy in copies:
         copy.wait()
 
@@ -225,13 +225,15 @@
           trace_matrix, lift_matrix, volume_matrix, block_inverse, low, high, *pieces)
 
     vmem = pl.BlockSpec(memory_space=pltpu.VMEM)
+    cuts = [0] + list(range(tile // 2, total, tile)) + [total]
     with jax.named_scope("update"):
         result = pl.pallas_call(
-            functools.partial(update_kernel, tile),
+            functools.partial(update_kernel, cuts),
             out_shape=jax.ShapeDtypeStruct((count, dof, total), bf16),
             in_specs=[vmem] * (2 + peers),
             out_specs=pl.BlockSpec(memory_space=pl.ANY),
-            scratch_shapes=[pltpu.VMEM((steps, count, dof, tile), bf16), pltpu.SemaphoreType.DMA((steps,))],
+            scratch_shapes=[pltpu.VMEM((count, dof, total), bf16),
+                            pltpu.SemaphoreType.DMA((len(cuts) - 1, count))],
             compiler_params=pltpu.CompilerParams(vmem_limit_bytes=VMEM_LIMIT),
             cost_estimate=pl.CostEstimate(flops=2 * count * total * dof * dof * (peers - 1),
                                           bytes_accessed=count * dof * total * 8, transcendentals=0),

time: 33.8 us -> 34.1 us (level)
    pallas_call x1, Pallas kernels: 1.64 us -> 2.03 us  [body(): pl.pallas_call(functools.partial(update_kernel, cuts), out_shape=jax.Shap...]
where the time goes in v8:
time: 34.1 us; the launch traced here: 34 us
  Pallas kernels  13.4 us (39%)
  starting transfers between devices  12.4 us (36%)
  waiting for transfers between devices  4.67 us (14%)
  local copies, waits for them, and re-layouts  2.58 us (8%)
  between operations  0.79 us (2%)
    pallas_call x1, Pallas kernels, body(): pl.pallas_call(functools.partial(couple_kernel, shards, peers), grid=(ste...  10.4 us
    ppermute x4, starting transfers between devices, body(): lax.ppermute(cross, ('space', 'row'), [(i * 2 + r, (i + d) % shards * 2 +...  5.62 us
    ppermute x1, starting transfers between devices, body(): lax.ppermute(current, 'inst', [(i, (i + d) % peers) for i in range(peers)])  2.94 us
    unnamed x20, local copies, waits for them, and re-layouts  2.58 us
    ppermute x1, waiting for transfers between devices, body(): lax.ppermute(current, 'inst', [(i, (i + d) % peers) for i in range(peers)])  2.5 us
    ppermute x1, starting transfers between devices, body(): lax.ppermute(down, 'space', [(i, (i - 1) % shards) for i in range(shards)])  2.25 us
    ppermute x4, waiting for transfers between devices, body(): lax.ppermute(cross, ('space', 'row'), [(i * 2 + r, (i + d) % shards * 2 +...  2.16 us
    pallas_call x1, Pallas kernels, body(): pl.pallas_call(functools.partial(update_kernel, cuts), out_shape=jax.Shap...  2.03 us
  transfers between devices with their start and end apart: 7, of which 3 were waited for; matrix products, arithmetic and copies ran while one was open for 4% of the time, Pallas kernels for 34%

profile of v8, /device:TPU:0, one launch (start us, length us, event | category | flops | bytes accessed | tf_op | source)
XLA Modules:
  0.0 34.0 jit_solution(1890759358105422979)
XLA Ops:
  0.0 2.9 %collective-permute-start.6 = (bf16[2,320,1024]{2,1,0:T(8,128)(2,1)}, bf16[2,320,1024]{2,1,0:T(8,128)(2,1)S(1)}, u32[]{:S(2)}, u32[]{:S(2)}) collective-permute-start(bf16[2,320,1024]{2,1,0:T(8,128)(2,1)} %bitcast.10), channel_id=1, source_target_pairs={{0,2},{2,0},{1,3},{3,1},{4,6},{6,4},{5,7},{7,5},{8,10},{10,8},{9,1... | collective-permute-start | bytes 3932168 | tf_op jit(solution)/shard_map/instances/ppermute | solution.py:174
  2.9 1.2 %copy.13.trace_ref = bf16[480,320]{1,0:T(8,128)(2,1)S(1)} copy(bf16[480,320]{0,1:T(8,128)(2,1)} %param.18) | data formatting | bytes 614400 | tf_op args[7]
  4.2 0.1 pad_add_fusion.place_ref
  4.2 0.0 copy-start
  4.2 1.3 %copy-done = bf16[1,2,320,1024]{3,2,1,0:T(8,128)(2,1)S(1)} copy-done((bf16[1,2,320,1024]{3,2,1,0:T(8,128)(2,1)S(1)}, bf16[1,2,320,1024]{3,2,1,0:T(8,128)(2,1)}, u32[]{:S(2)}) %copy-start) | copy-done | bytes 1310744
  5.6 0.0 copy-start.8
  5.6 0.0 copy-start.1
  5.6 0.0 copy-start.2
  5.6 0.0 copy-start.3
  5.6 0.0 copy-start.4
  5.6 0.0 copy-start.5
  5.6 0.0 copy-start.6
  5.6 0.0 copy-start.7
  5.6 1.0 %ends.1 = (bf16[2,160,64]{2,1,0:T(8,128)(2,1)S(1)}, bf16[2,160,64]{2,1,0:T(8,128)(2,1)S(1)}, bf16[2,80,64]{2,1,0:T(8,128)(2,1)S(1)}) custom-call(s32[3]{0:T(128)S(1)} %pad_add_fusion.place_ref, bf16[2,320,1024]{2,1,0:T(8,128)(2,1)S(1)} %bitcast.11, bf16[2,320,1024]{2,1,0:T(8,128)(2,1)S(1)} %bitcast.12, bf16[480,320]{1,0:T(8,128)(2,1)S(1)} %copy.13.trace_ref), custom_call_target="tpu_custom_call" | custom-call | flops 104857600 | bytes 1000000 | tf_op jit(solution)/shard_map/ends/ends/pallas_call | solution.py:178
  6.6 2.8 %collective-permute-start.5 = (bf16[2,80,64]{2,1,0:T(8,128)(2,1)S(1)}, bf16[2,80,64]{2,1,0:T(8,128)(2,1)S(1)}, u32[]{:S(2)}, u32[]{:S(2)}) collective-permute-start(bf16[2,80,64]{2,1,0:T(8,128)(2,1)S(1)} %get-tuple-element.12), channel_id=1, source_target_pairs={{0,13},{1,12},{4,1},{5,0},{8,5},{9,4},{12,9},{13,8},{2,15},{3,14},... | collective-permute-start | bytes 61448 | tf_op jit(solution)/shard_map/interface/ppermute | solution.py:201
  9.5 0.0 collective-permute-start.4
  9.5 1.6 %collective-permute-start = (bf16[2,160,64]{2,1,0:T(8,128)(2,1)S(1)}, bf16[2,160,64]{2,1,0:T(8,128)(2,1)S(1)}, u32[]{:S(2)}, u32[]{:S(2)}) collective-permute-start(bf16[2,160,64]{2,1,0:T(8,128)(2,1)S(1)} %get-tuple-element.10), channel_id=1, source_target_pairs={{0,4},{4,8},{8,12},{12,0},{1,5},{5,9},{9,13},{13,1},{2,6},{6,10},{... | collective-permute-start | bytes 122888 | tf_op jit(solution)/shard_map/halo/ppermute | solution.py:198
  11.0 2.2 %collective-permute-start.1 = (bf16[2,160,64]{2,1,0:T(8,128)(2,1)S(1)}, bf16[2,160,64]{2,1,0:T(8,128)(2,1)S(1)}, u32[]{:S(2)}, u32[]{:S(2)}) collective-permute-start(bf16[2,160,64]{2,1,0:T(8,128)(2,1)S(1)} %get-tuple-element.11), channel_id=1, source_target_pairs={{0,12},{4,0},{8,4},{12,8},{1,13},{5,1},{9,5},{13,9},{2,14},{6,2},{... | collective-permute-start | bytes 122888 | tf_op jit(solution)/shard_map/halo/ppermute | solution.py:199
  13.3 0.0 collective-permute-done.5.rest_3_
  13.3 0.0 collective-permute-start.3
  13.3 0.6 %collective-permute-done.4.rest_2_ = bf16[2,80,64]{2,1,0:T(8,128)(2,1)S(1)} collective-permute-done((bf16[2,80,64]{2,1,0:T(8,128)(2,1)S(1)}, bf16[2,80,64]{2,1,0:T(8,128)(2,1)S(1)}, u32[]{:S(2)}, u32[]{:S(2)}) %collective-permute-start.4) | collective-permute-done | bytes 20512 | tf_op jit(solution)/shard_map/interface/ppermute | solution.py:201
  13.9 2.8 %collective-permute-start.2 = (bf16[2,80,64]{2,1,0:T(8,128)(2,1)S(1)}, bf16[2,80,64]{2,1,0:T(8,128)(2,1)S(1)}, u32[]{:S(2)}, u32[]{:S(2)}) collective-permute-start(bf16[2,80,64]{2,1,0:T(8,128)(2,1)S(1)} %get-tuple-element.12), channel_id=1, source_target_pairs={{0,1},{1,0},{4,5},{5,4},{8,9},{9,8},{12,13},{13,12},{2,3},{3,2},{6... | collective-permute-start | bytes 61448 | tf_op jit(solution)/shard_map/interface/ppermute | solution.py:201
  17.4 0.0 copy-done.8
  17.4 1.5 %collective-permute-done.3.rest_1_ = bf16[2,80,64]{2,1,0:T(8,128)(2,1)S(1)} collective-permute-done((bf16[2,80,64]{2,1,0:T(8,128)(2,1)S(1)}, bf16[2,80,64]{2,1,0:T(8,128)(2,1)S(1)}, u32[]{:S(2)}, u32[]{:S(2)}) %collective-permute-start.3) | collective-permute-done | bytes 20512 | tf_op jit(solution)/shard_map/interface/ppermute | solution.py:201
  18.9 0.0 collective-permute-done.2.rest_0_
  18.9 0.0 collective-permute-done.low_ref
  18.9 0.0 collective-permute-done.1.high_ref
  18.9 0.0 copy-done.1
  18.9 0.0 copy-done.2
  19.0 0.0 copy-done.3
  19.0 0.0 copy-done.4
  19.0 0.0 copy-done.5
  19.0 0.0 copy-done.6
  19.0 0.0 copy-done.7
  19.0 10.4 %couple.1 = (f32[2,320,1024]{2,1,0:T(8,128)S(1)}, f32[4,1024]{1,0:T(4,128)S(1)}) custom-call(s32[3]{0:T(128)S(1)} %pad_add_fusion.place_ref, f32[1]{0:T(128)S(6)} %copy.17.freq_ref, f32[4,4]{1,0:T(4,128)S(1)} %copy-done.7, s32[6,1024]{1,0:T(8,128)S(1)} %bitcast.15, s32[2,64]{1,0:T(2,128)S(1)} %bitcast.17, bf16[2,320,1024]{2,1,0:T(8,128)(2,1)S(1)} %bitcast.13, ...), custom_call_target="tpu_custom_call" | custom-call | flops 3690987520 | bytes 6553600 | tf_op jit(solution)/shard_map/couple/couple/pallas_call | solution.py:209
  29.4 2.5 %collective-permute-done.6.rest_0_ = bf16[2,320,1024]{2,1,0:T(8,128)(2,1)S(1)} collective-permute-done((bf16[2,320,1024]{2,1,0:T(8,128)(2,1)}, bf16[2,320,1024]{2,1,0:T(8,128)(2,1)S(1)}, u32[]{:S(2)}, u32[]{:S(2)}) %collective-permute-start.6) | collective-permute-done | bytes 1310752 | tf_op jit(solution)/shard_map/instances/ppermute | solution.py:174
  31.9 2.0 %update.1 = bf16[2,320,1024]{2,1,0:T(8,128)(2,1)} custom-call(f32[2,320,1024]{2,1,0:T(8,128)S(1)} %get-tuple-element.13.ready_ref, f32[4,1024]{1,0:T(4,128)S(1)} %get-tuple-element.14.factor_ref, bf16[320,320]{1,0:T(8,128)(2,1)S(1)} %copy-done.1, bf16[2,320,1024]{2,1,0:T(8,128)(2,1)S(1)} %collective-permute-done.6.rest_0_), custom_call_target="tpu_custom_call" | custom-call | flops 419430400 | bytes 5242880 | tf_op jit(solution)/shard_map/update/update/pallas_call | solution.py:230
  (1 shorter events, 0.0 us)
Async XLA Ops:
  0.0 31.9 %collective-permute-start.6 = (bf16[2,320,1024]{2,1,0:T(8,128)(2,1)}, bf16[2,320,1024]{2,1,0:T(8,128)(2,1)S(1)}, u32[]{:S(2)}, u32[]{:S(2)}) collective-permute-start(bf16[2,320,1024]{2,1,0:T(8,128)(2,1)} %bitcast.10), channel_id=1, source_target_pairs={{0,2},{2,0},{1,3},{3,1},{4,6},{6,4},{5,7},{7,5},{8,10},{10,8},{9,1... | collective-permute-start | bytes 3932168 | tf_op jit(solution)/shard_map/instances/ppermute | solution.py:174
  4.2 1.3 %copy-start = (bf16[1,2,320,1024]{3,2,1,0:T(8,128)(2,1)S(1)}, bf16[1,2,320,1024]{3,2,1,0:T(8,128)(2,1)}, u32[]{:S(2)}) copy-start(bf16[1,2,320,1024]{3,2,1,0:T(8,128)(2,1)} %param.11) | copy-start | bytes 3932164
  5.6 11.8 %copy-start.8 = (s32[1,6,1024]{2,0,1:T(1,128)S(1)}, s32[1,6,1024]{2,0,1:T(1,128)}, u32[]{:S(2)}) copy-start(s32[1,6,1024]{2,0,1:T(1,128)} %param.15) | copy-start | bytes 73732
  5.6 13.4 %copy-start.1 = (bf16[320,320]{1,0:T(8,128)(2,1)S(1)}, bf16[320,320]{1,0:T(8,128)(2,1)}, u32[]{:S(2)}) copy-start(bf16[320,320]{1,0:T(8,128)(2,1)} %inverse_ref.3) | copy-start | bytes 614404
  5.6 13.4 %copy-start.2 = (bf16[1,2,320,1024]{3,2,1,0:T(8,128)(2,1)S(1)}, bf16[1,2,320,1024]{3,2,1,0:T(8,128)(2,1)}, u32[]{:S(2)}) copy-start(bf16[1,2,320,1024]{3,2,1,0:T(8,128)(2,1)} %param.12) | copy-start | bytes 3932164
  5.6 13.4 %copy-start.3 = (bf16[320,480]{1,0:T(8,128)(2,1)S(1)}, bf16[320,480]{1,0:T(8,128)(2,1)}, u32[]{:S(2)}) copy-start(bf16[320,480]{1,0:T(8,128)(2,1)} %lift_ref.1) | copy-start | bytes 921604
  5.6 13.4 %copy-start.4 = (bf16[320,320]{1,0:T(8,128)(2,1)S(1)}, bf16[320,320]{1,0:T(8,128)(2,1)}, u32[]{:S(2)}) copy-start(bf16[320,320]{1,0:T(8,128)(2,1)} %volume_ref.1) | copy-start | bytes 614404
  5.6 13.4 %copy-start.5 = (f32[1,1024]{1,0:T(1,128)S(1)}, f32[1,1024]{1,0:T(1,128)}, u32[]{:S(2)}) copy-start(f32[1,1024]{1,0:T(1,128)} %scale_ref.1) | copy-start | bytes 12292
  5.6 13.4 %copy-start.6 = (s32[1,2,64]{2,1,0:T(2,128)S(1)}, s32[1,2,64]{2,1,0:T(2,128)}, u32[]{:S(2)}) copy-start(s32[1,2,64]{2,1,0:T(2,128)} %param.16) | copy-start | bytes 1540
  5.6 13.4 %copy-start.7 = (f32[4,4]{1,0:T(4,128)S(1)}, f32[4,4]{1,0:T(4,128)}, u32[]{:S(2)}) copy-start(f32[4,4]{1,0:T(4,128)} %constant.13.clone.table_ref) | copy-start | bytes 196
  6.6 6.6 %collective-permute-start.5 = (bf16[2,80,64]{2,1,0:T(8,128)(2,1)S(1)}, bf16[2,80,64]{2,1,0:T(8,128)(2,1)S(1)}, u32[]{:S(2)}, u32[]{:S(2)}) collective-permute-start(bf16[2,80,64]{2,1,0:T(8,128)(2,1)S(1)} %get-tuple-element.12), channel_id=1, source_target_pairs={{0,13},{1,12},{4,1},{5,0},{8,5},{9,4},{12,9},{13,8},{2,15},{3,14},... | collective-permute-start | bytes 61448 | tf_op jit(solution)/shard_map/interface/ppermute | solution.py:201
  9.5 4.5 %collective-permute-start.4 = (bf16[2,80,64]{2,1,0:T(8,128)(2,1)S(1)}, bf16[2,80,64]{2,1,0:T(8,128)(2,1)S(1)}, u32[]{:S(2)}, u32[]{:S(2)}) collective-permute-start(bf16[2,80,64]{2,1,0:T(8,128)(2,1)S(1)} %get-tuple-element.12), channel_id=1, source_target_pairs={{0,9},{1,8},{4,13},{5,12},{8,1},{9,0},{12,5},{13,4},{2,11},{3,10},... | collective-permute-start | bytes 61448 | tf_op jit(solution)/shard_map/interface/ppermute | solution.py:201
  9.5 9.5 %collective-permute-start = (bf16[2,160,64]{2,1,0:T(8,128)(2,1)S(1)}, bf16[2,160,64]{2,1,0:T(8,128)(2,1)S(1)}, u32[]{:S(2)}, u32[]{:S(2)}) collective-permute-start(bf16[2,160,64]{2,1,0:T(8,128)(2,1)S(1)} %get-tuple-element.10), channel_id=1, source_target_pairs={{0,4},{4,8},{8,12},{12,0},{1,5},{5,9},{9,13},{13,1},{2,6},{6,10},{... | collective-permute-start | bytes 122888 | tf_op jit(solution)/shard_map/halo/ppermute | solution.py:198
  11.0 7.9 %collective-permute-start.1 = (bf16[2,160,64]{2,1,0:T(8,128)(2,1)S(1)}, bf16[2,160,64]{2,1,0:T(8,128)(2,1)S(1)}, u32[]{:S(2)}, u32[]{:S(2)}) collective-permute-start(bf16[2,160,64]{2,1,0:T(8,128)(2,1)S(1)} %get-tuple-element.11), channel_id=1, source_target_pairs={{0,12},{4,0},{8,4},{12,8},{1,13},{5,1},{9,5},{13,9},{2,14},{6,2},{... | collective-permute-start | bytes 122888 | tf_op jit(solution)/shard_map/halo/ppermute | solution.py:199
  13.3 5.6 %collective-permute-start.3 = (bf16[2,80,64]{2,1,0:T(8,128)(2,1)S(1)}, bf16[2,80,64]{2,1,0:T(8,128)(2,1)S(1)}, u32[]{:S(2)}, u32[]{:S(2)}) collective-permute-start(bf16[2,80,64]{2,1,0:T(8,128)(2,1)S(1)} %get-tuple-element.12), channel_id=1, source_target_pairs={{0,5},{1,4},{4,9},{5,8},{8,13},{9,12},{12,1},{13,0},{2,7},{3,6},{6... | collective-permute-start | bytes 61448 | tf_op jit(solution)/shard_map/interface/ppermute | solution.py:201
  13.9 5.0 %collective-permute-start.2 = (bf16[2,80,64]{2,1,0:T(8,128)(2,1)S(1)}, bf16[2,80,64]{2,1,0:T(8,128)(2,1)S(1)}, u32[]{:S(2)}, u32[]{:S(2)}) collective-permute-start(bf16[2,80,64]{2,1,0:T(8,128)(2,1)S(1)} %get-tuple-element.12), channel_id=1, source_target_pairs={{0,1},{1,0},{4,5},{5,4},{8,9},{9,8},{12,13},{13,12},{2,3},{3,2},{6... | collective-permute-start | bytes 61448 | tf_op jit(solution)/shard_map/interface/ppermute | solution.py:201

commit v9 on v4

--- a/solution.py
+++ b/solution.py
@@ -11,6 +11,7 @@
 LAYER = 64
 OPPOSITE = (1, 0, 3, 2, 5, 4)
 LANES = 128
+STRIP = 32
 VMEM_LIMIT = 40 * 1024 * 1024
 
 
@@ -130,18 +131,24 @@
 
 
 def update_kernel(tile, ready_ref, factor_ref, inverse_ref, *rest):
-    others, (out_ref, made, sems) = rest[:-3], rest[-3:]
+    others, (out_ref, made, moved, sems) = rest[:-4], rest[-4:]
     count, dof, total = ready_ref.shape
+    products = len(others) * count
     copies = []
     for t in range(total // tile):
         cols = slice(t * tile, (t + 1) * tile)
-        moved = [dot(inverse_ref[...], other[m, :, cols]) for other in others for m in range(count)]
-        for n in range(count):
-            value = ready_ref[n, :, cols]
-            for k, part in enumerate(moved):
-                at = n * len(moved) + k
-                value -= factor_ref[at : at + 1, cols] * part
-            made[t, n] = value.astype(jnp.bfloat16)
+        for k in range(products):
+            moved[t % 2, k] = dot(inverse_ref[...], others[k // count][k % count, :, cols])
+        factors = [[factor_ref[n * products + k : n * products + k + 1, cols] for k in range(products)]
+                   for n in range(count)]
+        for strip in range(0, dof, STRIP):
+            rows = slice(strip, strip + STRIP)
+            parts = [moved[t % 2, k, rows, :] for k in range(products)]
+            for n in range(count):
+                value = ready_ref[n, rows, cols]
+                for factor, part in zip(factors[n], parts):
+                    value -= factor * part
+                made[t, n, rows, :] = value.astype(jnp.bfloat16)
         copy = pltpu.make_async_copy(made.at[t], out_ref.at[:, :, cols], sems.at[t])
         copy.start()
         copies.append(copy)
@@ -231,7 +238,9 @@
             out_shape=jax.ShapeDtypeStruct((count, dof, total), bf16),
             in_specs=[vmem] * (2 + peers),
             out_specs=pl.BlockSpec(memory_space=pl.ANY),
-            scratch_shapes=[pltpu.VMEM((steps, count, dof, tile), bf16), pltpu.SemaphoreType.DMA((steps,))],
+            scratch_shapes=[pltpu.VMEM((steps, count, dof, tile), bf16),
+                            pltpu.VMEM((2, (peers - 1) * count, dof, tile), jnp.float32),
+                            pltpu.SemaphoreType.DMA((steps,))],
             compiler_params=pltpu.CompilerParams(vmem_limit_bytes=VMEM_LIMIT),
             cost_estimate=pl.CostEstimate(flops=2 * count * total * dof * dof * (peers - 1),
                                           bytes_accessed=count * dof * total * 8, transcendentals=0),

time: 33.8 us -> 33.8 us (level)
  no operation moved by 1% of the time
where the time goes in v9:
time: 33.8 us; the launch traced here: 33.6 us
  Pallas kernels  13.1 us (39%)
  starting transfers between devices  12.4 us (37%)
  waiting for transfers between devices  4.67 us (14%)
  local copies, waits for them, and re-layouts  2.58 us (8%)
  between operations  0.79 us (2%)
    pallas_call x1, Pallas kernels, body(): pl.pallas_call(functools.partial(couple_kernel, shards, peers), grid=(ste...  10.4 us
    ppermute x4, starting transfers between devices, body(): lax.ppermute(cross, ('space', 'row'), [(i * 2 + r, (i + d) % shards * 2 +...  5.62 us
    ppermute x1, starting transfers between devices, body(): lax.ppermute(current, 'inst', [(i, (i + d) % peers) for i in range(peers)])  2.94 us
    unnamed x20, local copies, waits for them, and re-layouts  2.58 us
    ppermute x1, waiting for transfers between devices, body(): lax.ppermute(current, 'inst', [(i, (i + d) % peers) for i in range(peers)])  2.5 us
    ppermute x1, starting transfers between devices, body(): lax.ppermute(down, 'space', [(i, (i - 1) % shards) for i in range(shards)])  2.25 us
    ppermute x4, waiting for transfers between devices, body(): lax.ppermute(cross, ('space', 'row'), [(i * 2 + r, (i + d) % shards * 2 +...  2.16 us
    pallas_call x1, Pallas kernels, body(): pl.pallas_call(functools.partial(update_kernel, tile), out_shape=jax.Shap...  1.64 us
  transfers between devices with their start and end apart: 7, of which 3 were waited for; matrix products, arithmetic and copies ran while one was open for 4% of the time, Pallas kernels for 34%

profile of v9, /device:TPU:0, one launch (start us, length us, event | category | flops | bytes accessed | tf_op | source)
XLA Modules:
  0.0 33.6 jit_solution(220306783451654093)
XLA Ops:
  0.0 2.9 %collective-permute-start.6 = (bf16[2,320,1024]{2,1,0:T(8,128)(2,1)}, bf16[2,320,1024]{2,1,0:T(8,128)(2,1)S(1)}, u32[]{:S(2)}, u32[]{:S(2)}) collective-permute-start(bf16[2,320,1024]{2,1,0:T(8,128)(2,1)} %bitcast.10), channel_id=1, source_target_pairs={{0,2},{2,0},{1,3},{3,1},{4,6},{6,4},{5,7},{7,5},{8,10},{10,8},{9,1... | collective-permute-start | bytes 3932168 | tf_op jit(solution)/shard_map/instances/ppermute | solution.py:181
  2.9 1.2 %copy.13.trace_ref = bf16[480,320]{1,0:T(8,128)(2,1)S(1)} copy(bf16[480,320]{0,1:T(8,128)(2,1)} %param.18) | data formatting | bytes 614400 | tf_op args[7]
  4.2 0.1 pad_add_fusion.place_ref
  4.2 0.0 copy-start
  4.2 1.3 %copy-done = bf16[1,2,320,1024]{3,2,1,0:T(8,128)(2,1)S(1)} copy-done((bf16[1,2,320,1024]{3,2,1,0:T(8,128)(2,1)S(1)}, bf16[1,2,320,1024]{3,2,1,0:T(8,128)(2,1)}, u32[]{:S(2)}) %copy-start) | copy-done | bytes 1310744
  5.6 0.0 copy-start.8
  5.6 0.0 copy-start.1
  5.6 0.0 copy-start.2
  5.6 0.0 copy-start.3
  5.6 0.0 copy-start.4
  5.6 0.0 copy-start.5
  5.6 0.0 copy-start.6
  5.6 0.0 copy-start.7
  5.6 1.0 %ends.1 = (bf16[2,160,64]{2,1,0:T(8,128)(2,1)S(1)}, bf16[2,160,64]{2,1,0:T(8,128)(2,1)S(1)}, bf16[2,80,64]{2,1,0:T(8,128)(2,1)S(1)}) custom-call(s32[3]{0:T(128)S(1)} %pad_add_fusion.place_ref, bf16[2,320,1024]{2,1,0:T(8,128)(2,1)S(1)} %bitcast.11, bf16[2,320,1024]{2,1,0:T(8,128)(2,1)S(1)} %bitcast.12, bf16[480,320]{1,0:T(8,128)(2,1)S(1)} %copy.13.trace_ref), custom_call_target="tpu_custom_call" | custom-call | flops 104857600 | bytes 1000000 | tf_op jit(solution)/shard_map/ends/ends/pallas_call | solution.py:185
  6.6 2.8 %collective-permute-start.5 = (bf16[2,80,64]{2,1,0:T(8,128)(2,1)S(1)}, bf16[2,80,64]{2,1,0:T(8,128)(2,1)S(1)}, u32[]{:S(2)}, u32[]{:S(2)}) collective-permute-start(bf16[2,80,64]{2,1,0:T(8,128)(2,1)S(1)} %get-tuple-element.12), channel_id=1, source_target_pairs={{0,13},{1,12},{4,1},{5,0},{8,5},{9,4},{12,9},{13,8},{2,15},{3,14},... | collective-permute-start | bytes 61448 | tf_op jit(solution)/shard_map/interface/ppermute | solution.py:208
  9.5 0.0 collective-permute-start.4
  9.5 1.6 %collective-permute-start = (bf16[2,160,64]{2,1,0:T(8,128)(2,1)S(1)}, bf16[2,160,64]{2,1,0:T(8,128)(2,1)S(1)}, u32[]{:S(2)}, u32[]{:S(2)}) collective-permute-start(bf16[2,160,64]{2,1,0:T(8,128)(2,1)S(1)} %get-tuple-element.10), channel_id=1, source_target_pairs={{0,4},{4,8},{8,12},{12,0},{1,5},{5,9},{9,13},{13,1},{2,6},{6,10},{... | collective-permute-start | bytes 122888 | tf_op jit(solution)/shard_map/halo/ppermute | solution.py:205
  11.0 2.2 %collective-permute-start.1 = (bf16[2,160,64]{2,1,0:T(8,128)(2,1)S(1)}, bf16[2,160,64]{2,1,0:T(8,128)(2,1)S(1)}, u32[]{:S(2)}, u32[]{:S(2)}) collective-permute-start(bf16[2,160,64]{2,1,0:T(8,128)(2,1)S(1)} %get-tuple-element.11), channel_id=1, source_target_pairs={{0,12},{4,0},{8,4},{12,8},{1,13},{5,1},{9,5},{13,9},{2,14},{6,2},{... | collective-permute-start | bytes 122888 | tf_op jit(solution)/shard_map/halo/ppermute | solution.py:206
  13.3 0.0 collective-permute-done.5.rest_3_
  13.3 0.0 collective-permute-start.3
  13.3 0.6 %collective-permute-done.4.rest_2_ = bf16[2,80,64]{2,1,0:T(8,128)(2,1)S(1)} collective-permute-done((bf16[2,80,64]{2,1,0:T(8,128)(2,1)S(1)}, bf16[2,80,64]{2,1,0:T(8,128)(2,1)S(1)}, u32[]{:S(2)}, u32[]{:S(2)}) %collective-permute-start.4) | collective-permute-done | bytes 20512 | tf_op jit(solution)/shard_map/interface/ppermute | solution.py:208
  13.9 2.8 %collective-permute-start.2 = (bf16[2,80,64]{2,1,0:T(8,128)(2,1)S(1)}, bf16[2,80,64]{2,1,0:T(8,128)(2,1)S(1)}, u32[]{:S(2)}, u32[]{:S(2)}) collective-permute-start(bf16[2,80,64]{2,1,0:T(8,128)(2,1)S(1)} %get-tuple-element.12), channel_id=1, source_target_pairs={{0,1},{1,0},{4,5},{5,4},{8,9},{9,8},{12,13},{13,12},{2,3},{3,2},{6... | collective-permute-start | bytes 61448 | tf_op jit(solution)/shard_map/interface/ppermute | solution.py:208
  17.4 0.0 copy-done.8
  17.4 1.5 %collective-permute-done.3.rest_1_ = bf16[2,80,64]{2,1,0:T(8,128)(2,1)S(1)} collective-permute-done((bf16[2,80,64]{2,1,0:T(8,128)(2,1)S(1)}, bf16[2,80,64]{2,1,0:T(8,128)(2,1)S(1)}, u32[]{:S(2)}, u32[]{:S(2)}) %collective-permute-start.3) | collective-permute-done | bytes 20512 | tf_op jit(solution)/shard_map/interface/ppermute | solution.py:208
  18.9 0.0 collective-permute-done.2.rest_0_
  18.9 0.0 collective-permute-done.low_ref
  18.9 0.0 collective-permute-done.1.high_ref
  18.9 0.0 copy-done.1
  18.9 0.0 copy-done.2
  19.0 0.0 copy-done.3
  19.0 0.0 copy-done.4
  19.0 0.0 copy-done.5
  19.0 0.0 copy-done.6
  19.0 0.0 copy-done.7
  19.0 10.4 %couple.1 = (f32[2,320,1024]{2,1,0:T(8,128)S(1)}, f32[4,1024]{1,0:T(4,128)S(1)}) custom-call(s32[3]{0:T(128)S(1)} %pad_add_fusion.place_ref, f32[1]{0:T(128)S(6)} %copy.17.freq_ref, f32[4,4]{1,0:T(4,128)S(1)} %copy-done.7, s32[6,1024]{1,0:T(8,128)S(1)} %bitcast.15, s32[2,64]{1,0:T(2,128)S(1)} %bitcast.17, bf16[2,320,1024]{2,1,0:T(8,128)(2,1)S(1)} %bitcast.13, ...), custom_call_target="tpu_custom_call" | custom-call | flops 3690987520 | bytes 6553600 | tf_op jit(solution)/shard_map/couple/couple/pallas_call | solution.py:216
  29.4 2.5 %collective-permute-done.6.rest_0_ = bf16[2,320,1024]{2,1,0:T(8,128)(2,1)S(1)} collective-permute-done((bf16[2,320,1024]{2,1,0:T(8,128)(2,1)}, bf16[2,320,1024]{2,1,0:T(8,128)(2,1)S(1)}, u32[]{:S(2)}, u32[]{:S(2)}) %collective-permute-start.6) | collective-permute-done | bytes 1310752 | tf_op jit(solution)/shard_map/instances/ppermute | solution.py:181
  31.9 1.6 %update.1 = bf16[2,320,1024]{2,1,0:T(8,128)(2,1)} custom-call(f32[2,320,1024]{2,1,0:T(8,128)S(1)} %get-tuple-element.13.ready_ref, f32[4,1024]{1,0:T(4,128)S(1)} %get-tuple-element.14.factor_ref, bf16[320,320]{1,0:T(8,128)(2,1)S(1)} %copy-done.1, bf16[2,320,1024]{2,1,0:T(8,128)(2,1)S(1)} %collective-permute-done.6.rest_0_), custom_call_target="tpu_custom_call" | custom-call | flops 419430400 | bytes 5242880 | tf_op jit(solution)/shard_map/update/update/pallas_call | solution.py:236
  (1 shorter events, 0.0 us)
Async XLA Ops:
  0.0 31.9 %collective-permute-start.6 = (bf16[2,320,1024]{2,1,0:T(8,128)(2,1)}, bf16[2,320,1024]{2,1,0:T(8,128)(2,1)S(1)}, u32[]{:S(2)}, u32[]{:S(2)}) collective-permute-start(bf16[2,320,1024]{2,1,0:T(8,128)(2,1)} %bitcast.10), channel_id=1, source_target_pairs={{0,2},{2,0},{1,3},{3,1},{4,6},{6,4},{5,7},{7,5},{8,10},{10,8},{9,1... | collective-permute-start | bytes 3932168 | tf_op jit(solution)/shard_map/instances/ppermute | solution.py:181
  4.2 1.3 %copy-start = (bf16[1,2,320,1024]{3,2,1,0:T(8,128)(2,1)S(1)}, bf16[1,2,320,1024]{3,2,1,0:T(8,128)(2,1)}, u32[]{:S(2)}) copy-start(bf16[1,2,320,1024]{3,2,1,0:T(8,128)(2,1)} %param.11) | copy-start | bytes 3932164
  5.6 11.8 %copy-start.8 = (s32[1,6,1024]{2,0,1:T(1,128)S(1)}, s32[1,6,1024]{2,0,1:T(1,128)}, u32[]{:S(2)}) copy-start(s32[1,6,1024]{2,0,1:T(1,128)} %param.15) | copy-start | bytes 73732
  5.6 13.4 %copy-start.1 = (bf16[320,320]{1,0:T(8,128)(2,1)S(1)}, bf16[320,320]{1,0:T(8,128)(2,1)}, u32[]{:S(2)}) copy-start(bf16[320,320]{1,0:T(8,128)(2,1)} %inverse_ref.3) | copy-start | bytes 614404
  5.6 13.4 %copy-start.2 = (bf16[1,2,320,1024]{3,2,1,0:T(8,128)(2,1)S(1)}, bf16[1,2,320,1024]{3,2,1,0:T(8,128)(2,1)}, u32[]{:S(2)}) copy-start(bf16[1,2,320,1024]{3,2,1,0:T(8,128)(2,1)} %param.12) | copy-start | bytes 3932164
  5.6 13.4 %copy-start.3 = (bf16[320,480]{1,0:T(8,128)(2,1)S(1)}, bf16[320,480]{1,0:T(8,128)(2,1)}, u32[]{:S(2)}) copy-start(bf16[320,480]{1,0:T(8,128)(2,1)} %lift_ref.1) | copy-start | bytes 921604
  5.6 13.4 %copy-start.4 = (bf16[320,320]{1,0:T(8,128)(2,1)S(1)}, bf16[320,320]{1,0:T(8,128)(2,1)}, u32[]{:S(2)}) copy-start(bf16[320,320]{1,0:T(8,128)(2,1)} %volume_ref.1) | copy-start | bytes 614404
  5.6 13.4 %copy-start.5 = (f32[1,1024]{1,0:T(1,128)S(1)}, f32[1,1024]{1,0:T(1,128)}, u32[]{:S(2)}) copy-start(f32[1,1024]{1,0:T(1,128)} %scale_ref.1) | copy-start | bytes 12292
  5.6 13.4 %copy-start.6 = (s32[1,2,64]{2,1,0:T(2,128)S(1)}, s32[1,2,64]{2,1,0:T(2,128)}, u32[]{:S(2)}) copy-start(s32[1,2,64]{2,1,0:T(2,128)} %param.16) | copy-start | bytes 1540
  5.6 13.4 %copy-start.7 = (f32[4,4]{1,0:T(4,128)S(1)}, f32[4,4]{1,0:T(4,128)}, u32[]{:S(2)}) copy-start(f32[4,4]{1,0:T(4,128)} %constant.13.clone.table_ref) | copy-start | bytes 196
  6.6 6.6 %collective-permute-start.5 = (bf16[2,80,64]{2,1,0:T(8,128)(2,1)S(1)}, bf16[2,80,64]{2,1,0:T(8,128)(2,1)S(1)}, u32[]{:S(2)}, u32[]{:S(2)}) collective-permute-start(bf16[2,80,64]{2,1,0:T(8,128)(2,1)S(1)} %get-tuple-element.12), channel_id=1, source_target_pairs={{0,13},{1,12},{4,1},{5,0},{8,5},{9,4},{12,9},{13,8},{2,15},{3,14},... | collective-permute-start | bytes 61448 | tf_op jit(solution)/shard_map/interface/ppermute | solution.py:208
  9.5 4.5 %collective-permute-start.4 = (bf16[2,80,64]{2,1,0:T(8,128)(2,1)S(1)}, bf16[2,80,64]{2,1,0:T(8,128)(2,1)S(1)}, u32[]{:S(2)}, u32[]{:S(2)}) collective-permute-start(bf16[2,80,64]{2,1,0:T(8,128)(2,1)S(1)} %get-tuple-element.12), channel_id=1, source_target_pairs={{0,9},{1,8},{4,13},{5,12},{8,1},{9,0},{12,5},{13,4},{2,11},{3,10},... | collective-permute-start | bytes 61448 | tf_op jit(solution)/shard_map/interface/ppermute | solution.py:208
  9.5 9.5 %collective-permute-start = (bf16[2,160,64]{2,1,0:T(8,128)(2,1)S(1)}, bf16[2,160,64]{2,1,0:T(8,128)(2,1)S(1)}, u32[]{:S(2)}, u32[]{:S(2)}) collective-permute-start(bf16[2,160,64]{2,1,0:T(8,128)(2,1)S(1)} %get-tuple-element.10), channel_id=1, source_target_pairs={{0,4},{4,8},{8,12},{12,0},{1,5},{5,9},{9,13},{13,1},{2,6},{6,10},{... | collective-permute-start | bytes 122888 | tf_op jit(solution)/shard_map/halo/ppermute | solution.py:205
  11.0 7.9 %collective-permute-start.1 = (bf16[2,160,64]{2,1,0:T(8,128)(2,1)S(1)}, bf16[2,160,64]{2,1,0:T(8,128)(2,1)S(1)}, u32[]{:S(2)}, u32[]{:S(2)}) collective-permute-start(bf16[2,160,64]{2,1,0:T(8,128)(2,1)S(1)} %get-tuple-element.11), channel_id=1, source_target_pairs={{0,12},{4,0},{8,4},{12,8},{1,13},{5,1},{9,5},{13,9},{2,14},{6,2},{... | collective-permute-start | bytes 122888 | tf_op jit(solution)/shard_map/halo/ppermute | solution.py:206
  13.3 5.6 %collective-permute-start.3 = (bf16[2,80,64]{2,1,0:T(8,128)(2,1)S(1)}, bf16[2,80,64]{2,1,0:T(8,128)(2,1)S(1)}, u32[]{:S(2)}, u32[]{:S(2)}) collective-permute-start(bf16[2,80,64]{2,1,0:T(8,128)(2,1)S(1)} %get-tuple-element.12), channel_id=1, source_target_pairs={{0,5},{1,4},{4,9},{5,8},{8,13},{9,12},{12,1},{13,0},{2,7},{3,6},{6... | collective-permute-start | bytes 61448 | tf_op jit(solution)/shard_map/interface/ppermute | solution.py:208
  13.9 5.0 %collective-permute-start.2 = (bf16[2,80,64]{2,1,0:T(8,128)(2,1)S(1)}, bf16[2,80,64]{2,1,0:T(8,128)(2,1)S(1)}, u32[]{:S(2)}, u32[]{:S(2)}) collective-permute-start(bf16[2,80,64]{2,1,0:T(8,128)(2,1)S(1)} %get-tuple-element.12), channel_id=1, source_target_pairs={{0,1},{1,0},{4,5},{5,4},{8,9},{9,8},{12,13},{13,12},{2,3},{3,2},{6... | collective-permute-start | bytes 61448 | tf_op jit(solution)/shard_map/interface/ppermute | solution.py:208

commit v10 on v6

--- a/solution.py
+++ b/solution.py
@@ -129,24 +129,25 @@
         finish(False)
 
 
-def update_kernel(tile, parts, ready_ref, factor_ref, inverse_ref, *rest):
+def update_kernel(tile, blocks, ready_ref, factor_ref, inverse_ref, *rest):
     others, (out_ref, made, sems) = rest[:-3], rest[-3:]
     count, dof, total = ready_ref.shape
     copies = []
-    for p in range(parts):
-        whole_part = slice(p * total // parts, (p + 1) * total // parts)
-        for start in range(whole_part.start, whole_part.stop, tile):
-            cols = slice(start, start + tile)
-            moved = [dot(inverse_ref[...], other[m, :, cols]) for other in others for m in range(count)]
+    for b in range(blocks):
+        rows = slice(b * dof // blocks, (b + 1) * dof // blocks)
+        for t in range(total // tile):
+            cols = slice(t * tile, (t + 1) * tile)
+            moved = [dot(inverse_ref[rows, :], other[m, :, cols]) for other in others for m in range(count)]
             for n in range(count):
-                value = ready_ref[n, :, cols]
+                value = ready_ref[n, rows, cols]
                 for k, part in enumerate(moved):
                     at = n * len(moved) + k
                     value -= factor_ref[at : at + 1, cols] * part
-                made[n, :, cols] = value.astype(jnp.bfloat16)
-        copy = pltpu.make_async_copy(made.at[:, :, whole_part], out_ref.at[:, :, whole_part], sems.at[p])
-        copy.start()
-        copies.append(copy)
+                made[n, rows, cols] = value.astype(jnp.bfloat16)
+        for n in range(count):
+            copy = pltpu.make_async_copy(made.at[n, rows, :], out_ref.at[n, rows, :], sems.at[b, n])
+            copy.start()
+            copies.append(copy)
     for copy in copies:
         copy.wait()
 
@@ -227,14 +228,14 @@
           trace_matrix, lift_matrix, volume_matrix, block_inverse, low, high, *pieces)
 
     vmem = pl.BlockSpec(memory_space=pltpu.VMEM)
-    parts = 2
+    blocks = 2
     with jax.named_scope("update"):
         result = pl.pallas_call(
-            functools.partial(update_kernel, tile, parts),
+            functools.partial(update_kernel, tile, blocks),
             out_shape=jax.ShapeDtypeStruct((count, dof, total), bf16),
             in_specs=[vmem] * (2 + peers),
             out_specs=pl.BlockSpec(memory_space=pl.ANY),
-            scratch_shapes=[pltpu.VMEM((count, dof, total), bf16), pltpu.SemaphoreType.DMA((parts,))],
+            scratch_shapes=[pltpu.VMEM((count, dof, total), bf16), pltpu.SemaphoreType.DMA((blocks, count))],
             compiler_params=pltpu.CompilerParams(vmem_limit_bytes=VMEM_LIMIT),
             cost_estimate=pl.CostEstimate(flops=2 * count * total * dof * dof * (peers - 1),
                                           bytes_accessed=count * dof * total * 8, transcendentals=0),

time: 33.9 us -> 33.9 us (level)
  no operation moved by 1% of the time
where the time goes in v10:
time: 33.9 us; the launch traced here: 33.7 us
  Pallas kernels  13.2 us (39%)
  starting transfers between devices  12.4 us (37%)
  waiting for transfers between devices  4.67 us (14%)
  local copies, waits for them, and re-layouts  2.58 us (8%)
  between operations  0.79 us (2%)
    pallas_call x1, Pallas kernels, body(): pl.pallas_call(functools.partial(couple_kernel, shards, peers), grid=(ste...  10.4 us
    ppermute x4, starting transfers between devices, body(): lax.ppermute(cross, ('space', 'row'), [(i * 2 + r, (i + d) % shards * 2 +...  5.62 us
    ppermute x1, starting transfers between devices, body(): lax.ppermute(current, 'inst', [(i, (i + d) % peers) for i in range(peers)])  2.94 us
    unnamed x20, local copies, waits for them, and re-layouts  2.58 us
    ppermute x1, waiting for transfers between devices, body(): lax.ppermute(current, 'inst', [(i, (i + d) % peers) for i in range(peers)])  2.5 us
    ppermute x1, starting transfers between devices, body(): lax.ppermute(down, 'space', [(i, (i - 1) % shards) for i in range(shards)])  2.25 us
    ppermute x4, waiting for transfers between devices, body(): lax.ppermute(cross, ('space', 'row'), [(i * 2 + r, (i + d) % shards * 2 +...  2.16 us
    pallas_call x1, Pallas kernels, body(): pl.pallas_call(functools.partial(update_kernel, tile, blocks), out_shape=...  1.76 us
  transfers between devices with their start and end apart: 7, of which 3 were waited for; matrix products, arithmetic and copies ran while one was open for 4% of the time, Pallas kernels for 34%

profile of v10, /device:TPU:0, one launch (start us, length us, event | category | flops | bytes accessed | tf_op | source)
XLA Modules:
  0.0 33.7 jit_solution(13160034305976501359)
XLA Ops:
  0.0 2.9 %collective-permute-start.6 = (bf16[2,320,1024]{2,1,0:T(8,128)(2,1)}, bf16[2,320,1024]{2,1,0:T(8,128)(2,1)S(1)}, u32[]{:S(2)}, u32[]{:S(2)}) collective-permute-start(bf16[2,320,1024]{2,1,0:T(8,128)(2,1)} %bitcast.10), channel_id=1, source_target_pairs={{0,2},{2,0},{1,3},{3,1},{4,6},{6,4},{5,7},{7,5},{8,10},{10,8},{9,1... | collective-permute-start | bytes 3932168 | tf_op jit(solution)/shard_map/instances/ppermute | solution.py:177
  2.9 1.2 %copy.13.trace_ref = bf16[480,320]{1,0:T(8,128)(2,1)S(1)} copy(bf16[480,320]{0,1:T(8,128)(2,1)} %param.18) | data formatting | bytes 614400 | tf_op args[7]
  4.2 0.1 pad_add_fusion.place_ref
  4.2 0.0 copy-start
  4.2 1.3 %copy-done = bf16[1,2,320,1024]{3,2,1,0:T(8,128)(2,1)S(1)} copy-done((bf16[1,2,320,1024]{3,2,1,0:T(8,128)(2,1)S(1)}, bf16[1,2,320,1024]{3,2,1,0:T(8,128)(2,1)}, u32[]{:S(2)}) %copy-start) | copy-done | bytes 1310744
  5.6 0.0 copy-start.8
  5.6 0.0 copy-start.1
  5.6 0.0 copy-start.2
  5.6 0.0 copy-start.3
  5.6 0.0 copy-start.4
  5.6 0.0 copy-start.5
  5.6 0.0 copy-start.6
  5.6 0.0 copy-start.7
  5.6 1.0 %ends.1 = (bf16[2,160,64]{2,1,0:T(8,128)(2,1)S(1)}, bf16[2,160,64]{2,1,0:T(8,128)(2,1)S(1)}, bf16[2,80,64]{2,1,0:T(8,128)(2,1)S(1)}) custom-call(s32[3]{0:T(128)S(1)} %pad_add_fusion.place_ref, bf16[2,320,1024]{2,1,0:T(8,128)(2,1)S(1)} %bitcast.11, bf16[2,320,1024]{2,1,0:T(8,128)(2,1)S(1)} %bitcast.12, bf16[480,320]{1,0:T(8,128)(2,1)S(1)} %copy.13.trace_ref), custom_call_target="tpu_custom_call" | custom-call | flops 104857600 | bytes 1000000 | tf_op jit(solution)/shard_map/ends/ends/pallas_call | solution.py:181
  6.6 2.8 %collective-permute-start.5 = (bf16[2,80,64]{2,1,0:T(8,128)(2,1)S(1)}, bf16[2,80,64]{2,1,0:T(8,128)(2,1)S(1)}, u32[]{:S(2)}, u32[]{:S(2)}) collective-permute-start(bf16[2,80,64]{2,1,0:T(8,128)(2,1)S(1)} %get-tuple-element.12), channel_id=1, source_target_pairs={{0,13},{1,12},{4,1},{5,0},{8,5},{9,4},{12,9},{13,8},{2,15},{3,14},... | collective-permute-start | bytes 61448 | tf_op jit(solution)/shard_map/interface/ppermute | solution.py:204
  9.5 0.0 collective-permute-start.4
  9.5 1.6 %collective-permute-start = (bf16[2,160,64]{2,1,0:T(8,128)(2,1)S(1)}, bf16[2,160,64]{2,1,0:T(8,128)(2,1)S(1)}, u32[]{:S(2)}, u32[]{:S(2)}) collective-permute-start(bf16[2,160,64]{2,1,0:T(8,128)(2,1)S(1)} %get-tuple-element.10), channel_id=1, source_target_pairs={{0,4},{4,8},{8,12},{12,0},{1,5},{5,9},{9,13},{13,1},{2,6},{6,10},{... | collective-permute-start | bytes 122888 | tf_op jit(solution)/shard_map/halo/ppermute | solution.py:201
  11.0 2.2 %collective-permute-start.1 = (bf16[2,160,64]{2,1,0:T(8,128)(2,1)S(1)}, bf16[2,160,64]{2,1,0:T(8,128)(2,1)S(1)}, u32[]{:S(2)}, u32[]{:S(2)}) collective-permute-start(bf16[2,160,64]{2,1,0:T(8,128)(2,1)S(1)} %get-tuple-element.11), channel_id=1, source_target_pairs={{0,12},{4,0},{8,4},{12,8},{1,13},{5,1},{9,5},{13,9},{2,14},{6,2},{... | collective-permute-start | bytes 122888 | tf_op jit(solution)/shard_map/halo/ppermute | solution.py:202
  13.3 0.0 collective-permute-done.5.rest_3_
  13.3 0.0 collective-permute-start.3
  13.3 0.6 %collective-permute-done.4.rest_2_ = bf16[2,80,64]{2,1,0:T(8,128)(2,1)S(1)} collective-permute-done((bf16[2,80,64]{2,1,0:T(8,128)(2,1)S(1)}, bf16[2,80,64]{2,1,0:T(8,128)(2,1)S(1)}, u32[]{:S(2)}, u32[]{:S(2)}) %collective-permute-start.4) | collective-permute-done | bytes 20512 | tf_op jit(solution)/shard_map/interface/ppermute | solution.py:204
  13.9 2.8 %collective-permute-start.2 = (bf16[2,80,64]{2,1,0:T(8,128)(2,1)S(1)}, bf16[2,80,64]{2,1,0:T(8,128)(2,1)S(1)}, u32[]{:S(2)}, u32[]{:S(2)}) collective-permute-start(bf16[2,80,64]{2,1,0:T(8,128)(2,1)S(1)} %get-tuple-element.12), channel_id=1, source_target_pairs={{0,1},{1,0},{4,5},{5,4},{8,9},{9,8},{12,13},{13,12},{2,3},{3,2},{6... | collective-permute-start | bytes 61448 | tf_op jit(solution)/shard_map/interface/ppermute | solution.py:204
  17.4 0.0 copy-done.8
  17.4 1.5 %collective-permute-done.3.rest_1_ = bf16[2,80,64]{2,1,0:T(8,128)(2,1)S(1)} collective-permute-done((bf16[2,80,64]{2,1,0:T(8,128)(2,1)S(1)}, bf16[2,80,64]{2,1,0:T(8,128)(2,1)S(1)}, u32[]{:S(2)}, u32[]{:S(2)}) %collective-permute-start.3) | collective-permute-done | bytes 20512 | tf_op jit(solution)/shard_map/interface/ppermute | solution.py:204
  18.9 0.0 collective-permute-done.2.rest_0_
  18.9 0.0 collective-permute-done.low_ref
  18.9 0.0 collective-permute-done.1.high_ref
  18.9 0.0 copy-done.1
  18.9 0.0 copy-done.2
  19.0 0.0 copy-done.3
  19.0 0.0 copy-done.4
  19.0 0.0 copy-done.5
  19.0 0.0 copy-done.6
  19.0 0.0 copy-done.7
  19.0 10.4 %couple.1 = (f32[2,320,1024]{2,1,0:T(8,128)S(1)}, f32[4,1024]{1,0:T(4,128)S(1)}) custom-call(s32[3]{0:T(128)S(1)} %pad_add_fusion.place_ref, f32[1]{0:T(128)S(6)} %copy.17.freq_ref, f32[4,4]{1,0:T(4,128)S(1)} %copy-done.7, s32[6,1024]{1,0:T(8,128)S(1)} %bitcast.15, s32[2,64]{1,0:T(2,128)S(1)} %bitcast.17, bf16[2,320,1024]{2,1,0:T(8,128)(2,1)S(1)} %bitcast.13, ...), custom_call_target="tpu_custom_call" | custom-call | flops 3690987520 | bytes 6553600 | tf_op jit(solution)/shard_map/couple/couple/pallas_call | solution.py:212
  29.4 2.5 %collective-permute-done.6.rest_0_ = bf16[2,320,1024]{2,1,0:T(8,128)(2,1)S(1)} collective-permute-done((bf16[2,320,1024]{2,1,0:T(8,128)(2,1)}, bf16[2,320,1024]{2,1,0:T(8,128)(2,1)S(1)}, u32[]{:S(2)}, u32[]{:S(2)}) %collective-permute-start.6) | collective-permute-done | bytes 1310752 | tf_op jit(solution)/shard_map/instances/ppermute | solution.py:177
  31.9 1.8 %update.1 = bf16[2,320,1024]{2,1,0:T(8,128)(2,1)} custom-call(f32[2,320,1024]{2,1,0:T(8,128)S(1)} %get-tuple-element.13.ready_ref, f32[4,1024]{1,0:T(4,128)S(1)} %get-tuple-element.14.factor_ref, bf16[320,320]{1,0:T(8,128)(2,1)S(1)} %copy-done.1, bf16[2,320,1024]{2,1,0:T(8,128)(2,1)S(1)} %collective-permute-done.6.rest_0_), custom_call_target="tpu_custom_call" | custom-call | flops 419430400 | bytes 5242880 | tf_op jit(solution)/shard_map/update/update/pallas_call | solution.py:233
  (1 shorter events, 0.0 us)
Async XLA Ops:
  0.0 31.9 %collective-permute-start.6 = (bf16[2,320,1024]{2,1,0:T(8,128)(2,1)}, bf16[2,320,1024]{2,1,0:T(8,128)(2,1)S(1)}, u32[]{:S(2)}, u32[]{:S(2)}) collective-permute-start(bf16[2,320,1024]{2,1,0:T(8,128)(2,1)} %bitcast.10), channel_id=1, source_target_pairs={{0,2},{2,0},{1,3},{3,1},{4,6},{6,4},{5,7},{7,5},{8,10},{10,8},{9,1... | collective-permute-start | bytes 3932168 | tf_op jit(solution)/shard_map/instances/ppermute | solution.py:177
  4.2 1.3 %copy-start = (bf16[1,2,320,1024]{3,2,1,0:T(8,128)(2,1)S(1)}, bf16[1,2,320,1024]{3,2,1,0:T(8,128)(2,1)}, u32[]{:S(2)}) copy-start(bf16[1,2,320,1024]{3,2,1,0:T(8,128)(2,1)} %param.11) | copy-start | bytes 3932164
  5.6 11.8 %copy-start.8 = (s32[1,6,1024]{2,0,1:T(1,128)S(1)}, s32[1,6,1024]{2,0,1:T(1,128)}, u32[]{:S(2)}) copy-start(s32[1,6,1024]{2,0,1:T(1,128)} %param.15) | copy-start | bytes 73732
  5.6 13.4 %copy-start.1 = (bf16[320,320]{1,0:T(8,128)(2,1)S(1)}, bf16[320,320]{1,0:T(8,128)(2,1)}, u32[]{:S(2)}) copy-start(bf16[320,320]{1,0:T(8,128)(2,1)} %inverse_ref.3) | copy-start | bytes 614404
  5.6 13.4 %copy-start.2 = (bf16[1,2,320,1024]{3,2,1,0:T(8,128)(2,1)S(1)}, bf16[1,2,320,1024]{3,2,1,0:T(8,128)(2,1)}, u32[]{:S(2)}) copy-start(bf16[1,2,320,1024]{3,2,1,0:T(8,128)(2,1)} %param.12) | copy-start | bytes 3932164
  5.6 13.4 %copy-start.3 = (bf16[320,480]{1,0:T(8,128)(2,1)S(1)}, bf16[320,480]{1,0:T(8,128)(2,1)}, u32[]{:S(2)}) copy-start(bf16[320,480]{1,0:T(8,128)(2,1)} %lift_ref.1) | copy-start | bytes 921604
  5.6 13.4 %copy-start.4 = (bf16[320,320]{1,0:T(8,128)(2,1)S(1)}, bf16[320,320]{1,0:T(8,128)(2,1)}, u32[]{:S(2)}) copy-start(bf16[320,320]{1,0:T(8,128)(2,1)} %volume_ref.1) | copy-start | bytes 614404
  5.6 13.4 %copy-start.5 = (f32[1,1024]{1,0:T(1,128)S(1)}, f32[1,1024]{1,0:T(1,128)}, u32[]{:S(2)}) copy-start(f32[1,1024]{1,0:T(1,128)} %scale_ref.1) | copy-start | bytes 12292
  5.6 13.4 %copy-start.6 = (s32[1,2,64]{2,1,0:T(2,128)S(1)}, s32[1,2,64]{2,1,0:T(2,128)}, u32[]{:S(2)}) copy-start(s32[1,2,64]{2,1,0:T(2,128)} %param.16) | copy-start | bytes 1540
  5.6 13.4 %copy-start.7 = (f32[4,4]{1,0:T(4,128)S(1)}, f32[4,4]{1,0:T(4,128)}, u32[]{:S(2)}) copy-start(f32[4,4]{1,0:T(4,128)} %constant.13.clone.table_ref) | copy-start | bytes 196
  6.6 6.6 %collective-permute-start.5 = (bf16[2,80,64]{2,1,0:T(8,128)(2,1)S(1)}, bf16[2,80,64]{2,1,0:T(8,128)(2,1)S(1)}, u32[]{:S(2)}, u32[]{:S(2)}) collective-permute-start(bf16[2,80,64]{2,1,0:T(8,128)(2,1)S(1)} %get-tuple-element.12), channel_id=1, source_target_pairs={{0,13},{1,12},{4,1},{5,0},{8,5},{9,4},{12,9},{13,8},{2,15},{3,14},... | collective-permute-start | bytes 61448 | tf_op jit(solution)/shard_map/interface/ppermute | solution.py:204
  9.5 4.5 %collective-permute-start.4 = (bf16[2,80,64]{2,1,0:T(8,128)(2,1)S(1)}, bf16[2,80,64]{2,1,0:T(8,128)(2,1)S(1)}, u32[]{:S(2)}, u32[]{:S(2)}) collective-permute-start(bf16[2,80,64]{2,1,0:T(8,128)(2,1)S(1)} %get-tuple-element.12), channel_id=1, source_target_pairs={{0,9},{1,8},{4,13},{5,12},{8,1},{9,0},{12,5},{13,4},{2,11},{3,10},... | collective-permute-start | bytes 61448 | tf_op jit(solution)/shard_map/interface/ppermute | solution.py:204
  9.5 9.5 %collective-permute-start = (bf16[2,160,64]{2,1,0:T(8,128)(2,1)S(1)}, bf16[2,160,64]{2,1,0:T(8,128)(2,1)S(1)}, u32[]{:S(2)}, u32[]{:S(2)}) collective-permute-start(bf16[2,160,64]{2,1,0:T(8,128)(2,1)S(1)} %get-tuple-element.10), channel_id=1, source_target_pairs={{0,4},{4,8},{8,12},{12,0},{1,5},{5,9},{9,13},{13,1},{2,6},{6,10},{... | collective-permute-start | bytes 122888 | tf_op jit(solution)/shard_map/halo/ppermute | solution.py:201
  11.0 7.9 %collective-permute-start.1 = (bf16[2,160,64]{2,1,0:T(8,128)(2,1)S(1)}, bf16[2,160,64]{2,1,0:T(8,128)(2,1)S(1)}, u32[]{:S(2)}, u32[]{:S(2)}) collective-permute-start(bf16[2,160,64]{2,1,0:T(8,128)(2,1)S(1)} %get-tuple-element.11), channel_id=1, source_target_pairs={{0,12},{4,0},{8,4},{12,8},{1,13},{5,1},{9,5},{13,9},{2,14},{6,2},{... | collective-permute-start | bytes 122888 | tf_op jit(solution)/shard_map/halo/ppermute | solution.py:202
  13.3 5.6 %collective-permute-start.3 = (bf16[2,80,64]{2,1,0:T(8,128)(2,1)S(1)}, bf16[2,80,64]{2,1,0:T(8,128)(2,1)S(1)}, u32[]{:S(2)}, u32[]{:S(2)}) collective-permute-start(bf16[2,80,64]{2,1,0:T(8,128)(2,1)S(1)} %get-tuple-element.12), channel_id=1, source_target_pairs={{0,5},{1,4},{4,9},{5,8},{8,13},{9,12},{12,1},{13,0},{2,7},{3,6},{6... | collective-permute-start | bytes 61448 | tf_op jit(solution)/shard_map/interface/ppermute | solution.py:204
  13.9 5.0 %collective-permute-start.2 = (bf16[2,80,64]{2,1,0:T(8,128)(2,1)S(1)}, bf16[2,80,64]{2,1,0:T(8,128)(2,1)S(1)}, u32[]{:S(2)}, u32[]{:S(2)}) collective-permute-start(bf16[2,80,64]{2,1,0:T(8,128)(2,1)S(1)} %get-tuple-element.12), channel_id=1, source_target_pairs={{0,1},{1,0},{4,5},{5,4},{8,9},{9,8},{12,13},{13,12},{2,3},{3,2},{6... | collective-permute-start | bytes 61448 | tf_op jit(solution)/shard_map/interface/ppermute | solution.py:204

commit v11 on v10

--- a/solution.py
+++ b/solution.py
@@ -129,23 +129,21 @@
         finish(False)
 
 
-def update_kernel(tile, blocks, ready_ref, factor_ref, inverse_ref, *rest):
+def update_kernel(tile, wide, ready_ref, factor_ref, inverse_ref, *rest):
     others, (out_ref, made, sems) = rest[:-3], rest[-3:]
     count, dof, total = ready_ref.shape
     copies = []
-    for b in range(blocks):
-        rows = slice(b * dof // blocks, (b + 1) * dof // blocks)
-        for t in range(total // tile):
+    for start in range(0, total, wide):
+        moved = [dot(inverse_ref[...], other[m, :, start : start + wide]) for other in others for m in range(count)]
+        for t in range(start // tile, min(start + wide, total) // tile):
             cols = slice(t * tile, (t + 1) * tile)
-            moved = [dot(inverse_ref[rows, :], other[m, :, cols]) for other in others for m in range(count)]
             for n in range(count):
-                value = ready_ref[n, rows, cols]
+                value = ready_ref[n, :, cols]
                 for k, part in enumerate(moved):
                     at = n * len(moved) + k
-                    value -= factor_ref[at : at + 1, cols] * part
-                made[n, rows, cols] = value.astype(jnp.bfloat16)
-        for n in range(count):
-            copy = pltpu.make_async_copy(made.at[n, rows, :], out_ref.at[n, rows, :], sems.at[b, n])
+                    value -= factor_ref[at : at + 1, cols] * part[:, t * tile - start : (t + 1) * tile - start]
+                made[t, n] = value.astype(jnp.bfloat16)
+            copy = pltpu.make_async_copy(made.at[t], out_ref.at[:, :, cols], sems.at[t])
             copy.start()
             copies.append(copy)
     for copy in copies:
@@ -228,14 +226,13 @@
           trace_matrix, lift_matrix, volume_matrix, block_inverse, low, high, *pieces)
 
     vmem = pl.BlockSpec(memory_space=pltpu.VMEM)
-    blocks = 2
     with jax.named_scope("update"):
         result = pl.pallas_call(
-            functools.partial(update_kernel, tile, blocks),
+            functools.partial(update_kernel, tile, 2 * tile),
             out_shape=jax.ShapeDtypeStruct((count, dof, total), bf16),
             in_specs=[vmem] * (2 + peers),
             out_specs=pl.BlockSpec(memory_space=pl.ANY),
-            scratch_shapes=[pltpu.VMEM((count, dof, total), bf16), pltpu.SemaphoreType.DMA((blocks, count))],
+            scratch_shapes=[pltpu.VMEM((steps, count, dof, tile), bf16), pltpu.SemaphoreType.DMA((steps,))],
             compiler_params=pltpu.CompilerParams(vmem_limit_bytes=VMEM_LIMIT),
             cost_estimate=pl.CostEstimate(flops=2 * count * total * dof * dof * (peers - 1),
                                           bytes_accessed=count * dof * total * 8, transcendentals=0),

time: 33.9 us -> 34.2 us (level)
  no operation moved by 1% of the time
where the time goes in v11:
time: 34.2 us; the launch traced here: 34 us
  Pallas kernels  13.5 us (39%)
  starting transfers between devices  12.4 us (36%)
  waiting for transfers between devices  4.67 us (14%)
  local copies, waits for them, and re-layouts  2.58 us (8%)
  between operations  0.79 us (2%)
    pallas_call x1, Pallas kernels, body(): pl.pallas_call(functools.partial(couple_kernel, shards, peers), grid=(ste...  10.4 us
    ppermute x4, starting transfers between devices, body(): lax.ppermute(cross, ('space', 'row'), [(i * 2 + r, (i + d) % shards * 2 +...  5.62 us
    ppermute x1, starting transfers between devices, body(): lax.ppermute(current, 'inst', [(i, (i + d) % peers) for i in range(peers)])  2.94 us
    unnamed x20, local copies, waits for them, and re-layouts  2.58 us
    ppermute x1, waiting for transfers between devices, body(): lax.ppermute(current, 'inst', [(i, (i + d) % peers) for i in range(peers)])  2.5 us
    ppermute x1, starting transfers between devices, body(): lax.ppermute(down, 'space', [(i, (i - 1) % shards) for i in range(shards)])  2.25 us
    ppermute x4, waiting for transfers between devices, body(): lax.ppermute(cross, ('space', 'row'), [(i * 2 + r, (i + d) % shards * 2 +...  2.16 us
    pallas_call x1, Pallas kernels, body(): pl.pallas_call(functools.partial(update_kernel, tile, 2 * tile), out_shap...  2.08 us
  transfers between devices with their start and end apart: 7, of which 3 were waited for; matrix products, arithmetic and copies ran while one was open for 4% of the time, Pallas kernels for 34%

profile of v11, /device:TPU:0, one launch (start us, length us, event | category | flops | bytes accessed | tf_op | source)
XLA Modules:
  0.0 34.0 jit_solution(6722768325808862850)
XLA Ops:
  0.0 2.9 %collective-permute-start.6 = (bf16[2,320,1024]{2,1,0:T(8,128)(2,1)}, bf16[2,320,1024]{2,1,0:T(8,128)(2,1)S(1)}, u32[]{:S(2)}, u32[]{:S(2)}) collective-permute-start(bf16[2,320,1024]{2,1,0:T(8,128)(2,1)} %bitcast.10), channel_id=1, source_target_pairs={{0,2},{2,0},{1,3},{3,1},{4,6},{6,4},{5,7},{7,5},{8,10},{10,8},{9,1... | collective-permute-start | bytes 3932168 | tf_op jit(solution)/shard_map/instances/ppermute | solution.py:175
  2.9 1.2 %copy.13.trace_ref = bf16[480,320]{1,0:T(8,128)(2,1)S(1)} copy(bf16[480,320]{0,1:T(8,128)(2,1)} %param.18) | data formatting | bytes 614400 | tf_op args[7]
  4.2 0.1 pad_add_fusion.place_ref
  4.2 0.0 copy-start
  4.2 1.3 %copy-done = bf16[1,2,320,1024]{3,2,1,0:T(8,128)(2,1)S(1)} copy-done((bf16[1,2,320,1024]{3,2,1,0:T(8,128)(2,1)S(1)}, bf16[1,2,320,1024]{3,2,1,0:T(8,128)(2,1)}, u32[]{:S(2)}) %copy-start) | copy-done | bytes 1310744
  5.6 0.0 copy-start.8
  5.6 0.0 copy-start.1
  5.6 0.0 copy-start.2
  5.6 0.0 copy-start.3
  5.6 0.0 copy-start.4
  5.6 0.0 copy-start.5
  5.6 0.0 copy-start.6
  5.6 0.0 copy-start.7
  5.6 1.0 %ends.1 = (bf16[2,160,64]{2,1,0:T(8,128)(2,1)S(1)}, bf16[2,160,64]{2,1,0:T(8,128)(2,1)S(1)}, bf16[2,80,64]{2,1,0:T(8,128)(2,1)S(1)}) custom-call(s32[3]{0:T(128)S(1)} %pad_add_fusion.place_ref, bf16[2,320,1024]{2,1,0:T(8,128)(2,1)S(1)} %bitcast.11, bf16[2,320,1024]{2,1,0:T(8,128)(2,1)S(1)} %bitcast.12, bf16[480,320]{1,0:T(8,128)(2,1)S(1)} %copy.13.trace_ref), custom_call_target="tpu_custom_call" | custom-call | flops 104857600 | bytes 1000000 | tf_op jit(solution)/shard_map/ends/ends/pallas_call | solution.py:179
  6.6 2.8 %collective-permute-start.5 = (bf16[2,80,64]{2,1,0:T(8,128)(2,1)S(1)}, bf16[2,80,64]{2,1,0:T(8,128)(2,1)S(1)}, u32[]{:S(2)}, u32[]{:S(2)}) collective-permute-start(bf16[2,80,64]{2,1,0:T(8,128)(2,1)S(1)} %get-tuple-element.12), channel_id=1, source_target_pairs={{0,13},{1,12},{4,1},{5,0},{8,5},{9,4},{12,9},{13,8},{2,15},{3,14},... | collective-permute-start | bytes 61448 | tf_op jit(solution)/shard_map/interface/ppermute | solution.py:202
  9.5 0.0 collective-permute-start.4
  9.5 1.6 %collective-permute-start = (bf16[2,160,64]{2,1,0:T(8,128)(2,1)S(1)}, bf16[2,160,64]{2,1,0:T(8,128)(2,1)S(1)}, u32[]{:S(2)}, u32[]{:S(2)}) collective-permute-start(bf16[2,160,64]{2,1,0:T(8,128)(2,1)S(1)} %get-tuple-element.10), channel_id=1, source_target_pairs={{0,4},{4,8},{8,12},{12,0},{1,5},{5,9},{9,13},{13,1},{2,6},{6,10},{... | collective-permute-start | bytes 122888 | tf_op jit(solution)/shard_map/halo/ppermute | solution.py:199
  11.0 2.2 %collective-permute-start.1 = (bf16[2,160,64]{2,1,0:T(8,128)(2,1)S(1)}, bf16[2,160,64]{2,1,0:T(8,128)(2,1)S(1)}, u32[]{:S(2)}, u32[]{:S(2)}) collective-permute-start(bf16[2,160,64]{2,1,0:T(8,128)(2,1)S(1)} %get-tuple-element.11), channel_id=1, source_target_pairs={{0,12},{4,0},{8,4},{12,8},{1,13},{5,1},{9,5},{13,9},{2,14},{6,2},{... | collective-permute-start | bytes 122888 | tf_op jit(solution)/shard_map/halo/ppermute | solution.py:200
  13.3 0.0 collective-permute-done.5.rest_3_
  13.3 0.0 collective-permute-start.3
  13.3 0.6 %collective-permute-done.4.rest_2_ = bf16[2,80,64]{2,1,0:T(8,128)(2,1)S(1)} collective-permute-done((bf16[2,80,64]{2,1,0:T(8,128)(2,1)S(1)}, bf16[2,80,64]{2,1,0:T(8,128)(2,1)S(1)}, u32[]{:S(2)}, u32[]{:S(2)}) %collective-permute-start.4) | collective-permute-done | bytes 20512 | tf_op jit(solution)/shard_map/interface/ppermute | solution.py:202
  13.9 2.8 %collective-permute-start.2 = (bf16[2,80,64]{2,1,0:T(8,128)(2,1)S(1)}, bf16[2,80,64]{2,1,0:T(8,128)(2,1)S(1)}, u32[]{:S(2)}, u32[]{:S(2)}) collective-permute-start(bf16[2,80,64]{2,1,0:T(8,128)(2,1)S(1)} %get-tuple-element.12), channel_id=1, source_target_pairs={{0,1},{1,0},{4,5},{5,4},{8,9},{9,8},{12,13},{13,12},{2,3},{3,2},{6... | collective-permute-start | bytes 61448 | tf_op jit(solution)/shard_map/interface/ppermute | solution.py:202
  17.4 0.0 copy-done.8
  17.4 1.5 %collective-permute-done.3.rest_1_ = bf16[2,80,64]{2,1,0:T(8,128)(2,1)S(1)} collective-permute-done((bf16[2,80,64]{2,1,0:T(8,128)(2,1)S(1)}, bf16[2,80,64]{2,1,0:T(8,128)(2,1)S(1)}, u32[]{:S(2)}, u32[]{:S(2)}) %collective-permute-start.3) | collective-permute-done | bytes 20512 | tf_op jit(solution)/shard_map/interface/ppermute | solution.py:202
  18.9 0.0 collective-permute-done.2.rest_0_
  18.9 0.0 collective-permute-done.low_ref
  18.9 0.0 collective-permute-done.1.high_ref
  18.9 0.0 copy-done.1
  18.9 0.0 copy-done.2
  19.0 0.0 copy-done.3
  19.0 0.0 copy-done.4
  19.0 0.0 copy-done.5
  19.0 0.0 copy-done.6
  19.0 0.0 copy-done.7
  19.0 10.4 %couple.1 = (f32[2,320,1024]{2,1,0:T(8,128)S(1)}, f32[4,1024]{1,0:T(4,128)S(1)}) custom-call(s32[3]{0:T(128)S(1)} %pad_add_fusion.place_ref, f32[1]{0:T(128)S(6)} %copy.17.freq_ref, f32[4,4]{1,0:T(4,128)S(1)} %copy-done.7, s32[6,1024]{1,0:T(8,128)S(1)} %bitcast.15, s32[2,64]{1,0:T(2,128)S(1)} %bitcast.17, bf16[2,320,1024]{2,1,0:T(8,128)(2,1)S(1)} %bitcast.13, ...), custom_call_target="tpu_custom_call" | custom-call | flops 3690987520 | bytes 6553600 | tf_op jit(solution)/shard_map/couple/couple/pallas_call | solution.py:210
  29.4 2.5 %collective-permute-done.6.rest_0_ = bf16[2,320,1024]{2,1,0:T(8,128)(2,1)S(1)} collective-permute-done((bf16[2,320,1024]{2,1,0:T(8,128)(2,1)}, bf16[2,320,1024]{2,1,0:T(8,128)(2,1)S(1)}, u32[]{:S(2)}, u32[]{:S(2)}) %collective-permute-start.6) | collective-permute-done | bytes 1310752 | tf_op jit(solution)/shard_map/instances/ppermute | solution.py:175
  31.9 2.1 %update.1 = bf16[2,320,1024]{2,1,0:T(8,128)(2,1)} custom-call(f32[2,320,1024]{2,1,0:T(8,128)S(1)} %get-tuple-element.13.ready_ref, f32[4,1024]{1,0:T(4,128)S(1)} %get-tuple-element.14.factor_ref, bf16[320,320]{1,0:T(8,128)(2,1)S(1)} %copy-done.1, bf16[2,320,1024]{2,1,0:T(8,128)(2,1)S(1)} %collective-permute-done.6.rest_0_), custom_call_target="tpu_custom_call" | custom-call | flops 419430400 | bytes 5242880 | tf_op jit(solution)/shard_map/update/update/pallas_call | solution.py:230
  (1 shorter events, 0.0 us)
Async XLA Ops:
  0.0 31.9 %collective-permute-start.6 = (bf16[2,320,1024]{2,1,0:T(8,128)(2,1)}, bf16[2,320,1024]{2,1,0:T(8,128)(2,1)S(1)}, u32[]{:S(2)}, u32[]{:S(2)}) collective-permute-start(bf16[2,320,1024]{2,1,0:T(8,128)(2,1)} %bitcast.10), channel_id=1, source_target_pairs={{0,2},{2,0},{1,3},{3,1},{4,6},{6,4},{5,7},{7,5},{8,10},{10,8},{9,1... | collective-permute-start | bytes 3932168 | tf_op jit(solution)/shard_map/instances/ppermute | solution.py:175
  4.2 1.3 %copy-start = (bf16[1,2,320,1024]{3,2,1,0:T(8,128)(2,1)S(1)}, bf16[1,2,320,1024]{3,2,1,0:T(8,128)(2,1)}, u32[]{:S(2)}) copy-start(bf16[1,2,320,1024]{3,2,1,0:T(8,128)(2,1)} %param.11) | copy-start | bytes 3932164
  5.6 11.8 %copy-start.8 = (s32[1,6,1024]{2,0,1:T(1,128)S(1)}, s32[1,6,1024]{2,0,1:T(1,128)}, u32[]{:S(2)}) copy-start(s32[1,6,1024]{2,0,1:T(1,128)} %param.15) | copy-start | bytes 73732
  5.6 13.4 %copy-start.1 = (bf16[320,320]{1,0:T(8,128)(2,1)S(1)}, bf16[320,320]{1,0:T(8,128)(2,1)}, u32[]{:S(2)}) copy-start(bf16[320,320]{1,0:T(8,128)(2,1)} %inverse_ref.3) | copy-start | bytes 614404
  5.6 13.4 %copy-start.2 = (bf16[1,2,320,1024]{3,2,1,0:T(8,128)(2,1)S(1)}, bf16[1,2,320,1024]{3,2,1,0:T(8,128)(2,1)}, u32[]{:S(2)}) copy-start(bf16[1,2,320,1024]{3,2,1,0:T(8,128)(2,1)} %param.12) | copy-start | bytes 3932164
  5.6 13.4 %copy-start.3 = (bf16[320,480]{1,0:T(8,128)(2,1)S(1)}, bf16[320,480]{1,0:T(8,128)(2,1)}, u32[]{:S(2)}) copy-start(bf16[320,480]{1,0:T(8,128)(2,1)} %lift_ref.1) | copy-start | bytes 921604
  5.6 13.4 %copy-start.4 = (bf16[320,320]{1,0:T(8,128)(2,1)S(1)}, bf16[320,320]{1,0:T(8,128)(2,1)}, u32[]{:S(2)}) copy-start(bf16[320,320]{1,0:T(8,128)(2,1)} %volume_ref.1) | copy-start | bytes 614404
  5.6 13.4 %copy-start.5 = (f32[1,1024]{1,0:T(1,128)S(1)}, f32[1,1024]{1,0:T(1,128)}, u32[]{:S(2)}) copy-start(f32[1,1024]{1,0:T(1,128)} %scale_ref.1) | copy-start | bytes 12292
  5.6 13.4 %copy-start.6 = (s32[1,2,64]{2,1,0:T(2,128)S(1)}, s32[1,2,64]{2,1,0:T(2,128)}, u32[]{:S(2)}) copy-start(s32[1,2,64]{2,1,0:T(2,128)} %param.16) | copy-start | bytes 1540
  5.6 13.4 %copy-start.7 = (f32[4,4]{1,0:T(4,128)S(1)}, f32[4,4]{1,0:T(4,128)}, u32[]{:S(2)}) copy-start(f32[4,4]{1,0:T(4,128)} %constant.13.clone.table_ref) | copy-start | bytes 196
  6.6 6.6 %collective-permute-start.5 = (bf16[2,80,64]{2,1,0:T(8,128)(2,1)S(1)}, bf16[2,80,64]{2,1,0:T(8,128)(2,1)S(1)}, u32[]{:S(2)}, u32[]{:S(2)}) collective-permute-start(bf16[2,80,64]{2,1,0:T(8,128)(2,1)S(1)} %get-tuple-element.12), channel_id=1, source_target_pairs={{0,13},{1,12},{4,1},{5,0},{8,5},{9,4},{12,9},{13,8},{2,15},{3,14},... | collective-permute-start | bytes 61448 | tf_op jit(solution)/shard_map/interface/ppermute | solution.py:202
  9.5 4.5 %collective-permute-start.4 = (bf16[2,80,64]{2,1,0:T(8,128)(2,1)S(1)}, bf16[2,80,64]{2,1,0:T(8,128)(2,1)S(1)}, u32[]{:S(2)}, u32[]{:S(2)}) collective-permute-start(bf16[2,80,64]{2,1,0:T(8,128)(2,1)S(1)} %get-tuple-element.12), channel_id=1, source_target_pairs={{0,9},{1,8},{4,13},{5,12},{8,1},{9,0},{12,5},{13,4},{2,11},{3,10},... | collective-permute-start | bytes 61448 | tf_op jit(solution)/shard_map/interface/ppermute | solution.py:202
  9.5 9.5 %collective-permute-start = (bf16[2,160,64]{2,1,0:T(8,128)(2,1)S(1)}, bf16[2,160,64]{2,1,0:T(8,128)(2,1)S(1)}, u32[]{:S(2)}, u32[]{:S(2)}) collective-permute-start(bf16[2,160,64]{2,1,0:T(8,128)(2,1)S(1)} %get-tuple-element.10), channel_id=1, source_target_pairs={{0,4},{4,8},{8,12},{12,0},{1,5},{5,9},{9,13},{13,1},{2,6},{6,10},{... | collective-permute-start | bytes 122888 | tf_op jit(solution)/shard_map/halo/ppermute | solution.py:199
  11.0 7.9 %collective-permute-start.1 = (bf16[2,160,64]{2,1,0:T(8,128)(2,1)S(1)}, bf16[2,160,64]{2,1,0:T(8,128)(2,1)S(1)}, u32[]{:S(2)}, u32[]{:S(2)}) collective-permute-start(bf16[2,160,64]{2,1,0:T(8,128)(2,1)S(1)} %get-tuple-element.11), channel_id=1, source_target_pairs={{0,12},{4,0},{8,4},{12,8},{1,13},{5,1},{9,5},{13,9},{2,14},{6,2},{... | collective-permute-start | bytes 122888 | tf_op jit(solution)/shard_map/halo/ppermute | solution.py:200
  13.3 5.6 %collective-permute-start.3 = (bf16[2,80,64]{2,1,0:T(8,128)(2,1)S(1)}, bf16[2,80,64]{2,1,0:T(8,128)(2,1)S(1)}, u32[]{:S(2)}, u32[]{:S(2)}) collective-permute-start(bf16[2,80,64]{2,1,0:T(8,128)(2,1)S(1)} %get-tuple-element.12), channel_id=1, source_target_pairs={{0,5},{1,4},{4,9},{5,8},{8,13},{9,12},{12,1},{13,0},{2,7},{3,6},{6... | collective-permute-start | bytes 61448 | tf_op jit(solution)/shard_map/interface/ppermute | solution.py:202
  13.9 5.0 %collective-permute-start.2 = (bf16[2,80,64]{2,1,0:T(8,128)(2,1)S(1)}, bf16[2,80,64]{2,1,0:T(8,128)(2,1)S(1)}, u32[]{:S(2)}, u32[]{:S(2)}) collective-permute-start(bf16[2,80,64]{2,1,0:T(8,128)(2,1)S(1)} %get-tuple-element.12), channel_id=1, source_target_pairs={{0,1},{1,0},{4,5},{5,4},{8,9},{9,8},{12,13},{13,12},{2,3},{3,2},{6... | collective-permute-start | bytes 61448 | tf_op jit(solution)/shard_map/interface/ppermute | solution.py:202

commit v12 on v4

--- a/solution.py
+++ b/solution.py
@@ -12,6 +12,8 @@
 OPPOSITE = (1, 0, 3, 2, 5, 4)
 LANES = 128
 VMEM_LIMIT = 40 * 1024 * 1024
+CUT_LIMIT = 56 * 1024 * 1024
+COUPLE_FLOPS = 7_500_000_000
 
 
 def spectral_table(instances):
@@ -31,6 +33,16 @@
 
 def dot(left, right):
     return jnp.dot(left, right, preferred_element_type=jnp.float32)
+
+
+def cut_kernel(bounds, head_ref, all_ref, *rest):
+    out_refs, sems = rest[:-1], rest[-1]
+    copies = []
+    for k, (first, last) in enumerate(bounds):
+        copies.append(pltpu.make_async_copy(all_ref.at[:, :, first:last], out_refs[k], sems.at[k]))
+        copies[k].start()
+    for copy in copies:
+        copy.wait()
 
 
 def ends_kernel(place_ref, first_ref, last_ref, trace_ref, up_ref, down_ref, cross_ref):
@@ -47,7 +59,7 @@
 
 def couple_kernel(shards, peers, place_ref, freq_ref, table_ref, adj_ref, partner_ref, all_ref, tile_ref, forcing_ref,
                   scale_ref, trace_ref, lift_ref, volume_ref, inverse_ref, low_ref, high_ref, *rest):
-    pieces, (out_ref, factor_ref, traces) = rest[:shards], rest[shards:]
+    pieces, heads, (out_ref, factor_ref, traces) = rest[:shards], rest[shards:-3], rest[-3:]
     step = pl.program_id(0)
     steps = pl.num_programs(0)
     count, dof, total = all_ref.shape
@@ -120,6 +132,14 @@
             update = dot(inverse_ref[...], value.astype(jnp.bfloat16))
             out_ref[n] = tile_ref[n].astype(jnp.float32) + update * inverse_scale
 
+        @pl.when(step == 0)
+        def _():
+            moved = [dot(inverse_ref[...], head[m]) for head in heads for m in range(count)]
+            for n in range(count):
+                for k, part in enumerate(moved):
+                    row = n * len(moved) + k
+                    out_ref[n, :, :LANES] -= factor_ref[row : row + 1, :LANES] * part
+
     @pl.when(at_edge)
     def _():
         finish(True)
@@ -129,22 +149,35 @@
         finish(False)
 
 
-def update_kernel(tile, ready_ref, factor_ref, inverse_ref, *rest):
-    others, (out_ref, made, sems) = rest[:-3], rest[-3:]
+def update_kernel(base, bounds, peers, tile, ready_ref, factor_ref, inverse_ref, *rest):
+    pieces = len(bounds) * (peers - 1)
+    arrived, (out_ref, made, sems) = rest[:pieces], rest[-3:]
     count, dof, total = ready_ref.shape
     copies = []
-    for t in range(total // tile):
-        cols = slice(t * tile, (t + 1) * tile)
-        moved = [dot(inverse_ref[...], other[m, :, cols]) for other in others for m in range(count)]
-        for n in range(count):
-            value = ready_ref[n, :, cols]
-            for k, part in enumerate(moved):
-                at = n * len(moved) + k
-                value -= factor_ref[at : at + 1, cols] * part
-            made[t, n] = value.astype(jnp.bfloat16)
-        copy = pltpu.make_async_copy(made.at[t], out_ref.at[:, :, cols], sems.at[t])
+
+    def send(first, last):
+        copy = pltpu.make_async_copy(
+            made.at[:, :, first - base : last - base], out_ref.at[:, :, first:last], sems.at[len(copies)])
         copy.start()
         copies.append(copy)
+
+    if base < bounds[0][0]:
+        for n in range(count):
+            made[n, :, : bounds[0][0] - base] = ready_ref[n, :, base : bounds[0][0]].astype(jnp.bfloat16)
+        send(base, bounds[0][0])
+    for b, (first, last) in enumerate(bounds):
+        others = arrived[b * (peers - 1) : (b + 1) * (peers - 1)]
+        for start in range(first, last, tile):
+            stop = min(start + tile, last)
+            moved = [dot(inverse_ref[...], other[m, :, start - first : stop - first])
+                     for other in others for m in range(count)]
+            for n in range(count):
+                value = ready_ref[n, :, start:stop]
+                for k, part in enumerate(moved):
+                    row = n * len(moved) + k
+                    value -= factor_ref[row : row + 1, start:stop] * part
+                made[n, :, start - base : stop - base] = value.astype(jnp.bfloat16)
+            send(start, stop)
     for copy in copies:
         copy.wait()
 
@@ -171,8 +204,21 @@
     bf16 = jnp.bfloat16
 
     with jax.named_scope("instances"):
-        others = [lax.ppermute(current, "inst", [(i, (i + d) % peers) for i in range(peers)])
-                  for d in range(1, peers)]
+        tile = 256
+        bounds = [(0, LANES), (LANES, total - tile), (total - tile, total)]
+        head = current[:, :, :LANES]
+        chunks = [head] + list(pl.pallas_call(
+            functools.partial(cut_kernel, bounds[1:]),
+            out_shape=tuple(jax.ShapeDtypeStruct((count, dof, last - first), bf16) for first, last in bounds[1:]),
+            in_specs=[pl.BlockSpec(memory_space=pl.ANY)] * 2,
+            out_specs=tuple([pl.BlockSpec(memory_space=pl.ANY)] * (len(bounds) - 1)),
+            scratch_shapes=[pltpu.SemaphoreType.DMA((len(bounds) - 1,))],
+            compiler_params=pltpu.CompilerParams(vmem_limit_bytes=CUT_LIMIT),
+            cost_estimate=pl.CostEstimate(flops=0, bytes_accessed=0, transcendentals=0),
+            name="cut",
+        )(head, current))
+        arriving = [[lax.ppermute(chunk, "inst", [(i, (i + d) % peers) for i in range(peers)])
+                     for d in range(1, peers)] for chunk in chunks]
 
     with jax.named_scope("ends"):
         up, down, cross = pl.pallas_call(
@@ -182,7 +228,7 @@
                        jax.ShapeDtypeStruct((count, 2 * width, LAYER), bf16),
                        jax.ShapeDtypeStruct((count, width, iface_rows), bf16)),
             in_specs=[smem,
-                      pl.BlockSpec((count, dof, LANES), lambda j: (0, 0, 0)),
+                      whole(head),
                       pl.BlockSpec((count, dof, LANES), lambda j: (0, 0, total // LANES - 1)),
                       whole(trace_matrix)],
             out_specs=(pl.BlockSpec((count, 2 * width, LAYER), lambda j: (0, 0, 0)),
@@ -192,7 +238,7 @@
             cost_estimate=pl.CostEstimate(flops=8 * width * dof * LANES * 2 * count,
                                           bytes_accessed=1_000_000, transcendentals=0),
             name="ends",
-        )(place, current, current, trace_matrix)
+        )(place, head, current, trace_matrix)
 
     with jax.named_scope("halo"):
         low = lax.ppermute(up, "space", [(i, (i + 1) % shards) for i in range(shards)])
@@ -202,7 +248,6 @@
                                [(i * 2 + r, (i + d) % shards * 2 + 1 - r) for i in range(shards) for r in range(2)])
                   for d in range(shards)]
 
-    tile = 256
     steps = total // tile
     by_tile = lambda *lead: pl.BlockSpec(lead + (tile,), lambda j: (0,) * len(lead) + (j,))
     with jax.named_scope("couple"):
@@ -213,30 +258,35 @@
                        jax.ShapeDtypeStruct((count * count * (peers - 1), total), jnp.float32)),
             in_specs=[smem, smem, smem, by_tile(6), whole(partner_rows), whole(current), by_tile(count, dof),
                       by_tile(count, dof), by_tile(1), whole(trace_matrix), whole(lift_matrix),
-                      whole(volume_matrix), whole(block_inverse), whole(low), whole(high)] + [whole(p) for p in pieces],
+                      whole(volume_matrix), whole(block_inverse), whole(low), whole(high)] + [whole(p) for p in pieces + arriving[0]],
             out_specs=(by_tile(count, dof), by_tile(count * count * (peers - 1))),
             scratch_shapes=[pltpu.VMEM((6, count * width, total), bf16)],
             compiler_params=pltpu.CompilerParams(vmem_limit_bytes=VMEM_LIMIT),
             cost_estimate=pl.CostEstimate(
-                flops=2 * count * total * (6 * width * dof * 2 + dof * dof + 6 * width * total),
+                flops=COUPLE_FLOPS,
                 bytes_accessed=count * dof * total * 10, transcendentals=0),
             name="couple",
         )(place, frequency, table, neighbours, partner_rows, current, current, forcing_local, metric_scale,
-          trace_matrix, lift_matrix, volume_matrix, block_inverse, low, high, *pieces)
+          trace_matrix, lift_matrix, volume_matrix, block_inverse, low, high, *pieces, *arriving[0])
 
     vmem = pl.BlockSpec(memory_space=pltpu.VMEM)
     with jax.named_scope("update"):
-        result = pl.pallas_call(
-            functools.partial(update_kernel, tile),
-            out_shape=jax.ShapeDtypeStruct((count, dof, total), bf16),
-            in_specs=[vmem] * (2 + peers),
-            out_specs=pl.BlockSpec(memory_space=pl.ANY),
-            scratch_shapes=[pltpu.VMEM((steps, count, dof, tile), bf16), pltpu.SemaphoreType.DMA((steps,))],
-            compiler_params=pltpu.CompilerParams(vmem_limit_bytes=VMEM_LIMIT),
-            cost_estimate=pl.CostEstimate(flops=2 * count * total * dof * dof * (peers - 1),
-                                          bytes_accessed=count * dof * total * 8, transcendentals=0),
-            name="update",
-        )(ready, factors, block_inverse, *others)
+        result = None
+        for base, mine, others in ((0, bounds[1:2], arriving[1]), (bounds[2][0], bounds[2:], arriving[2])):
+            more = [] if result is None else [result]
+            span = mine[-1][1] - base
+            result = pl.pallas_call(
+                functools.partial(update_kernel, base, mine, peers, tile),
+                out_shape=jax.ShapeDtypeStruct((count, dof, total), bf16),
+                in_specs=[vmem] * (3 + len(others)) + [pl.BlockSpec(memory_space=pl.ANY)] * len(more),
+                out_specs=pl.BlockSpec(memory_space=pl.ANY),
+                scratch_shapes=[pltpu.VMEM((count, dof, span), bf16), pltpu.SemaphoreType.DMA((steps,))],
+                input_output_aliases={3 + len(others): 0} if more else {},
+                compiler_params=pltpu.CompilerParams(vmem_limit_bytes=VMEM_LIMIT),
+                cost_estimate=pl.CostEstimate(flops=2 * count * span * dof * dof * (peers - 1),
+                                              bytes_accessed=count * dof * span * 8, transcendentals=0),
+                name="update",
+            )(ready, factors, block_inverse, *others, *more)
     return result[None]
 
 

time: 33.8 us -> 70.8 us (2.09)
  Pallas kernels: 13.1 us -> 50 us
  waiting for transfers between devices: 4.67 us -> 2.81 us
  starting transfers between devices: 12.4 us -> 13.5 us
  local copies, waits for them, and re-layouts: 2.58 us -> 3.31 us
    pallas_call x1 -> x3, Pallas kernels: 1.64 us -> 38.3 us  [the longest x1 35.9 us: body(): pl.pallas_call(functools.partial(cut_kernel, bounds[1:]), out_shape=tuple...]
    ppermute x1 -> x3, waiting for transfers between devices: 2.5 us -> 0.01 us  [body(): lax.ppermute(chunk, 'inst', [(i, (i + d) % peers) for i in range(peers)])]
    ppermute x1 -> x3, starting transfers between devices: 2.94 us -> 5.2 us  [body(): lax.ppermute(chunk, 'inst', [(i, (i + d) % peers) for i in range(peers)])]
    slice x0 -> x1, local copies, waits for them, and re-layouts: none -> 1.03 us  [body(): head = current[:, :, :LANES]]
    ppermute x4, starting transfers between devices: 5.62 us -> 4.67 us  [body(): lax.ppermute(cross, ('space', 'row'), [(i * 2 + r, (i + d) % shards * 2 +...]
    ppermute x1, waiting for transfers between devices: 0.01 us -> 0.88 us  [body(): lax.ppermute(down, 'space', [(i, (i - 1) % shards) for i in range(shards)])]
    unnamed x20 -> x26, local copies, waits for them, and re-layouts: 2.58 us -> 2.27 us
  transfers between devices with their start and end apart: 7 -> 9, of which waited for: 3 -> 4; matrix products, arithmetic and copies ran while one was open for 4% -> 2% of each run, Pallas kernels for 34% -> 69%
where the time goes in v12:
time: 70.8 us; the launch traced here: 70.6 us
  Pallas kernels  50 us (71%)
  starting transfers between devices  13.5 us (19%)
  local copies, waits for them, and re-layouts  3.31 us (5%)
  waiting for transfers between devices  2.81 us (4%)
  between operations  0.82 us (1%)
    pallas_call x1, Pallas kernels, body(): pl.pallas_call(functools.partial(cut_kernel, bounds[1:]), out_shape=tuple...  35.9 us
    pallas_call x1, Pallas kernels, body(): pl.pallas_call(functools.partial(couple_kernel, shards, peers), grid=(ste...  10.7 us
    ppermute x3, starting transfers between devices, body(): lax.ppermute(chunk, 'inst', [(i, (i + d) % peers) for i in range(peers)])  5.2 us
    ppermute x4, starting transfers between devices, body(): lax.ppermute(cross, ('space', 'row'), [(i * 2 + r, (i + d) % shards * 2 +...  4.67 us
    pallas_call x2, Pallas kernels, body(): pl.pallas_call(functools.partial(update_kernel, base, mine, peers, tile),...  2.48 us
    unnamed x26, local copies, waits for them, and re-layouts  2.27 us
    ppermute x1, starting transfers between devices, body(): lax.ppermute(down, 'space', [(i, (i - 1) % shards) for i in range(shards)])  2.16 us
    ppermute x4, waiting for transfers between devices, body(): lax.ppermute(cross, ('space', 'row'), [(i * 2 + r, (i + d) % shards * 2 +...  1.92 us
  transfers between devices with their start and end apart: 9, of which 4 were waited for; matrix products, arithmetic and copies ran while one was open for 2% of the time, Pallas kernels for 69%

profile of v12, /device:TPU:0, one launch (start us, length us, event | category | flops | bytes accessed | tf_op | source)
XLA Modules:
  0.0 70.6 jit_solution(8489159322696821837)
XLA Ops:
  0.0 0.0 copy-start
  0.0 1.0 %slice.4.first_ref.head_ref = bf16[2,320,128]{2,1,0:T(8,128)(2,1)S(1)} slice(bf16[2,320,1024]{2,1,0:T(8,128)(2,1)} %bitcast.10), slice={[0:2], [0:320], [0:128]} | slice | bytes 327680 | tf_op jit(solution)/shard_map/instances/slice | solution.py:209
  1.0 0.0 copy-start.1
  1.0 3.0 %collective-permute-start.6 = (bf16[2,320,128]{2,1,0:T(8,128)(2,1)S(1)}, bf16[2,320,128]{2,1,0:T(8,128)(2,1)S(1)}, u32[]{:S(2)}, u32[]{:S(2)}) collective-permute-start(bf16[2,320,128]{2,1,0:T(8,128)(2,1)S(1)} %slice.4.first_ref.head_ref), channel_id=1, source_target_pairs={{0,2},{2,0},{1,3},{3,1},{4,6},{6,4},{5,7},{7,5},{8,10},{10,8},{9,1... | collective-permute-start | bytes 491528 | tf_op jit(solution)/shard_map/instances/ppermute | solution.py:220
  4.1 0.0 copy-done.1
  4.1 35.9 %cut.1 = (bf16[2,320,640]{2,1,0:T(8,128)(2,1)}, bf16[2,320,256]{2,1,0:T(8,128)(2,1)}) custom-call(bf16[2,320,128]{2,1,0:T(8,128)(2,1)} %copy-done.1, bf16[2,320,1024]{2,1,0:T(8,128)(2,1)} %bitcast.11), custom_call_target="tpu_custom_call" | custom-call | tf_op jit(solution)/shard_map/instances/cut/pallas_call | solution.py:210
  39.9 0.0 copy-start.10
  39.9 0.6 collective-permute-start.8
  40.6 0.0 copy-start.3
  40.6 0.0 copy-start.5
  40.6 0.0 copy-start.7
  40.6 0.0 copy-start.8
  40.6 0.0 copy-start.9
  40.6 0.1 pad_add_fusion.place_ref
  40.7 1.3 %copy.14.trace_ref = bf16[480,320]{1,0:T(8,128)(2,1)S(1)} copy(bf16[480,320]{0,1:T(8,128)(2,1)} %param.18) | data formatting | bytes 614400 | tf_op args[7]
  42.0 0.0 copy-done
  42.0 0.0 copy-start.2
  42.0 0.9 %copy-done.2 = bf16[2,320,128]{2,1,0:T(8,128)(2,1)S(1)} copy-done((bf16[2,320,128]{2,1,0:T(8,128)(2,1)S(1)}, bf16[2,320,128]{2,1,0:T(8,128)(2,1)}, u32[]{:S(2)}) %copy-start.2) | copy-done | bytes 163864
  42.9 0.0 copy-start.11
  42.9 1.0 %ends.1 = (bf16[2,160,64]{2,1,0:T(8,128)(2,1)S(1)}, bf16[2,160,64]{2,1,0:T(8,128)(2,1)S(1)}, bf16[2,80,64]{2,1,0:T(8,128)(2,1)S(1)}) custom-call(s32[3]{0:T(128)S(1)} %pad_add_fusion.place_ref, bf16[2,320,128]{2,1,0:T(8,128)(2,1)S(1)} %copy-done.2, bf16[2,320,1024]{2,1,0:T(8,128)(2,1)S(1)} %bitcast.12, bf16[480,320]{1,0:T(8,128)(2,1)S(1)} %copy.14.trace_ref), custom_call_target="tpu_custom_call" | custom-call | flops 104857600 | bytes 1000000 | tf_op jit(solution)/shard_map/ends/ends/pallas_call | solution.py:224
  43.9 2.8 %collective-permute-start.5 = (bf16[2,80,64]{2,1,0:T(8,128)(2,1)S(1)}, bf16[2,80,64]{2,1,0:T(8,128)(2,1)S(1)}, u32[]{:S(2)}, u32[]{:S(2)}) collective-permute-start(bf16[2,80,64]{2,1,0:T(8,128)(2,1)S(1)} %get-tuple-element.14), channel_id=1, source_target_pairs={{0,13},{1,12},{4,1},{5,0},{8,5},{9,4},{12,9},{13,8},{2,15},{3,14},... | collective-permute-start | bytes 61448 | tf_op jit(solution)/shard_map/interface/ppermute | solution.py:247
  46.8 0.0 collective-permute-start.4
  46.8 1.2 %collective-permute-start.3 = (bf16[2,80,64]{2,1,0:T(8,128)(2,1)S(1)}, bf16[2,80,64]{2,1,0:T(8,128)(2,1)S(1)}, u32[]{:S(2)}, u32[]{:S(2)}) collective-permute-start(bf16[2,80,64]{2,1,0:T(8,128)(2,1)S(1)} %get-tuple-element.14), channel_id=1, source_target_pairs={{0,5},{1,4},{4,9},{5,8},{8,13},{9,12},{12,1},{13,0},{2,7},{3,6},{6... | collective-permute-start | bytes 61448 | tf_op jit(solution)/shard_map/interface/ppermute | solution.py:247
  48.0 0.5 collective-permute-done.5.rest_3_
  48.4 1.5 %collective-permute-start = (bf16[2,160,64]{2,1,0:T(8,128)(2,1)S(1)}, bf16[2,160,64]{2,1,0:T(8,128)(2,1)S(1)}, u32[]{:S(2)}, u32[]{:S(2)}) collective-permute-start(bf16[2,160,64]{2,1,0:T(8,128)(2,1)S(1)} %get-tuple-element.12), channel_id=1, source_target_pairs={{0,4},{4,8},{8,12},{12,0},{1,5},{5,9},{9,13},{13,1},{2,6},{6,10},{... | collective-permute-start | bytes 122888 | tf_op jit(solution)/shard_map/halo/ppermute | solution.py:244
  50.0 1.2 %collective-permute-done.4.rest_2_ = bf16[2,80,64]{2,1,0:T(8,128)(2,1)S(1)} collective-permute-done((bf16[2,80,64]{2,1,0:T(8,128)(2,1)S(1)}, bf16[2,80,64]{2,1,0:T(8,128)(2,1)S(1)}, u32[]{:S(2)}, u32[]{:S(2)}) %collective-permute-start.4) | collective-permute-done | bytes 20512 | tf_op jit(solution)/shard_map/interface/ppermute | solution.py:247
  51.2 2.2 %collective-permute-start.1 = (bf16[2,160,64]{2,1,0:T(8,128)(2,1)S(1)}, bf16[2,160,64]{2,1,0:T(8,128)(2,1)S(1)}, u32[]{:S(2)}, u32[]{:S(2)}) collective-permute-start(bf16[2,160,64]{2,1,0:T(8,128)(2,1)S(1)} %get-tuple-element.13), channel_id=1, source_target_pairs={{0,12},{4,0},{8,4},{12,8},{1,13},{5,1},{9,5},{13,9},{2,14},{6,2},{... | collective-permute-start | bytes 122888 | tf_op jit(solution)/shard_map/halo/ppermute | solution.py:245
  53.4 0.0 collective-permute-done.3.rest_1_
  53.4 0.7 collective-permute-start.2
  54.7 0.0 copy-done.10
  54.7 0.2 collective-permute-done.2.rest_0_
  54.9 0.0 copy-done.11
  54.9 1.6 %collective-permute-start.7 = (bf16[2,320,256]{2,1,0:T(8,128)(2,1)S(1)}, bf16[2,320,256]{2,1,0:T(8,128)(2,1)S(1)}, u32[]{:S(2)}, u32[]{:S(2)}) collective-permute-start(bf16[2,320,256]{2,1,0:T(8,128)(2,1)S(1)} %copy-done.11), channel_id=1, source_target_pairs={{0,2},{2,0},{1,3},{3,1},{4,6},{6,4},{5,7},{7,5},{8,10},{10,8},{9,1... | collective-permute-start | bytes 983048 | tf_op jit(solution)/shard_map/instances/ppermute | solution.py:220
  56.5 0.0 collective-permute-done.low_ref
  56.5 0.9 %collective-permute-done.1.high_ref = bf16[2,160,64]{2,1,0:T(8,128)(2,1)S(1)} collective-permute-done((bf16[2,160,64]{2,1,0:T(8,128)(2,1)S(1)}, bf16[2,160,64]{2,1,0:T(8,128)(2,1)S(1)}, u32[]{:S(2)}, u32[]{:S(2)}) %collective-permute-start.1) | collective-permute-done | bytes 40992 | tf_op jit(solution)/shard_map/halo/ppermute | solution.py:245
  57.3 0.0 collective-permute-done.6.rest_4_
  57.3 0.0 copy-done.3
  57.3 0.0 copy-done.5
  57.4 0.0 copy-done.7
  57.4 0.0 copy-done.8
  57.4 0.0 copy-done.9
  57.4 0.0 copy-done.4
  57.4 0.0 copy-done.6
  57.4 10.7 %couple.1 = (f32[2,320,1024]{2,1,0:T(8,128)S(1)}, f32[4,1024]{1,0:T(4,128)S(1)}) custom-call(s32[3]{0:T(128)S(1)} %pad_add_fusion.place_ref, f32[1]{0:T(128)S(6)} %copy.19.freq_ref, f32[4,4]{1,0:T(4,128)S(1)} %copy-done.9, s32[6,1024]{1,0:T(8,128)S(1)} %bitcast.15, s32[2,64]{1,0:T(2,128)S(1)} %bitcast.17, bf16[2,320,1024]{2,1,0:T(8,128)(2,1)S(1)} %bitcast.13, ...), custom_call_target="tpu_custom_call" | custom-call | flops 7500000256 | bytes 6553600 | tf_op jit(solution)/shard_map/couple/couple/pallas_call | solution.py:254
  68.1 0.0 collective-permute-done.8.rest_0_
  68.1 1.4 %update.2.rest_1_ = bf16[2,320,1024]{2,1,0:T(8,128)(2,1)} custom-call(f32[2,320,1024]{2,1,0:T(8,128)S(1)} %get-tuple-element.15.ready_ref, f32[4,1024]{1,0:T(4,128)S(1)} %get-tuple-element.16.factor_ref, bf16[320,320]{1,0:T(8,128)(2,1)S(1)} %copy-done.3, bf16[2,320,640]{2,1,0:T(8,128)(2,1)S(1)} %collective-permute-done.8.rest_0_), custom_call_target="tpu_custom_call" | custom-call | flops 314572800 | bytes 3932160 | tf_op jit(solution)/shard_map/update/update/pallas_call | solution.py:278
  69.5 0.0 collective-permute-done.7.rest_0_
  69.5 1.1 %update.3 = bf16[2,320,1024]{2,1,0:T(8,128)(2,1)} custom-call(f32[2,320,1024]{2,1,0:T(8,128)S(1)} %get-tuple-element.15.ready_ref, f32[4,1024]{1,0:T(4,128)S(1)} %get-tuple-element.16.factor_ref, bf16[320,320]{1,0:T(8,128)(2,1)S(1)} %copy-done.3, bf16[2,320,256]{2,1,0:T(8,128)(2,1)S(1)} %collective-permute-done.7.rest_0_, ...), custom_call_target="tpu_custom_call", output_to_operand_aliasing={{}: (4, {})} | custom-call | flops 104857600 | bytes 1310720 | tf_op jit(solution)/shard_map/update/update/pallas_call | solution.py:278
  (3 shorter events, 0.0 us)
Async XLA Ops:
  0.0 42.0 %copy-start = (bf16[1,2,320,1024]{3,2,1,0:T(8,128)(2,1)S(1)}, bf16[1,2,320,1024]{3,2,1,0:T(8,128)(2,1)}, u32[]{:S(2)}) copy-start(bf16[1,2,320,1024]{3,2,1,0:T(8,128)(2,1)} %param.11) | copy-start | bytes 3932164
  1.0 3.0 %copy-start.1 = (bf16[2,320,128]{2,1,0:T(8,128)(2,1)}, bf16[2,320,128]{2,1,0:T(8,128)(2,1)S(1)}, u32[]{:S(2)}) copy-start(bf16[2,320,128]{2,1,0:T(8,128)(2,1)S(1)} %slice.4.first_ref.head_ref) | copy-start | bytes 491524
  1.0 56.3 %collective-permute-start.6 = (bf16[2,320,128]{2,1,0:T(8,128)(2,1)S(1)}, bf16[2,320,128]{2,1,0:T(8,128)(2,1)S(1)}, u32[]{:S(2)}, u32[]{:S(2)}) collective-permute-start(bf16[2,320,128]{2,1,0:T(8,128)(2,1)S(1)} %slice.4.first_ref.head_ref), channel_id=1, source_target_pairs={{0,2},{2,0},{1,3},{3,1},{4,6},{6,4},{5,7},{7,5},{8,10},{10,8},{9,1... | collective-permute-start | bytes 491528 | tf_op jit(solution)/shard_map/instances/ppermute | solution.py:220
  39.9 14.8 %copy-start.10 = (s32[1,6,1024]{2,0,1:T(1,128)S(1)}, s32[1,6,1024]{2,0,1:T(1,128)}, u32[]{:S(2)}) copy-start(s32[1,6,1024]{2,0,1:T(1,128)} %param.15) | copy-start | bytes 73732
  39.9 28.1 %collective-permute-start.8 = (bf16[2,320,640]{2,1,0:T(8,128)(2,1)}, bf16[2,320,640]{2,1,0:T(8,128)(2,1)S(1)}, u32[]{:S(2)}, u32[]{:S(2)}) collective-permute-start(bf16[2,320,640]{2,1,0:T(8,128)(2,1)} %get-tuple-element.18), channel_id=1, source_target_pairs={{0,2},{2,0},{1,3},{3,1},{4,6},{6,4},{5,7},{7,5},{8,10},{10,8},{9,1... | collective-permute-start | bytes 2457608 | tf_op jit(solution)/shard_map/instances/ppermute | solution.py:220
  40.6 16.8 %copy-start.3 = (bf16[320,320]{1,0:T(8,128)(2,1)S(1)}, bf16[320,320]{1,0:T(8,128)(2,1)}, u32[]{:S(2)}) copy-start(bf16[320,320]{1,0:T(8,128)(2,1)} %inverse_ref.5) | copy-start | bytes 614404
  40.6 16.8 %copy-start.5 = (bf16[320,480]{1,0:T(8,128)(2,1)S(1)}, bf16[320,480]{1,0:T(8,128)(2,1)}, u32[]{:S(2)}) copy-start(bf16[320,480]{1,0:T(8,128)(2,1)} %lift_ref.1) | copy-start | bytes 921604
  40.6 16.8 %copy-start.7 = (f32[1,1024]{1,0:T(1,128)S(1)}, f32[1,1024]{1,0:T(1,128)}, u32[]{:S(2)}) copy-start(f32[1,1024]{1,0:T(1,128)} %scale_ref.1) | copy-start | bytes 12292
  40.6 16.8 %copy-start.8 = (s32[1,2,64]{2,1,0:T(2,128)S(1)}, s32[1,2,64]{2,1,0:T(2,128)}, u32[]{:S(2)}) copy-start(s32[1,2,64]{2,1,0:T(2,128)} %param.16) | copy-start | bytes 1540
  40.6 16.8 %copy-start.9 = (f32[4,4]{1,0:T(4,128)S(1)}, f32[4,4]{1,0:T(4,128)}, u32[]{:S(2)}) copy-start(f32[4,4]{1,0:T(4,128)} %constant.13.clone.table_ref) | copy-start | bytes 196
  42.0 0.9 %copy-start.2 = (bf16[2,320,128]{2,1,0:T(8,128)(2,1)S(1)}, bf16[2,320,128]{2,1,0:T(8,128)(2,1)}, u32[]{:S(2)}) copy-start(bf16[2,320,128]{2,1,0:T(8,128)(2,1)} %copy-done.1) | copy-start | bytes 491524
  42.9 12.0 %copy-start.11 = (bf16[2,320,256]{2,1,0:T(8,128)(2,1)S(1)}, bf16[2,320,256]{2,1,0:T(8,128)(2,1)}, u32[]{:S(2)}) copy-start(bf16[2,320,256]{2,1,0:T(8,128)(2,1)} %get-tuple-element.17) | copy-start | bytes 983044
  42.9 14.5 %copy-start.4 = (bf16[1,2,320,1024]{3,2,1,0:T(8,128)(2,1)S(1)}, bf16[1,2,320,1024]{3,2,1,0:T(8,128)(2,1)}, u32[]{:S(2)}) copy-start(bf16[1,2,320,1024]{3,2,1,0:T(8,128)(2,1)} %param.12) | copy-start | bytes 3932164
  42.9 14.5 %copy-start.6 = (bf16[320,320]{1,0:T(8,128)(2,1)S(1)}, bf16[320,320]{1,0:T(8,128)(2,1)}, u32[]{:S(2)}) copy-start(bf16[320,320]{1,0:T(8,128)(2,1)} %volume_ref.1) | copy-start | bytes 614404
  43.9 4.5 %collective-permute-start.5 = (bf16[2,80,64]{2,1,0:T(8,128)(2,1)S(1)}, bf16[2,80,64]{2,1,0:T(8,128)(2,1)S(1)}, u32[]{:S(2)}, u32[]{:S(2)}) collective-permute-start(bf16[2,80,64]{2,1,0:T(8,128)(2,1)S(1)} %get-tuple-element.14), channel_id=1, source_target_pairs={{0,13},{1,12},{4,1},{5,0},{8,5},{9,4},{12,9},{13,8},{2,15},{3,14},... | collective-permute-start | bytes 61448 | tf_op jit(solution)/shard_map/interface/ppermute | solution.py:247
  46.8 4.5 %collective-permute-start.4 = (bf16[2,80,64]{2,1,0:T(8,128)(2,1)S(1)}, bf16[2,80,64]{2,1,0:T(8,128)(2,1)S(1)}, u32[]{:S(2)}, u32[]{:S(2)}) collective-permute-start(bf16[2,80,64]{2,1,0:T(8,128)(2,1)S(1)} %get-tuple-element.14), channel_id=1, source_target_pairs={{0,9},{1,8},{4,13},{5,12},{8,1},{9,0},{12,5},{13,4},{2,11},{3,10},... | collective-permute-start | bytes 61448 | tf_op jit(solution)/shard_map/interface/ppermute | solution.py:247
  46.8 6.6 %collective-permute-start.3 = (bf16[2,80,64]{2,1,0:T(8,128)(2,1)S(1)}, bf16[2,80,64]{2,1,0:T(8,128)(2,1)S(1)}, u32[]{:S(2)}, u32[]{:S(2)}) collective-permute-start(bf16[2,80,64]{2,1,0:T(8,128)(2,1)S(1)} %get-tuple-element.14), channel_id=1, source_target_pairs={{0,5},{1,4},{4,9},{5,8},{8,13},{9,12},{12,1},{13,0},{2,7},{3,6},{6... | collective-permute-start | bytes 61448 | tf_op jit(solution)/shard_map/interface/ppermute | solution.py:247
  48.4 8.0 %collective-permute-start = (bf16[2,160,64]{2,1,0:T(8,128)(2,1)S(1)}, bf16[2,160,64]{2,1,0:T(8,128)(2,1)S(1)}, u32[]{:S(2)}, u32[]{:S(2)}) collective-permute-start(bf16[2,160,64]{2,1,0:T(8,128)(2,1)S(1)} %get-tuple-element.12), channel_id=1, source_target_pairs={{0,4},{4,8},{8,12},{12,0},{1,5},{5,9},{9,13},{13,1},{2,6},{6,10},{... | collective-permute-start | bytes 122888 | tf_op jit(solution)/shard_map/halo/ppermute | solution.py:244
  51.2 6.1 %collective-permute-start.1 = (bf16[2,160,64]{2,1,0:T(8,128)(2,1)S(1)}, bf16[2,160,64]{2,1,0:T(8,128)(2,1)S(1)}, u32[]{:S(2)}, u32[]{:S(2)}) collective-permute-start(bf16[2,160,64]{2,1,0:T(8,128)(2,1)S(1)} %get-tuple-element.13), channel_id=1, source_target_pairs={{0,12},{4,0},{8,4},{12,8},{1,13},{5,1},{9,5},{13,9},{2,14},{6,2},{... | collective-permute-start | bytes 122888 | tf_op jit(solution)/shard_map/halo/ppermute | solution.py:245
  53.4 1.5 %collective-permute-start.2 = (bf16[2,80,64]{2,1,0:T(8,128)(2,1)S(1)}, bf16[2,80,64]{2,1,0:T(8,128)(2,1)S(1)}, u32[]{:S(2)}, u32[]{:S(2)}) collective-permute-start(bf16[2,80,64]{2,1,0:T(8,128)(2,1)S(1)} %get-tuple-element.14), channel_id=1, source_target_pairs={{0,1},{1,0},{4,5},{5,4},{8,9},{9,8},{12,13},{13,12},{2,3},{3,2},{6... | collective-permute-start | bytes 61448 | tf_op jit(solution)/shard_map/interface/ppermute | solution.py:247
  54.9 14.6 %collective-permute-start.7 = (bf16[2,320,256]{2,1,0:T(8,128)(2,1)S(1)}, bf16[2,320,256]{2,1,0:T(8,128)(2,1)S(1)}, u32[]{:S(2)}, u32[]{:S(2)}) collective-permute-start(bf16[2,320,256]{2,1,0:T(8,128)(2,1)S(1)} %copy-done.11), channel_id=1, source_target_pairs={{0,2},{2,0},{1,3},{3,1},{4,6},{6,4},{5,7},{7,5},{8,10},{10,8},{9,1... | collective-permute-start | bytes 983048 | tf_op jit(solution)/shard_map/instances/ppermute | solution.py:220

commit v13 on v5

--- a/solution.py
+++ b/solution.py
@@ -12,6 +12,8 @@
 OPPOSITE = (1, 0, 3, 2, 5, 4)
 LANES = 128
 VMEM_LIMIT = 40 * 1024 * 1024
+ENDS_LIMIT = 63 * 1024 * 1024
+UPDATE_LIMIT = 40 * 1024 * 1024
 
 
 def spectral_table(instances):
@@ -129,24 +131,23 @@
         finish(False)
 
 
-def update_kernel(tile, place_ref, ready_ref, factor_ref, inverse_ref, all_ref, out_ref, taken, made, in_sems, sems):
+def update_kernel(tile, ready_ref, factor_ref, inverse_ref, *rest):
+    others, (out_ref, taken, made, in_sems, sems) = rest[:-5], rest[-5:]
     count, dof, total = ready_ref.shape
-    peers = all_ref.shape[0]
     steps = total // tile
     loads = []
     for t in range(steps):
-        cols = slice(t * tile, (t + 1) * tile)
-        for d in range(1, peers):
-            owner = lax.rem(place_ref[1] - d + peers, peers)
-            load = pltpu.make_async_copy(all_ref.at[owner, :, :, cols], taken.at[t, d - 1], in_sems.at[t, d - 1])
+        for d, other in enumerate(others):
+            load = pltpu.make_async_copy(
+                other.at[:, :, t * tile : (t + 1) * tile], taken.at[t, d], in_sems.at[t, d])
             load.start()
             loads.append(load)
     copies = []
     for t in range(steps):
         cols = slice(t * tile, (t + 1) * tile)
-        for load in loads[t * (peers - 1) : (t + 1) * (peers - 1)]:
+        for load in loads[t * len(others) : (t + 1) * len(others)]:
             load.wait()
-        moved = [dot(inverse_ref[...], taken[t, d, m]) for d in range(peers - 1) for m in range(count)]
+        moved = [dot(inverse_ref[...], taken[t, d, m]) for d in range(len(others)) for m in range(count)]
         for n in range(count):
             value = ready_ref[n, :, cols]
             for k, part in enumerate(moved):
@@ -182,7 +183,8 @@
     bf16 = jnp.bfloat16
 
     with jax.named_scope("instances"):
-        gathered = lax.all_gather(current, "inst")
+        others = [lax.ppermute(current, "inst", [(i, (i + d) % peers) for i in range(peers)])
+                  for d in range(1, peers)]
 
     with jax.named_scope("ends"):
         up, down, cross = pl.pallas_call(
@@ -198,7 +200,7 @@
             out_specs=(pl.BlockSpec((count, 2 * width, LAYER), lambda j: (0, 0, 0)),
                        pl.BlockSpec((count, 2 * width, LAYER), lambda j: (0, 0, 0)),
                        pl.BlockSpec((count, width, iface_rows), lambda j: (0, 0, 0))),
-            compiler_params=pltpu.CompilerParams(vmem_limit_bytes=VMEM_LIMIT),
+            compiler_params=pltpu.CompilerParams(vmem_limit_bytes=ENDS_LIMIT),
             cost_estimate=pl.CostEstimate(flops=8 * width * dof * LANES * 2 * count,
                                           bytes_accessed=1_000_000, transcendentals=0),
             name="ends",
@@ -239,16 +241,16 @@
         result = pl.pallas_call(
             functools.partial(update_kernel, tile),
             out_shape=jax.ShapeDtypeStruct((count, dof, total), bf16),
-            in_specs=[smem, vmem, vmem, vmem, pl.BlockSpec(memory_space=pl.ANY)],
+            in_specs=[vmem] * 3 + [pl.BlockSpec(memory_space=pl.ANY)] * (peers - 1),
             out_specs=pl.BlockSpec(memory_space=pl.ANY),
             scratch_shapes=[pltpu.VMEM((steps, peers - 1, count, dof, tile), bf16),
                             pltpu.VMEM((steps, count, dof, tile), bf16),
                             pltpu.SemaphoreType.DMA((steps, peers - 1)), pltpu.SemaphoreType.DMA((steps,))],
-            compiler_params=pltpu.CompilerParams(vmem_limit_bytes=VMEM_LIMIT),
+            compiler_params=pltpu.CompilerParams(vmem_limit_bytes=UPDATE_LIMIT),
             cost_estimate=pl.CostEstimate(flops=2 * count * total * dof * dof * (peers - 1),
                                           bytes_accessed=count * dof * total * 8, transcendentals=0),
             name="update",
-        )(place, ready, factors, block_inverse, gathered)
+        )(ready, factors, block_inverse, *others)
     return result[None]
 
 

time: 64.2 us -> 37.9 us (0.59)
  waiting for transfers between devices: 19.9 us -> 2.38 us
  between operations: 14.2 us -> 0.8 us
  starting transfers between devices: 9.08 us -> 12.3 us
  Pallas kernels: 14.3 us -> 15.9 us
  local copies, waits for them, and re-layouts: 6.28 us -> 5.53 us
    all_gather x1 -> x0, waiting for transfers between devices: 14.4 us -> none  [body(): gathered = lax.all_gather(current, 'inst')]
    ppermute x0 -> x1, starting transfers between devices: none -> 2.94 us  [body(): lax.ppermute(current, 'inst', [(i, (i + d) % peers) for i in range(peers)])]
    ppermute x4, waiting for transfers between devices: 4.83 us -> 2.37 us  [body(): lax.ppermute(cross, ('space', 'row'), [(i * 2 + r, (i + d) % shards * 2 +...]
    ppermute x1, starting transfers between devices: 0.01 us -> 1.57 us  [body(): lax.ppermute(up, 'space', [(i, (i + 1) % shards) for i in range(shards)])]
    ppermute x1, starting transfers between devices: 3.82 us -> 2.25 us  [body(): lax.ppermute(down, 'space', [(i, (i - 1) % shards) for i in range(shards)])]
    pallas_call x1, Pallas kernels: 1.01 us -> 2.35 us  [body(): pl.pallas_call(ends_kernel, grid=(1,), out_shape=(jax.ShapeDtypeStruct((c...]
    unnamed x26 -> x24, local copies, waits for them, and re-layouts: 6.28 us -> 5.53 us
    unnamed x1 -> x0, waiting for transfers between devices: 0.71 us -> none
  transfers between devices with their start and end apart: 7 -> 7, of which waited for: 3 -> 2; matrix products, arithmetic and copies ran while one was open for 2% -> 7% of each run, Pallas kernels for 18% -> 34%
where the time goes in v13:
time: 37.9 us; the launch traced here: 37.6 us
  Pallas kernels  15.9 us (42%)
  starting transfers between devices  12.3 us (32%)
  local copies, waits for them, and re-layouts  5.53 us (15%)
  waiting for transfers between devices  2.38 us (6%)
  between operations  0.8 us (2%)
  other arithmetic  0.66 us (2%)
    pallas_call x1, Pallas kernels, body(): pl.pallas_call(functools.partial(couple_kernel, shards, peers), grid=(ste...  10.4 us
    ppermute x4, starting transfers between devices, body(): lax.ppermute(cross, ('space', 'row'), [(i * 2 + r, (i + d) % shards * 2 +...  5.57 us
    unnamed x24, local copies, waits for them, and re-layouts  5.53 us
    pallas_call x1, Pallas kernels, body(): pl.pallas_call(functools.partial(update_kernel, tile), out_shape=jax.Shap...  3.18 us
    ppermute x1, starting transfers between devices, body(): lax.ppermute(current, 'inst', [(i, (i + d) % peers) for i in range(peers)])  2.94 us
    ppermute x4, waiting for transfers between devices, body(): lax.ppermute(cross, ('space', 'row'), [(i * 2 + r, (i + d) % shards * 2 +...  2.37 us
    pallas_call x1, Pallas kernels, body(): pl.pallas_call(ends_kernel, grid=(1,), out_shape=(jax.ShapeDtypeStruct((c...  2.35 us
    ppermute x1, starting transfers between devices, body(): lax.ppermute(down, 'space', [(i, (i - 1) % shards) for i in range(shards)])  2.25 us
  transfers between devices with their start and end apart: 7, of which 2 were waited for; matrix products, arithmetic and copies ran while one was open for 7% of the time, Pallas kernels for 34%

profile of v13, /device:TPU:0, one launch (start us, length us, event | category | flops | bytes accessed | tf_op | source)
XLA Modules:
  0.0 37.6 jit_solution(16373160376140205000)
XLA Ops:
  0.0 2.9 %collective-permute-start.6 = (bf16[2,320,1024]{2,1,0:T(8,128)(2,1)}, bf16[2,320,1024]{2,1,0:T(8,128)(2,1)}, u32[]{:S(2)}, u32[]{:S(2)}) collective-permute-start(bf16[2,320,1024]{2,1,0:T(8,128)(2,1)} %bitcast.10), channel_id=1, source_target_pairs={{0,2},{2,0},{1,3},{3,1},{4,6},{6,4},{5,7},{7,5},{8,10},{10,8},{9,1... | collective-permute-start | bytes 3932168 | tf_op jit(solution)/shard_map/instances/ppermute | solution.py:186
  2.9 1.9 %copy.13.trace_ref = bf16[480,320]{1,0:T(8,128)(2,1)} copy(bf16[480,320]{0,1:T(8,128)(2,1)} %param.18) | data formatting | bytes 614400 | tf_op args[7]
  4.8 0.7 %pad_add_fusion.place_ref = s32[3]{0:T(128)} fusion(s32[1]{0:T(128)} %bitcast.2, s32[1]{0:T(128)} %bitcast.1, s32[1]{0:T(128)} %bitcast), kind=kLoop, calls=%fused_computation.1 | loop fusion | flops 6 | bytes 24 | tf_op jit(solution)/shard_map/stack | solution.py:180
  5.5 0.0 copy-start.10
  5.5 0.0 copy-start.1
  5.5 0.0 copy-start.2
  5.5 0.0 copy-start.3
  5.5 0.0 copy-start.5
  5.5 0.0 copy-start.7
  5.5 0.0 copy-start.8
  5.6 0.0 copy-start.9
  5.6 2.3 %ends.1 = (bf16[2,160,64]{2,1,0:T(8,128)(2,1)}, bf16[2,160,64]{2,1,0:T(8,128)(2,1)}, bf16[2,80,64]{2,1,0:T(8,128)(2,1)}) custom-call(s32[3]{0:T(128)} %pad_add_fusion.place_ref, bf16[2,320,1024]{2,1,0:T(8,128)(2,1)} %bitcast.11, bf16[2,320,1024]{2,1,0:T(8,128)(2,1)} %bitcast.12, bf16[480,320]{1,0:T(8,128)(2,1)} %copy.13.trace_ref), custom_call_target="tpu_custom_call" | custom-call | flops 104857600 | bytes 1000000 | tf_op jit(solution)/shard_map/ends/ends/pallas_call | solution.py:190
  7.9 2.8 %collective-permute-start.5 = (bf16[2,80,64]{2,1,0:T(8,128)(2,1)}, bf16[2,80,64]{2,1,0:T(8,128)(2,1)S(1)}, u32[]{:S(2)}, u32[]{:S(2)}) collective-permute-start(bf16[2,80,64]{2,1,0:T(8,128)(2,1)} %get-tuple-element.12), channel_id=1, source_target_pairs={{0,13},{1,12},{4,1},{5,0},{8,5},{9,4},{12,9},{13,8},{2,15},{3,14},... | collective-permute-start | bytes 61448 | tf_op jit(solution)/shard_map/interface/ppermute | solution.py:213
  10.7 0.0 collective-permute-start.4
  10.7 1.6 %collective-permute-start = (bf16[2,160,64]{2,1,0:T(8,128)(2,1)}, bf16[2,160,64]{2,1,0:T(8,128)(2,1)S(1)}, u32[]{:S(2)}, u32[]{:S(2)}) collective-permute-start(bf16[2,160,64]{2,1,0:T(8,128)(2,1)} %get-tuple-element.10), channel_id=1, source_target_pairs={{0,4},{4,8},{8,12},{12,0},{1,5},{5,9},{9,13},{13,1},{2,6},{6,10},{... | collective-permute-start | bytes 122888 | tf_op jit(solution)/shard_map/halo/ppermute | solution.py:210
  12.3 2.3 %collective-permute-start.1 = (bf16[2,160,64]{2,1,0:T(8,128)(2,1)}, bf16[2,160,64]{2,1,0:T(8,128)(2,1)S(1)}, u32[]{:S(2)}, u32[]{:S(2)}) collective-permute-start(bf16[2,160,64]{2,1,0:T(8,128)(2,1)} %get-tuple-element.11), channel_id=1, source_target_pairs={{0,12},{4,0},{8,4},{12,8},{1,13},{5,1},{9,5},{13,9},{2,14},{6,2},{... | collective-permute-start | bytes 122888 | tf_op jit(solution)/shard_map/halo/ppermute | solution.py:211
  14.5 0.0 collective-permute-done.5.rest_3_
  14.5 0.0 collective-permute-start.3
  14.5 0.9 %collective-permute-done.4.rest_2_ = bf16[2,80,64]{2,1,0:T(8,128)(2,1)S(1)} collective-permute-done((bf16[2,80,64]{2,1,0:T(8,128)(2,1)}, bf16[2,80,64]{2,1,0:T(8,128)(2,1)S(1)}, u32[]{:S(2)}, u32[]{:S(2)}) %collective-permute-start.4) | collective-permute-done | bytes 20512 | tf_op jit(solution)/shard_map/interface/ppermute | solution.py:213
  15.4 2.8 %collective-permute-start.2 = (bf16[2,80,64]{2,1,0:T(8,128)(2,1)}, bf16[2,80,64]{2,1,0:T(8,128)(2,1)S(1)}, u32[]{:S(2)}, u32[]{:S(2)}) collective-permute-start(bf16[2,80,64]{2,1,0:T(8,128)(2,1)} %get-tuple-element.12), channel_id=1, source_target_pairs={{0,1},{1,0},{4,5},{5,4},{8,9},{9,8},{12,13},{13,12},{2,3},{3,2},{6... | collective-permute-start | bytes 61448 | tf_op jit(solution)/shard_map/interface/ppermute | solution.py:213
  18.8 0.0 copy-done.10
  18.8 1.5 %collective-permute-done.3.rest_1_ = bf16[2,80,64]{2,1,0:T(8,128)(2,1)S(1)} collective-permute-done((bf16[2,80,64]{2,1,0:T(8,128)(2,1)}, bf16[2,80,64]{2,1,0:T(8,128)(2,1)S(1)}, u32[]{:S(2)}, u32[]{:S(2)}) %collective-permute-start.3) | collective-permute-done | bytes 20512 | tf_op jit(solution)/shard_map/interface/ppermute | solution.py:213
  20.4 0.0 collective-permute-done.2.rest_0_
  20.4 0.0 collective-permute-done.low_ref
  20.4 0.0 collective-permute-done.1.high_ref
  20.4 0.0 copy-done.1
  20.4 0.0 copy-done.2
  20.4 0.0 copy-done.3
  20.4 0.0 copy-done.5
  20.4 0.0 copy-done.7
  20.4 0.0 copy-done.8
  20.4 0.0 copy-done.9
  20.4 0.0 copy-start
  20.5 1.3 %copy-done = bf16[1,2,320,1024]{3,2,1,0:T(8,128)(2,1)S(1)} copy-done((bf16[1,2,320,1024]{3,2,1,0:T(8,128)(2,1)S(1)}, bf16[1,2,320,1024]{3,2,1,0:T(8,128)(2,1)}, u32[]{:S(2)}) %copy-start) | copy-done | bytes 1310744
  21.8 0.0 copy-start.4
  21.8 1.3 %copy-done.4 = bf16[1,2,320,1024]{3,2,1,0:T(8,128)(2,1)S(1)} copy-done((bf16[1,2,320,1024]{3,2,1,0:T(8,128)(2,1)S(1)}, bf16[1,2,320,1024]{3,2,1,0:T(8,128)(2,1)}, u32[]{:S(2)}) %copy-start.4) | copy-done | bytes 1310744
  23.1 0.0 copy-start.6
  23.1 0.9 %copy-done.6 = bf16[320,320]{1,0:T(8,128)(2,1)S(1)} copy-done((bf16[320,320]{1,0:T(8,128)(2,1)S(1)}, bf16[320,320]{1,0:T(8,128)(2,1)}, u32[]{:S(2)}) %copy-start.6) | copy-done | bytes 204824
  24.0 10.4 %couple.1 = (f32[2,320,1024]{2,1,0:T(8,128)S(1)}, f32[4,1024]{1,0:T(4,128)S(1)}) custom-call(s32[3]{0:T(128)S(1)} %copy-done.3, f32[1]{0:T(128)S(6)} %copy.17.freq_ref, f32[4,4]{1,0:T(4,128)S(1)} %copy-done.9, s32[6,1024]{1,0:T(8,128)S(1)} %bitcast.15, s32[2,64]{1,0:T(2,128)S(1)} %bitcast.17, bf16[2,320,1024]{2,1,0:T(8,128)(2,1)S(1)} %bitcast.13, ...), custom_call_target="tpu_custom_call" | custom-call | flops 3690987520 | bytes 6553600 | tf_op jit(solution)/shard_map/couple/couple/pallas_call | solution.py:221
  34.4 0.0 collective-permute-done.6.rest_0_
  34.4 3.2 %update.1 = bf16[2,320,1024]{2,1,0:T(8,128)(2,1)} custom-call(f32[2,320,1024]{2,1,0:T(8,128)S(1)} %get-tuple-element.13.ready_ref, f32[4,1024]{1,0:T(4,128)S(1)} %get-tuple-element.14.factor_ref, bf16[320,320]{1,0:T(8,128)(2,1)S(1)} %copy-done.2, bf16[2,320,1024]{2,1,0:T(8,128)(2,1)} %collective-permute-done.6.rest_0_), custom_call_target="tpu_custom_call" | custom-call | flops 419430400 | bytes 5242880 | tf_op jit(solution)/shard_map/update/update/pallas_call | solution.py:241
  (1 shorter events, 0.0 us)
Async XLA Ops:
  0.0 34.4 %collective-permute-start.6 = (bf16[2,320,1024]{2,1,0:T(8,128)(2,1)}, bf16[2,320,1024]{2,1,0:T(8,128)(2,1)}, u32[]{:S(2)}, u32[]{:S(2)}) collective-permute-start(bf16[2,320,1024]{2,1,0:T(8,128)(2,1)} %bitcast.10), channel_id=1, source_target_pairs={{0,2},{2,0},{1,3},{3,1},{4,6},{6,4},{5,7},{7,5},{8,10},{10,8},{9,1... | collective-permute-start | bytes 3932168 | tf_op jit(solution)/shard_map/instances/ppermute | solution.py:186
  5.5 13.3 %copy-start.10 = (s32[1,6,1024]{2,0,1:T(1,128)S(1)}, s32[1,6,1024]{2,0,1:T(1,128)}, u32[]{:S(2)}) copy-start(s32[1,6,1024]{2,0,1:T(1,128)} %param.15) | copy-start | bytes 73732
  5.5 14.9 %copy-start.1 = (bf16[480,320]{1,0:T(8,128)(2,1)S(1)}, bf16[480,320]{1,0:T(8,128)(2,1)}, u32[]{:S(2)}) copy-start(bf16[480,320]{1,0:T(8,128)(2,1)} %copy.13.trace_ref) | copy-start | bytes 921604
  5.5 14.9 %copy-start.2 = (bf16[320,320]{1,0:T(8,128)(2,1)S(1)}, bf16[320,320]{1,0:T(8,128)(2,1)}, u32[]{:S(2)}) copy-start(bf16[320,320]{1,0:T(8,128)(2,1)} %inverse_ref.3) | copy-start | bytes 614404
  5.5 14.9 %copy-start.3 = (s32[3]{0:T(128)S(1)}, s32[3]{0:T(128)}, u32[]{:S(2)}) copy-start(s32[3]{0:T(128)} %pad_add_fusion.place_ref) | copy-start | bytes 40
  5.5 14.9 %copy-start.5 = (bf16[320,480]{1,0:T(8,128)(2,1)S(1)}, bf16[320,480]{1,0:T(8,128)(2,1)}, u32[]{:S(2)}) copy-start(bf16[320,480]{1,0:T(8,128)(2,1)} %lift_ref.1) | copy-start | bytes 921604
  5.5 14.9 %copy-start.7 = (f32[1,1024]{1,0:T(1,128)S(1)}, f32[1,1024]{1,0:T(1,128)}, u32[]{:S(2)}) copy-start(f32[1,1024]{1,0:T(1,128)} %scale_ref.1) | copy-start | bytes 12292
  5.5 14.9 %copy-start.8 = (s32[1,2,64]{2,1,0:T(2,128)S(1)}, s32[1,2,64]{2,1,0:T(2,128)}, u32[]{:S(2)}) copy-start(s32[1,2,64]{2,1,0:T(2,128)} %param.16) | copy-start | bytes 1540
  5.6 14.9 %copy-start.9 = (f32[4,4]{1,0:T(4,128)S(1)}, f32[4,4]{1,0:T(4,128)}, u32[]{:S(2)}) copy-start(f32[4,4]{1,0:T(4,128)} %constant.13.clone.table_ref) | copy-start | bytes 196
  7.9 6.6 %collective-permute-start.5 = (bf16[2,80,64]{2,1,0:T(8,128)(2,1)}, bf16[2,80,64]{2,1,0:T(8,128)(2,1)S(1)}, u32[]{:S(2)}, u32[]{:S(2)}) collective-permute-start(bf16[2,80,64]{2,1,0:T(8,128)(2,1)} %get-tuple-element.12), channel_id=1, source_target_pairs={{0,13},{1,12},{4,1},{5,0},{8,5},{9,4},{12,9},{13,8},{2,15},{3,14},... | collective-permute-start | bytes 61448 | tf_op jit(solution)/shard_map/interface/ppermute | solution.py:213
  10.7 4.7 %collective-permute-start.4 = (bf16[2,80,64]{2,1,0:T(8,128)(2,1)}, bf16[2,80,64]{2,1,0:T(8,128)(2,1)S(1)}, u32[]{:S(2)}, u32[]{:S(2)}) collective-permute-start(bf16[2,80,64]{2,1,0:T(8,128)(2,1)} %get-tuple-element.12), channel_id=1, source_target_pairs={{0,9},{1,8},{4,13},{5,12},{8,1},{9,0},{12,5},{13,4},{2,11},{3,10},... | collective-permute-start | bytes 61448 | tf_op jit(solution)/shard_map/interface/ppermute | solution.py:213
  10.7 9.7 %collective-permute-start = (bf16[2,160,64]{2,1,0:T(8,128)(2,1)}, bf16[2,160,64]{2,1,0:T(8,128)(2,1)S(1)}, u32[]{:S(2)}, u32[]{:S(2)}) collective-permute-start(bf16[2,160,64]{2,1,0:T(8,128)(2,1)} %get-tuple-element.10), channel_id=1, source_target_pairs={{0,4},{4,8},{8,12},{12,0},{1,5},{5,9},{9,13},{13,1},{2,6},{6,10},{... | collective-permute-start | bytes 122888 | tf_op jit(solution)/shard_map/halo/ppermute | solution.py:210
  12.3 8.1 %collective-permute-start.1 = (bf16[2,160,64]{2,1,0:T(8,128)(2,1)}, bf16[2,160,64]{2,1,0:T(8,128)(2,1)S(1)}, u32[]{:S(2)}, u32[]{:S(2)}) collective-permute-start(bf16[2,160,64]{2,1,0:T(8,128)(2,1)} %get-tuple-element.11), channel_id=1, source_target_pairs={{0,12},{4,0},{8,4},{12,8},{1,13},{5,1},{9,5},{13,9},{2,14},{6,2},{... | collective-permute-start | bytes 122888 | tf_op jit(solution)/shard_map/halo/ppermute | solution.py:211
  14.5 5.9 %collective-permute-start.3 = (bf16[2,80,64]{2,1,0:T(8,128)(2,1)}, bf16[2,80,64]{2,1,0:T(8,128)(2,1)S(1)}, u32[]{:S(2)}, u32[]{:S(2)}) collective-permute-start(bf16[2,80,64]{2,1,0:T(8,128)(2,1)} %get-tuple-element.12), channel_id=1, source_target_pairs={{0,5},{1,4},{4,9},{5,8},{8,13},{9,12},{12,1},{13,0},{2,7},{3,6},{6... | collective-permute-start | bytes 61448 | tf_op jit(solution)/shard_map/interface/ppermute | solution.py:213
  15.4 5.0 %collective-permute-start.2 = (bf16[2,80,64]{2,1,0:T(8,128)(2,1)}, bf16[2,80,64]{2,1,0:T(8,128)(2,1)S(1)}, u32[]{:S(2)}, u32[]{:S(2)}) collective-permute-start(bf16[2,80,64]{2,1,0:T(8,128)(2,1)} %get-tuple-element.12), channel_id=1, source_target_pairs={{0,1},{1,0},{4,5},{5,4},{8,9},{9,8},{12,13},{13,12},{2,3},{3,2},{6... | collective-permute-start | bytes 61448 | tf_op jit(solution)/shard_map/interface/ppermute | solution.py:213
  20.4 1.3 %copy-start = (bf16[1,2,320,1024]{3,2,1,0:T(8,128)(2,1)S(1)}, bf16[1,2,320,1024]{3,2,1,0:T(8,128)(2,1)}, u32[]{:S(2)}) copy-start(bf16[1,2,320,1024]{3,2,1,0:T(8,128)(2,1)} %param.11) | copy-start | bytes 3932164
  21.8 1.3 %copy-start.4 = (bf16[1,2,320,1024]{3,2,1,0:T(8,128)(2,1)S(1)}, bf16[1,2,320,1024]{3,2,1,0:T(8,128)(2,1)}, u32[]{:S(2)}) copy-start(bf16[1,2,320,1024]{3,2,1,0:T(8,128)(2,1)} %param.12) | copy-start | bytes 3932164
  23.1 0.9 %copy-start.6 = (bf16[320,320]{1,0:T(8,128)(2,1)S(1)}, bf16[320,320]{1,0:T(8,128)(2,1)}, u32[]{:S(2)}) copy-start(bf16[320,320]{1,0:T(8,128)(2,1)} %volume_ref.1) | copy-start | bytes 614404

commit v14 on v4

--- a/solution.py
+++ b/solution.py
@@ -143,7 +143,7 @@
                 value -= factor_ref[at : at + 1, cols] * part
             made[t, n] = value.astype(jnp.bfloat16)
         copy = pltpu.make_async_copy(made.at[t], out_ref.at[:, :, cols], sems.at[t])
-        copy.start()
+        copy.start(priority=t % 2)
         copies.append(copy)
     for copy in copies:
         copy.wait()

time: 33.8 us -> 33.8 us (level)
  no operation moved by 1% of the time
where the time goes in v14:
time: 33.8 us; the launch traced here: 33.6 us
  Pallas kernels  13.1 us (39%)
  starting transfers between devices  12.4 us (37%)
  waiting for transfers between devices  4.67 us (14%)
  local copies, waits for them, and re-layouts  2.58 us (8%)
  between operations  0.79 us (2%)
    pallas_call x1, Pallas kernels, body(): pl.pallas_call(functools.partial(couple_kernel, shards, peers), grid=(ste...  10.4 us
    ppermute x4, starting transfers between devices, body(): lax.ppermute(cross, ('space', 'row'), [(i * 2 + r, (i + d) % shards * 2 +...  5.62 us
    ppermute x1, starting transfers between devices, body(): lax.ppermute(current, 'inst', [(i, (i + d) % peers) for i in range(peers)])  2.94 us
    unnamed x20, local copies, waits for them, and re-layouts  2.58 us
    ppermute x1, waiting for transfers between devices, body(): lax.ppermute(current, 'inst', [(i, (i + d) % peers) for i in range(peers)])  2.5 us
    ppermute x1, starting transfers between devices, body(): lax.ppermute(down, 'space', [(i, (i - 1) % shards) for i in range(shards)])  2.25 us
    ppermute x4, waiting for transfers between devices, body(): lax.ppermute(cross, ('space', 'row'), [(i * 2 + r, (i + d) % shards * 2 +...  2.16 us
    pallas_call x1, Pallas kernels, body(): pl.pallas_call(functools.partial(update_kernel, tile), out_shape=jax.Shap...  1.64 us
  transfers between devices with their start and end apart: 7, of which 3 were waited for; matrix products, arithmetic and copies ran while one was open for 4% of the time, Pallas kernels for 34%

profile of v14, /device:TPU:0, one launch (start us, length us, event | category | flops | bytes accessed | tf_op | source)
XLA Modules:
  0.0 33.6 jit_solution(7306924839292614989)
XLA Ops:
  0.0 2.9 %collective-permute-start.6 = (bf16[2,320,1024]{2,1,0:T(8,128)(2,1)}, bf16[2,320,1024]{2,1,0:T(8,128)(2,1)S(1)}, u32[]{:S(2)}, u32[]{:S(2)}) collective-permute-start(bf16[2,320,1024]{2,1,0:T(8,128)(2,1)} %bitcast.10), channel_id=1, source_target_pairs={{0,2},{2,0},{1,3},{3,1},{4,6},{6,4},{5,7},{7,5},{8,10},{10,8},{9,1... | collective-permute-start | bytes 3932168 | tf_op jit(solution)/shard_map/instances/ppermute | solution.py:174
  2.9 1.2 %copy.13.trace_ref = bf16[480,320]{1,0:T(8,128)(2,1)S(1)} copy(bf16[480,320]{0,1:T(8,128)(2,1)} %param.18) | data formatting | bytes 614400 | tf_op args[7]
  4.2 0.1 pad_add_fusion.place_ref
  4.2 0.0 copy-start
  4.2 1.3 %copy-done = bf16[1,2,320,1024]{3,2,1,0:T(8,128)(2,1)S(1)} copy-done((bf16[1,2,320,1024]{3,2,1,0:T(8,128)(2,1)S(1)}, bf16[1,2,320,1024]{3,2,1,0:T(8,128)(2,1)}, u32[]{:S(2)}) %copy-start) | copy-done | bytes 1310744
  5.6 0.0 copy-start.8
  5.6 0.0 copy-start.1
  5.6 0.0 copy-start.2
  5.6 0.0 copy-start.3
  5.6 0.0 copy-start.4
  5.6 0.0 copy-start.5
  5.6 0.0 copy-start.6
  5.6 0.0 copy-start.7
  5.6 1.0 %ends.1 = (bf16[2,160,64]{2,1,0:T(8,128)(2,1)S(1)}, bf16[2,160,64]{2,1,0:T(8,128)(2,1)S(1)}, bf16[2,80,64]{2,1,0:T(8,128)(2,1)S(1)}) custom-call(s32[3]{0:T(128)S(1)} %pad_add_fusion.place_ref, bf16[2,320,1024]{2,1,0:T(8,128)(2,1)S(1)} %bitcast.11, bf16[2,320,1024]{2,1,0:T(8,128)(2,1)S(1)} %bitcast.12, bf16[480,320]{1,0:T(8,128)(2,1)S(1)} %copy.13.trace_ref), custom_call_target="tpu_custom_call" | custom-call | flops 104857600 | bytes 1000000 | tf_op jit(solution)/shard_map/ends/ends/pallas_call | solution.py:178
  6.6 2.8 %collective-permute-start.5 = (bf16[2,80,64]{2,1,0:T(8,128)(2,1)S(1)}, bf16[2,80,64]{2,1,0:T(8,128)(2,1)S(1)}, u32[]{:S(2)}, u32[]{:S(2)}) collective-permute-start(bf16[2,80,64]{2,1,0:T(8,128)(2,1)S(1)} %get-tuple-element.12), channel_id=1, source_target_pairs={{0,13},{1,12},{4,1},{5,0},{8,5},{9,4},{12,9},{13,8},{2,15},{3,14},... | collective-permute-start | bytes 61448 | tf_op jit(solution)/shard_map/interface/ppermute | solution.py:201
  9.5 0.0 collective-permute-start.4
  9.5 1.6 %collective-permute-start = (bf16[2,160,64]{2,1,0:T(8,128)(2,1)S(1)}, bf16[2,160,64]{2,1,0:T(8,128)(2,1)S(1)}, u32[]{:S(2)}, u32[]{:S(2)}) collective-permute-start(bf16[2,160,64]{2,1,0:T(8,128)(2,1)S(1)} %get-tuple-element.10), channel_id=1, source_target_pairs={{0,4},{4,8},{8,12},{12,0},{1,5},{5,9},{9,13},{13,1},{2,6},{6,10},{... | collective-permute-start | bytes 122888 | tf_op jit(solution)/shard_map/halo/ppermute | solution.py:198
  11.0 2.2 %collective-permute-start.1 = (bf16[2,160,64]{2,1,0:T(8,128)(2,1)S(1)}, bf16[2,160,64]{2,1,0:T(8,128)(2,1)S(1)}, u32[]{:S(2)}, u32[]{:S(2)}) collective-permute-start(bf16[2,160,64]{2,1,0:T(8,128)(2,1)S(1)} %get-tuple-element.11), channel_id=1, source_target_pairs={{0,12},{4,0},{8,4},{12,8},{1,13},{5,1},{9,5},{13,9},{2,14},{6,2},{... | collective-permute-start | bytes 122888 | tf_op jit(solution)/shard_map/halo/ppermute | solution.py:199
  13.3 0.0 collective-permute-done.5.rest_3_
  13.3 0.0 collective-permute-start.3
  13.3 0.6 %collective-permute-done.4.rest_2_ = bf16[2,80,64]{2,1,0:T(8,128)(2,1)S(1)} collective-permute-done((bf16[2,80,64]{2,1,0:T(8,128)(2,1)S(1)}, bf16[2,80,64]{2,1,0:T(8,128)(2,1)S(1)}, u32[]{:S(2)}, u32[]{:S(2)}) %collective-permute-start.4) | collective-permute-done | bytes 20512 | tf_op jit(solution)/shard_map/interface/ppermute | solution.py:201
  13.9 2.8 %collective-permute-start.2 = (bf16[2,80,64]{2,1,0:T(8,128)(2,1)S(1)}, bf16[2,80,64]{2,1,0:T(8,128)(2,1)S(1)}, u32[]{:S(2)}, u32[]{:S(2)}) collective-permute-start(bf16[2,80,64]{2,1,0:T(8,128)(2,1)S(1)} %get-tuple-element.12), channel_id=1, source_target_pairs={{0,1},{1,0},{4,5},{5,4},{8,9},{9,8},{12,13},{13,12},{2,3},{3,2},{6... | collective-permute-start | bytes 61448 | tf_op jit(solution)/shard_map/interface/ppermute | solution.py:201
  17.4 0.0 copy-done.8
  17.4 1.5 %collective-permute-done.3.rest_1_ = bf16[2,80,64]{2,1,0:T(8,128)(2,1)S(1)} collective-permute-done((bf16[2,80,64]{2,1,0:T(8,128)(2,1)S(1)}, bf16[2,80,64]{2,1,0:T(8,128)(2,1)S(1)}, u32[]{:S(2)}, u32[]{:S(2)}) %collective-permute-start.3) | collective-permute-done | bytes 20512 | tf_op jit(solution)/shard_map/interface/ppermute | solution.py:201
  18.9 0.0 collective-permute-done.2.rest_0_
  18.9 0.0 collective-permute-done.low_ref
  18.9 0.0 collective-permute-done.1.high_ref
  18.9 0.0 copy-done.1
  18.9 0.0 copy-done.2
  19.0 0.0 copy-done.3
  19.0 0.0 copy-done.4
  19.0 0.0 copy-done.5
  19.0 0.0 copy-done.6
  19.0 0.0 copy-done.7
  19.0 10.4 %couple.1 = (f32[2,320,1024]{2,1,0:T(8,128)S(1)}, f32[4,1024]{1,0:T(4,128)S(1)}) custom-call(s32[3]{0:T(128)S(1)} %pad_add_fusion.place_ref, f32[1]{0:T(128)S(6)} %copy.17.freq_ref, f32[4,4]{1,0:T(4,128)S(1)} %copy-done.7, s32[6,1024]{1,0:T(8,128)S(1)} %bitcast.15, s32[2,64]{1,0:T(2,128)S(1)} %bitcast.17, bf16[2,320,1024]{2,1,0:T(8,128)(2,1)S(1)} %bitcast.13, ...), custom_call_target="tpu_custom_call" | custom-call | flops 3690987520 | bytes 6553600 | tf_op jit(solution)/shard_map/couple/couple/pallas_call | solution.py:209
  29.4 2.5 %collective-permute-done.6.rest_0_ = bf16[2,320,1024]{2,1,0:T(8,128)(2,1)S(1)} collective-permute-done((bf16[2,320,1024]{2,1,0:T(8,128)(2,1)}, bf16[2,320,1024]{2,1,0:T(8,128)(2,1)S(1)}, u32[]{:S(2)}, u32[]{:S(2)}) %collective-permute-start.6) | collective-permute-done | bytes 1310752 | tf_op jit(solution)/shard_map/instances/ppermute | solution.py:174
  31.9 1.6 %update.1 = bf16[2,320,1024]{2,1,0:T(8,128)(2,1)} custom-call(f32[2,320,1024]{2,1,0:T(8,128)S(1)} %get-tuple-element.13.ready_ref, f32[4,1024]{1,0:T(4,128)S(1)} %get-tuple-element.14.factor_ref, bf16[320,320]{1,0:T(8,128)(2,1)S(1)} %copy-done.1, bf16[2,320,1024]{2,1,0:T(8,128)(2,1)S(1)} %collective-permute-done.6.rest_0_), custom_call_target="tpu_custom_call" | custom-call | flops 419430400 | bytes 5242880 | tf_op jit(solution)/shard_map/update/update/pallas_call | solution.py:229
  (1 shorter events, 0.0 us)
Async XLA Ops:
  0.0 31.9 %collective-permute-start.6 = (bf16[2,320,1024]{2,1,0:T(8,128)(2,1)}, bf16[2,320,1024]{2,1,0:T(8,128)(2,1)S(1)}, u32[]{:S(2)}, u32[]{:S(2)}) collective-permute-start(bf16[2,320,1024]{2,1,0:T(8,128)(2,1)} %bitcast.10), channel_id=1, source_target_pairs={{0,2},{2,0},{1,3},{3,1},{4,6},{6,4},{5,7},{7,5},{8,10},{10,8},{9,1... | collective-permute-start | bytes 3932168 | tf_op jit(solution)/shard_map/instances/ppermute | solution.py:174
  4.2 1.3 %copy-start = (bf16[1,2,320,1024]{3,2,1,0:T(8,128)(2,1)S(1)}, bf16[1,2,320,1024]{3,2,1,0:T(8,128)(2,1)}, u32[]{:S(2)}) copy-start(bf16[1,2,320,1024]{3,2,1,0:T(8,128)(2,1)} %param.11) | copy-start | bytes 3932164
  5.6 11.8 %copy-start.8 = (s32[1,6,1024]{2,0,1:T(1,128)S(1)}, s32[1,6,1024]{2,0,1:T(1,128)}, u32[]{:S(2)}) copy-start(s32[1,6,1024]{2,0,1:T(1,128)} %param.15) | copy-start | bytes 73732
  5.6 13.4 %copy-start.1 = (bf16[320,320]{1,0:T(8,128)(2,1)S(1)}, bf16[320,320]{1,0:T(8,128)(2,1)}, u32[]{:S(2)}) copy-start(bf16[320,320]{1,0:T(8,128)(2,1)} %inverse_ref.3) | copy-start | bytes 614404
  5.6 13.4 %copy-start.2 = (bf16[1,2,320,1024]{3,2,1,0:T(8,128)(2,1)S(1)}, bf16[1,2,320,1024]{3,2,1,0:T(8,128)(2,1)}, u32[]{:S(2)}) copy-start(bf16[1,2,320,1024]{3,2,1,0:T(8,128)(2,1)} %param.12) | copy-start | bytes 3932164
  5.6 13.4 %copy-start.3 = (bf16[320,480]{1,0:T(8,128)(2,1)S(1)}, bf16[320,480]{1,0:T(8,128)(2,1)}, u32[]{:S(2)}) copy-start(bf16[320,480]{1,0:T(8,128)(2,1)} %lift_ref.1) | copy-start | bytes 921604
  5.6 13.4 %copy-start.4 = (bf16[320,320]{1,0:T(8,128)(2,1)S(1)}, bf16[320,320]{1,0:T(8,128)(2,1)}, u32[]{:S(2)}) copy-start(bf16[320,320]{1,0:T(8,128)(2,1)} %volume_ref.1) | copy-start | bytes 614404
  5.6 13.4 %copy-start.5 = (f32[1,1024]{1,0:T(1,128)S(1)}, f32[1,1024]{1,0:T(1,128)}, u32[]{:S(2)}) copy-start(f32[1,1024]{1,0:T(1,128)} %scale_ref.1) | copy-start | bytes 12292
  5.6 13.4 %copy-start.6 = (s32[1,2,64]{2,1,0:T(2,128)S(1)}, s32[1,2,64]{2,1,0:T(2,128)}, u32[]{:S(2)}) copy-start(s32[1,2,64]{2,1,0:T(2,128)} %param.16) | copy-start | bytes 1540
  5.6 13.4 %copy-start.7 = (f32[4,4]{1,0:T(4,128)S(1)}, f32[4,4]{1,0:T(4,128)}, u32[]{:S(2)}) copy-start(f32[4,4]{1,0:T(4,128)} %constant.13.clone.table_ref) | copy-start | bytes 196
  6.6 6.6 %collective-permute-start.5 = (bf16[2,80,64]{2,1,0:T(8,128)(2,1)S(1)}, bf16[2,80,64]{2,1,0:T(8,128)(2,1)S(1)}, u32[]{:S(2)}, u32[]{:S(2)}) collective-permute-start(bf16[2,80,64]{2,1,0:T(8,128)(2,1)S(1)} %get-tuple-element.12), channel_id=1, source_target_pairs={{0,13},{1,12},{4,1},{5,0},{8,5},{9,4},{12,9},{13,8},{2,15},{3,14},... | collective-permute-start | bytes 61448 | tf_op jit(solution)/shard_map/interface/ppermute | solution.py:201
  9.5 4.5 %collective-permute-start.4 = (bf16[2,80,64]{2,1,0:T(8,128)(2,1)S(1)}, bf16[2,80,64]{2,1,0:T(8,128)(2,1)S(1)}, u32[]{:S(2)}, u32[]{:S(2)}) collective-permute-start(bf16[2,80,64]{2,1,0:T(8,128)(2,1)S(1)} %get-tuple-element.12), channel_id=1, source_target_pairs={{0,9},{1,8},{4,13},{5,12},{8,1},{9,0},{12,5},{13,4},{2,11},{3,10},... | collective-permute-start | bytes 61448 | tf_op jit(solution)/shard_map/interface/ppermute | solution.py:201
  9.5 9.5 %collective-permute-start = (bf16[2,160,64]{2,1,0:T(8,128)(2,1)S(1)}, bf16[2,160,64]{2,1,0:T(8,128)(2,1)S(1)}, u32[]{:S(2)}, u32[]{:S(2)}) collective-permute-start(bf16[2,160,64]{2,1,0:T(8,128)(2,1)S(1)} %get-tuple-element.10), channel_id=1, source_target_pairs={{0,4},{4,8},{8,12},{12,0},{1,5},{5,9},{9,13},{13,1},{2,6},{6,10},{... | collective-permute-start | bytes 122888 | tf_op jit(solution)/shard_map/halo/ppermute | solution.py:198
  11.0 7.9 %collective-permute-start.1 = (bf16[2,160,64]{2,1,0:T(8,128)(2,1)S(1)}, bf16[2,160,64]{2,1,0:T(8,128)(2,1)S(1)}, u32[]{:S(2)}, u32[]{:S(2)}) collective-permute-start(bf16[2,160,64]{2,1,0:T(8,128)(2,1)S(1)} %get-tuple-element.11), channel_id=1, source_target_pairs={{0,12},{4,0},{8,4},{12,8},{1,13},{5,1},{9,5},{13,9},{2,14},{6,2},{... | collective-permute-start | bytes 122888 | tf_op jit(solution)/shard_map/halo/ppermute | solution.py:199
  13.3 5.6 %collective-permute-start.3 = (bf16[2,80,64]{2,1,0:T(8,128)(2,1)S(1)}, bf16[2,80,64]{2,1,0:T(8,128)(2,1)S(1)}, u32[]{:S(2)}, u32[]{:S(2)}) collective-permute-start(bf16[2,80,64]{2,1,0:T(8,128)(2,1)S(1)} %get-tuple-element.12), channel_id=1, source_target_pairs={{0,5},{1,4},{4,9},{5,8},{8,13},{9,12},{12,1},{13,0},{2,7},{3,6},{6... | collective-permute-start | bytes 61448 | tf_op jit(solution)/shard_map/interface/ppermute | solution.py:201
  13.9 5.0 %collective-permute-start.2 = (bf16[2,80,64]{2,1,0:T(8,128)(2,1)S(1)}, bf16[2,80,64]{2,1,0:T(8,128)(2,1)S(1)}, u32[]{:S(2)}, u32[]{:S(2)}) collective-permute-start(bf16[2,80,64]{2,1,0:T(8,128)(2,1)S(1)} %get-tuple-element.12), channel_id=1, source_target_pairs={{0,1},{1,0},{4,5},{5,4},{8,9},{9,8},{12,13},{13,12},{2,3},{3,2},{6... | collective-permute-start | bytes 61448 | tf_op jit(solution)/shard_map/interface/ppermute | solution.py:201

commit v15 on v14

--- a/solution.py
+++ b/solution.py
@@ -132,9 +132,14 @@
 def update_kernel(tile, ready_ref, factor_ref, inverse_ref, *rest):
     others, (out_ref, made, sems) = rest[:-3], rest[-3:]
     count, dof, total = ready_ref.shape
-    copies = []
-    for t in range(total // tile):
-        cols = slice(t * tile, (t + 1) * tile)
+
+    def copy(t):
+        cols = pl.ds(pl.multiple_of(t * tile, tile), tile)
+        return pltpu.make_async_copy(made.at[t], out_ref.at[:, :, cols], sems.at[t])
+
+    @pl.loop(0, total // tile)
+    def _(t):
+        cols = pl.ds(pl.multiple_of(t * tile, tile), tile)
         moved = [dot(inverse_ref[...], other[m, :, cols]) for other in others for m in range(count)]
         for n in range(count):
             value = ready_ref[n, :, cols]
@@ -142,11 +147,11 @@
                 at = n * len(moved) + k
                 value -= factor_ref[at : at + 1, cols] * part
             made[t, n] = value.astype(jnp.bfloat16)
-        copy = pltpu.make_async_copy(made.at[t], out_ref.at[:, :, cols], sems.at[t])
-        copy.start(priority=t % 2)
-        copies.append(copy)
-    for copy in copies:
-        copy.wait()
+        copy(t).start()
+
+    @pl.loop(0, total // tile)
+    def _(t):
+        copy(t).wait()
 
 
 def whole(array):

time: 33.8 us -> 34.3 us (1.015)
  Pallas kernels: 13.1 us -> 13.6 us
    pallas_call x1, Pallas kernels: 1.64 us -> 2.19 us  [body(): pl.pallas_call(functools.partial(update_kernel, tile), out_shape=jax.Shap...]
  transfers between devices with their start and end apart: 7 -> 7, of which waited for: 3 -> 3; matrix products, arithmetic and copies ran while one was open for 4% -> 4% of each run, Pallas kernels for 34% -> 33%
where the time goes in v15:
time: 34.3 us; the launch traced here: 34.1 us
  Pallas kernels  13.6 us (40%)
  starting transfers between devices  12.4 us (36%)
  waiting for transfers between devices  4.67 us (14%)
  local copies, waits for them, and re-layouts  2.58 us (8%)
  between operations  0.79 us (2%)
    pallas_call x1, Pallas kernels, body(): pl.pallas_call(functools.partial(couple_kernel, shards, peers), grid=(ste...  10.4 us
    ppermute x4, starting transfers between devices, body(): lax.ppermute(cross, ('space', 'row'), [(i * 2 + r, (i + d) % shards * 2 +...  5.62 us
    ppermute x1, starting transfers between devices, body(): lax.ppermute(current, 'inst', [(i, (i + d) % peers) for i in range(peers)])  2.94 us
    unnamed x20, local copies, waits for them, and re-layouts  2.58 us
    ppermute x1, waiting for transfers between devices, body(): lax.ppermute(current, 'inst', [(i, (i + d) % peers) for i in range(peers)])  2.5 us
    ppermute x1, starting transfers between devices, body(): lax.ppermute(down, 'space', [(i, (i - 1) % shards) for i in range(shards)])  2.25 us
    pallas_call x1, Pallas kernels, body(): pl.pallas_call(functools.partial(update_kernel, tile), out_shape=jax.Shap...  2.19 us
    ppermute x4, waiting for transfers between devices, body(): lax.ppermute(cross, ('space', 'row'), [(i * 2 + r, (i + d) % shards * 2 +...  2.16 us
  transfers between devices with their start and end apart: 7, of which 3 were waited for; matrix products, arithmetic and copies ran while one was open for 4% of the time, Pallas kernels for 33%

profile of v15, /device:TPU:0, one launch (start us, length us, event | category | flops | bytes accessed | tf_op | source)
XLA Modules:
  0.0 34.1 jit_solution(3303456253345711471)
XLA Ops:
  0.0 2.9 %collective-permute-start.6 = (bf16[2,320,1024]{2,1,0:T(8,128)(2,1)}, bf16[2,320,1024]{2,1,0:T(8,128)(2,1)S(1)}, u32[]{:S(2)}, u32[]{:S(2)}) collective-permute-start(bf16[2,320,1024]{2,1,0:T(8,128)(2,1)} %bitcast.10), channel_id=1, source_target_pairs={{0,2},{2,0},{1,3},{3,1},{4,6},{6,4},{5,7},{7,5},{8,10},{10,8},{9,1... | collective-permute-start | bytes 3932168 | tf_op jit(solution)/shard_map/instances/ppermute | solution.py:179
  2.9 1.2 %copy.13.trace_ref = bf16[480,320]{1,0:T(8,128)(2,1)S(1)} copy(bf16[480,320]{0,1:T(8,128)(2,1)} %param.18) | data formatting | bytes 614400 | tf_op args[7]
  4.2 0.1 pad_add_fusion.place_ref
  4.2 0.0 copy-start
  4.2 1.3 %copy-done = bf16[1,2,320,1024]{3,2,1,0:T(8,128)(2,1)S(1)} copy-done((bf16[1,2,320,1024]{3,2,1,0:T(8,128)(2,1)S(1)}, bf16[1,2,320,1024]{3,2,1,0:T(8,128)(2,1)}, u32[]{:S(2)}) %copy-start) | copy-done | bytes 1310744
  5.6 0.0 copy-start.8
  5.6 0.0 copy-start.1
  5.6 0.0 copy-start.2
  5.6 0.0 copy-start.3
  5.6 0.0 copy-start.4
  5.6 0.0 copy-start.5
  5.6 0.0 copy-start.6
  5.6 0.0 copy-start.7
  5.6 1.0 %ends.1 = (bf16[2,160,64]{2,1,0:T(8,128)(2,1)S(1)}, bf16[2,160,64]{2,1,0:T(8,128)(2,1)S(1)}, bf16[2,80,64]{2,1,0:T(8,128)(2,1)S(1)}) custom-call(s32[3]{0:T(128)S(1)} %pad_add_fusion.place_ref, bf16[2,320,1024]{2,1,0:T(8,128)(2,1)S(1)} %bitcast.11, bf16[2,320,1024]{2,1,0:T(8,128)(2,1)S(1)} %bitcast.12, bf16[480,320]{1,0:T(8,128)(2,1)S(1)} %copy.13.trace_ref), custom_call_target="tpu_custom_call" | custom-call | flops 104857600 | bytes 1000000 | tf_op jit(solution)/shard_map/ends/ends/pallas_call | solution.py:183
  6.6 2.8 %collective-permute-start.5 = (bf16[2,80,64]{2,1,0:T(8,128)(2,1)S(1)}, bf16[2,80,64]{2,1,0:T(8,128)(2,1)S(1)}, u32[]{:S(2)}, u32[]{:S(2)}) collective-permute-start(bf16[2,80,64]{2,1,0:T(8,128)(2,1)S(1)} %get-tuple-element.12), channel_id=1, source_target_pairs={{0,13},{1,12},{4,1},{5,0},{8,5},{9,4},{12,9},{13,8},{2,15},{3,14},... | collective-permute-start | bytes 61448 | tf_op jit(solution)/shard_map/interface/ppermute | solution.py:206
  9.5 0.0 collective-permute-start.4
  9.5 1.6 %collective-permute-start = (bf16[2,160,64]{2,1,0:T(8,128)(2,1)S(1)}, bf16[2,160,64]{2,1,0:T(8,128)(2,1)S(1)}, u32[]{:S(2)}, u32[]{:S(2)}) collective-permute-start(bf16[2,160,64]{2,1,0:T(8,128)(2,1)S(1)} %get-tuple-element.10), channel_id=1, source_target_pairs={{0,4},{4,8},{8,12},{12,0},{1,5},{5,9},{9,13},{13,1},{2,6},{6,10},{... | collective-permute-start | bytes 122888 | tf_op jit(solution)/shard_map/halo/ppermute | solution.py:203
  11.0 2.2 %collective-permute-start.1 = (bf16[2,160,64]{2,1,0:T(8,128)(2,1)S(1)}, bf16[2,160,64]{2,1,0:T(8,128)(2,1)S(1)}, u32[]{:S(2)}, u32[]{:S(2)}) collective-permute-start(bf16[2,160,64]{2,1,0:T(8,128)(2,1)S(1)} %get-tuple-element.11), channel_id=1, source_target_pairs={{0,12},{4,0},{8,4},{12,8},{1,13},{5,1},{9,5},{13,9},{2,14},{6,2},{... | collective-permute-start | bytes 122888 | tf_op jit(solution)/shard_map/halo/ppermute | solution.py:204
  13.3 0.0 collective-permute-done.5.rest_3_
  13.3 0.0 collective-permute-start.3
  13.3 0.6 %collective-permute-done.4.rest_2_ = bf16[2,80,64]{2,1,0:T(8,128)(2,1)S(1)} collective-permute-done((bf16[2,80,64]{2,1,0:T(8,128)(2,1)S(1)}, bf16[2,80,64]{2,1,0:T(8,128)(2,1)S(1)}, u32[]{:S(2)}, u32[]{:S(2)}) %collective-permute-start.4) | collective-permute-done | bytes 20512 | tf_op jit(solution)/shard_map/interface/ppermute | solution.py:206
  13.9 2.8 %collective-permute-start.2 = (bf16[2,80,64]{2,1,0:T(8,128)(2,1)S(1)}, bf16[2,80,64]{2,1,0:T(8,128)(2,1)S(1)}, u32[]{:S(2)}, u32[]{:S(2)}) collective-permute-start(bf16[2,80,64]{2,1,0:T(8,128)(2,1)S(1)} %get-tuple-element.12), channel_id=1, source_target_pairs={{0,1},{1,0},{4,5},{5,4},{8,9},{9,8},{12,13},{13,12},{2,3},{3,2},{6... | collective-permute-start | bytes 61448 | tf_op jit(solution)/shard_map/interface/ppermute | solution.py:206
  17.4 0.0 copy-done.8
  17.4 1.5 %collective-permute-done.3.rest_1_ = bf16[2,80,64]{2,1,0:T(8,128)(2,1)S(1)} collective-permute-done((bf16[2,80,64]{2,1,0:T(8,128)(2,1)S(1)}, bf16[2,80,64]{2,1,0:T(8,128)(2,1)S(1)}, u32[]{:S(2)}, u32[]{:S(2)}) %collective-permute-start.3) | collective-permute-done | bytes 20512 | tf_op jit(solution)/shard_map/interface/ppermute | solution.py:206
  18.9 0.0 collective-permute-done.2.rest_0_
  18.9 0.0 collective-permute-done.low_ref
  18.9 0.0 collective-permute-done.1.high_ref
  18.9 0.0 copy-done.1
  18.9 0.0 copy-done.2
  19.0 0.0 copy-done.3
  19.0 0.0 copy-done.4
  19.0 0.0 copy-done.5
  19.0 0.0 copy-done.6
  19.0 0.0 copy-done.7
  19.0 10.4 %couple.1 = (f32[2,320,1024]{2,1,0:T(8,128)S(1)}, f32[4,1024]{1,0:T(4,128)S(1)}) custom-call(s32[3]{0:T(128)S(1)} %pad_add_fusion.place_ref, f32[1]{0:T(128)S(6)} %copy.17.freq_ref, f32[4,4]{1,0:T(4,128)S(1)} %copy-done.7, s32[6,1024]{1,0:T(8,128)S(1)} %bitcast.15, s32[2,64]{1,0:T(2,128)S(1)} %bitcast.17, bf16[2,320,1024]{2,1,0:T(8,128)(2,1)S(1)} %bitcast.13, ...), custom_call_target="tpu_custom_call" | custom-call | flops 3690987520 | bytes 6553600 | tf_op jit(solution)/shard_map/couple/couple/pallas_call | solution.py:214
  29.4 2.5 %collective-permute-done.6.rest_0_ = bf16[2,320,1024]{2,1,0:T(8,128)(2,1)S(1)} collective-permute-done((bf16[2,320,1024]{2,1,0:T(8,128)(2,1)}, bf16[2,320,1024]{2,1,0:T(8,128)(2,1)S(1)}, u32[]{:S(2)}, u32[]{:S(2)}) %collective-permute-start.6) | collective-permute-done | bytes 1310752 | tf_op jit(solution)/shard_map/instances/ppermute | solution.py:179
  31.9 2.2 %update.1 = bf16[2,320,1024]{2,1,0:T(8,128)(2,1)} custom-call(f32[2,320,1024]{2,1,0:T(8,128)S(1)} %get-tuple-element.13.ready_ref, f32[4,1024]{1,0:T(4,128)S(1)} %get-tuple-element.14.factor_ref, bf16[320,320]{1,0:T(8,128)(2,1)S(1)} %copy-done.1, bf16[2,320,1024]{2,1,0:T(8,128)(2,1)S(1)} %collective-permute-done.6.rest_0_), custom_call_target="tpu_custom_call" | custom-call | flops 419430400 | bytes 5242880 | tf_op jit(solution)/shard_map/update/update/pallas_call | solution.py:234
  (1 shorter events, 0.0 us)
Async XLA Ops:
  0.0 31.9 %collective-permute-start.6 = (bf16[2,320,1024]{2,1,0:T(8,128)(2,1)}, bf16[2,320,1024]{2,1,0:T(8,128)(2,1)S(1)}, u32[]{:S(2)}, u32[]{:S(2)}) collective-permute-start(bf16[2,320,1024]{2,1,0:T(8,128)(2,1)} %bitcast.10), channel_id=1, source_target_pairs={{0,2},{2,0},{1,3},{3,1},{4,6},{6,4},{5,7},{7,5},{8,10},{10,8},{9,1... | collective-permute-start | bytes 3932168 | tf_op jit(solution)/shard_map/instances/ppermute | solution.py:179
  4.2 1.3 %copy-start = (bf16[1,2,320,1024]{3,2,1,0:T(8,128)(2,1)S(1)}, bf16[1,2,320,1024]{3,2,1,0:T(8,128)(2,1)}, u32[]{:S(2)}) copy-start(bf16[1,2,320,1024]{3,2,1,0:T(8,128)(2,1)} %param.11) | copy-start | bytes 3932164
  5.6 11.8 %copy-start.8 = (s32[1,6,1024]{2,0,1:T(1,128)S(1)}, s32[1,6,1024]{2,0,1:T(1,128)}, u32[]{:S(2)}) copy-start(s32[1,6,1024]{2,0,1:T(1,128)} %param.15) | copy-start | bytes 73732
  5.6 13.4 %copy-start.1 = (bf16[320,320]{1,0:T(8,128)(2,1)S(1)}, bf16[320,320]{1,0:T(8,128)(2,1)}, u32[]{:S(2)}) copy-start(bf16[320,320]{1,0:T(8,128)(2,1)} %inverse_ref.3) | copy-start | bytes 614404
  5.6 13.4 %copy-start.2 = (bf16[1,2,320,1024]{3,2,1,0:T(8,128)(2,1)S(1)}, bf16[1,2,320,1024]{3,2,1,0:T(8,128)(2,1)}, u32[]{:S(2)}) copy-start(bf16[1,2,320,1024]{3,2,1,0:T(8,128)(2,1)} %param.12) | copy-start | bytes 3932164
  5.6 13.4 %copy-start.3 = (bf16[320,480]{1,0:T(8,128)(2,1)S(1)}, bf16[320,480]{1,0:T(8,128)(2,1)}, u32[]{:S(2)}) copy-start(bf16[320,480]{1,0:T(8,128)(2,1)} %lift_ref.1) | copy-start | bytes 921604
  5.6 13.4 %copy-start.4 = (bf16[320,320]{1,0:T(8,128)(2,1)S(1)}, bf16[320,320]{1,0:T(8,128)(2,1)}, u32[]{:S(2)}) copy-start(bf16[320,320]{1,0:T(8,128)(2,1)} %volume_ref.1) | copy-start | bytes 614404
  5.6 13.4 %copy-start.5 = (f32[1,1024]{1,0:T(1,128)S(1)}, f32[1,1024]{1,0:T(1,128)}, u32[]{:S(2)}) copy-start(f32[1,1024]{1,0:T(1,128)} %scale_ref.1) | copy-start | bytes 12292
  5.6 13.4 %copy-start.6 = (s32[1,2,64]{2,1,0:T(2,128)S(1)}, s32[1,2,64]{2,1,0:T(2,128)}, u32[]{:S(2)}) copy-start(s32[1,2,64]{2,1,0:T(2,128)} %param.16) | copy-start | bytes 1540
  5.6 13.4 %copy-start.7 = (f32[4,4]{1,0:T(4,128)S(1)}, f32[4,4]{1,0:T(4,128)}, u32[]{:S(2)}) copy-start(f32[4,4]{1,0:T(4,128)} %constant.13.clone.table_ref) | copy-start | bytes 196
  6.6 6.6 %collective-permute-start.5 = (bf16[2,80,64]{2,1,0:T(8,128)(2,1)S(1)}, bf16[2,80,64]{2,1,0:T(8,128)(2,1)S(1)}, u32[]{:S(2)}, u32[]{:S(2)}) collective-permute-start(bf16[2,80,64]{2,1,0:T(8,128)(2,1)S(1)} %get-tuple-element.12), channel_id=1, source_target_pairs={{0,13},{1,12},{4,1},{5,0},{8,5},{9,4},{12,9},{13,8},{2,15},{3,14},... | collective-permute-start | bytes 61448 | tf_op jit(solution)/shard_map/interface/ppermute | solution.py:206
  9.5 4.5 %collective-permute-start.4 = (bf16[2,80,64]{2,1,0:T(8,128)(2,1)S(1)}, bf16[2,80,64]{2,1,0:T(8,128)(2,1)S(1)}, u32[]{:S(2)}, u32[]{:S(2)}) collective-permute-start(bf16[2,80,64]{2,1,0:T(8,128)(2,1)S(1)} %get-tuple-element.12), channel_id=1, source_target_pairs={{0,9},{1,8},{4,13},{5,12},{8,1},{9,0},{12,5},{13,4},{2,11},{3,10},... | collective-permute-start | bytes 61448 | tf_op jit(solution)/shard_map/interface/ppermute | solution.py:206
  9.5 9.5 %collective-permute-start = (bf16[2,160,64]{2,1,0:T(8,128)(2,1)S(1)}, bf16[2,160,64]{2,1,0:T(8,128)(2,1)S(1)}, u32[]{:S(2)}, u32[]{:S(2)}) collective-permute-start(bf16[2,160,64]{2,1,0:T(8,128)(2,1)S(1)} %get-tuple-element.10), channel_id=1, source_target_pairs={{0,4},{4,8},{8,12},{12,0},{1,5},{5,9},{9,13},{13,1},{2,6},{6,10},{... | collective-permute-start | bytes 122888 | tf_op jit(solution)/shard_map/halo/ppermute | solution.py:203
  11.0 7.9 %collective-permute-start.1 = (bf16[2,160,64]{2,1,0:T(8,128)(2,1)S(1)}, bf16[2,160,64]{2,1,0:T(8,128)(2,1)S(1)}, u32[]{:S(2)}, u32[]{:S(2)}) collective-permute-start(bf16[2,160,64]{2,1,0:T(8,128)(2,1)S(1)} %get-tuple-element.11), channel_id=1, source_target_pairs={{0,12},{4,0},{8,4},{12,8},{1,13},{5,1},{9,5},{13,9},{2,14},{6,2},{... | collective-permute-start | bytes 122888 | tf_op jit(solution)/shard_map/halo/ppermute | solution.py:204
  13.3 5.6 %collective-permute-start.3 = (bf16[2,80,64]{2,1,0:T(8,128)(2,1)S(1)}, bf16[2,80,64]{2,1,0:T(8,128)(2,1)S(1)}, u32[]{:S(2)}, u32[]{:S(2)}) collective-permute-start(bf16[2,80,64]{2,1,0:T(8,128)(2,1)S(1)} %get-tuple-element.12), channel_id=1, source_target_pairs={{0,5},{1,4},{4,9},{5,8},{8,13},{9,12},{12,1},{13,0},{2,7},{3,6},{6... | collective-permute-start | bytes 61448 | tf_op jit(solution)/shard_map/interface/ppermute | solution.py:206
  13.9 5.0 %collective-permute-start.2 = (bf16[2,80,64]{2,1,0:T(8,128)(2,1)S(1)}, bf16[2,80,64]{2,1,0:T(8,128)(2,1)S(1)}, u32[]{:S(2)}, u32[]{:S(2)}) collective-permute-start(bf16[2,80,64]{2,1,0:T(8,128)(2,1)S(1)} %get-tuple-element.12), channel_id=1, source_target_pairs={{0,1},{1,0},{4,5},{5,4},{8,9},{9,8},{12,13},{13,12},{2,3},{3,2},{6... | collective-permute-start | bytes 61448 | tf_op jit(solution)/shard_map/interface/ppermute | solution.py:206

commit v16 on v9

--- a/solution.py
+++ b/solution.py
@@ -134,11 +134,18 @@
     others, (out_ref, made, moved, sems) = rest[:-4], rest[-4:]
     count, dof, total = ready_ref.shape
     products = len(others) * count
+    steps = total // tile
     copies = []
-    for t in range(total // tile):
+
+    def multiply(t):
+        for k in range(products):
+            moved[t % 2, k] = dot(inverse_ref[...], others[k // count][k % count, :, t * tile : (t + 1) * tile])
+
+    multiply(0)
+    for t in range(steps):
         cols = slice(t * tile, (t + 1) * tile)
-        for k in range(products):
-            moved[t % 2, k] = dot(inverse_ref[...], others[k // count][k % count, :, cols])
+        if t + 1 < steps:
+            multiply(t + 1)
         factors = [[factor_ref[n * products + k : n * products + k + 1, cols] for k in range(products)]
                    for n in range(count)]
         for strip in range(0, dof, STRIP):

time: 33.8 us -> 33.8 us (level)
  no operation moved by 1% of the time
where the time goes in v16:
time: 33.8 us; the launch traced here: 33.6 us
  Pallas kernels  13.1 us (39%)
  starting transfers between devices  12.4 us (37%)
  waiting for transfers between devices  4.67 us (14%)
  local copies, waits for them, and re-layouts  2.58 us (8%)
  between operations  0.79 us (2%)
    pallas_call x1, Pallas kernels, body(): pl.pallas_call(functools.partial(couple_kernel, shards, peers), grid=(ste...  10.4 us
    ppermute x4, starting transfers between devices, body(): lax.ppermute(cross, ('space', 'row'), [(i * 2 + r, (i + d) % shards * 2 +...  5.62 us
    ppermute x1, starting transfers between devices, body(): lax.ppermute(current, 'inst', [(i, (i + d) % peers) for i in range(peers)])  2.94 us
    unnamed x20, local copies, waits for them, and re-layouts  2.58 us
    ppermute x1, waiting for transfers between devices, body(): lax.ppermute(current, 'inst', [(i, (i + d) % peers) for i in range(peers)])  2.5 us
    ppermute x1, starting transfers between devices, body(): lax.ppermute(down, 'space', [(i, (i - 1) % shards) for i in range(shards)])  2.25 us
    ppermute x4, waiting for transfers between devices, body(): lax.ppermute(cross, ('space', 'row'), [(i * 2 + r, (i + d) % shards * 2 +...  2.16 us
    pallas_call x1, Pallas kernels, body(): pl.pallas_call(functools.partial(update_kernel, tile), out_shape=jax.Shap...  1.64 us
  transfers between devices with their start and end apart: 7, of which 3 were waited for; matrix products, arithmetic and copies ran while one was open for 4% of the time, Pallas kernels for 34%

profile of v16, /device:TPU:0, one launch (start us, length us, event | category | flops | bytes accessed | tf_op | source)
XLA Modules:
  0.0 33.6 jit_solution(1381746905268175217)
XLA Ops:
  0.0 2.9 %collective-permute-start.6 = (bf16[2,320,1024]{2,1,0:T(8,128)(2,1)}, bf16[2,320,1024]{2,1,0:T(8,128)(2,1)S(1)}, u32[]{:S(2)}, u32[]{:S(2)}) collective-permute-start(bf16[2,320,1024]{2,1,0:T(8,128)(2,1)} %bitcast.10), channel_id=1, source_target_pairs={{0,2},{2,0},{1,3},{3,1},{4,6},{6,4},{5,7},{7,5},{8,10},{10,8},{9,1... | collective-permute-start | bytes 3932168 | tf_op jit(solution)/shard_map/instances/ppermute | solution.py:188
  2.9 1.2 %copy.13.trace_ref = bf16[480,320]{1,0:T(8,128)(2,1)S(1)} copy(bf16[480,320]{0,1:T(8,128)(2,1)} %param.18) | data formatting | bytes 614400 | tf_op args[7]
  4.2 0.1 pad_add_fusion.place_ref
  4.2 0.0 copy-start
  4.2 1.3 %copy-done = bf16[1,2,320,1024]{3,2,1,0:T(8,128)(2,1)S(1)} copy-done((bf16[1,2,320,1024]{3,2,1,0:T(8,128)(2,1)S(1)}, bf16[1,2,320,1024]{3,2,1,0:T(8,128)(2,1)}, u32[]{:S(2)}) %copy-start) | copy-done | bytes 1310744
  5.6 0.0 copy-start.8
  5.6 0.0 copy-start.1
  5.6 0.0 copy-start.2
  5.6 0.0 copy-start.3
  5.6 0.0 copy-start.4
  5.6 0.0 copy-start.5
  5.6 0.0 copy-start.6
  5.6 0.0 copy-start.7
  5.6 1.0 %ends.1 = (bf16[2,160,64]{2,1,0:T(8,128)(2,1)S(1)}, bf16[2,160,64]{2,1,0:T(8,128)(2,1)S(1)}, bf16[2,80,64]{2,1,0:T(8,128)(2,1)S(1)}) custom-call(s32[3]{0:T(128)S(1)} %pad_add_fusion.place_ref, bf16[2,320,1024]{2,1,0:T(8,128)(2,1)S(1)} %bitcast.11, bf16[2,320,1024]{2,1,0:T(8,128)(2,1)S(1)} %bitcast.12, bf16[480,320]{1,0:T(8,128)(2,1)S(1)} %copy.13.trace_ref), custom_call_target="tpu_custom_call" | custom-call | flops 104857600 | bytes 1000000 | tf_op jit(solution)/shard_map/ends/ends/pallas_call | solution.py:192
  6.6 2.8 %collective-permute-start.5 = (bf16[2,80,64]{2,1,0:T(8,128)(2,1)S(1)}, bf16[2,80,64]{2,1,0:T(8,128)(2,1)S(1)}, u32[]{:S(2)}, u32[]{:S(2)}) collective-permute-start(bf16[2,80,64]{2,1,0:T(8,128)(2,1)S(1)} %get-tuple-element.12), channel_id=1, source_target_pairs={{0,13},{1,12},{4,1},{5,0},{8,5},{9,4},{12,9},{13,8},{2,15},{3,14},... | collective-permute-start | bytes 61448 | tf_op jit(solution)/shard_map/interface/ppermute | solution.py:215
  9.5 0.0 collective-permute-start.4
  9.5 1.6 %collective-permute-start = (bf16[2,160,64]{2,1,0:T(8,128)(2,1)S(1)}, bf16[2,160,64]{2,1,0:T(8,128)(2,1)S(1)}, u32[]{:S(2)}, u32[]{:S(2)}) collective-permute-start(bf16[2,160,64]{2,1,0:T(8,128)(2,1)S(1)} %get-tuple-element.10), channel_id=1, source_target_pairs={{0,4},{4,8},{8,12},{12,0},{1,5},{5,9},{9,13},{13,1},{2,6},{6,10},{... | collective-permute-start | bytes 122888 | tf_op jit(solution)/shard_map/halo/ppermute | solution.py:212
  11.0 2.2 %collective-permute-start.1 = (bf16[2,160,64]{2,1,0:T(8,128)(2,1)S(1)}, bf16[2,160,64]{2,1,0:T(8,128)(2,1)S(1)}, u32[]{:S(2)}, u32[]{:S(2)}) collective-permute-start(bf16[2,160,64]{2,1,0:T(8,128)(2,1)S(1)} %get-tuple-element.11), channel_id=1, source_target_pairs={{0,12},{4,0},{8,4},{12,8},{1,13},{5,1},{9,5},{13,9},{2,14},{6,2},{... | collective-permute-start | bytes 122888 | tf_op jit(solution)/shard_map/halo/ppermute | solution.py:213
  13.3 0.0 collective-permute-done.5.rest_3_
  13.3 0.0 collective-permute-start.3
  13.3 0.6 %collective-permute-done.4.rest_2_ = bf16[2,80,64]{2,1,0:T(8,128)(2,1)S(1)} collective-permute-done((bf16[2,80,64]{2,1,0:T(8,128)(2,1)S(1)}, bf16[2,80,64]{2,1,0:T(8,128)(2,1)S(1)}, u32[]{:S(2)}, u32[]{:S(2)}) %collective-permute-start.4) | collective-permute-done | bytes 20512 | tf_op jit(solution)/shard_map/interface/ppermute | solution.py:215
  13.9 2.8 %collective-permute-start.2 = (bf16[2,80,64]{2,1,0:T(8,128)(2,1)S(1)}, bf16[2,80,64]{2,1,0:T(8,128)(2,1)S(1)}, u32[]{:S(2)}, u32[]{:S(2)}) collective-permute-start(bf16[2,80,64]{2,1,0:T(8,128)(2,1)S(1)} %get-tuple-element.12), channel_id=1, source_target_pairs={{0,1},{1,0},{4,5},{5,4},{8,9},{9,8},{12,13},{13,12},{2,3},{3,2},{6... | collective-permute-start | bytes 61448 | tf_op jit(solution)/shard_map/interface/ppermute | solution.py:215
  17.4 0.0 copy-done.8
  17.4 1.5 %collective-permute-done.3.rest_1_ = bf16[2,80,64]{2,1,0:T(8,128)(2,1)S(1)} collective-permute-done((bf16[2,80,64]{2,1,0:T(8,128)(2,1)S(1)}, bf16[2,80,64]{2,1,0:T(8,128)(2,1)S(1)}, u32[]{:S(2)}, u32[]{:S(2)}) %collective-permute-start.3) | collective-permute-done | bytes 20512 | tf_op jit(solution)/shard_map/interface/ppermute | solution.py:215
  18.9 0.0 collective-permute-done.2.rest_0_
  18.9 0.0 collective-permute-done.low_ref
  18.9 0.0 collective-permute-done.1.high_ref
  18.9 0.0 copy-done.1
  18.9 0.0 copy-done.2
  19.0 0.0 copy-done.3
  19.0 0.0 copy-done.4
  19.0 0.0 copy-done.5
  19.0 0.0 copy-done.6
  19.0 0.0 copy-done.7
  19.0 10.4 %couple.1 = (f32[2,320,1024]{2,1,0:T(8,128)S(1)}, f32[4,1024]{1,0:T(4,128)S(1)}) custom-call(s32[3]{0:T(128)S(1)} %pad_add_fusion.place_ref, f32[1]{0:T(128)S(6)} %copy.17.freq_ref, f32[4,4]{1,0:T(4,128)S(1)} %copy-done.7, s32[6,1024]{1,0:T(8,128)S(1)} %bitcast.15, s32[2,64]{1,0:T(2,128)S(1)} %bitcast.17, bf16[2,320,1024]{2,1,0:T(8,128)(2,1)S(1)} %bitcast.13, ...), custom_call_target="tpu_custom_call" | custom-call | flops 3690987520 | bytes 6553600 | tf_op jit(solution)/shard_map/couple/couple/pallas_call | solution.py:223
  29.4 2.5 %collective-permute-done.6.rest_0_ = bf16[2,320,1024]{2,1,0:T(8,128)(2,1)S(1)} collective-permute-done((bf16[2,320,1024]{2,1,0:T(8,128)(2,1)}, bf16[2,320,1024]{2,1,0:T(8,128)(2,1)S(1)}, u32[]{:S(2)}, u32[]{:S(2)}) %collective-permute-start.6) | collective-permute-done | bytes 1310752 | tf_op jit(solution)/shard_map/instances/ppermute | solution.py:188
  31.9 1.6 %update.1 = bf16[2,320,1024]{2,1,0:T(8,128)(2,1)} custom-call(f32[2,320,1024]{2,1,0:T(8,128)S(1)} %get-tuple-element.13.ready_ref, f32[4,1024]{1,0:T(4,128)S(1)} %get-tuple-element.14.factor_ref, bf16[320,320]{1,0:T(8,128)(2,1)S(1)} %copy-done.1, bf16[2,320,1024]{2,1,0:T(8,128)(2,1)S(1)} %collective-permute-done.6.rest_0_), custom_call_target="tpu_custom_call" | custom-call | flops 419430400 | bytes 5242880 | tf_op jit(solution)/shard_map/update/update/pallas_call | solution.py:243
  (1 shorter events, 0.0 us)
Async XLA Ops:
  0.0 31.9 %collective-permute-start.6 = (bf16[2,320,1024]{2,1,0:T(8,128)(2,1)}, bf16[2,320,1024]{2,1,0:T(8,128)(2,1)S(1)}, u32[]{:S(2)}, u32[]{:S(2)}) collective-permute-start(bf16[2,320,1024]{2,1,0:T(8,128)(2,1)} %bitcast.10), channel_id=1, source_target_pairs={{0,2},{2,0},{1,3},{3,1},{4,6},{6,4},{5,7},{7,5},{8,10},{10,8},{9,1... | collective-permute-start | bytes 3932168 | tf_op jit(solution)/shard_map/instances/ppermute | solution.py:188
  4.2 1.3 %copy-start = (bf16[1,2,320,1024]{3,2,1,0:T(8,128)(2,1)S(1)}, bf16[1,2,320,1024]{3,2,1,0:T(8,128)(2,1)}, u32[]{:S(2)}) copy-start(bf16[1,2,320,1024]{3,2,1,0:T(8,128)(2,1)} %param.11) | copy-start | bytes 3932164
  5.6 11.8 %copy-start.8 = (s32[1,6,1024]{2,0,1:T(1,128)S(1)}, s32[1,6,1024]{2,0,1:T(1,128)}, u32[]{:S(2)}) copy-start(s32[1,6,1024]{2,0,1:T(1,128)} %param.15) | copy-start | bytes 73732
  5.6 13.4 %copy-start.1 = (bf16[320,320]{1,0:T(8,128)(2,1)S(1)}, bf16[320,320]{1,0:T(8,128)(2,1)}, u32[]{:S(2)}) copy-start(bf16[320,320]{1,0:T(8,128)(2,1)} %inverse_ref.3) | copy-start | bytes 614404
  5.6 13.4 %copy-start.2 = (bf16[1,2,320,1024]{3,2,1,0:T(8,128)(2,1)S(1)}, bf16[1,2,320,1024]{3,2,1,0:T(8,128)(2,1)}, u32[]{:S(2)}) copy-start(bf16[1,2,320,1024]{3,2,1,0:T(8,128)(2,1)} %param.12) | copy-start | bytes 3932164
  5.6 13.4 %copy-start.3 = (bf16[320,480]{1,0:T(8,128)(2,1)S(1)}, bf16[320,480]{1,0:T(8,128)(2,1)}, u32[]{:S(2)}) copy-start(bf16[320,480]{1,0:T(8,128)(2,1)} %lift_ref.1) | copy-start | bytes 921604
  5.6 13.4 %copy-start.4 = (bf16[320,320]{1,0:T(8,128)(2,1)S(1)}, bf16[320,320]{1,0:T(8,128)(2,1)}, u32[]{:S(2)}) copy-start(bf16[320,320]{1,0:T(8,128)(2,1)} %volume_ref.1) | copy-start | bytes 614404
  5.6 13.4 %copy-start.5 = (f32[1,1024]{1,0:T(1,128)S(1)}, f32[1,1024]{1,0:T(1,128)}, u32[]{:S(2)}) copy-start(f32[1,1024]{1,0:T(1,128)} %scale_ref.1) | copy-start | bytes 12292
  5.6 13.4 %copy-start.6 = (s32[1,2,64]{2,1,0:T(2,128)S(1)}, s32[1,2,64]{2,1,0:T(2,128)}, u32[]{:S(2)}) copy-start(s32[1,2,64]{2,1,0:T(2,128)} %param.16) | copy-start | bytes 1540
  5.6 13.4 %copy-start.7 = (f32[4,4]{1,0:T(4,128)S(1)}, f32[4,4]{1,0:T(4,128)}, u32[]{:S(2)}) copy-start(f32[4,4]{1,0:T(4,128)} %constant.13.clone.table_ref) | copy-start | bytes 196
  6.6 6.6 %collective-permute-start.5 = (bf16[2,80,64]{2,1,0:T(8,128)(2,1)S(1)}, bf16[2,80,64]{2,1,0:T(8,128)(2,1)S(1)}, u32[]{:S(2)}, u32[]{:S(2)}) collective-permute-start(bf16[2,80,64]{2,1,0:T(8,128)(2,1)S(1)} %get-tuple-element.12), channel_id=1, source_target_pairs={{0,13},{1,12},{4,1},{5,0},{8,5},{9,4},{12,9},{13,8},{2,15},{3,14},... | collective-permute-start | bytes 61448 | tf_op jit(solution)/shard_map/interface/ppermute | solution.py:215
  9.5 4.5 %collective-permute-start.4 = (bf16[2,80,64]{2,1,0:T(8,128)(2,1)S(1)}, bf16[2,80,64]{2,1,0:T(8,128)(2,1)S(1)}, u32[]{:S(2)}, u32[]{:S(2)}) collective-permute-start(bf16[2,80,64]{2,1,0:T(8,128)(2,1)S(1)} %get-tuple-element.12), channel_id=1, source_target_pairs={{0,9},{1,8},{4,13},{5,12},{8,1},{9,0},{12,5},{13,4},{2,11},{3,10},... | collective-permute-start | bytes 61448 | tf_op jit(solution)/shard_map/interface/ppermute | solution.py:215
  9.5 9.5 %collective-permute-start = (bf16[2,160,64]{2,1,0:T(8,128)(2,1)S(1)}, bf16[2,160,64]{2,1,0:T(8,128)(2,1)S(1)}, u32[]{:S(2)}, u32[]{:S(2)}) collective-permute-start(bf16[2,160,64]{2,1,0:T(8,128)(2,1)S(1)} %get-tuple-element.10), channel_id=1, source_target_pairs={{0,4},{4,8},{8,12},{12,0},{1,5},{5,9},{9,13},{13,1},{2,6},{6,10},{... | collective-permute-start | bytes 122888 | tf_op jit(solution)/shard_map/halo/ppermute | solution.py:212
  11.0 7.9 %collective-permute-start.1 = (bf16[2,160,64]{2,1,0:T(8,128)(2,1)S(1)}, bf16[2,160,64]{2,1,0:T(8,128)(2,1)S(1)}, u32[]{:S(2)}, u32[]{:S(2)}) collective-permute-start(bf16[2,160,64]{2,1,0:T(8,128)(2,1)S(1)} %get-tuple-element.11), channel_id=1, source_target_pairs={{0,12},{4,0},{8,4},{12,8},{1,13},{5,1},{9,5},{13,9},{2,14},{6,2},{... | collective-permute-start | bytes 122888 | tf_op jit(solution)/shard_map/halo/ppermute | solution.py:213
  13.3 5.6 %collective-permute-start.3 = (bf16[2,80,64]{2,1,0:T(8,128)(2,1)S(1)}, bf16[2,80,64]{2,1,0:T(8,128)(2,1)S(1)}, u32[]{:S(2)}, u32[]{:S(2)}) collective-permute-start(bf16[2,80,64]{2,1,0:T(8,128)(2,1)S(1)} %get-tuple-element.12), channel_id=1, source_target_pairs={{0,5},{1,4},{4,9},{5,8},{8,13},{9,12},{12,1},{13,0},{2,7},{3,6},{6... | collective-permute-start | bytes 61448 | tf_op jit(solution)/shard_map/interface/ppermute | solution.py:215
  13.9 5.0 %collective-permute-start.2 = (bf16[2,80,64]{2,1,0:T(8,128)(2,1)S(1)}, bf16[2,80,64]{2,1,0:T(8,128)(2,1)S(1)}, u32[]{:S(2)}, u32[]{:S(2)}) collective-permute-start(bf16[2,80,64]{2,1,0:T(8,128)(2,1)S(1)} %get-tuple-element.12), channel_id=1, source_target_pairs={{0,1},{1,0},{4,5},{5,4},{8,9},{9,8},{12,13},{13,12},{2,3},{3,2},{6... | collective-permute-start | bytes 61448 | tf_op jit(solution)/shard_map/interface/ppermute | solution.py:215

commit v17 on v14

--- a/solution.py
+++ b/solution.py
@@ -142,9 +142,13 @@
                 at = n * len(moved) + k
                 value -= factor_ref[at : at + 1, cols] * part
             made[t, n] = value.astype(jnp.bfloat16)
-        copy = pltpu.make_async_copy(made.at[t], out_ref.at[:, :, cols], sems.at[t])
-        copy.start(priority=t % 2)
-        copies.append(copy)
+        for n in range(count):
+            for half in range(2):
+                rows = slice(half * dof // 2, (half + 1) * dof // 2)
+                copy = pltpu.make_async_copy(
+                    made.at[t, n, rows, :], out_ref.at[n, rows, cols], sems.at[t, n, half])
+                copy.start(priority=half)
+                copies.append(copy)
     for copy in copies:
         copy.wait()
 
@@ -231,7 +235,7 @@
             out_shape=jax.ShapeDtypeStruct((count, dof, total), bf16),
             in_specs=[vmem] * (2 + peers),
             out_specs=pl.BlockSpec(memory_space=pl.ANY),
-            scratch_shapes=[pltpu.VMEM((steps, count, dof, tile), bf16), pltpu.SemaphoreType.DMA((steps,))],
+            scratch_shapes=[pltpu.VMEM((steps, count, dof, tile), bf16), pltpu.SemaphoreType.DMA((steps, count, 2))],
             compiler_params=pltpu.CompilerParams(vmem_limit_bytes=VMEM_LIMIT),
             cost_estimate=pl.CostEstimate(flops=2 * count * total * dof * dof * (peers - 1),
                                           bytes_accessed=count * dof * total * 8, transcendentals=0),

time: 33.8 us -> 33.8 us (level)
  no operation moved by 1% of the time
where the time goes in v17:
time: 33.8 us; the launch traced here: 33.7 us
  Pallas kernels  13.2 us (39%)
  starting transfers between devices  12.4 us (37%)
  waiting for transfers between devices  4.67 us (14%)
  local copies, waits for them, and re-layouts  2.58 us (8%)
  between operations  0.79 us (2%)
    pallas_call x1, Pallas kernels, body(): pl.pallas_call(functools.partial(couple_kernel, shards, peers), grid=(ste...  10.4 us
    ppermute x4, starting transfers between devices, body(): lax.ppermute(cross, ('space', 'row'), [(i * 2 + r, (i + d) % shards * 2 +...  5.62 us
    ppermute x1, starting transfers between devices, body(): lax.ppermute(current, 'inst', [(i, (i + d) % peers) for i in range(peers)])  2.94 us
    unnamed x20, local copies, waits for them, and re-layouts  2.58 us
    ppermute x1, waiting for transfers between devices, body(): lax.ppermute(current, 'inst', [(i, (i + d) % peers) for i in range(peers)])  2.5 us
    ppermute x1, starting transfers between devices, body(): lax.ppermute(down, 'space', [(i, (i - 1) % shards) for i in range(shards)])  2.25 us
    ppermute x4, waiting for transfers between devices, body(): lax.ppermute(cross, ('space', 'row'), [(i * 2 + r, (i + d) % shards * 2 +...  2.16 us
    pallas_call x1, Pallas kernels, body(): pl.pallas_call(functools.partial(update_kernel, tile), out_shape=jax.Shap...  1.74 us
  transfers between devices with their start and end apart: 7, of which 3 were waited for; matrix products, arithmetic and copies ran while one was open for 4% of the time, Pallas kernels for 34%

profile of v17, /device:TPU:0, one launch (start us, length us, event | category | flops | bytes accessed | tf_op | source)
XLA Modules:
  0.0 33.7 jit_solution(17388102990216135353)
XLA Ops:
  0.0 2.9 %collective-permute-start.6 = (bf16[2,320,1024]{2,1,0:T(8,128)(2,1)}, bf16[2,320,1024]{2,1,0:T(8,128)(2,1)S(1)}, u32[]{:S(2)}, u32[]{:S(2)}) collective-permute-start(bf16[2,320,1024]{2,1,0:T(8,128)(2,1)} %bitcast.10), channel_id=1, source_target_pairs={{0,2},{2,0},{1,3},{3,1},{4,6},{6,4},{5,7},{7,5},{8,10},{10,8},{9,1... | collective-permute-start | bytes 3932168 | tf_op jit(solution)/shard_map/instances/ppermute | solution.py:178
  2.9 1.2 %copy.13.trace_ref = bf16[480,320]{1,0:T(8,128)(2,1)S(1)} copy(bf16[480,320]{0,1:T(8,128)(2,1)} %param.18) | data formatting | bytes 614400 | tf_op args[7]
  4.2 0.1 pad_add_fusion.place_ref
  4.2 0.0 copy-start
  4.2 1.3 %copy-done = bf16[1,2,320,1024]{3,2,1,0:T(8,128)(2,1)S(1)} copy-done((bf16[1,2,320,1024]{3,2,1,0:T(8,128)(2,1)S(1)}, bf16[1,2,320,1024]{3,2,1,0:T(8,128)(2,1)}, u32[]{:S(2)}) %copy-start) | copy-done | bytes 1310744
  5.6 0.0 copy-start.8
  5.6 0.0 copy-start.1
  5.6 0.0 copy-start.2
  5.6 0.0 copy-start.3
  5.6 0.0 copy-start.4
  5.6 0.0 copy-start.5
  5.6 0.0 copy-start.6
  5.6 0.0 copy-start.7
  5.6 1.0 %ends.1 = (bf16[2,160,64]{2,1,0:T(8,128)(2,1)S(1)}, bf16[2,160,64]{2,1,0:T(8,128)(2,1)S(1)}, bf16[2,80,64]{2,1,0:T(8,128)(2,1)S(1)}) custom-call(s32[3]{0:T(128)S(1)} %pad_add_fusion.place_ref, bf16[2,320,1024]{2,1,0:T(8,128)(2,1)S(1)} %bitcast.11, bf16[2,320,1024]{2,1,0:T(8,128)(2,1)S(1)} %bitcast.12, bf16[480,320]{1,0:T(8,128)(2,1)S(1)} %copy.13.trace_ref), custom_call_target="tpu_custom_call" | custom-call | flops 104857600 | bytes 1000000 | tf_op jit(solution)/shard_map/ends/ends/pallas_call | solution.py:182
  6.6 2.8 %collective-permute-start.5 = (bf16[2,80,64]{2,1,0:T(8,128)(2,1)S(1)}, bf16[2,80,64]{2,1,0:T(8,128)(2,1)S(1)}, u32[]{:S(2)}, u32[]{:S(2)}) collective-permute-start(bf16[2,80,64]{2,1,0:T(8,128)(2,1)S(1)} %get-tuple-element.12), channel_id=1, source_target_pairs={{0,13},{1,12},{4,1},{5,0},{8,5},{9,4},{12,9},{13,8},{2,15},{3,14},... | collective-permute-start | bytes 61448 | tf_op jit(solution)/shard_map/interface/ppermute | solution.py:205
  9.5 0.0 collective-permute-start.4
  9.5 1.6 %collective-permute-start = (bf16[2,160,64]{2,1,0:T(8,128)(2,1)S(1)}, bf16[2,160,64]{2,1,0:T(8,128)(2,1)S(1)}, u32[]{:S(2)}, u32[]{:S(2)}) collective-permute-start(bf16[2,160,64]{2,1,0:T(8,128)(2,1)S(1)} %get-tuple-element.10), channel_id=1, source_target_pairs={{0,4},{4,8},{8,12},{12,0},{1,5},{5,9},{9,13},{13,1},{2,6},{6,10},{... | collective-permute-start | bytes 122888 | tf_op jit(solution)/shard_map/halo/ppermute | solution.py:202
  11.0 2.2 %collective-permute-start.1 = (bf16[2,160,64]{2,1,0:T(8,128)(2,1)S(1)}, bf16[2,160,64]{2,1,0:T(8,128)(2,1)S(1)}, u32[]{:S(2)}, u32[]{:S(2)}) collective-permute-start(bf16[2,160,64]{2,1,0:T(8,128)(2,1)S(1)} %get-tuple-element.11), channel_id=1, source_target_pairs={{0,12},{4,0},{8,4},{12,8},{1,13},{5,1},{9,5},{13,9},{2,14},{6,2},{... | collective-permute-start | bytes 122888 | tf_op jit(solution)/shard_map/halo/ppermute | solution.py:203
  13.3 0.0 collective-permute-done.5.rest_3_
  13.3 0.0 collective-permute-start.3
  13.3 0.6 %collective-permute-done.4.rest_2_ = bf16[2,80,64]{2,1,0:T(8,128)(2,1)S(1)} collective-permute-done((bf16[2,80,64]{2,1,0:T(8,128)(2,1)S(1)}, bf16[2,80,64]{2,1,0:T(8,128)(2,1)S(1)}, u32[]{:S(2)}, u32[]{:S(2)}) %collective-permute-start.4) | collective-permute-done | bytes 20512 | tf_op jit(solution)/shard_map/interface/ppermute | solution.py:205
  13.9 2.8 %collective-permute-start.2 = (bf16[2,80,64]{2,1,0:T(8,128)(2,1)S(1)}, bf16[2,80,64]{2,1,0:T(8,128)(2,1)S(1)}, u32[]{:S(2)}, u32[]{:S(2)}) collective-permute-start(bf16[2,80,64]{2,1,0:T(8,128)(2,1)S(1)} %get-tuple-element.12), channel_id=1, source_target_pairs={{0,1},{1,0},{4,5},{5,4},{8,9},{9,8},{12,13},{13,12},{2,3},{3,2},{6... | collective-permute-start | bytes 61448 | tf_op jit(solution)/shard_map/interface/ppermute | solution.py:205
  17.4 0.0 copy-done.8
  17.4 1.5 %collective-permute-done.3.rest_1_ = bf16[2,80,64]{2,1,0:T(8,128)(2,1)S(1)} collective-permute-done((bf16[2,80,64]{2,1,0:T(8,128)(2,1)S(1)}, bf16[2,80,64]{2,1,0:T(8,128)(2,1)S(1)}, u32[]{:S(2)}, u32[]{:S(2)}) %collective-permute-start.3) | collective-permute-done | bytes 20512 | tf_op jit(solution)/shard_map/interface/ppermute | solution.py:205
  18.9 0.0 collective-permute-done.2.rest_0_
  18.9 0.0 collective-permute-done.low_ref
  18.9 0.0 collective-permute-done.1.high_ref
  18.9 0.0 copy-done.1
  18.9 0.0 copy-done.2
  19.0 0.0 copy-done.3
  19.0 0.0 copy-done.4
  19.0 0.0 copy-done.5
  19.0 0.0 copy-done.6
  19.0 0.0 copy-done.7
  19.0 10.4 %couple.1 = (f32[2,320,1024]{2,1,0:T(8,128)S(1)}, f32[4,1024]{1,0:T(4,128)S(1)}) custom-call(s32[3]{0:T(128)S(1)} %pad_add_fusion.place_ref, f32[1]{0:T(128)S(6)} %copy.17.freq_ref, f32[4,4]{1,0:T(4,128)S(1)} %copy-done.7, s32[6,1024]{1,0:T(8,128)S(1)} %bitcast.15, s32[2,64]{1,0:T(2,128)S(1)} %bitcast.17, bf16[2,320,1024]{2,1,0:T(8,128)(2,1)S(1)} %bitcast.13, ...), custom_call_target="tpu_custom_call" | custom-call | flops 3690987520 | bytes 6553600 | tf_op jit(solution)/shard_map/couple/couple/pallas_call | solution.py:213
  29.4 2.5 %collective-permute-done.6.rest_0_ = bf16[2,320,1024]{2,1,0:T(8,128)(2,1)S(1)} collective-permute-done((bf16[2,320,1024]{2,1,0:T(8,128)(2,1)}, bf16[2,320,1024]{2,1,0:T(8,128)(2,1)S(1)}, u32[]{:S(2)}, u32[]{:S(2)}) %collective-permute-start.6) | collective-permute-done | bytes 1310752 | tf_op jit(solution)/shard_map/instances/ppermute | solution.py:178
  31.9 1.7 %update.1 = bf16[2,320,1024]{2,1,0:T(8,128)(2,1)} custom-call(f32[2,320,1024]{2,1,0:T(8,128)S(1)} %get-tuple-element.13.ready_ref, f32[4,1024]{1,0:T(4,128)S(1)} %get-tuple-element.14.factor_ref, bf16[320,320]{1,0:T(8,128)(2,1)S(1)} %copy-done.1, bf16[2,320,1024]{2,1,0:T(8,128)(2,1)S(1)} %collective-permute-done.6.rest_0_), custom_call_target="tpu_custom_call" | custom-call | flops 419430400 | bytes 5242880 | tf_op jit(solution)/shard_map/update/update/pallas_call | solution.py:233
  (1 shorter events, 0.0 us)
Async XLA Ops:
  0.0 31.9 %collective-permute-start.6 = (bf16[2,320,1024]{2,1,0:T(8,128)(2,1)}, bf16[2,320,1024]{2,1,0:T(8,128)(2,1)S(1)}, u32[]{:S(2)}, u32[]{:S(2)}) collective-permute-start(bf16[2,320,1024]{2,1,0:T(8,128)(2,1)} %bitcast.10), channel_id=1, source_target_pairs={{0,2},{2,0},{1,3},{3,1},{4,6},{6,4},{5,7},{7,5},{8,10},{10,8},{9,1... | collective-permute-start | bytes 3932168 | tf_op jit(solution)/shard_map/instances/ppermute | solution.py:178
  4.2 1.3 %copy-start = (bf16[1,2,320,1024]{3,2,1,0:T(8,128)(2,1)S(1)}, bf16[1,2,320,1024]{3,2,1,0:T(8,128)(2,1)}, u32[]{:S(2)}) copy-start(bf16[1,2,320,1024]{3,2,1,0:T(8,128)(2,1)} %param.11) | copy-start | bytes 3932164
  5.6 11.8 %copy-start.8 = (s32[1,6,1024]{2,0,1:T(1,128)S(1)}, s32[1,6,1024]{2,0,1:T(1,128)}, u32[]{:S(2)}) copy-start(s32[1,6,1024]{2,0,1:T(1,128)} %param.15) | copy-start | bytes 73732
  5.6 13.4 %copy-start.1 = (bf16[320,320]{1,0:T(8,128)(2,1)S(1)}, bf16[320,320]{1,0:T(8,128)(2,1)}, u32[]{:S(2)}) copy-start(bf16[320,320]{1,0:T(8,128)(2,1)} %inverse_ref.3) | copy-start | bytes 614404
  5.6 13.4 %copy-start.2 = (bf16[1,2,320,1024]{3,2,1,0:T(8,128)(2,1)S(1)}, bf16[1,2,320,1024]{3,2,1,0:T(8,128)(2,1)}, u32[]{:S(2)}) copy-start(bf16[1,2,320,1024]{3,2,1,0:T(8,128)(2,1)} %param.12) | copy-start | bytes 3932164
  5.6 13.4 %copy-start.3 = (bf16[320,480]{1,0:T(8,128)(2,1)S(1)}, bf16[320,480]{1,0:T(8,128)(2,1)}, u32[]{:S(2)}) copy-start(bf16[320,480]{1,0:T(8,128)(2,1)} %lift_ref.1) | copy-start | bytes 921604
  5.6 13.4 %copy-start.4 = (bf16[320,320]{1,0:T(8,128)(2,1)S(1)}, bf16[320,320]{1,0:T(8,128)(2,1)}, u32[]{:S(2)}) copy-start(bf16[320,320]{1,0:T(8,128)(2,1)} %volume_ref.1) | copy-start | bytes 614404
  5.6 13.4 %copy-start.5 = (f32[1,1024]{1,0:T(1,128)S(1)}, f32[1,1024]{1,0:T(1,128)}, u32[]{:S(2)}) copy-start(f32[1,1024]{1,0:T(1,128)} %scale_ref.1) | copy-start | bytes 12292
  5.6 13.4 %copy-start.6 = (s32[1,2,64]{2,1,0:T(2,128)S(1)}, s32[1,2,64]{2,1,0:T(2,128)}, u32[]{:S(2)}) copy-start(s32[1,2,64]{2,1,0:T(2,128)} %param.16) | copy-start | bytes 1540
  5.6 13.4 %copy-start.7 = (f32[4,4]{1,0:T(4,128)S(1)}, f32[4,4]{1,0:T(4,128)}, u32[]{:S(2)}) copy-start(f32[4,4]{1,0:T(4,128)} %constant.13.clone.table_ref) | copy-start | bytes 196
  6.6 6.6 %collective-permute-start.5 = (bf16[2,80,64]{2,1,0:T(8,128)(2,1)S(1)}, bf16[2,80,64]{2,1,0:T(8,128)(2,1)S(1)}, u32[]{:S(2)}, u32[]{:S(2)}) collective-permute-start(bf16[2,80,64]{2,1,0:T(8,128)(2,1)S(1)} %get-tuple-element.12), channel_id=1, source_target_pairs={{0,13},{1,12},{4,1},{5,0},{8,5},{9,4},{12,9},{13,8},{2,15},{3,14},... | collective-permute-start | bytes 61448 | tf_op jit(solution)/shard_map/interface/ppermute | solution.py:205
  9.5 4.5 %collective-permute-start.4 = (bf16[2,80,64]{2,1,0:T(8,128)(2,1)S(1)}, bf16[2,80,64]{2,1,0:T(8,128)(2,1)S(1)}, u32[]{:S(2)}, u32[]{:S(2)}) collective-permute-start(bf16[2,80,64]{2,1,0:T(8,128)(2,1)S(1)} %get-tuple-element.12), channel_id=1, source_target_pairs={{0,9},{1,8},{4,13},{5,12},{8,1},{9,0},{12,5},{13,4},{2,11},{3,10},... | collective-permute-start | bytes 61448 | tf_op jit(solution)/shard_map/interface/ppermute | solution.py:205
  9.5 9.5 %collective-permute-start = (bf16[2,160,64]{2,1,0:T(8,128)(2,1)S(1)}, bf16[2,160,64]{2,1,0:T(8,128)(2,1)S(1)}, u32[]{:S(2)}, u32[]{:S(2)}) collective-permute-start(bf16[2,160,64]{2,1,0:T(8,128)(2,1)S(1)} %get-tuple-element.10), channel_id=1, source_target_pairs={{0,4},{4,8},{8,12},{12,0},{1,5},{5,9},{9,13},{13,1},{2,6},{6,10},{... | collective-permute-start | bytes 122888 | tf_op jit(solution)/shard_map/halo/ppermute | solution.py:202
  11.0 7.9 %collective-permute-start.1 = (bf16[2,160,64]{2,1,0:T(8,128)(2,1)S(1)}, bf16[2,160,64]{2,1,0:T(8,128)(2,1)S(1)}, u32[]{:S(2)}, u32[]{:S(2)}) collective-permute-start(bf16[2,160,64]{2,1,0:T(8,128)(2,1)S(1)} %get-tuple-element.11), channel_id=1, source_target_pairs={{0,12},{4,0},{8,4},{12,8},{1,13},{5,1},{9,5},{13,9},{2,14},{6,2},{... | collective-permute-start | bytes 122888 | tf_op jit(solution)/shard_map/halo/ppermute | solution.py:203
  13.3 5.6 %collective-permute-start.3 = (bf16[2,80,64]{2,1,0:T(8,128)(2,1)S(1)}, bf16[2,80,64]{2,1,0:T(8,128)(2,1)S(1)}, u32[]{:S(2)}, u32[]{:S(2)}) collective-permute-start(bf16[2,80,64]{2,1,0:T(8,128)(2,1)S(1)} %get-tuple-element.12), channel_id=1, source_target_pairs={{0,5},{1,4},{4,9},{5,8},{8,13},{9,12},{12,1},{13,0},{2,7},{3,6},{6... | collective-permute-start | bytes 61448 | tf_op jit(solution)/shard_map/interface/ppermute | solution.py:205
  13.9 5.0 %collective-permute-start.2 = (bf16[2,80,64]{2,1,0:T(8,128)(2,1)S(1)}, bf16[2,80,64]{2,1,0:T(8,128)(2,1)S(1)}, u32[]{:S(2)}, u32[]{:S(2)}) collective-permute-start(bf16[2,80,64]{2,1,0:T(8,128)(2,1)S(1)} %get-tuple-element.12), channel_id=1, source_target_pairs={{0,1},{1,0},{4,5},{5,4},{8,9},{9,8},{12,13},{13,12},{2,3},{3,2},{6... | collective-permute-start | bytes 61448 | tf_op jit(solution)/shard_map/interface/ppermute | solution.py:205

commit v18 on v4

--- a/solution.py
+++ b/solution.py
@@ -132,10 +132,13 @@
 def update_kernel(tile, ready_ref, factor_ref, inverse_ref, *rest):
     others, (out_ref, made, sems) = rest[:-3], rest[-3:]
     count, dof, total = ready_ref.shape
+    depths = [(low, min(low + tile, dof)) for low in range(0, dof, tile)]
     copies = []
     for t in range(total // tile):
         cols = slice(t * tile, (t + 1) * tile)
-        moved = [dot(inverse_ref[...], other[m, :, cols]) for other in others for m in range(count)]
+        moved = [[dot(inverse_ref[:, low:high], other[m, low:high, cols]) for low, high in depths]
+                 for other in others for m in range(count)]
+        moved = [functools.reduce(jnp.add, parts) for parts in moved]
         for n in range(count):
             value = ready_ref[n, :, cols]
             for k, part in enumerate(moved):

time: 33.8 us -> 33.7 us (level)
  no operation moved by 1% of the time
where the time goes in v18:
time: 33.7 us; the launch traced here: 33.5 us
  Pallas kernels  13 us (39%)
  starting transfers between devices  12.4 us (37%)
  waiting for transfers between devices  4.67 us (14%)
  local copies, waits for them, and re-layouts  2.58 us (8%)
  between operations  0.79 us (2%)
    pallas_call x1, Pallas kernels, body(): pl.pallas_call(functools.partial(couple_kernel, shards, peers), grid=(ste...  10.4 us
    ppermute x4, starting transfers between devices, body(): lax.ppermute(cross, ('space', 'row'), [(i * 2 + r, (i + d) % shards * 2 +...  5.62 us
    ppermute x1, starting transfers between devices, body(): lax.ppermute(current, 'inst', [(i, (i + d) % peers) for i in range(peers)])  2.94 us
    unnamed x20, local copies, waits for them, and re-layouts  2.58 us
    ppermute x1, waiting for transfers between devices, body(): lax.ppermute(current, 'inst', [(i, (i + d) % peers) for i in range(peers)])  2.5 us
    ppermute x1, starting transfers between devices, body(): lax.ppermute(down, 'space', [(i, (i - 1) % shards) for i in range(shards)])  2.25 us
    ppermute x4, waiting for transfers between devices, body(): lax.ppermute(cross, ('space', 'row'), [(i * 2 + r, (i + d) % shards * 2 +...  2.16 us
    pallas_call x1, Pallas kernels, body(): pl.pallas_call(functools.partial(update_kernel, tile), out_shape=jax.Shap...  1.61 us
  transfers between devices with their start and end apart: 7, of which 3 were waited for; matrix products, arithmetic and copies ran while one was open for 4% of the time, Pallas kernels for 34%

profile of v18, /device:TPU:0, one launch (start us, length us, event | category | flops | bytes accessed | tf_op | source)
XLA Modules:
  0.0 33.5 jit_solution(8312357954844662571)
XLA Ops:
  0.0 2.9 %collective-permute-start.6 = (bf16[2,320,1024]{2,1,0:T(8,128)(2,1)}, bf16[2,320,1024]{2,1,0:T(8,128)(2,1)S(1)}, u32[]{:S(2)}, u32[]{:S(2)}) collective-permute-start(bf16[2,320,1024]{2,1,0:T(8,128)(2,1)} %bitcast.10), channel_id=1, source_target_pairs={{0,2},{2,0},{1,3},{3,1},{4,6},{6,4},{5,7},{7,5},{8,10},{10,8},{9,1... | collective-permute-start | bytes 3932168 | tf_op jit(solution)/shard_map/instances/ppermute | solution.py:177
  2.9 1.2 %copy.13.trace_ref = bf16[480,320]{1,0:T(8,128)(2,1)S(1)} copy(bf16[480,320]{0,1:T(8,128)(2,1)} %param.18) | data formatting | bytes 614400 | tf_op args[7]
  4.2 0.1 pad_add_fusion.place_ref
  4.2 0.0 copy-start
  4.2 1.3 %copy-done = bf16[1,2,320,1024]{3,2,1,0:T(8,128)(2,1)S(1)} copy-done((bf16[1,2,320,1024]{3,2,1,0:T(8,128)(2,1)S(1)}, bf16[1,2,320,1024]{3,2,1,0:T(8,128)(2,1)}, u32[]{:S(2)}) %copy-start) | copy-done | bytes 1310744
  5.6 0.0 copy-start.8
  5.6 0.0 copy-start.1
  5.6 0.0 copy-start.2
  5.6 0.0 copy-start.3
  5.6 0.0 copy-start.4
  5.6 0.0 copy-start.5
  5.6 0.0 copy-start.6
  5.6 0.0 copy-start.7
  5.6 1.0 %ends.1 = (bf16[2,160,64]{2,1,0:T(8,128)(2,1)S(1)}, bf16[2,160,64]{2,1,0:T(8,128)(2,1)S(1)}, bf16[2,80,64]{2,1,0:T(8,128)(2,1)S(1)}) custom-call(s32[3]{0:T(128)S(1)} %pad_add_fusion.place_ref, bf16[2,320,1024]{2,1,0:T(8,128)(2,1)S(1)} %bitcast.11, bf16[2,320,1024]{2,1,0:T(8,128)(2,1)S(1)} %bitcast.12, bf16[480,320]{1,0:T(8,128)(2,1)S(1)} %copy.13.trace_ref), custom_call_target="tpu_custom_call" | custom-call | flops 104857600 | bytes 1000000 | tf_op jit(solution)/shard_map/ends/ends/pallas_call | solution.py:181
  6.6 2.8 %collective-permute-start.5 = (bf16[2,80,64]{2,1,0:T(8,128)(2,1)S(1)}, bf16[2,80,64]{2,1,0:T(8,128)(2,1)S(1)}, u32[]{:S(2)}, u32[]{:S(2)}) collective-permute-start(bf16[2,80,64]{2,1,0:T(8,128)(2,1)S(1)} %get-tuple-element.12), channel_id=1, source_target_pairs={{0,13},{1,12},{4,1},{5,0},{8,5},{9,4},{12,9},{13,8},{2,15},{3,14},... | collective-permute-start | bytes 61448 | tf_op jit(solution)/shard_map/interface/ppermute | solution.py:204
  9.5 0.0 collective-permute-start.4
  9.5 1.6 %collective-permute-start = (bf16[2,160,64]{2,1,0:T(8,128)(2,1)S(1)}, bf16[2,160,64]{2,1,0:T(8,128)(2,1)S(1)}, u32[]{:S(2)}, u32[]{:S(2)}) collective-permute-start(bf16[2,160,64]{2,1,0:T(8,128)(2,1)S(1)} %get-tuple-element.10), channel_id=1, source_target_pairs={{0,4},{4,8},{8,12},{12,0},{1,5},{5,9},{9,13},{13,1},{2,6},{6,10},{... | collective-permute-start | bytes 122888 | tf_op jit(solution)/shard_map/halo/ppermute | solution.py:201
  11.0 2.2 %collective-permute-start.1 = (bf16[2,160,64]{2,1,0:T(8,128)(2,1)S(1)}, bf16[2,160,64]{2,1,0:T(8,128)(2,1)S(1)}, u32[]{:S(2)}, u32[]{:S(2)}) collective-permute-start(bf16[2,160,64]{2,1,0:T(8,128)(2,1)S(1)} %get-tuple-element.11), channel_id=1, source_target_pairs={{0,12},{4,0},{8,4},{12,8},{1,13},{5,1},{9,5},{13,9},{2,14},{6,2},{... | collective-permute-start | bytes 122888 | tf_op jit(solution)/shard_map/halo/ppermute | solution.py:202
  13.3 0.0 collective-permute-done.5.rest_3_
  13.3 0.0 collective-permute-start.3
  13.3 0.6 %collective-permute-done.4.rest_2_ = bf16[2,80,64]{2,1,0:T(8,128)(2,1)S(1)} collective-permute-done((bf16[2,80,64]{2,1,0:T(8,128)(2,1)S(1)}, bf16[2,80,64]{2,1,0:T(8,128)(2,1)S(1)}, u32[]{:S(2)}, u32[]{:S(2)}) %collective-permute-start.4) | collective-permute-done | bytes 20512 | tf_op jit(solution)/shard_map/interface/ppermute | solution.py:204
  13.9 2.8 %collective-permute-start.2 = (bf16[2,80,64]{2,1,0:T(8,128)(2,1)S(1)}, bf16[2,80,64]{2,1,0:T(8,128)(2,1)S(1)}, u32[]{:S(2)}, u32[]{:S(2)}) collective-permute-start(bf16[2,80,64]{2,1,0:T(8,128)(2,1)S(1)} %get-tuple-element.12), channel_id=1, source_target_pairs={{0,1},{1,0},{4,5},{5,4},{8,9},{9,8},{12,13},{13,12},{2,3},{3,2},{6... | collective-permute-start | bytes 61448 | tf_op jit(solution)/shard_map/interface/ppermute | solution.py:204
  17.4 0.0 copy-done.8
  17.4 1.5 %collective-permute-done.3.rest_1_ = bf16[2,80,64]{2,1,0:T(8,128)(2,1)S(1)} collective-permute-done((bf16[2,80,64]{2,1,0:T(8,128)(2,1)S(1)}, bf16[2,80,64]{2,1,0:T(8,128)(2,1)S(1)}, u32[]{:S(2)}, u32[]{:S(2)}) %collective-permute-start.3) | collective-permute-done | bytes 20512 | tf_op jit(solution)/shard_map/interface/ppermute | solution.py:204
  18.9 0.0 collective-permute-done.2.rest_0_
  18.9 0.0 collective-permute-done.low_ref
  18.9 0.0 collective-permute-done.1.high_ref
  18.9 0.0 copy-done.1
  18.9 0.0 copy-done.2
  19.0 0.0 copy-done.3
  19.0 0.0 copy-done.4
  19.0 0.0 copy-done.5
  19.0 0.0 copy-done.6
  19.0 0.0 copy-done.7
  19.0 10.4 %couple.1 = (f32[2,320,1024]{2,1,0:T(8,128)S(1)}, f32[4,1024]{1,0:T(4,128)S(1)}) custom-call(s32[3]{0:T(128)S(1)} %pad_add_fusion.place_ref, f32[1]{0:T(128)S(6)} %copy.17.freq_ref, f32[4,4]{1,0:T(4,128)S(1)} %copy-done.7, s32[6,1024]{1,0:T(8,128)S(1)} %bitcast.15, s32[2,64]{1,0:T(2,128)S(1)} %bitcast.17, bf16[2,320,1024]{2,1,0:T(8,128)(2,1)S(1)} %bitcast.13, ...), custom_call_target="tpu_custom_call" | custom-call | flops 3690987520 | bytes 6553600 | tf_op jit(solution)/shard_map/couple/couple/pallas_call | solution.py:212
  29.4 2.5 %collective-permute-done.6.rest_0_ = bf16[2,320,1024]{2,1,0:T(8,128)(2,1)S(1)} collective-permute-done((bf16[2,320,1024]{2,1,0:T(8,128)(2,1)}, bf16[2,320,1024]{2,1,0:T(8,128)(2,1)S(1)}, u32[]{:S(2)}, u32[]{:S(2)}) %collective-permute-start.6) | collective-permute-done | bytes 1310752 | tf_op jit(solution)/shard_map/instances/ppermute | solution.py:177
  31.9 1.6 %update.1 = bf16[2,320,1024]{2,1,0:T(8,128)(2,1)} custom-call(f32[2,320,1024]{2,1,0:T(8,128)S(1)} %get-tuple-element.13.ready_ref, f32[4,1024]{1,0:T(4,128)S(1)} %get-tuple-element.14.factor_ref, bf16[320,320]{1,0:T(8,128)(2,1)S(1)} %copy-done.1, bf16[2,320,1024]{2,1,0:T(8,128)(2,1)S(1)} %collective-permute-done.6.rest_0_), custom_call_target="tpu_custom_call" | custom-call | flops 419430400 | bytes 5242880 | tf_op jit(solution)/shard_map/update/update/pallas_call | solution.py:232
  (1 shorter events, 0.0 us)
Async XLA Ops:
  0.0 31.9 %collective-permute-start.6 = (bf16[2,320,1024]{2,1,0:T(8,128)(2,1)}, bf16[2,320,1024]{2,1,0:T(8,128)(2,1)S(1)}, u32[]{:S(2)}, u32[]{:S(2)}) collective-permute-start(bf16[2,320,1024]{2,1,0:T(8,128)(2,1)} %bitcast.10), channel_id=1, source_target_pairs={{0,2},{2,0},{1,3},{3,1},{4,6},{6,4},{5,7},{7,5},{8,10},{10,8},{9,1... | collective-permute-start | bytes 3932168 | tf_op jit(solution)/shard_map/instances/ppermute | solution.py:177
  4.2 1.3 %copy-start = (bf16[1,2,320,1024]{3,2,1,0:T(8,128)(2,1)S(1)}, bf16[1,2,320,1024]{3,2,1,0:T(8,128)(2,1)}, u32[]{:S(2)}) copy-start(bf16[1,2,320,1024]{3,2,1,0:T(8,128)(2,1)} %param.11) | copy-start | bytes 3932164
  5.6 11.8 %copy-start.8 = (s32[1,6,1024]{2,0,1:T(1,128)S(1)}, s32[1,6,1024]{2,0,1:T(1,128)}, u32[]{:S(2)}) copy-start(s32[1,6,1024]{2,0,1:T(1,128)} %param.15) | copy-start | bytes 73732
  5.6 13.4 %copy-start.1 = (bf16[320,320]{1,0:T(8,128)(2,1)S(1)}, bf16[320,320]{1,0:T(8,128)(2,1)}, u32[]{:S(2)}) copy-start(bf16[320,320]{1,0:T(8,128)(2,1)} %inverse_ref.3) | copy-start | bytes 614404
  5.6 13.4 %copy-start.2 = (bf16[1,2,320,1024]{3,2,1,0:T(8,128)(2,1)S(1)}, bf16[1,2,320,1024]{3,2,1,0:T(8,128)(2,1)}, u32[]{:S(2)}) copy-start(bf16[1,2,320,1024]{3,2,1,0:T(8,128)(2,1)} %param.12) | copy-start | bytes 3932164
  5.6 13.4 %copy-start.3 = (bf16[320,480]{1,0:T(8,128)(2,1)S(1)}, bf16[320,480]{1,0:T(8,128)(2,1)}, u32[]{:S(2)}) copy-start(bf16[320,480]{1,0:T(8,128)(2,1)} %lift_ref.1) | copy-start | bytes 921604
  5.6 13.4 %copy-start.4 = (bf16[320,320]{1,0:T(8,128)(2,1)S(1)}, bf16[320,320]{1,0:T(8,128)(2,1)}, u32[]{:S(2)}) copy-start(bf16[320,320]{1,0:T(8,128)(2,1)} %volume_ref.1) | copy-start | bytes 614404
  5.6 13.4 %copy-start.5 = (f32[1,1024]{1,0:T(1,128)S(1)}, f32[1,1024]{1,0:T(1,128)}, u32[]{:S(2)}) copy-start(f32[1,1024]{1,0:T(1,128)} %scale_ref.1) | copy-start | bytes 12292
  5.6 13.4 %copy-start.6 = (s32[1,2,64]{2,1,0:T(2,128)S(1)}, s32[1,2,64]{2,1,0:T(2,128)}, u32[]{:S(2)}) copy-start(s32[1,2,64]{2,1,0:T(2,128)} %param.16) | copy-start | bytes 1540
  5.6 13.4 %copy-start.7 = (f32[4,4]{1,0:T(4,128)S(1)}, f32[4,4]{1,0:T(4,128)}, u32[]{:S(2)}) copy-start(f32[4,4]{1,0:T(4,128)} %constant.13.clone.table_ref) | copy-start | bytes 196
  6.6 6.6 %collective-permute-start.5 = (bf16[2,80,64]{2,1,0:T(8,128)(2,1)S(1)}, bf16[2,80,64]{2,1,0:T(8,128)(2,1)S(1)}, u32[]{:S(2)}, u32[]{:S(2)}) collective-permute-start(bf16[2,80,64]{2,1,0:T(8,128)(2,1)S(1)} %get-tuple-element.12), channel_id=1, source_target_pairs={{0,13},{1,12},{4,1},{5,0},{8,5},{9,4},{12,9},{13,8},{2,15},{3,14},... | collective-permute-start | bytes 61448 | tf_op jit(solution)/shard_map/interface/ppermute | solution.py:204
  9.5 4.5 %collective-permute-start.4 = (bf16[2,80,64]{2,1,0:T(8,128)(2,1)S(1)}, bf16[2,80,64]{2,1,0:T(8,128)(2,1)S(1)}, u32[]{:S(2)}, u32[]{:S(2)}) collective-permute-start(bf16[2,80,64]{2,1,0:T(8,128)(2,1)S(1)} %get-tuple-element.12), channel_id=1, source_target_pairs={{0,9},{1,8},{4,13},{5,12},{8,1},{9,0},{12,5},{13,4},{2,11},{3,10},... | collective-permute-start | bytes 61448 | tf_op jit(solution)/shard_map/interface/ppermute | solution.py:204
  9.5 9.5 %collective-permute-start = (bf16[2,160,64]{2,1,0:T(8,128)(2,1)S(1)}, bf16[2,160,64]{2,1,0:T(8,128)(2,1)S(1)}, u32[]{:S(2)}, u32[]{:S(2)}) collective-permute-start(bf16[2,160,64]{2,1,0:T(8,128)(2,1)S(1)} %get-tuple-element.10), channel_id=1, source_target_pairs={{0,4},{4,8},{8,12},{12,0},{1,5},{5,9},{9,13},{13,1},{2,6},{6,10},{... | collective-permute-start | bytes 122888 | tf_op jit(solution)/shard_map/halo/ppermute | solution.py:201
  11.0 7.9 %collective-permute-start.1 = (bf16[2,160,64]{2,1,0:T(8,128)(2,1)S(1)}, bf16[2,160,64]{2,1,0:T(8,128)(2,1)S(1)}, u32[]{:S(2)}, u32[]{:S(2)}) collective-permute-start(bf16[2,160,64]{2,1,0:T(8,128)(2,1)S(1)} %get-tuple-element.11), channel_id=1, source_target_pairs={{0,12},{4,0},{8,4},{12,8},{1,13},{5,1},{9,5},{13,9},{2,14},{6,2},{... | collective-permute-start | bytes 122888 | tf_op jit(solution)/shard_map/halo/ppermute | solution.py:202
  13.3 5.6 %collective-permute-start.3 = (bf16[2,80,64]{2,1,0:T(8,128)(2,1)S(1)}, bf16[2,80,64]{2,1,0:T(8,128)(2,1)S(1)}, u32[]{:S(2)}, u32[]{:S(2)}) collective-permute-start(bf16[2,80,64]{2,1,0:T(8,128)(2,1)S(1)} %get-tuple-element.12), channel_id=1, source_target_pairs={{0,5},{1,4},{4,9},{5,8},{8,13},{9,12},{12,1},{13,0},{2,7},{3,6},{6... | collective-permute-start | bytes 61448 | tf_op jit(solution)/shard_map/interface/ppermute | solution.py:204
  13.9 5.0 %collective-permute-start.2 = (bf16[2,80,64]{2,1,0:T(8,128)(2,1)S(1)}, bf16[2,80,64]{2,1,0:T(8,128)(2,1)S(1)}, u32[]{:S(2)}, u32[]{:S(2)}) collective-permute-start(bf16[2,80,64]{2,1,0:T(8,128)(2,1)S(1)} %get-tuple-element.12), channel_id=1, source_target_pairs={{0,1},{1,0},{4,5},{5,4},{8,9},{9,8},{12,13},{13,12},{2,3},{3,2},{6... | collective-permute-start | bytes 61448 | tf_op jit(solution)/shard_map/interface/ppermute | solution.py:204

commit v19 on v12

--- a/solution.py
+++ b/solution.py
@@ -12,7 +12,7 @@
 OPPOSITE = (1, 0, 3, 2, 5, 4)
 LANES = 128
 VMEM_LIMIT = 40 * 1024 * 1024
-CUT_LIMIT = 56 * 1024 * 1024
+CUT_LIMIT = 8 * 1024 * 1024
 COUPLE_FLOPS = 7_500_000_000
 
 
@@ -35,7 +35,7 @@
     return jnp.dot(left, right, preferred_element_type=jnp.float32)
 
 
-def cut_kernel(bounds, head_ref, all_ref, *rest):
+def cut_kernel(bounds, before_ref, all_ref, *rest):
     out_refs, sems = rest[:-1], rest[-1]
     copies = []
     for k, (first, last) in enumerate(bounds):
@@ -206,17 +206,27 @@
     with jax.named_scope("instances"):
         tile = 256
         bounds = [(0, LANES), (LANES, total - tile), (total - tile, total)]
-        head = current[:, :, :LANES]
+        vmem = pl.BlockSpec(memory_space=pltpu.VMEM)
+        (head,) = pl.pallas_call(
+            functools.partial(cut_kernel, bounds[:1], None),
+            out_shape=(jax.ShapeDtypeStruct((count, dof, LANES), bf16),),
+            in_specs=[pl.BlockSpec(memory_space=pltpu.HBM)],
+            out_specs=(vmem,),
+            scratch_shapes=[pltpu.SemaphoreType.DMA((1,))],
+            compiler_params=pltpu.CompilerParams(vmem_limit_bytes=CUT_LIMIT),
+            cost_estimate=pl.CostEstimate(flops=0, bytes_accessed=0, transcendentals=0),
+            name="head",
+        )(pltpu.with_memory_space_constraint(current, pltpu.HBM))
         chunks = [head] + list(pl.pallas_call(
             functools.partial(cut_kernel, bounds[1:]),
             out_shape=tuple(jax.ShapeDtypeStruct((count, dof, last - first), bf16) for first, last in bounds[1:]),
-            in_specs=[pl.BlockSpec(memory_space=pl.ANY)] * 2,
-            out_specs=tuple([pl.BlockSpec(memory_space=pl.ANY)] * (len(bounds) - 1)),
+            in_specs=[pl.BlockSpec(memory_space=pl.ANY), pl.BlockSpec(memory_space=pltpu.HBM)],
+            out_specs=tuple([vmem] * (len(bounds) - 1)),
             scratch_shapes=[pltpu.SemaphoreType.DMA((len(bounds) - 1,))],
             compiler_params=pltpu.CompilerParams(vmem_limit_bytes=CUT_LIMIT),
             cost_estimate=pl.CostEstimate(flops=0, bytes_accessed=0, transcendentals=0),
             name="cut",
-        )(head, current))
+        )(head, pltpu.with_memory_space_constraint(current, pltpu.HBM)))
         arriving = [[lax.ppermute(chunk, "inst", [(i, (i + d) % peers) for i in range(peers)])
                      for d in range(1, peers)] for chunk in chunks]
 
@@ -269,7 +279,6 @@
         )(place, frequency, table, neighbours, partner_rows, current, current, forcing_local, metric_scale,
           trace_matrix, lift_matrix, volume_matrix, block_inverse, low, high, *pieces, *arriving[0])
 
-    vmem = pl.BlockSpec(memory_space=pltpu.VMEM)
     with jax.named_scope("update"):
         result = None
         for base, mine, others in ((0, bounds[1:2], arriving[1]), (bounds[2][0], bounds[2:], arriving[2])):

time: 70.8 us -> 37.1 us (0.52)
  Pallas kernels: 50 us -> 17.6 us
  local copies, waits for them, and re-layouts: 3.31 us -> 2.09 us
    pallas_call x1, Pallas kernels: 35.9 us -> 2.12 us  [body(): pl.pallas_call(functools.partial(cut_kernel, bounds[1:]), out_shape=tuple...]
    slice x1 -> x0, local copies, waits for them, and re-layouts: 1.03 us -> none  [body(): head = current[:, :, :LANES]]
    pallas_call x0 -> x1, Pallas kernels: none -> 0.92 us  [body(): pl.pallas_call(functools.partial(cut_kernel, bounds[:1], None), out_shape...]
    unnamed x26 -> x24, local copies, waits for them, and re-layouts: 2.27 us -> 2.09 us
  transfers between devices with their start and end apart: 9 -> 9, of which waited for: 4 -> 4; matrix products, arithmetic and copies ran while one was open for 2% -> 4% of each run, Pallas kernels for 69% -> 42%
where the time goes in v19:
time: 37.1 us; the launch traced here: 36.9 us
  Pallas kernels  17.6 us (47%)
  starting transfers between devices  13.5 us (36%)
  waiting for transfers between devices  2.74 us (7%)
  local copies, waits for them, and re-layouts  2.09 us (6%)
  between operations  0.84 us (2%)
    pallas_call x1, Pallas kernels, body(): pl.pallas_call(functools.partial(couple_kernel, shards, peers), grid=(ste...  11 us
    ppermute x3, starting transfers between devices, body(): lax.ppermute(chunk, 'inst', [(i, (i + d) % peers) for i in range(peers)])  5.02 us
    ppermute x4, starting transfers between devices, body(): lax.ppermute(cross, ('space', 'row'), [(i * 2 + r, (i + d) % shards * 2 +...  4.89 us
    pallas_call x2, Pallas kernels, body(): pl.pallas_call(functools.partial(update_kernel, base, mine, peers, tile),...  2.5 us
    pallas_call x1, Pallas kernels, body(): pl.pallas_call(functools.partial(cut_kernel, bounds[1:]), out_shape=tuple...  2.12 us
    unnamed x24, local copies, waits for them, and re-layouts  2.09 us
    ppermute x1, starting transfers between devices, body(): lax.ppermute(down, 'space', [(i, (i - 1) % shards) for i in range(shards)])  2.08 us
    ppermute x4, waiting for transfers between devices, body(): lax.ppermute(cross, ('space', 'row'), [(i * 2 + r, (i + d) % shards * 2 +...  1.91 us
  transfers between devices with their start and end apart: 9, of which 4 were waited for; matrix products, arithmetic and copies ran while one was open for 4% of the time, Pallas kernels for 42%

profile of v19, /device:TPU:0, one launch (start us, length us, event | category | flops | bytes accessed | tf_op | source)
XLA Modules:
  0.0 36.9 jit_solution(8000358834872829423)
XLA Ops:
  0.0 0.9 %head.1.first_ref.before_ref = bf16[2,320,128]{2,1,0:T(8,128)(2,1)S(1)} custom-call(bf16[2,320,1024]{2,1,0:T(8,128)(2,1)} %bitcast.10), custom_call_target="tpu_custom_call" | custom-call | tf_op jit(solution)/shard_map/instances/head/pallas_call | solution.py:210
  0.9 0.0 copy-start
  0.9 3.0 %collective-permute-start.6 = (bf16[2,320,128]{2,1,0:T(8,128)(2,1)S(1)}, bf16[2,320,128]{2,1,0:T(8,128)(2,1)}, u32[]{:S(2)}, u32[]{:S(2)}) collective-permute-start(bf16[2,320,128]{2,1,0:T(8,128)(2,1)S(1)} %head.1.first_ref.before_ref), channel_id=1, source_target_pairs={{0,2},{2,0},{1,3},{3,1},{4,6},{6,4},{5,7},{7,5},{8,10},{10,8},{9,1... | collective-permute-start | bytes 491528 | tf_op jit(solution)/shard_map/instances/ppermute | solution.py:230
  3.9 2.1 %cut.1 = (bf16[2,320,640]{2,1,0:T(8,128)(2,1)}, bf16[2,320,256]{2,1,0:T(8,128)(2,1)S(1)}) custom-call(bf16[2,320,128]{2,1,0:T(8,128)(2,1)S(1)} %head.1.first_ref.before_ref, bf16[2,320,1024]{2,1,0:T(8,128)(2,1)} %bitcast.11), custom_call_target="tpu_custom_call" | custom-call | tf_op jit(solution)/shard_map/instances/cut/pallas_call | solution.py:220
  6.1 0.0 copy-start.4
  6.1 0.7 %copy-done.4 = bf16[2,320,256]{2,1,0:T(8,128)(2,1)} copy-done((bf16[2,320,256]{2,1,0:T(8,128)(2,1)}, bf16[2,320,256]{2,1,0:T(8,128)(2,1)S(1)}, u32[]{:S(2)}) %copy-start.4) | copy-done | bytes 327704
  6.8 0.0 copy-start.10
  6.8 0.1 collective-permute-start.8
  6.9 0.0 copy-start.1
  6.9 0.0 copy-start.3
  6.9 0.0 copy-start.6
  6.9 0.0 copy-start.7
  6.9 0.0 copy-start.8
  6.9 0.0 copy-start.9
  6.9 0.1 pad_add_fusion.place_ref
  7.0 1.3 %copy.14.trace_ref = bf16[480,320]{1,0:T(8,128)(2,1)S(1)} copy(bf16[480,320]{0,1:T(8,128)(2,1)} %param.18) | data formatting | bytes 614400 | tf_op args[7]
  8.3 0.0 copy-done
  8.4 0.0 copy-start.5
  8.4 0.0 copy-start.2
  8.4 1.0 %ends.1 = (bf16[2,160,64]{2,1,0:T(8,128)(2,1)S(1)}, bf16[2,160,64]{2,1,0:T(8,128)(2,1)S(1)}, bf16[2,80,64]{2,1,0:T(8,128)(2,1)S(1)}) custom-call(s32[3]{0:T(128)S(1)} %pad_add_fusion.place_ref, bf16[2,320,128]{2,1,0:T(8,128)(2,1)S(1)} %head.1.first_ref.before_ref, bf16[2,320,1024]{2,1,0:T(8,128)(2,1)S(1)} %bitcast.12, bf16[480,320]{1,0:T(8,128)(2,1)S(1)} %copy.14.trace_ref), custom_call_target="tpu_custom_call" | custom-call | flops 104857600 | bytes 1000000 | tf_op jit(solution)/shard_map/ends/ends/pallas_call | solution.py:234
  9.4 3.0 %collective-permute-start.5 = (bf16[2,80,64]{2,1,0:T(8,128)(2,1)S(1)}, bf16[2,80,64]{2,1,0:T(8,128)(2,1)S(1)}, u32[]{:S(2)}, u32[]{:S(2)}) collective-permute-start(bf16[2,80,64]{2,1,0:T(8,128)(2,1)S(1)} %get-tuple-element.14), channel_id=1, source_target_pairs={{0,13},{1,12},{4,1},{5,0},{8,5},{9,4},{12,9},{13,8},{2,15},{3,14},... | collective-permute-start | bytes 61448 | tf_op jit(solution)/shard_map/interface/ppermute | solution.py:257
  12.4 0.2 collective-permute-start.4
  12.6 1.2 %collective-permute-start.3 = (bf16[2,80,64]{2,1,0:T(8,128)(2,1)S(1)}, bf16[2,80,64]{2,1,0:T(8,128)(2,1)S(1)}, u32[]{:S(2)}, u32[]{:S(2)}) collective-permute-start(bf16[2,80,64]{2,1,0:T(8,128)(2,1)S(1)} %get-tuple-element.14), channel_id=1, source_target_pairs={{0,5},{1,4},{4,9},{5,8},{8,13},{9,12},{12,1},{13,0},{2,7},{3,6},{6... | collective-permute-start | bytes 61448 | tf_op jit(solution)/shard_map/interface/ppermute | solution.py:257
  13.8 0.3 collective-permute-done.5.rest_3_
  14.1 1.5 %collective-permute-start = (bf16[2,160,64]{2,1,0:T(8,128)(2,1)S(1)}, bf16[2,160,64]{2,1,0:T(8,128)(2,1)S(1)}, u32[]{:S(2)}, u32[]{:S(2)}) collective-permute-start(bf16[2,160,64]{2,1,0:T(8,128)(2,1)S(1)} %get-tuple-element.12), channel_id=1, source_target_pairs={{0,4},{4,8},{8,12},{12,0},{1,5},{5,9},{9,13},{13,1},{2,6},{6,10},{... | collective-permute-start | bytes 122888 | tf_op jit(solution)/shard_map/halo/ppermute | solution.py:254
  15.6 1.5 %collective-permute-done.4.rest_2_ = bf16[2,80,64]{2,1,0:T(8,128)(2,1)S(1)} collective-permute-done((bf16[2,80,64]{2,1,0:T(8,128)(2,1)S(1)}, bf16[2,80,64]{2,1,0:T(8,128)(2,1)S(1)}, u32[]{:S(2)}, u32[]{:S(2)}) %collective-permute-start.4) | collective-permute-done | bytes 20512 | tf_op jit(solution)/shard_map/interface/ppermute | solution.py:257
  17.1 2.1 %collective-permute-start.1 = (bf16[2,160,64]{2,1,0:T(8,128)(2,1)S(1)}, bf16[2,160,64]{2,1,0:T(8,128)(2,1)S(1)}, u32[]{:S(2)}, u32[]{:S(2)}) collective-permute-start(bf16[2,160,64]{2,1,0:T(8,128)(2,1)S(1)} %get-tuple-element.13), channel_id=1, source_target_pairs={{0,12},{4,0},{8,4},{12,8},{1,13},{5,1},{9,5},{13,9},{2,14},{6,2},{... | collective-permute-start | bytes 122888 | tf_op jit(solution)/shard_map/halo/ppermute | solution.py:255
  19.2 0.0 collective-permute-done.3.rest_1_
  19.2 0.4 %collective-permute-start.2 = (bf16[2,80,64]{2,1,0:T(8,128)(2,1)S(1)}, bf16[2,80,64]{2,1,0:T(8,128)(2,1)S(1)}, u32[]{:S(2)}, u32[]{:S(2)}) collective-permute-start(bf16[2,80,64]{2,1,0:T(8,128)(2,1)S(1)} %get-tuple-element.14), channel_id=1, source_target_pairs={{0,1},{1,0},{4,5},{5,4},{8,9},{9,8},{12,13},{13,12},{2,3},{3,2},{6... | collective-permute-start | bytes 61448 | tf_op jit(solution)/shard_map/interface/ppermute | solution.py:257
  20.3 0.0 copy-done.10
  20.3 0.2 collective-permute-done.2.rest_0_
  20.5 0.0 copy-done.5
  20.5 1.9 %collective-permute-start.7 = (bf16[2,320,256]{2,1,0:T(8,128)(2,1)S(1)}, bf16[2,320,256]{2,1,0:T(8,128)(2,1)S(1)}, u32[]{:S(2)}, u32[]{:S(2)}) collective-permute-start(bf16[2,320,256]{2,1,0:T(8,128)(2,1)S(1)} %copy-done.5), channel_id=1, source_target_pairs={{0,2},{2,0},{1,3},{3,1},{4,6},{6,4},{5,7},{7,5},{8,10},{10,8},{9,1... | collective-permute-start | bytes 983048 | tf_op jit(solution)/shard_map/instances/ppermute | solution.py:230
  22.4 0.0 collective-permute-done.low_ref
  22.4 0.8 %collective-permute-done.1.high_ref = bf16[2,160,64]{2,1,0:T(8,128)(2,1)S(1)} collective-permute-done((bf16[2,160,64]{2,1,0:T(8,128)(2,1)S(1)}, bf16[2,160,64]{2,1,0:T(8,128)(2,1)S(1)}, u32[]{:S(2)}, u32[]{:S(2)}) %collective-permute-start.1) | collective-permute-done | bytes 40992 | tf_op jit(solution)/shard_map/halo/ppermute | solution.py:255
  23.2 0.0 collective-permute-done.6.rest_4_
  23.2 0.0 copy-done.1
  23.2 0.0 copy-done.3
  23.2 0.0 copy-done.6
  23.3 0.0 copy-done.7
  23.3 0.0 copy-done.8
  23.3 0.0 copy-done.9
  23.3 0.0 copy-done.2
  23.3 11.0 %couple.1 = (f32[2,320,1024]{2,1,0:T(8,128)S(1)}, f32[4,1024]{1,0:T(4,128)S(1)}) custom-call(s32[3]{0:T(128)S(1)} %pad_add_fusion.place_ref, f32[1]{0:T(128)S(6)} %copy.19.freq_ref, f32[4,4]{1,0:T(4,128)S(1)} %copy-done.9, s32[6,1024]{1,0:T(8,128)S(1)} %bitcast.15, s32[2,64]{1,0:T(2,128)S(1)} %bitcast.17, bf16[2,320,1024]{2,1,0:T(8,128)(2,1)S(1)} %bitcast.13, ...), custom_call_target="tpu_custom_call" | custom-call | flops 7500000256 | bytes 6553600 | tf_op jit(solution)/shard_map/couple/couple/pallas_call | solution.py:264
  34.3 0.0 collective-permute-done.8.rest_0_
  34.3 1.4 %update.2.rest_1_ = bf16[2,320,1024]{2,1,0:T(8,128)(2,1)} custom-call(f32[2,320,1024]{2,1,0:T(8,128)S(1)} %get-tuple-element.15.ready_ref, f32[4,1024]{1,0:T(4,128)S(1)} %get-tuple-element.16.factor_ref, bf16[320,320]{1,0:T(8,128)(2,1)S(1)} %copy-done.1, bf16[2,320,640]{2,1,0:T(8,128)(2,1)S(1)} %collective-permute-done.8.rest_0_), custom_call_target="tpu_custom_call" | custom-call | flops 314572800 | bytes 3932160 | tf_op jit(solution)/shard_map/update/update/pallas_call | solution.py:287
  35.7 0.0 collective-permute-done.7.rest_0_
  35.7 1.1 %update.3 = bf16[2,320,1024]{2,1,0:T(8,128)(2,1)} custom-call(f32[2,320,1024]{2,1,0:T(8,128)S(1)} %get-tuple-element.15.ready_ref, f32[4,1024]{1,0:T(4,128)S(1)} %get-tuple-element.16.factor_ref, bf16[320,320]{1,0:T(8,128)(2,1)S(1)} %copy-done.1, bf16[2,320,256]{2,1,0:T(8,128)(2,1)S(1)} %collective-permute-done.7.rest_0_, ...), custom_call_target="tpu_custom_call", output_to_operand_aliasing={{}: (4, {})} | custom-call | flops 104857600 | bytes 1310720 | tf_op jit(solution)/shard_map/update/update/pallas_call | solution.py:287
  (1 shorter events, 0.0 us)
Async XLA Ops:
  0.9 7.4 %copy-start = (bf16[1,2,320,1024]{3,2,1,0:T(8,128)(2,1)S(1)}, bf16[1,2,320,1024]{3,2,1,0:T(8,128)(2,1)}, u32[]{:S(2)}) copy-start(bf16[1,2,320,1024]{3,2,1,0:T(8,128)(2,1)} %param.11) | copy-start | bytes 3932164
  0.9 22.3 %collective-permute-start.6 = (bf16[2,320,128]{2,1,0:T(8,128)(2,1)S(1)}, bf16[2,320,128]{2,1,0:T(8,128)(2,1)}, u32[]{:S(2)}, u32[]{:S(2)}) collective-permute-start(bf16[2,320,128]{2,1,0:T(8,128)(2,1)S(1)} %head.1.first_ref.before_ref), channel_id=1, source_target_pairs={{0,2},{2,0},{1,3},{3,1},{4,6},{6,4},{5,7},{7,5},{8,10},{10,8},{9,1... | collective-permute-start | bytes 491528 | tf_op jit(solution)/shard_map/instances/ppermute | solution.py:230
  6.1 0.7 %copy-start.4 = (bf16[2,320,256]{2,1,0:T(8,128)(2,1)}, bf16[2,320,256]{2,1,0:T(8,128)(2,1)S(1)}, u32[]{:S(2)}) copy-start(bf16[2,320,256]{2,1,0:T(8,128)(2,1)S(1)} %get-tuple-element.17) | copy-start | bytes 983044
  6.8 13.5 %copy-start.10 = (s32[1,6,1024]{2,0,1:T(1,128)S(1)}, s32[1,6,1024]{2,0,1:T(1,128)}, u32[]{:S(2)}) copy-start(s32[1,6,1024]{2,0,1:T(1,128)} %param.15) | copy-start | bytes 73732
  6.8 27.5 %collective-permute-start.8 = (bf16[2,320,640]{2,1,0:T(8,128)(2,1)}, bf16[2,320,640]{2,1,0:T(8,128)(2,1)S(1)}, u32[]{:S(2)}, u32[]{:S(2)}) collective-permute-start(bf16[2,320,640]{2,1,0:T(8,128)(2,1)} %get-tuple-element.18), channel_id=1, source_target_pairs={{0,2},{2,0},{1,3},{3,1},{4,6},{6,4},{5,7},{7,5},{8,10},{10,8},{9,1... | collective-permute-start | bytes 2457608 | tf_op jit(solution)/shard_map/instances/ppermute | solution.py:230
  6.9 16.3 %copy-start.1 = (bf16[320,320]{1,0:T(8,128)(2,1)S(1)}, bf16[320,320]{1,0:T(8,128)(2,1)}, u32[]{:S(2)}) copy-start(bf16[320,320]{1,0:T(8,128)(2,1)} %inverse_ref.5) | copy-start | bytes 614404
  6.9 16.3 %copy-start.3 = (bf16[320,480]{1,0:T(8,128)(2,1)S(1)}, bf16[320,480]{1,0:T(8,128)(2,1)}, u32[]{:S(2)}) copy-start(bf16[320,480]{1,0:T(8,128)(2,1)} %lift_ref.1) | copy-start | bytes 921604
  6.9 16.3 %copy-start.6 = (bf16[320,320]{1,0:T(8,128)(2,1)S(1)}, bf16[320,320]{1,0:T(8,128)(2,1)}, u32[]{:S(2)}) copy-start(bf16[320,320]{1,0:T(8,128)(2,1)} %volume_ref.1) | copy-start | bytes 614404
  6.9 16.3 %copy-start.7 = (f32[1,1024]{1,0:T(1,128)S(1)}, f32[1,1024]{1,0:T(1,128)}, u32[]{:S(2)}) copy-start(f32[1,1024]{1,0:T(1,128)} %scale_ref.1) | copy-start | bytes 12292
  6.9 16.3 %copy-start.8 = (s32[1,2,64]{2,1,0:T(2,128)S(1)}, s32[1,2,64]{2,1,0:T(2,128)}, u32[]{:S(2)}) copy-start(s32[1,2,64]{2,1,0:T(2,128)} %param.16) | copy-start | bytes 1540
  6.9 16.3 %copy-start.9 = (f32[4,4]{1,0:T(4,128)S(1)}, f32[4,4]{1,0:T(4,128)}, u32[]{:S(2)}) copy-start(f32[4,4]{1,0:T(4,128)} %constant.13.clone.table_ref) | copy-start | bytes 196
  8.4 12.1 %copy-start.5 = (bf16[2,320,256]{2,1,0:T(8,128)(2,1)S(1)}, bf16[2,320,256]{2,1,0:T(8,128)(2,1)}, u32[]{:S(2)}) copy-start(bf16[2,320,256]{2,1,0:T(8,128)(2,1)} %copy-done.4) | copy-start | bytes 983044
  8.4 14.9 %copy-start.2 = (bf16[1,2,320,1024]{3,2,1,0:T(8,128)(2,1)S(1)}, bf16[1,2,320,1024]{3,2,1,0:T(8,128)(2,1)}, u32[]{:S(2)}) copy-start(bf16[1,2,320,1024]{3,2,1,0:T(8,128)(2,1)} %param.12) | copy-start | bytes 3932164
  9.4 4.7 %collective-permute-start.5 = (bf16[2,80,64]{2,1,0:T(8,128)(2,1)S(1)}, bf16[2,80,64]{2,1,0:T(8,128)(2,1)S(1)}, u32[]{:S(2)}, u32[]{:S(2)}) collective-permute-start(bf16[2,80,64]{2,1,0:T(8,128)(2,1)S(1)} %get-tuple-element.14), channel_id=1, source_target_pairs={{0,13},{1,12},{4,1},{5,0},{8,5},{9,4},{12,9},{13,8},{2,15},{3,14},... | collective-permute-start | bytes 61448 | tf_op jit(solution)/shard_map/interface/ppermute | solution.py:257
  12.4 4.7 %collective-permute-start.4 = (bf16[2,80,64]{2,1,0:T(8,128)(2,1)S(1)}, bf16[2,80,64]{2,1,0:T(8,128)(2,1)S(1)}, u32[]{:S(2)}, u32[]{:S(2)}) collective-permute-start(bf16[2,80,64]{2,1,0:T(8,128)(2,1)S(1)} %get-tuple-element.14), channel_id=1, source_target_pairs={{0,9},{1,8},{4,13},{5,12},{8,1},{9,0},{12,5},{13,4},{2,11},{3,10},... | collective-permute-start | bytes 61448 | tf_op jit(solution)/shard_map/interface/ppermute | solution.py:257
  12.6 6.5 %collective-permute-start.3 = (bf16[2,80,64]{2,1,0:T(8,128)(2,1)S(1)}, bf16[2,80,64]{2,1,0:T(8,128)(2,1)S(1)}, u32[]{:S(2)}, u32[]{:S(2)}) collective-permute-start(bf16[2,80,64]{2,1,0:T(8,128)(2,1)S(1)} %get-tuple-element.14), channel_id=1, source_target_pairs={{0,5},{1,4},{4,9},{5,8},{8,13},{9,12},{12,1},{13,0},{2,7},{3,6},{6... | collective-permute-start | bytes 61448 | tf_op jit(solution)/shard_map/interface/ppermute | solution.py:257
  14.1 8.3 %collective-permute-start = (bf16[2,160,64]{2,1,0:T(8,128)(2,1)S(1)}, bf16[2,160,64]{2,1,0:T(8,128)(2,1)S(1)}, u32[]{:S(2)}, u32[]{:S(2)}) collective-permute-start(bf16[2,160,64]{2,1,0:T(8,128)(2,1)S(1)} %get-tuple-element.12), channel_id=1, source_target_pairs={{0,4},{4,8},{8,12},{12,0},{1,5},{5,9},{9,13},{13,1},{2,6},{6,10},{... | collective-permute-start | bytes 122888 | tf_op jit(solution)/shard_map/halo/ppermute | solution.py:254
  17.1 6.1 %collective-permute-start.1 = (bf16[2,160,64]{2,1,0:T(8,128)(2,1)S(1)}, bf16[2,160,64]{2,1,0:T(8,128)(2,1)S(1)}, u32[]{:S(2)}, u32[]{:S(2)}) collective-permute-start(bf16[2,160,64]{2,1,0:T(8,128)(2,1)S(1)} %get-tuple-element.13), channel_id=1, source_target_pairs={{0,12},{4,0},{8,4},{12,8},{1,13},{5,1},{9,5},{13,9},{2,14},{6,2},{... | collective-permute-start | bytes 122888 | tf_op jit(solution)/shard_map/halo/ppermute | solution.py:255
  19.2 1.3 %collective-permute-start.2 = (bf16[2,80,64]{2,1,0:T(8,128)(2,1)S(1)}, bf16[2,80,64]{2,1,0:T(8,128)(2,1)S(1)}, u32[]{:S(2)}, u32[]{:S(2)}) collective-permute-start(bf16[2,80,64]{2,1,0:T(8,128)(2,1)S(1)} %get-tuple-element.14), channel_id=1, source_target_pairs={{0,1},{1,0},{4,5},{5,4},{8,9},{9,8},{12,13},{13,12},{2,3},{3,2},{6... | collective-permute-start | bytes 61448 | tf_op jit(solution)/shard_map/interface/ppermute | solution.py:257
  20.5 15.2 %collective-permute-start.7 = (bf16[2,320,256]{2,1,0:T(8,128)(2,1)S(1)}, bf16[2,320,256]{2,1,0:T(8,128)(2,1)S(1)}, u32[]{:S(2)}, u32[]{:S(2)}) collective-permute-start(bf16[2,320,256]{2,1,0:T(8,128)(2,1)S(1)} %copy-done.5), channel_id=1, source_target_pairs={{0,2},{2,0},{1,3},{3,1},{4,6},{6,4},{5,7},{7,5},{8,10},{10,8},{9,1... | collective-permute-start | bytes 983048 | tf_op jit(solution)/shard_map/instances/ppermute | solution.py:230

commit v20 on v4

--- a/solution.py
+++ b/solution.py
@@ -132,17 +132,19 @@
 def update_kernel(tile, ready_ref, factor_ref, inverse_ref, *rest):
     others, (out_ref, made, sems) = rest[:-3], rest[-3:]
     count, dof, total = ready_ref.shape
+    pieces = [(t, slice(0, dof)) for t in range(total // tile - 1)]
+    pieces += [(total // tile - 1, slice(0, dof // 2)), (total // tile - 1, slice(dof // 2, dof))]
     copies = []
-    for t in range(total // tile):
+    for p, (t, rows) in enumerate(pieces):
         cols = slice(t * tile, (t + 1) * tile)
-        moved = [dot(inverse_ref[...], other[m, :, cols]) for other in others for m in range(count)]
-        for n in range(count):
-            value = ready_ref[n, :, cols]
+        moved = [dot(inverse_ref[rows, :], other[m, :, cols]) for other in others for m in range(count)]
+        for n in range(count):
+            value = ready_ref[n, rows, cols]
             for k, part in enumerate(moved):
                 at = n * len(moved) + k
                 value -= factor_ref[at : at + 1, cols] * part
-            made[t, n] = value.astype(jnp.bfloat16)
-        copy = pltpu.make_async_copy(made.at[t], out_ref.at[:, :, cols], sems.at[t])
+            made[t, n, rows, :] = value.astype(jnp.bfloat16)
+        copy = pltpu.make_async_copy(made.at[t, :, rows, :], out_ref.at[:, rows, cols], sems.at[p])
         copy.start()
         copies.append(copy)
     for copy in copies:
@@ -231,7 +233,7 @@
             out_shape=jax.ShapeDtypeStruct((count, dof, total), bf16),
             in_specs=[vmem] * (2 + peers),
             out_specs=pl.BlockSpec(memory_space=pl.ANY),
-            scratch_shapes=[pltpu.VMEM((steps, count, dof, tile), bf16), pltpu.SemaphoreType.DMA((steps,))],
+            scratch_shapes=[pltpu.VMEM((steps, count, dof, tile), bf16), pltpu.SemaphoreType.DMA((steps + 1,))],
             compiler_params=pltpu.CompilerParams(vmem_limit_bytes=VMEM_LIMIT),
             cost_estimate=pl.CostEstimate(flops=2 * count * total * dof * dof * (peers - 1),
                                           bytes_accessed=count * dof * total * 8, transcendentals=0),

time: 33.8 us -> 33.9 us (level)
  no operation moved by 1% of the time
where the time goes in v20:
time: 33.9 us; the launch traced here: 33.7 us
  Pallas kernels  13.2 us (39%)
  starting transfers between devices  12.4 us (37%)
  waiting for transfers between devices  4.67 us (14%)
  local copies, waits for them, and re-layouts  2.58 us (8%)
  between operations  0.79 us (2%)
    pallas_call x1, Pallas kernels, body(): pl.pallas_call(functools.partial(couple_kernel, shards, peers), grid=(ste...  10.4 us
    ppermute x4, starting transfers between devices, body(): lax.ppermute(cross, ('space', 'row'), [(i * 2 + r, (i + d) % shards * 2 +...  5.62 us
    ppermute x1, starting transfers between devices, body(): lax.ppermute(current, 'inst', [(i, (i + d) % peers) for i in range(peers)])  2.94 us
    unnamed x20, local copies, waits for them, and re-layouts  2.58 us
    ppermute x1, waiting for transfers between devices, body(): lax.ppermute(current, 'inst', [(i, (i + d) % peers) for i in range(peers)])  2.5 us
    ppermute x1, starting transfers between devices, body(): lax.ppermute(down, 'space', [(i, (i - 1) % shards) for i in range(shards)])  2.25 us
    ppermute x4, waiting for transfers between devices, body(): lax.ppermute(cross, ('space', 'row'), [(i * 2 + r, (i + d) % shards * 2 +...  2.16 us
    pallas_call x1, Pallas kernels, body(): pl.pallas_call(functools.partial(update_kernel, tile), out_shape=jax.Shap...  1.76 us
  transfers between devices with their start and end apart: 7, of which 3 were waited for; matrix products, arithmetic and copies ran while one was open for 4% of the time, Pallas kernels for 34%

profile of v20, /device:TPU:0, one launch (start us, length us, event | category | flops | bytes accessed | tf_op | source)
XLA Modules:
  0.0 33.7 jit_solution(13461740295071129063)
XLA Ops:
  0.0 2.9 %collective-permute-start.6 = (bf16[2,320,1024]{2,1,0:T(8,128)(2,1)}, bf16[2,320,1024]{2,1,0:T(8,128)(2,1)S(1)}, u32[]{:S(2)}, u32[]{:S(2)}) collective-permute-start(bf16[2,320,1024]{2,1,0:T(8,128)(2,1)} %bitcast.10), channel_id=1, source_target_pairs={{0,2},{2,0},{1,3},{3,1},{4,6},{6,4},{5,7},{7,5},{8,10},{10,8},{9,1... | collective-permute-start | bytes 3932168 | tf_op jit(solution)/shard_map/instances/ppermute | solution.py:176
  2.9 1.2 %copy.13.trace_ref = bf16[480,320]{1,0:T(8,128)(2,1)S(1)} copy(bf16[480,320]{0,1:T(8,128)(2,1)} %param.18) | data formatting | bytes 614400 | tf_op args[7]
  4.2 0.1 pad_add_fusion.place_ref
  4.2 0.0 copy-start
  4.2 1.3 %copy-done = bf16[1,2,320,1024]{3,2,1,0:T(8,128)(2,1)S(1)} copy-done((bf16[1,2,320,1024]{3,2,1,0:T(8,128)(2,1)S(1)}, bf16[1,2,320,1024]{3,2,1,0:T(8,128)(2,1)}, u32[]{:S(2)}) %copy-start) | copy-done | bytes 1310744
  5.6 0.0 copy-start.8
  5.6 0.0 copy-start.1
  5.6 0.0 copy-start.2
  5.6 0.0 copy-start.3
  5.6 0.0 copy-start.4
  5.6 0.0 copy-start.5
  5.6 0.0 copy-start.6
  5.6 0.0 copy-start.7
  5.6 1.0 %ends.1 = (bf16[2,160,64]{2,1,0:T(8,128)(2,1)S(1)}, bf16[2,160,64]{2,1,0:T(8,128)(2,1)S(1)}, bf16[2,80,64]{2,1,0:T(8,128)(2,1)S(1)}) custom-call(s32[3]{0:T(128)S(1)} %pad_add_fusion.place_ref, bf16[2,320,1024]{2,1,0:T(8,128)(2,1)S(1)} %bitcast.11, bf16[2,320,1024]{2,1,0:T(8,128)(2,1)S(1)} %bitcast.12, bf16[480,320]{1,0:T(8,128)(2,1)S(1)} %copy.13.trace_ref), custom_call_target="tpu_custom_call" | custom-call | flops 104857600 | bytes 1000000 | tf_op jit(solution)/shard_map/ends/ends/pallas_call | solution.py:180
  6.6 2.8 %collective-permute-start.5 = (bf16[2,80,64]{2,1,0:T(8,128)(2,1)S(1)}, bf16[2,80,64]{2,1,0:T(8,128)(2,1)S(1)}, u32[]{:S(2)}, u32[]{:S(2)}) collective-permute-start(bf16[2,80,64]{2,1,0:T(8,128)(2,1)S(1)} %get-tuple-element.12), channel_id=1, source_target_pairs={{0,13},{1,12},{4,1},{5,0},{8,5},{9,4},{12,9},{13,8},{2,15},{3,14},... | collective-permute-start | bytes 61448 | tf_op jit(solution)/shard_map/interface/ppermute | solution.py:203
  9.5 0.0 collective-permute-start.4
  9.5 1.6 %collective-permute-start = (bf16[2,160,64]{2,1,0:T(8,128)(2,1)S(1)}, bf16[2,160,64]{2,1,0:T(8,128)(2,1)S(1)}, u32[]{:S(2)}, u32[]{:S(2)}) collective-permute-start(bf16[2,160,64]{2,1,0:T(8,128)(2,1)S(1)} %get-tuple-element.10), channel_id=1, source_target_pairs={{0,4},{4,8},{8,12},{12,0},{1,5},{5,9},{9,13},{13,1},{2,6},{6,10},{... | collective-permute-start | bytes 122888 | tf_op jit(solution)/shard_map/halo/ppermute | solution.py:200
  11.0 2.2 %collective-permute-start.1 = (bf16[2,160,64]{2,1,0:T(8,128)(2,1)S(1)}, bf16[2,160,64]{2,1,0:T(8,128)(2,1)S(1)}, u32[]{:S(2)}, u32[]{:S(2)}) collective-permute-start(bf16[2,160,64]{2,1,0:T(8,128)(2,1)S(1)} %get-tuple-element.11), channel_id=1, source_target_pairs={{0,12},{4,0},{8,4},{12,8},{1,13},{5,1},{9,5},{13,9},{2,14},{6,2},{... | collective-permute-start | bytes 122888 | tf_op jit(solution)/shard_map/halo/ppermute | solution.py:201
  13.3 0.0 collective-permute-done.5.rest_3_
  13.3 0.0 collective-permute-start.3
  13.3 0.6 %collective-permute-done.4.rest_2_ = bf16[2,80,64]{2,1,0:T(8,128)(2,1)S(1)} collective-permute-done((bf16[2,80,64]{2,1,0:T(8,128)(2,1)S(1)}, bf16[2,80,64]{2,1,0:T(8,128)(2,1)S(1)}, u32[]{:S(2)}, u32[]{:S(2)}) %collective-permute-start.4) | collective-permute-done | bytes 20512 | tf_op jit(solution)/shard_map/interface/ppermute | solution.py:203
  13.9 2.8 %collective-permute-start.2 = (bf16[2,80,64]{2,1,0:T(8,128)(2,1)S(1)}, bf16[2,80,64]{2,1,0:T(8,128)(2,1)S(1)}, u32[]{:S(2)}, u32[]{:S(2)}) collective-permute-start(bf16[2,80,64]{2,1,0:T(8,128)(2,1)S(1)} %get-tuple-element.12), channel_id=1, source_target_pairs={{0,1},{1,0},{4,5},{5,4},{8,9},{9,8},{12,13},{13,12},{2,3},{3,2},{6... | collective-permute-start | bytes 61448 | tf_op jit(solution)/shard_map/interface/ppermute | solution.py:203
  17.4 0.0 copy-done.8
  17.4 1.5 %collective-permute-done.3.rest_1_ = bf16[2,80,64]{2,1,0:T(8,128)(2,1)S(1)} collective-permute-done((bf16[2,80,64]{2,1,0:T(8,128)(2,1)S(1)}, bf16[2,80,64]{2,1,0:T(8,128)(2,1)S(1)}, u32[]{:S(2)}, u32[]{:S(2)}) %collective-permute-start.3) | collective-permute-done | bytes 20512 | tf_op jit(solution)/shard_map/interface/ppermute | solution.py:203
  18.9 0.0 collective-permute-done.2.rest_0_
  18.9 0.0 collective-permute-done.low_ref
  18.9 0.0 collective-permute-done.1.high_ref
  18.9 0.0 copy-done.1
  18.9 0.0 copy-done.2
  19.0 0.0 copy-done.3
  19.0 0.0 copy-done.4
  19.0 0.0 copy-done.5
  19.0 0.0 copy-done.6
  19.0 0.0 copy-done.7
  19.0 10.4 %couple.1 = (f32[2,320,1024]{2,1,0:T(8,128)S(1)}, f32[4,1024]{1,0:T(4,128)S(1)}) custom-call(s32[3]{0:T(128)S(1)} %pad_add_fusion.place_ref, f32[1]{0:T(128)S(6)} %copy.17.freq_ref, f32[4,4]{1,0:T(4,128)S(1)} %copy-done.7, s32[6,1024]{1,0:T(8,128)S(1)} %bitcast.15, s32[2,64]{1,0:T(2,128)S(1)} %bitcast.17, bf16[2,320,1024]{2,1,0:T(8,128)(2,1)S(1)} %bitcast.13, ...), custom_call_target="tpu_custom_call" | custom-call | flops 3690987520 | bytes 6553600 | tf_op jit(solution)/shard_map/couple/couple/pallas_call | solution.py:211
  29.4 2.5 %collective-permute-done.6.rest_0_ = bf16[2,320,1024]{2,1,0:T(8,128)(2,1)S(1)} collective-permute-done((bf16[2,320,1024]{2,1,0:T(8,128)(2,1)}, bf16[2,320,1024]{2,1,0:T(8,128)(2,1)S(1)}, u32[]{:S(2)}, u32[]{:S(2)}) %collective-permute-start.6) | collective-permute-done | bytes 1310752 | tf_op jit(solution)/shard_map/instances/ppermute | solution.py:176
  31.9 1.8 %update.1 = bf16[2,320,1024]{2,1,0:T(8,128)(2,1)} custom-call(f32[2,320,1024]{2,1,0:T(8,128)S(1)} %get-tuple-element.13.ready_ref, f32[4,1024]{1,0:T(4,128)S(1)} %get-tuple-element.14.factor_ref, bf16[320,320]{1,0:T(8,128)(2,1)S(1)} %copy-done.1, bf16[2,320,1024]{2,1,0:T(8,128)(2,1)S(1)} %collective-permute-done.6.rest_0_), custom_call_target="tpu_custom_call" | custom-call | flops 419430400 | bytes 5242880 | tf_op jit(solution)/shard_map/update/update/pallas_call | solution.py:231
  (1 shorter events, 0.0 us)
Async XLA Ops:
  0.0 31.9 %collective-permute-start.6 = (bf16[2,320,1024]{2,1,0:T(8,128)(2,1)}, bf16[2,320,1024]{2,1,0:T(8,128)(2,1)S(1)}, u32[]{:S(2)}, u32[]{:S(2)}) collective-permute-start(bf16[2,320,1024]{2,1,0:T(8,128)(2,1)} %bitcast.10), channel_id=1, source_target_pairs={{0,2},{2,0},{1,3},{3,1},{4,6},{6,4},{5,7},{7,5},{8,10},{10,8},{9,1... | collective-permute-start | bytes 3932168 | tf_op jit(solution)/shard_map/instances/ppermute | solution.py:176
  4.2 1.3 %copy-start = (bf16[1,2,320,1024]{3,2,1,0:T(8,128)(2,1)S(1)}, bf16[1,2,320,1024]{3,2,1,0:T(8,128)(2,1)}, u32[]{:S(2)}) copy-start(bf16[1,2,320,1024]{3,2,1,0:T(8,128)(2,1)} %param.11) | copy-start | bytes 3932164
  5.6 11.8 %copy-start.8 = (s32[1,6,1024]{2,0,1:T(1,128)S(1)}, s32[1,6,1024]{2,0,1:T(1,128)}, u32[]{:S(2)}) copy-start(s32[1,6,1024]{2,0,1:T(1,128)} %param.15) | copy-start | bytes 73732
  5.6 13.4 %copy-start.1 = (bf16[320,320]{1,0:T(8,128)(2,1)S(1)}, bf16[320,320]{1,0:T(8,128)(2,1)}, u32[]{:S(2)}) copy-start(bf16[320,320]{1,0:T(8,128)(2,1)} %inverse_ref.3) | copy-start | bytes 614404
  5.6 13.4 %copy-start.2 = (bf16[1,2,320,1024]{3,2,1,0:T(8,128)(2,1)S(1)}, bf16[1,2,320,1024]{3,2,1,0:T(8,128)(2,1)}, u32[]{:S(2)}) copy-start(bf16[1,2,320,1024]{3,2,1,0:T(8,128)(2,1)} %param.12) | copy-start | bytes 3932164
  5.6 13.4 %copy-start.3 = (bf16[320,480]{1,0:T(8,128)(2,1)S(1)}, bf16[320,480]{1,0:T(8,128)(2,1)}, u32[]{:S(2)}) copy-start(bf16[320,480]{1,0:T(8,128)(2,1)} %lift_ref.1) | copy-start | bytes 921604
  5.6 13.4 %copy-start.4 = (bf16[320,320]{1,0:T(8,128)(2,1)S(1)}, bf16[320,320]{1,0:T(8,128)(2,1)}, u32[]{:S(2)}) copy-start(bf16[320,320]{1,0:T(8,128)(2,1)} %volume_ref.1) | copy-start | bytes 614404
  5.6 13.4 %copy-start.5 = (f32[1,1024]{1,0:T(1,128)S(1)}, f32[1,1024]{1,0:T(1,128)}, u32[]{:S(2)}) copy-start(f32[1,1024]{1,0:T(1,128)} %scale_ref.1) | copy-start | bytes 12292
  5.6 13.4 %copy-start.6 = (s32[1,2,64]{2,1,0:T(2,128)S(1)}, s32[1,2,64]{2,1,0:T(2,128)}, u32[]{:S(2)}) copy-start(s32[1,2,64]{2,1,0:T(2,128)} %param.16) | copy-start | bytes 1540
  5.6 13.4 %copy-start.7 = (f32[4,4]{1,0:T(4,128)S(1)}, f32[4,4]{1,0:T(4,128)}, u32[]{:S(2)}) copy-start(f32[4,4]{1,0:T(4,128)} %constant.13.clone.table_ref) | copy-start | bytes 196
  6.6 6.6 %collective-permute-start.5 = (bf16[2,80,64]{2,1,0:T(8,128)(2,1)S(1)}, bf16[2,80,64]{2,1,0:T(8,128)(2,1)S(1)}, u32[]{:S(2)}, u32[]{:S(2)}) collective-permute-start(bf16[2,80,64]{2,1,0:T(8,128)(2,1)S(1)} %get-tuple-element.12), channel_id=1, source_target_pairs={{0,13},{1,12},{4,1},{5,0},{8,5},{9,4},{12,9},{13,8},{2,15},{3,14},... | collective-permute-start | bytes 61448 | tf_op jit(solution)/shard_map/interface/ppermute | solution.py:203
  9.5 4.5 %collective-permute-start.4 = (bf16[2,80,64]{2,1,0:T(8,128)(2,1)S(1)}, bf16[2,80,64]{2,1,0:T(8,128)(2,1)S(1)}, u32[]{:S(2)}, u32[]{:S(2)}) collective-permute-start(bf16[2,80,64]{2,1,0:T(8,128)(2,1)S(1)} %get-tuple-element.12), channel_id=1, source_target_pairs={{0,9},{1,8},{4,13},{5,12},{8,1},{9,0},{12,5},{13,4},{2,11},{3,10},... | collective-permute-start | bytes 61448 | tf_op jit(solution)/shard_map/interface/ppermute | solution.py:203
  9.5 9.5 %collective-permute-start = (bf16[2,160,64]{2,1,0:T(8,128)(2,1)S(1)}, bf16[2,160,64]{2,1,0:T(8,128)(2,1)S(1)}, u32[]{:S(2)}, u32[]{:S(2)}) collective-permute-start(bf16[2,160,64]{2,1,0:T(8,128)(2,1)S(1)} %get-tuple-element.10), channel_id=1, source_target_pairs={{0,4},{4,8},{8,12},{12,0},{1,5},{5,9},{9,13},{13,1},{2,6},{6,10},{... | collective-permute-start | bytes 122888 | tf_op jit(solution)/shard_map/halo/ppermute | solution.py:200
  11.0 7.9 %collective-permute-start.1 = (bf16[2,160,64]{2,1,0:T(8,128)(2,1)S(1)}, bf16[2,160,64]{2,1,0:T(8,128)(2,1)S(1)}, u32[]{:S(2)}, u32[]{:S(2)}) collective-permute-start(bf16[2,160,64]{2,1,0:T(8,128)(2,1)S(1)} %get-tuple-element.11), channel_id=1, source_target_pairs={{0,12},{4,0},{8,4},{12,8},{1,13},{5,1},{9,5},{13,9},{2,14},{6,2},{... | collective-permute-start | bytes 122888 | tf_op jit(solution)/shard_map/halo/ppermute | solution.py:201
  13.3 5.6 %collective-permute-start.3 = (bf16[2,80,64]{2,1,0:T(8,128)(2,1)S(1)}, bf16[2,80,64]{2,1,0:T(8,128)(2,1)S(1)}, u32[]{:S(2)}, u32[]{:S(2)}) collective-permute-start(bf16[2,80,64]{2,1,0:T(8,128)(2,1)S(1)} %get-tuple-element.12), channel_id=1, source_target_pairs={{0,5},{1,4},{4,9},{5,8},{8,13},{9,12},{12,1},{13,0},{2,7},{3,6},{6... | collective-permute-start | bytes 61448 | tf_op jit(solution)/shard_map/interface/ppermute | solution.py:203
  13.9 5.0 %collective-permute-start.2 = (bf16[2,80,64]{2,1,0:T(8,128)(2,1)S(1)}, bf16[2,80,64]{2,1,0:T(8,128)(2,1)S(1)}, u32[]{:S(2)}, u32[]{:S(2)}) collective-permute-start(bf16[2,80,64]{2,1,0:T(8,128)(2,1)S(1)} %get-tuple-element.12), channel_id=1, source_target_pairs={{0,1},{1,0},{4,5},{5,4},{8,9},{9,8},{12,13},{13,12},{2,3},{3,2},{6... | collective-permute-start | bytes 61448 | tf_op jit(solution)/shard_map/interface/ppermute | solution.py:203

commit v21 on v4

--- a/solution.py
+++ b/solution.py
@@ -45,9 +45,9 @@
         cross_ref[n] = jnp.where(section == 0, first[width : 2 * width, :rows], first[:width, :rows])
 
 
-def couple_kernel(shards, peers, place_ref, freq_ref, table_ref, adj_ref, partner_ref, all_ref, tile_ref, forcing_ref,
+def couple_kernel(shards, peers, deep, place_ref, freq_ref, table_ref, adj_ref, partner_ref, all_ref, tile_ref, forcing_ref,
                   scale_ref, trace_ref, lift_ref, volume_ref, inverse_ref, low_ref, high_ref, *rest):
-    pieces, (out_ref, factor_ref, traces) = rest[:shards], rest[shards:]
+    pieces, (out_ref, factor_ref, spread_ref, traces) = rest[:shards], rest[shards:]
     step = pl.program_id(0)
     steps = pl.num_programs(0)
     count, dof, total = all_ref.shape
@@ -63,6 +63,11 @@
                 made = dot(trace_ref[...], all_ref[n, :, cols]).astype(jnp.bfloat16)
                 for f in range(6):
                     traces[f, n * width : (n + 1) * width, cols] = made[f * width : (f + 1) * width]
+
+        left = dof - deep
+        spread_ref[...] = jnp.zeros_like(spread_ref)
+        for m in range(count):
+            spread_ref[m, :, m * left : (m + 1) * left] = inverse_ref[:, deep:]
 
     column = lax.broadcasted_iota(jnp.int32, (1, tile), 1)
     at_edge = jnp.logical_or(step == 0, step == steps - 1)
@@ -129,13 +134,17 @@
         finish(False)
 
 
-def update_kernel(tile, ready_ref, factor_ref, inverse_ref, *rest):
+def update_kernel(tile, deep, ready_ref, factor_ref, inverse_ref, spread_ref, *rest):
     others, (out_ref, made, sems) = rest[:-3], rest[-3:]
     count, dof, total = ready_ref.shape
     copies = []
     for t in range(total // tile):
         cols = slice(t * tile, (t + 1) * tile)
-        moved = [dot(inverse_ref[...], other[m, :, cols]) for other in others for m in range(count)]
+        moved = []
+        for other in others:
+            stack = jnp.concatenate([other[m, deep:, cols] for m in range(count)], axis=0)
+            for m in range(count):
+                moved.append(dot(inverse_ref[:, :deep], other[m, :deep, cols]) + dot(spread_ref[m], stack))
         for n in range(count):
             value = ready_ref[n, :, cols]
             for k, part in enumerate(moved):
@@ -204,17 +213,20 @@
 
     tile = 256
     steps = total // tile
+    deep = dof // tile * tile
     by_tile = lambda *lead: pl.BlockSpec(lead + (tile,), lambda j: (0,) * len(lead) + (j,))
     with jax.named_scope("couple"):
-        ready, factors = pl.pallas_call(
-            functools.partial(couple_kernel, shards, peers),
+        ready, factors, spread = pl.pallas_call(
+            functools.partial(couple_kernel, shards, peers, deep),
             grid=(steps,),
             out_shape=(jax.ShapeDtypeStruct((count, dof, total), jnp.float32),
-                       jax.ShapeDtypeStruct((count * count * (peers - 1), total), jnp.float32)),
+                       jax.ShapeDtypeStruct((count * count * (peers - 1), total), jnp.float32),
+                       jax.ShapeDtypeStruct((count, dof, count * (dof - deep)), bf16)),
             in_specs=[smem, smem, smem, by_tile(6), whole(partner_rows), whole(current), by_tile(count, dof),
                       by_tile(count, dof), by_tile(1), whole(trace_matrix), whole(lift_matrix),
                       whole(volume_matrix), whole(block_inverse), whole(low), whole(high)] + [whole(p) for p in pieces],
-            out_specs=(by_tile(count, dof), by_tile(count * count * (peers - 1))),
+            out_specs=(by_tile(count, dof), by_tile(count * count * (peers - 1)),
+                       pl.BlockSpec((count, dof, count * (dof - deep)), lambda j: (0, 0, 0))),
             scratch_shapes=[pltpu.VMEM((6, count * width, total), bf16)],
             compiler_params=pltpu.CompilerParams(vmem_limit_bytes=VMEM_LIMIT),
             cost_estimate=pl.CostEstimate(
@@ -227,16 +239,16 @@
     vmem = pl.BlockSpec(memory_space=pltpu.VMEM)
     with jax.named_scope("update"):
         result = pl.pallas_call(
-            functools.partial(update_kernel, tile),
+            functools.partial(update_kernel, tile, deep),
             out_shape=jax.ShapeDtypeStruct((count, dof, total), bf16),
-            in_specs=[vmem] * (2 + peers),
+            in_specs=[vmem] * (3 + peers),
             out_specs=pl.BlockSpec(memory_space=pl.ANY),
             scratch_shapes=[pltpu.VMEM((steps, count, dof, tile), bf16), pltpu.SemaphoreType.DMA((steps,))],
             compiler_params=pltpu.CompilerParams(vmem_limit_bytes=VMEM_LIMIT),
             cost_estimate=pl.CostEstimate(flops=2 * count * total * dof * dof * (peers - 1),
                                           bytes_accessed=count * dof * total * 8, transcendentals=0),
             name="update",
-        )(ready, factors, block_inverse, *others)
+        )(ready, factors, block_inverse, spread, *others)
     return result[None]
 
 

time: 33.8 us -> 33.7 us (level)
  no operation moved by 1% of the time
where the time goes in v21:
time: 33.7 us; the launch traced here: 33.5 us
  Pallas kernels  13 us (39%)
  starting transfers between devices  12.4 us (37%)
  waiting for transfers between devices  4.67 us (14%)
  local copies, waits for them, and re-layouts  2.58 us (8%)
  between operations  0.79 us (2%)
    pallas_call x1, Pallas kernels, body(): pl.pallas_call(functools.partial(couple_kernel, shards, peers, deep), gri...  10.4 us
    ppermute x4, starting transfers between devices, body(): lax.ppermute(cross, ('space', 'row'), [(i * 2 + r, (i + d) % shards * 2 +...  5.62 us
    ppermute x1, starting transfers between devices, body(): lax.ppermute(current, 'inst', [(i, (i + d) % peers) for i in range(peers)])  2.94 us
    unnamed x20, local copies, waits for them, and re-layouts  2.58 us
    ppermute x1, waiting for transfers between devices, body(): lax.ppermute(current, 'inst', [(i, (i + d) % peers) for i in range(peers)])  2.5 us
    ppermute x1, starting transfers between devices, body(): lax.ppermute(down, 'space', [(i, (i - 1) % shards) for i in range(shards)])  2.25 us
    ppermute x4, waiting for transfers between devices, body(): lax.ppermute(cross, ('space', 'row'), [(i * 2 + r, (i + d) % shards * 2 +...  2.16 us
    pallas_call x1, Pallas kernels, body(): pl.pallas_call(functools.partial(update_kernel, tile, deep), out_shape=ja...  1.62 us
  transfers between devices with their start and end apart: 7, of which 3 were waited for; matrix products, arithmetic and copies ran while one was open for 4% of the time, Pallas kernels for 34%

profile of v21, /device:TPU:0, one launch (start us, length us, event | category | flops | bytes accessed | tf_op | source)
XLA Modules:
  0.0 33.5 jit_solution(17800287085983461045)
XLA Ops:
  0.0 2.9 %collective-permute-start.6 = (bf16[2,320,1024]{2,1,0:T(8,128)(2,1)}, bf16[2,320,1024]{2,1,0:T(8,128)(2,1)S(1)}, u32[]{:S(2)}, u32[]{:S(2)}) collective-permute-start(bf16[2,320,1024]{2,1,0:T(8,128)(2,1)} %bitcast.10), channel_id=1, source_target_pairs={{0,2},{2,0},{1,3},{3,1},{4,6},{6,4},{5,7},{7,5},{8,10},{10,8},{9,1... | collective-permute-start | bytes 3932168 | tf_op jit(solution)/shard_map/instances/ppermute | solution.py:183
  2.9 1.2 %copy.13.trace_ref = bf16[480,320]{1,0:T(8,128)(2,1)S(1)} copy(bf16[480,320]{0,1:T(8,128)(2,1)} %param.18) | data formatting | bytes 614400 | tf_op args[7]
  4.2 0.1 pad_add_fusion.place_ref
  4.2 0.0 copy-start
  4.2 1.3 %copy-done = bf16[1,2,320,1024]{3,2,1,0:T(8,128)(2,1)S(1)} copy-done((bf16[1,2,320,1024]{3,2,1,0:T(8,128)(2,1)S(1)}, bf16[1,2,320,1024]{3,2,1,0:T(8,128)(2,1)}, u32[]{:S(2)}) %copy-start) | copy-done | bytes 1310744
  5.6 0.0 copy-start.8
  5.6 0.0 copy-start.1
  5.6 0.0 copy-start.2
  5.6 0.0 copy-start.3
  5.6 0.0 copy-start.4
  5.6 0.0 copy-start.5
  5.6 0.0 copy-start.6
  5.6 0.0 copy-start.7
  5.6 1.0 %ends.1 = (bf16[2,160,64]{2,1,0:T(8,128)(2,1)S(1)}, bf16[2,160,64]{2,1,0:T(8,128)(2,1)S(1)}, bf16[2,80,64]{2,1,0:T(8,128)(2,1)S(1)}) custom-call(s32[3]{0:T(128)S(1)} %pad_add_fusion.place_ref, bf16[2,320,1024]{2,1,0:T(8,128)(2,1)S(1)} %bitcast.11, bf16[2,320,1024]{2,1,0:T(8,128)(2,1)S(1)} %bitcast.12, bf16[480,320]{1,0:T(8,128)(2,1)S(1)} %copy.13.trace_ref), custom_call_target="tpu_custom_call" | custom-call | flops 104857600 | bytes 1000000 | tf_op jit(solution)/shard_map/ends/ends/pallas_call | solution.py:187
  6.6 2.8 %collective-permute-start.5 = (bf16[2,80,64]{2,1,0:T(8,128)(2,1)S(1)}, bf16[2,80,64]{2,1,0:T(8,128)(2,1)S(1)}, u32[]{:S(2)}, u32[]{:S(2)}) collective-permute-start(bf16[2,80,64]{2,1,0:T(8,128)(2,1)S(1)} %get-tuple-element.13), channel_id=1, source_target_pairs={{0,13},{1,12},{4,1},{5,0},{8,5},{9,4},{12,9},{13,8},{2,15},{3,14},... | collective-permute-start | bytes 61448 | tf_op jit(solution)/shard_map/interface/ppermute | solution.py:210
  9.5 0.0 collective-permute-start.4
  9.5 1.6 %collective-permute-start = (bf16[2,160,64]{2,1,0:T(8,128)(2,1)S(1)}, bf16[2,160,64]{2,1,0:T(8,128)(2,1)S(1)}, u32[]{:S(2)}, u32[]{:S(2)}) collective-permute-start(bf16[2,160,64]{2,1,0:T(8,128)(2,1)S(1)} %get-tuple-element.11), channel_id=1, source_target_pairs={{0,4},{4,8},{8,12},{12,0},{1,5},{5,9},{9,13},{13,1},{2,6},{6,10},{... | collective-permute-start | bytes 122888 | tf_op jit(solution)/shard_map/halo/ppermute | solution.py:207
  11.0 2.2 %collective-permute-start.1 = (bf16[2,160,64]{2,1,0:T(8,128)(2,1)S(1)}, bf16[2,160,64]{2,1,0:T(8,128)(2,1)S(1)}, u32[]{:S(2)}, u32[]{:S(2)}) collective-permute-start(bf16[2,160,64]{2,1,0:T(8,128)(2,1)S(1)} %get-tuple-element.12), channel_id=1, source_target_pairs={{0,12},{4,0},{8,4},{12,8},{1,13},{5,1},{9,5},{13,9},{2,14},{6,2},{... | collective-permute-start | bytes 122888 | tf_op jit(solution)/shard_map/halo/ppermute | solution.py:208
  13.3 0.0 collective-permute-done.5.rest_3_
  13.3 0.0 collective-permute-start.3
  13.3 0.6 %collective-permute-done.4.rest_2_ = bf16[2,80,64]{2,1,0:T(8,128)(2,1)S(1)} collective-permute-done((bf16[2,80,64]{2,1,0:T(8,128)(2,1)S(1)}, bf16[2,80,64]{2,1,0:T(8,128)(2,1)S(1)}, u32[]{:S(2)}, u32[]{:S(2)}) %collective-permute-start.4) | collective-permute-done | bytes 20512 | tf_op jit(solution)/shard_map/interface/ppermute | solution.py:210
  13.9 2.8 %collective-permute-start.2 = (bf16[2,80,64]{2,1,0:T(8,128)(2,1)S(1)}, bf16[2,80,64]{2,1,0:T(8,128)(2,1)S(1)}, u32[]{:S(2)}, u32[]{:S(2)}) collective-permute-start(bf16[2,80,64]{2,1,0:T(8,128)(2,1)S(1)} %get-tuple-element.13), channel_id=1, source_target_pairs={{0,1},{1,0},{4,5},{5,4},{8,9},{9,8},{12,13},{13,12},{2,3},{3,2},{6... | collective-permute-start | bytes 61448 | tf_op jit(solution)/shard_map/interface/ppermute | solution.py:210
  17.4 0.0 copy-done.8
  17.4 1.5 %collective-permute-done.3.rest_1_ = bf16[2,80,64]{2,1,0:T(8,128)(2,1)S(1)} collective-permute-done((bf16[2,80,64]{2,1,0:T(8,128)(2,1)S(1)}, bf16[2,80,64]{2,1,0:T(8,128)(2,1)S(1)}, u32[]{:S(2)}, u32[]{:S(2)}) %collective-permute-start.3) | collective-permute-done | bytes 20512 | tf_op jit(solution)/shard_map/interface/ppermute | solution.py:210
  18.9 0.0 collective-permute-done.2.rest_0_
  18.9 0.0 collective-permute-done.low_ref
  18.9 0.0 collective-permute-done.1.high_ref
  18.9 0.0 copy-done.1
  18.9 0.0 copy-done.2
  19.0 0.0 copy-done.3
  19.0 0.0 copy-done.4
  19.0 0.0 copy-done.5
  19.0 0.0 copy-done.6
  19.0 0.0 copy-done.7
  19.0 10.4 %couple.1 = (f32[2,320,1024]{2,1,0:T(8,128)S(1)}, f32[4,1024]{1,0:T(4,128)S(1)}, bf16[2,320,128]{2,1,0:T(8,128)(2,1)S(1)}) custom-call(s32[3]{0:T(128)S(1)} %pad_add_fusion.place_ref, f32[1]{0:T(128)S(6)} %copy.17.freq_ref, f32[4,4]{1,0:T(4,128)S(1)} %copy-done.7, s32[6,1024]{1,0:T(8,128)S(1)} %bitcast.15, s32[2,64]{1,0:T(2,128)S(1)} %bitcast.17, ...), custom_call_target="tpu_custom_call" | custom-call | flops 3690987520 | bytes 6553600 | tf_op jit(solution)/shard_map/couple/couple/pallas_call | solution.py:219
  29.4 2.5 %collective-permute-done.6.rest_0_ = bf16[2,320,1024]{2,1,0:T(8,128)(2,1)S(1)} collective-permute-done((bf16[2,320,1024]{2,1,0:T(8,128)(2,1)}, bf16[2,320,1024]{2,1,0:T(8,128)(2,1)S(1)}, u32[]{:S(2)}, u32[]{:S(2)}) %collective-permute-start.6) | collective-permute-done | bytes 1310752 | tf_op jit(solution)/shard_map/instances/ppermute | solution.py:183
  31.9 1.6 %update.1 = bf16[2,320,1024]{2,1,0:T(8,128)(2,1)} custom-call(f32[2,320,1024]{2,1,0:T(8,128)S(1)} %get-tuple-element.14.ready_ref, f32[4,1024]{1,0:T(4,128)S(1)} %get-tuple-element.15.factor_ref, bf16[320,320]{1,0:T(8,128)(2,1)S(1)} %copy-done.1, bf16[2,320,128]{2,1,0:T(8,128)(2,1)S(1)} %get-tuple-element.16.spread_ref, ...), custom_call_target="tpu_custom_call" | custom-call | flops 419430400 | bytes 5242880 | tf_op jit(solution)/shard_map/update/update/pallas_call | solution.py:241
  (1 shorter events, 0.0 us)
Async XLA Ops:
  0.0 31.9 %collective-permute-start.6 = (bf16[2,320,1024]{2,1,0:T(8,128)(2,1)}, bf16[2,320,1024]{2,1,0:T(8,128)(2,1)S(1)}, u32[]{:S(2)}, u32[]{:S(2)}) collective-permute-start(bf16[2,320,1024]{2,1,0:T(8,128)(2,1)} %bitcast.10), channel_id=1, source_target_pairs={{0,2},{2,0},{1,3},{3,1},{4,6},{6,4},{5,7},{7,5},{8,10},{10,8},{9,1... | collective-permute-start | bytes 3932168 | tf_op jit(solution)/shard_map/instances/ppermute | solution.py:183
  4.2 1.3 %copy-start = (bf16[1,2,320,1024]{3,2,1,0:T(8,128)(2,1)S(1)}, bf16[1,2,320,1024]{3,2,1,0:T(8,128)(2,1)}, u32[]{:S(2)}) copy-start(bf16[1,2,320,1024]{3,2,1,0:T(8,128)(2,1)} %param.11) | copy-start | bytes 3932164
  5.6 11.8 %copy-start.8 = (s32[1,6,1024]{2,0,1:T(1,128)S(1)}, s32[1,6,1024]{2,0,1:T(1,128)}, u32[]{:S(2)}) copy-start(s32[1,6,1024]{2,0,1:T(1,128)} %param.15) | copy-start | bytes 73732
  5.6 13.4 %copy-start.1 = (bf16[320,320]{1,0:T(8,128)(2,1)S(1)}, bf16[320,320]{1,0:T(8,128)(2,1)}, u32[]{:S(2)}) copy-start(bf16[320,320]{1,0:T(8,128)(2,1)} %inverse_ref.3) | copy-start | bytes 614404
  5.6 13.4 %copy-start.2 = (bf16[1,2,320,1024]{3,2,1,0:T(8,128)(2,1)S(1)}, bf16[1,2,320,1024]{3,2,1,0:T(8,128)(2,1)}, u32[]{:S(2)}) copy-start(bf16[1,2,320,1024]{3,2,1,0:T(8,128)(2,1)} %param.12) | copy-start | bytes 3932164
  5.6 13.4 %copy-start.3 = (bf16[320,480]{1,0:T(8,128)(2,1)S(1)}, bf16[320,480]{1,0:T(8,128)(2,1)}, u32[]{:S(2)}) copy-start(bf16[320,480]{1,0:T(8,128)(2,1)} %lift_ref.1) | copy-start | bytes 921604
  5.6 13.4 %copy-start.4 = (bf16[320,320]{1,0:T(8,128)(2,1)S(1)}, bf16[320,320]{1,0:T(8,128)(2,1)}, u32[]{:S(2)}) copy-start(bf16[320,320]{1,0:T(8,128)(2,1)} %volume_ref.1) | copy-start | bytes 614404
  5.6 13.4 %copy-start.5 = (f32[1,1024]{1,0:T(1,128)S(1)}, f32[1,1024]{1,0:T(1,128)}, u32[]{:S(2)}) copy-start(f32[1,1024]{1,0:T(1,128)} %scale_ref.1) | copy-start | bytes 12292
  5.6 13.4 %copy-start.6 = (s32[1,2,64]{2,1,0:T(2,128)S(1)}, s32[1,2,64]{2,1,0:T(2,128)}, u32[]{:S(2)}) copy-start(s32[1,2,64]{2,1,0:T(2,128)} %param.16) | copy-start | bytes 1540
  5.6 13.4 %copy-start.7 = (f32[4,4]{1,0:T(4,128)S(1)}, f32[4,4]{1,0:T(4,128)}, u32[]{:S(2)}) copy-start(f32[4,4]{1,0:T(4,128)} %constant.13.clone.table_ref) | copy-start | bytes 196
  6.6 6.6 %collective-permute-start.5 = (bf16[2,80,64]{2,1,0:T(8,128)(2,1)S(1)}, bf16[2,80,64]{2,1,0:T(8,128)(2,1)S(1)}, u32[]{:S(2)}, u32[]{:S(2)}) collective-permute-start(bf16[2,80,64]{2,1,0:T(8,128)(2,1)S(1)} %get-tuple-element.13), channel_id=1, source_target_pairs={{0,13},{1,12},{4,1},{5,0},{8,5},{9,4},{12,9},{13,8},{2,15},{3,14},... | collective-permute-start | bytes 61448 | tf_op jit(solution)/shard_map/interface/ppermute | solution.py:210
  9.5 4.5 %collective-permute-start.4 = (bf16[2,80,64]{2,1,0:T(8,128)(2,1)S(1)}, bf16[2,80,64]{2,1,0:T(8,128)(2,1)S(1)}, u32[]{:S(2)}, u32[]{:S(2)}) collective-permute-start(bf16[2,80,64]{2,1,0:T(8,128)(2,1)S(1)} %get-tuple-element.13), channel_id=1, source_target_pairs={{0,9},{1,8},{4,13},{5,12},{8,1},{9,0},{12,5},{13,4},{2,11},{3,10},... | collective-permute-start | bytes 61448 | tf_op jit(solution)/shard_map/interface/ppermute | solution.py:210
  9.5 9.5 %collective-permute-start = (bf16[2,160,64]{2,1,0:T(8,128)(2,1)S(1)}, bf16[2,160,64]{2,1,0:T(8,128)(2,1)S(1)}, u32[]{:S(2)}, u32[]{:S(2)}) collective-permute-start(bf16[2,160,64]{2,1,0:T(8,128)(2,1)S(1)} %get-tuple-element.11), channel_id=1, source_target_pairs={{0,4},{4,8},{8,12},{12,0},{1,5},{5,9},{9,13},{13,1},{2,6},{6,10},{... | collective-permute-start | bytes 122888 | tf_op jit(solution)/shard_map/halo/ppermute | solution.py:207
  11.0 7.9 %collective-permute-start.1 = (bf16[2,160,64]{2,1,0:T(8,128)(2,1)S(1)}, bf16[2,160,64]{2,1,0:T(8,128)(2,1)S(1)}, u32[]{:S(2)}, u32[]{:S(2)}) collective-permute-start(bf16[2,160,64]{2,1,0:T(8,128)(2,1)S(1)} %get-tuple-element.12), channel_id=1, source_target_pairs={{0,12},{4,0},{8,4},{12,8},{1,13},{5,1},{9,5},{13,9},{2,14},{6,2},{... | collective-permute-start | bytes 122888 | tf_op jit(solution)/shard_map/halo/ppermute | solution.py:208
  13.3 5.6 %collective-permute-start.3 = (bf16[2,80,64]{2,1,0:T(8,128)(2,1)S(1)}, bf16[2,80,64]{2,1,0:T(8,128)(2,1)S(1)}, u32[]{:S(2)}, u32[]{:S(2)}) collective-permute-start(bf16[2,80,64]{2,1,0:T(8,128)(2,1)S(1)} %get-tuple-element.13), channel_id=1, source_target_pairs={{0,5},{1,4},{4,9},{5,8},{8,13},{9,12},{12,1},{13,0},{2,7},{3,6},{6... | collective-permute-start | bytes 61448 | tf_op jit(solution)/shard_map/interface/ppermute | solution.py:210
  13.9 5.0 %collective-permute-start.2 = (bf16[2,80,64]{2,1,0:T(8,128)(2,1)S(1)}, bf16[2,80,64]{2,1,0:T(8,128)(2,1)S(1)}, u32[]{:S(2)}, u32[]{:S(2)}) collective-permute-start(bf16[2,80,64]{2,1,0:T(8,128)(2,1)S(1)} %get-tuple-element.13), channel_id=1, source_target_pairs={{0,1},{1,0},{4,5},{5,4},{8,9},{9,8},{12,13},{13,12},{2,3},{3,2},{6... | collective-permute-start | bytes 61448 | tf_op jit(solution)/shard_map/interface/ppermute | solution.py:210

commit v22 on v21

--- a/solution.py
+++ b/solution.py
@@ -137,21 +137,23 @@
 def update_kernel(tile, deep, ready_ref, factor_ref, inverse_ref, spread_ref, *rest):
     others, (out_ref, made, sems) = rest[:-3], rest[-3:]
     count, dof, total = ready_ref.shape
+    pieces = [(0, slice(0, dof // 2)), (0, slice(dof // 2, dof))]
+    pieces += [(t, slice(0, dof)) for t in range(1, total // tile)]
     copies = []
-    for t in range(total // tile):
+    for p, (t, rows) in enumerate(pieces):
         cols = slice(t * tile, (t + 1) * tile)
         moved = []
         for other in others:
             stack = jnp.concatenate([other[m, deep:, cols] for m in range(count)], axis=0)
             for m in range(count):
-                moved.append(dot(inverse_ref[:, :deep], other[m, :deep, cols]) + dot(spread_ref[m], stack))
-        for n in range(count):
-            value = ready_ref[n, :, cols]
+                moved.append(dot(inverse_ref[rows, :deep], other[m, :deep, cols]) + dot(spread_ref[m, rows, :], stack))
+        for n in range(count):
+            value = ready_ref[n, rows, cols]
             for k, part in enumerate(moved):
                 at = n * len(moved) + k
                 value -= factor_ref[at : at + 1, cols] * part
-            made[t, n] = value.astype(jnp.bfloat16)
-        copy = pltpu.make_async_copy(made.at[t], out_ref.at[:, :, cols], sems.at[t])
+            made[t, n, rows, :] = value.astype(jnp.bfloat16)
+        copy = pltpu.make_async_copy(made.at[t, :, rows, :], out_ref.at[:, rows, cols], sems.at[p])
         copy.start()
         copies.append(copy)
     for copy in copies:
@@ -243,7 +245,7 @@
             out_shape=jax.ShapeDtypeStruct((count, dof, total), bf16),
             in_specs=[vmem] * (3 + peers),
             out_specs=pl.BlockSpec(memory_space=pl.ANY),
-            scratch_shapes=[pltpu.VMEM((steps, count, dof, tile), bf16), pltpu.SemaphoreType.DMA((steps,))],
+            scratch_shapes=[pltpu.VMEM((steps, count, dof, tile), bf16), pltpu.SemaphoreType.DMA((steps + 1,))],
             compiler_params=pltpu.CompilerParams(vmem_limit_bytes=VMEM_LIMIT),
             cost_estimate=pl.CostEstimate(flops=2 * count * total * dof * dof * (peers - 1),
                                           bytes_accessed=count * dof * total * 8, transcendentals=0),

time: 33.7 us -> 34.1 us (1.012)
  Pallas kernels: 13 us -> 13.4 us
where the time goes in v22:
time: 34.1 us; the launch traced here: 33.9 us
  Pallas kernels  13.4 us (39%)
  starting transfers between devices  12.4 us (36%)
  waiting for transfers between devices  4.67 us (14%)
  local copies, waits for them, and re-layouts  2.58 us (8%)
  between operations  0.79 us (2%)
    pallas_call x1, Pallas kernels, body(): pl.pallas_call(functools.partial(couple_kernel, shards, peers, deep), gri...  10.4 us
    ppermute x4, starting transfers between devices, body(): lax.ppermute(cross, ('space', 'row'), [(i * 2 + r, (i + d) % shards * 2 +...  5.62 us
    ppermute x1, starting transfers between devices, body(): lax.ppermute(current, 'inst', [(i, (i + d) % peers) for i in range(peers)])  2.94 us
    unnamed x20, local copies, waits for them, and re-layouts  2.58 us
    ppermute x1, waiting for transfers between devices, body(): lax.ppermute(current, 'inst', [(i, (i + d) % peers) for i in range(peers)])  2.5 us
    ppermute x1, starting transfers between devices, body(): lax.ppermute(down, 'space', [(i, (i - 1) % shards) for i in range(shards)])  2.25 us
    ppermute x4, waiting for transfers between devices, body(): lax.ppermute(cross, ('space', 'row'), [(i * 2 + r, (i + d) % shards * 2 +...  2.16 us
    pallas_call x1, Pallas kernels, body(): pl.pallas_call(functools.partial(update_kernel, tile, deep), out_shape=ja...  1.95 us
  transfers between devices with their start and end apart: 7, of which 3 were waited for; matrix products, arithmetic and copies ran while one was open for 4% of the time, Pallas kernels for 34%

profile of v22, /device:TPU:0, one launch (start us, length us, event | category | flops | bytes accessed | tf_op | source)
XLA Modules:
  0.0 33.9 jit_solution(1053903051932073402)
XLA Ops:
  0.0 2.9 %collective-permute-start.6 = (bf16[2,320,1024]{2,1,0:T(8,128)(2,1)}, bf16[2,320,1024]{2,1,0:T(8,128)(2,1)S(1)}, u32[]{:S(2)}, u32[]{:S(2)}) collective-permute-start(bf16[2,320,1024]{2,1,0:T(8,128)(2,1)} %bitcast.10), channel_id=1, source_target_pairs={{0,2},{2,0},{1,3},{3,1},{4,6},{6,4},{5,7},{7,5},{8,10},{10,8},{9,1... | collective-permute-start | bytes 3932168 | tf_op jit(solution)/shard_map/instances/ppermute | solution.py:185
  2.9 1.2 %copy.13.trace_ref = bf16[480,320]{1,0:T(8,128)(2,1)S(1)} copy(bf16[480,320]{0,1:T(8,128)(2,1)} %param.18) | data formatting | bytes 614400 | tf_op args[7]
  4.2 0.1 pad_add_fusion.place_ref
  4.2 0.0 copy-start
  4.2 1.3 %copy-done = bf16[1,2,320,1024]{3,2,1,0:T(8,128)(2,1)S(1)} copy-done((bf16[1,2,320,1024]{3,2,1,0:T(8,128)(2,1)S(1)}, bf16[1,2,320,1024]{3,2,1,0:T(8,128)(2,1)}, u32[]{:S(2)}) %copy-start) | copy-done | bytes 1310744
  5.6 0.0 copy-start.8
  5.6 0.0 copy-start.1
  5.6 0.0 copy-start.2
  5.6 0.0 copy-start.3
  5.6 0.0 copy-start.4
  5.6 0.0 copy-start.5
  5.6 0.0 copy-start.6
  5.6 0.0 copy-start.7
  5.6 1.0 %ends.1 = (bf16[2,160,64]{2,1,0:T(8,128)(2,1)S(1)}, bf16[2,160,64]{2,1,0:T(8,128)(2,1)S(1)}, bf16[2,80,64]{2,1,0:T(8,128)(2,1)S(1)}) custom-call(s32[3]{0:T(128)S(1)} %pad_add_fusion.place_ref, bf16[2,320,1024]{2,1,0:T(8,128)(2,1)S(1)} %bitcast.11, bf16[2,320,1024]{2,1,0:T(8,128)(2,1)S(1)} %bitcast.12, bf16[480,320]{1,0:T(8,128)(2,1)S(1)} %copy.13.trace_ref), custom_call_target="tpu_custom_call" | custom-call | flops 104857600 | bytes 1000000 | tf_op jit(solution)/shard_map/ends/ends/pallas_call | solution.py:189
  6.6 2.8 %collective-permute-start.5 = (bf16[2,80,64]{2,1,0:T(8,128)(2,1)S(1)}, bf16[2,80,64]{2,1,0:T(8,128)(2,1)S(1)}, u32[]{:S(2)}, u32[]{:S(2)}) collective-permute-start(bf16[2,80,64]{2,1,0:T(8,128)(2,1)S(1)} %get-tuple-element.13), channel_id=1, source_target_pairs={{0,13},{1,12},{4,1},{5,0},{8,5},{9,4},{12,9},{13,8},{2,15},{3,14},... | collective-permute-start | bytes 61448 | tf_op jit(solution)/shard_map/interface/ppermute | solution.py:212
  9.5 0.0 collective-permute-start.4
  9.5 1.6 %collective-permute-start = (bf16[2,160,64]{2,1,0:T(8,128)(2,1)S(1)}, bf16[2,160,64]{2,1,0:T(8,128)(2,1)S(1)}, u32[]{:S(2)}, u32[]{:S(2)}) collective-permute-start(bf16[2,160,64]{2,1,0:T(8,128)(2,1)S(1)} %get-tuple-element.11), channel_id=1, source_target_pairs={{0,4},{4,8},{8,12},{12,0},{1,5},{5,9},{9,13},{13,1},{2,6},{6,10},{... | collective-permute-start | bytes 122888 | tf_op jit(solution)/shard_map/halo/ppermute | solution.py:209
  11.0 2.2 %collective-permute-start.1 = (bf16[2,160,64]{2,1,0:T(8,128)(2,1)S(1)}, bf16[2,160,64]{2,1,0:T(8,128)(2,1)S(1)}, u32[]{:S(2)}, u32[]{:S(2)}) collective-permute-start(bf16[2,160,64]{2,1,0:T(8,128)(2,1)S(1)} %get-tuple-element.12), channel_id=1, source_target_pairs={{0,12},{4,0},{8,4},{12,8},{1,13},{5,1},{9,5},{13,9},{2,14},{6,2},{... | collective-permute-start | bytes 122888 | tf_op jit(solution)/shard_map/halo/ppermute | solution.py:210
  13.3 0.0 collective-permute-done.5.rest_3_
  13.3 0.0 collective-permute-start.3
  13.3 0.6 %collective-permute-done.4.rest_2_ = bf16[2,80,64]{2,1,0:T(8,128)(2,1)S(1)} collective-permute-done((bf16[2,80,64]{2,1,0:T(8,128)(2,1)S(1)}, bf16[2,80,64]{2,1,0:T(8,128)(2,1)S(1)}, u32[]{:S(2)}, u32[]{:S(2)}) %collective-permute-start.4) | collective-permute-done | bytes 20512 | tf_op jit(solution)/shard_map/interface/ppermute | solution.py:212
  13.9 2.8 %collective-permute-start.2 = (bf16[2,80,64]{2,1,0:T(8,128)(2,1)S(1)}, bf16[2,80,64]{2,1,0:T(8,128)(2,1)S(1)}, u32[]{:S(2)}, u32[]{:S(2)}) collective-permute-start(bf16[2,80,64]{2,1,0:T(8,128)(2,1)S(1)} %get-tuple-element.13), channel_id=1, source_target_pairs={{0,1},{1,0},{4,5},{5,4},{8,9},{9,8},{12,13},{13,12},{2,3},{3,2},{6... | collective-permute-start | bytes 61448 | tf_op jit(solution)/shard_map/interface/ppermute | solution.py:212
  17.4 0.0 copy-done.8
  17.4 1.5 %collective-permute-done.3.rest_1_ = bf16[2,80,64]{2,1,0:T(8,128)(2,1)S(1)} collective-permute-done((bf16[2,80,64]{2,1,0:T(8,128)(2,1)S(1)}, bf16[2,80,64]{2,1,0:T(8,128)(2,1)S(1)}, u32[]{:S(2)}, u32[]{:S(2)}) %collective-permute-start.3) | collective-permute-done | bytes 20512 | tf_op jit(solution)/shard_map/interface/ppermute | solution.py:212
  18.9 0.0 collective-permute-done.2.rest_0_
  18.9 0.0 collective-permute-done.low_ref
  18.9 0.0 collective-permute-done.1.high_ref
  18.9 0.0 copy-done.1
  18.9 0.0 copy-done.2
  19.0 0.0 copy-done.3
  19.0 0.0 copy-done.4
  19.0 0.0 copy-done.5
  19.0 0.0 copy-done.6
  19.0 0.0 copy-done.7
  19.0 10.4 %couple.1 = (f32[2,320,1024]{2,1,0:T(8,128)S(1)}, f32[4,1024]{1,0:T(4,128)S(1)}, bf16[2,320,128]{2,1,0:T(8,128)(2,1)S(1)}) custom-call(s32[3]{0:T(128)S(1)} %pad_add_fusion.place_ref, f32[1]{0:T(128)S(6)} %copy.17.freq_ref, f32[4,4]{1,0:T(4,128)S(1)} %copy-done.7, s32[6,1024]{1,0:T(8,128)S(1)} %bitcast.15, s32[2,64]{1,0:T(2,128)S(1)} %bitcast.17, ...), custom_call_target="tpu_custom_call" | custom-call | flops 3690987520 | bytes 6553600 | tf_op jit(solution)/shard_map/couple/couple/pallas_call | solution.py:221
  29.4 2.5 %collective-permute-done.6.rest_0_ = bf16[2,320,1024]{2,1,0:T(8,128)(2,1)S(1)} collective-permute-done((bf16[2,320,1024]{2,1,0:T(8,128)(2,1)}, bf16[2,320,1024]{2,1,0:T(8,128)(2,1)S(1)}, u32[]{:S(2)}, u32[]{:S(2)}) %collective-permute-start.6) | collective-permute-done | bytes 1310752 | tf_op jit(solution)/shard_map/instances/ppermute | solution.py:185
  31.9 2.0 %update.1 = bf16[2,320,1024]{2,1,0:T(8,128)(2,1)} custom-call(f32[2,320,1024]{2,1,0:T(8,128)S(1)} %get-tuple-element.14.ready_ref, f32[4,1024]{1,0:T(4,128)S(1)} %get-tuple-element.15.factor_ref, bf16[320,320]{1,0:T(8,128)(2,1)S(1)} %copy-done.1, bf16[2,320,128]{2,1,0:T(8,128)(2,1)S(1)} %get-tuple-element.16.spread_ref, ...), custom_call_target="tpu_custom_call" | custom-call | flops 419430400 | bytes 5242880 | tf_op jit(solution)/shard_map/update/update/pallas_call | solution.py:243
  (1 shorter events, 0.0 us)
Async XLA Ops:
  0.0 31.9 %collective-permute-start.6 = (bf16[2,320,1024]{2,1,0:T(8,128)(2,1)}, bf16[2,320,1024]{2,1,0:T(8,128)(2,1)S(1)}, u32[]{:S(2)}, u32[]{:S(2)}) collective-permute-start(bf16[2,320,1024]{2,1,0:T(8,128)(2,1)} %bitcast.10), channel_id=1, source_target_pairs={{0,2},{2,0},{1,3},{3,1},{4,6},{6,4},{5,7},{7,5},{8,10},{10,8},{9,1... | collective-permute-start | bytes 3932168 | tf_op jit(solution)/shard_map/instances/ppermute | solution.py:185
  4.2 1.3 %copy-start = (bf16[1,2,320,1024]{3,2,1,0:T(8,128)(2,1)S(1)}, bf16[1,2,320,1024]{3,2,1,0:T(8,128)(2,1)}, u32[]{:S(2)}) copy-start(bf16[1,2,320,1024]{3,2,1,0:T(8,128)(2,1)} %param.11) | copy-start | bytes 3932164
  5.6 11.8 %copy-start.8 = (s32[1,6,1024]{2,0,1:T(1,128)S(1)}, s32[1,6,1024]{2,0,1:T(1,128)}, u32[]{:S(2)}) copy-start(s32[1,6,1024]{2,0,1:T(1,128)} %param.15) | copy-start | bytes 73732
  5.6 13.4 %copy-start.1 = (bf16[320,320]{1,0:T(8,128)(2,1)S(1)}, bf16[320,320]{1,0:T(8,128)(2,1)}, u32[]{:S(2)}) copy-start(bf16[320,320]{1,0:T(8,128)(2,1)} %inverse_ref.3) | copy-start | bytes 614404
  5.6 13.4 %copy-start.2 = (bf16[1,2,320,1024]{3,2,1,0:T(8,128)(2,1)S(1)}, bf16[1,2,320,1024]{3,2,1,0:T(8,128)(2,1)}, u32[]{:S(2)}) copy-start(bf16[1,2,320,1024]{3,2,1,0:T(8,128)(2,1)} %param.12) | copy-start | bytes 3932164
  5.6 13.4 %copy-start.3 = (bf16[320,480]{1,0:T(8,128)(2,1)S(1)}, bf16[320,480]{1,0:T(8,128)(2,1)}, u32[]{:S(2)}) copy-start(bf16[320,480]{1,0:T(8,128)(2,1)} %lift_ref.1) | copy-start | bytes 921604
  5.6 13.4 %copy-start.4 = (bf16[320,320]{1,0:T(8,128)(2,1)S(1)}, bf16[320,320]{1,0:T(8,128)(2,1)}, u32[]{:S(2)}) copy-start(bf16[320,320]{1,0:T(8,128)(2,1)} %volume_ref.1) | copy-start | bytes 614404
  5.6 13.4 %copy-start.5 = (f32[1,1024]{1,0:T(1,128)S(1)}, f32[1,1024]{1,0:T(1,128)}, u32[]{:S(2)}) copy-start(f32[1,1024]{1,0:T(1,128)} %scale_ref.1) | copy-start | bytes 12292
  5.6 13.4 %copy-start.6 = (s32[1,2,64]{2,1,0:T(2,128)S(1)}, s32[1,2,64]{2,1,0:T(2,128)}, u32[]{:S(2)}) copy-start(s32[1,2,64]{2,1,0:T(2,128)} %param.16) | copy-start | bytes 1540
  5.6 13.4 %copy-start.7 = (f32[4,4]{1,0:T(4,128)S(1)}, f32[4,4]{1,0:T(4,128)}, u32[]{:S(2)}) copy-start(f32[4,4]{1,0:T(4,128)} %constant.13.clone.table_ref) | copy-start | bytes 196
  6.6 6.6 %collective-permute-start.5 = (bf16[2,80,64]{2,1,0:T(8,128)(2,1)S(1)}, bf16[2,80,64]{2,1,0:T(8,128)(2,1)S(1)}, u32[]{:S(2)}, u32[]{:S(2)}) collective-permute-start(bf16[2,80,64]{2,1,0:T(8,128)(2,1)S(1)} %get-tuple-element.13), channel_id=1, source_target_pairs={{0,13},{1,12},{4,1},{5,0},{8,5},{9,4},{12,9},{13,8},{2,15},{3,14},... | collective-permute-start | bytes 61448 | tf_op jit(solution)/shard_map/interface/ppermute | solution.py:212
  9.5 4.5 %collective-permute-start.4 = (bf16[2,80,64]{2,1,0:T(8,128)(2,1)S(1)}, bf16[2,80,64]{2,1,0:T(8,128)(2,1)S(1)}, u32[]{:S(2)}, u32[]{:S(2)}) collective-permute-start(bf16[2,80,64]{2,1,0:T(8,128)(2,1)S(1)} %get-tuple-element.13), channel_id=1, source_target_pairs={{0,9},{1,8},{4,13},{5,12},{8,1},{9,0},{12,5},{13,4},{2,11},{3,10},... | collective-permute-start | bytes 61448 | tf_op jit(solution)/shard_map/interface/ppermute | solution.py:212
  9.5 9.5 %collective-permute-start = (bf16[2,160,64]{2,1,0:T(8,128)(2,1)S(1)}, bf16[2,160,64]{2,1,0:T(8,128)(2,1)S(1)}, u32[]{:S(2)}, u32[]{:S(2)}) collective-permute-start(bf16[2,160,64]{2,1,0:T(8,128)(2,1)S(1)} %get-tuple-element.11), channel_id=1, source_target_pairs={{0,4},{4,8},{8,12},{12,0},{1,5},{5,9},{9,13},{13,1},{2,6},{6,10},{... | collective-permute-start | bytes 122888 | tf_op jit(solution)/shard_map/halo/ppermute | solution.py:209
  11.0 7.9 %collective-permute-start.1 = (bf16[2,160,64]{2,1,0:T(8,128)(2,1)S(1)}, bf16[2,160,64]{2,1,0:T(8,128)(2,1)S(1)}, u32[]{:S(2)}, u32[]{:S(2)}) collective-permute-start(bf16[2,160,64]{2,1,0:T(8,128)(2,1)S(1)} %get-tuple-element.12), channel_id=1, source_target_pairs={{0,12},{4,0},{8,4},{12,8},{1,13},{5,1},{9,5},{13,9},{2,14},{6,2},{... | collective-permute-start | bytes 122888 | tf_op jit(solution)/shard_map/halo/ppermute | solution.py:210
  13.3 5.6 %collective-permute-start.3 = (bf16[2,80,64]{2,1,0:T(8,128)(2,1)S(1)}, bf16[2,80,64]{2,1,0:T(8,128)(2,1)S(1)}, u32[]{:S(2)}, u32[]{:S(2)}) collective-permute-start(bf16[2,80,64]{2,1,0:T(8,128)(2,1)S(1)} %get-tuple-element.13), channel_id=1, source_target_pairs={{0,5},{1,4},{4,9},{5,8},{8,13},{9,12},{12,1},{13,0},{2,7},{3,6},{6... | collective-permute-start | bytes 61448 | tf_op jit(solution)/shard_map/interface/ppermute | solution.py:212
  13.9 5.0 %collective-permute-start.2 = (bf16[2,80,64]{2,1,0:T(8,128)(2,1)S(1)}, bf16[2,80,64]{2,1,0:T(8,128)(2,1)S(1)}, u32[]{:S(2)}, u32[]{:S(2)}) collective-permute-start(bf16[2,80,64]{2,1,0:T(8,128)(2,1)S(1)} %get-tuple-element.13), channel_id=1, source_target_pairs={{0,1},{1,0},{4,5},{5,4},{8,9},{9,8},{12,13},{13,12},{2,3},{3,2},{6... | collective-permute-start | bytes 61448 | tf_op jit(solution)/shard_map/interface/ppermute | solution.py:212

commit v23 on v21

--- a/solution.py
+++ b/solution.py
@@ -135,21 +135,30 @@
 
 
 def update_kernel(tile, deep, ready_ref, factor_ref, inverse_ref, spread_ref, *rest):
-    others, (out_ref, made, sems) = rest[:-3], rest[-3:]
+    others, (out_ref, made, moved, sems) = rest[:-4], rest[-4:]
     count, dof, total = ready_ref.shape
+    products = len(others) * count
+    steps = total // tile
     copies = []
-    for t in range(total // tile):
+
+    def multiply(t):
         cols = slice(t * tile, (t + 1) * tile)
-        moved = []
-        for other in others:
+        for d, other in enumerate(others):
             stack = jnp.concatenate([other[m, deep:, cols] for m in range(count)], axis=0)
             for m in range(count):
-                moved.append(dot(inverse_ref[:, :deep], other[m, :deep, cols]) + dot(spread_ref[m], stack))
+                moved[t % 2, d * count + m] = (
+                    dot(inverse_ref[:, :deep], other[m, :deep, cols]) + dot(spread_ref[m], stack))
+
+    multiply(0)
+    for t in range(steps):
+        cols = slice(t * tile, (t + 1) * tile)
+        if t + 1 < steps:
+            multiply(t + 1)
         for n in range(count):
             value = ready_ref[n, :, cols]
-            for k, part in enumerate(moved):
-                at = n * len(moved) + k
-                value -= factor_ref[at : at + 1, cols] * part
+            for k in range(products):
+                at = n * products + k
+                value -= factor_ref[at : at + 1, cols] * moved[t % 2, k]
             made[t, n] = value.astype(jnp.bfloat16)
         copy = pltpu.make_async_copy(made.at[t], out_ref.at[:, :, cols], sems.at[t])
         copy.start()
@@ -243,7 +252,9 @@
             out_shape=jax.ShapeDtypeStruct((count, dof, total), bf16),
             in_specs=[vmem] * (3 + peers),
             out_specs=pl.BlockSpec(memory_space=pl.ANY),
-            scratch_shapes=[pltpu.VMEM((steps, count, dof, tile), bf16), pltpu.SemaphoreType.DMA((steps,))],
+            scratch_shapes=[pltpu.VMEM((steps, count, dof, tile), bf16),
+                            pltpu.VMEM((2, (peers - 1) * count, dof, tile), jnp.float32),
+                            pltpu.SemaphoreType.DMA((steps,))],
             compiler_params=pltpu.CompilerParams(vmem_limit_bytes=VMEM_LIMIT),
             cost_estimate=pl.CostEstimate(flops=2 * count * total * dof * dof * (peers - 1),
                                           bytes_accessed=count * dof * total * 8, transcendentals=0),

time: 33.7 us -> 33.7 us (level)
  no operation moved by 1% of the time
where the time goes in v23:
time: 33.7 us; the launch traced here: 33.5 us
  Pallas kernels  13 us (39%)
  starting transfers between devices  12.4 us (37%)
  waiting for transfers between devices  4.67 us (14%)
  local copies, waits for them, and re-layouts  2.58 us (8%)
  between operations  0.79 us (2%)
    pallas_call x1, Pallas kernels, body(): pl.pallas_call(functools.partial(couple_kernel, shards, peers, deep), gri...  10.4 us
    ppermute x4, starting transfers between devices, body(): lax.ppermute(cross, ('space', 'row'), [(i * 2 + r, (i + d) % shards * 2 +...  5.62 us
    ppermute x1, starting transfers between devices, body(): lax.ppermute(current, 'inst', [(i, (i + d) % peers) for i in range(peers)])  2.94 us
    unnamed x20, local copies, waits for them, and re-layouts  2.58 us
    ppermute x1, waiting for transfers between devices, body(): lax.ppermute(current, 'inst', [(i, (i + d) % peers) for i in range(peers)])  2.5 us
    ppermute x1, starting transfers between devices, body(): lax.ppermute(down, 'space', [(i, (i - 1) % shards) for i in range(shards)])  2.25 us
    ppermute x4, waiting for transfers between devices, body(): lax.ppermute(cross, ('space', 'row'), [(i * 2 + r, (i + d) % shards * 2 +...  2.16 us
    pallas_call x1, Pallas kernels, body(): pl.pallas_call(functools.partial(update_kernel, tile, deep), out_shape=ja...  1.62 us
  transfers between devices with their start and end apart: 7, of which 3 were waited for; matrix products, arithmetic and copies ran while one was open for 4% of the time, Pallas kernels for 34%

profile of v23, /device:TPU:0, one launch (start us, length us, event | category | flops | bytes accessed | tf_op | source)
XLA Modules:
  0.0 33.5 jit_solution(11669663289867143291)
XLA Ops:
  0.0 2.9 %collective-permute-start.6 = (bf16[2,320,1024]{2,1,0:T(8,128)(2,1)}, bf16[2,320,1024]{2,1,0:T(8,128)(2,1)S(1)}, u32[]{:S(2)}, u32[]{:S(2)}) collective-permute-start(bf16[2,320,1024]{2,1,0:T(8,128)(2,1)} %bitcast.10), channel_id=1, source_target_pairs={{0,2},{2,0},{1,3},{3,1},{4,6},{6,4},{5,7},{7,5},{8,10},{10,8},{9,1... | collective-permute-start | bytes 3932168 | tf_op jit(solution)/shard_map/instances/ppermute | solution.py:192
  2.9 1.2 %copy.13.trace_ref = bf16[480,320]{1,0:T(8,128)(2,1)S(1)} copy(bf16[480,320]{0,1:T(8,128)(2,1)} %param.18) | data formatting | bytes 614400 | tf_op args[7]
  4.2 0.1 pad_add_fusion.place_ref
  4.2 0.0 copy-start
  4.2 1.3 %copy-done = bf16[1,2,320,1024]{3,2,1,0:T(8,128)(2,1)S(1)} copy-done((bf16[1,2,320,1024]{3,2,1,0:T(8,128)(2,1)S(1)}, bf16[1,2,320,1024]{3,2,1,0:T(8,128)(2,1)}, u32[]{:S(2)}) %copy-start) | copy-done | bytes 1310744
  5.6 0.0 copy-start.8
  5.6 0.0 copy-start.1
  5.6 0.0 copy-start.2
  5.6 0.0 copy-start.3
  5.6 0.0 copy-start.4
  5.6 0.0 copy-start.5
  5.6 0.0 copy-start.6
  5.6 0.0 copy-start.7
  5.6 1.0 %ends.1 = (bf16[2,160,64]{2,1,0:T(8,128)(2,1)S(1)}, bf16[2,160,64]{2,1,0:T(8,128)(2,1)S(1)}, bf16[2,80,64]{2,1,0:T(8,128)(2,1)S(1)}) custom-call(s32[3]{0:T(128)S(1)} %pad_add_fusion.place_ref, bf16[2,320,1024]{2,1,0:T(8,128)(2,1)S(1)} %bitcast.11, bf16[2,320,1024]{2,1,0:T(8,128)(2,1)S(1)} %bitcast.12, bf16[480,320]{1,0:T(8,128)(2,1)S(1)} %copy.13.trace_ref), custom_call_target="tpu_custom_call" | custom-call | flops 104857600 | bytes 1000000 | tf_op jit(solution)/shard_map/ends/ends/pallas_call | solution.py:196
  6.6 2.8 %collective-permute-start.5 = (bf16[2,80,64]{2,1,0:T(8,128)(2,1)S(1)}, bf16[2,80,64]{2,1,0:T(8,128)(2,1)S(1)}, u32[]{:S(2)}, u32[]{:S(2)}) collective-permute-start(bf16[2,80,64]{2,1,0:T(8,128)(2,1)S(1)} %get-tuple-element.13), channel_id=1, source_target_pairs={{0,13},{1,12},{4,1},{5,0},{8,5},{9,4},{12,9},{13,8},{2,15},{3,14},... | collective-permute-start | bytes 61448 | tf_op jit(solution)/shard_map/interface/ppermute | solution.py:219
  9.5 0.0 collective-permute-start.4
  9.5 1.6 %collective-permute-start = (bf16[2,160,64]{2,1,0:T(8,128)(2,1)S(1)}, bf16[2,160,64]{2,1,0:T(8,128)(2,1)S(1)}, u32[]{:S(2)}, u32[]{:S(2)}) collective-permute-start(bf16[2,160,64]{2,1,0:T(8,128)(2,1)S(1)} %get-tuple-element.11), channel_id=1, source_target_pairs={{0,4},{4,8},{8,12},{12,0},{1,5},{5,9},{9,13},{13,1},{2,6},{6,10},{... | collective-permute-start | bytes 122888 | tf_op jit(solution)/shard_map/halo/ppermute | solution.py:216
  11.0 2.2 %collective-permute-start.1 = (bf16[2,160,64]{2,1,0:T(8,128)(2,1)S(1)}, bf16[2,160,64]{2,1,0:T(8,128)(2,1)S(1)}, u32[]{:S(2)}, u32[]{:S(2)}) collective-permute-start(bf16[2,160,64]{2,1,0:T(8,128)(2,1)S(1)} %get-tuple-element.12), channel_id=1, source_target_pairs={{0,12},{4,0},{8,4},{12,8},{1,13},{5,1},{9,5},{13,9},{2,14},{6,2},{... | collective-permute-start | bytes 122888 | tf_op jit(solution)/shard_map/halo/ppermute | solution.py:217
  13.3 0.0 collective-permute-done.5.rest_3_
  13.3 0.0 collective-permute-start.3
  13.3 0.6 %collective-permute-done.4.rest_2_ = bf16[2,80,64]{2,1,0:T(8,128)(2,1)S(1)} collective-permute-done((bf16[2,80,64]{2,1,0:T(8,128)(2,1)S(1)}, bf16[2,80,64]{2,1,0:T(8,128)(2,1)S(1)}, u32[]{:S(2)}, u32[]{:S(2)}) %collective-permute-start.4) | collective-permute-done | bytes 20512 | tf_op jit(solution)/shard_map/interface/ppermute | solution.py:219
  13.9 2.8 %collective-permute-start.2 = (bf16[2,80,64]{2,1,0:T(8,128)(2,1)S(1)}, bf16[2,80,64]{2,1,0:T(8,128)(2,1)S(1)}, u32[]{:S(2)}, u32[]{:S(2)}) collective-permute-start(bf16[2,80,64]{2,1,0:T(8,128)(2,1)S(1)} %get-tuple-element.13), channel_id=1, source_target_pairs={{0,1},{1,0},{4,5},{5,4},{8,9},{9,8},{12,13},{13,12},{2,3},{3,2},{6... | collective-permute-start | bytes 61448 | tf_op jit(solution)/shard_map/interface/ppermute | solution.py:219
  17.4 0.0 copy-done.8
  17.4 1.5 %collective-permute-done.3.rest_1_ = bf16[2,80,64]{2,1,0:T(8,128)(2,1)S(1)} collective-permute-done((bf16[2,80,64]{2,1,0:T(8,128)(2,1)S(1)}, bf16[2,80,64]{2,1,0:T(8,128)(2,1)S(1)}, u32[]{:S(2)}, u32[]{:S(2)}) %collective-permute-start.3) | collective-permute-done | bytes 20512 | tf_op jit(solution)/shard_map/interface/ppermute | solution.py:219
  18.9 0.0 collective-permute-done.2.rest_0_
  18.9 0.0 collective-permute-done.low_ref
  18.9 0.0 collective-permute-done.1.high_ref
  18.9 0.0 copy-done.1
  18.9 0.0 copy-done.2
  19.0 0.0 copy-done.3
  19.0 0.0 copy-done.4
  19.0 0.0 copy-done.5
  19.0 0.0 copy-done.6
  19.0 0.0 copy-done.7
  19.0 10.4 %couple.1 = (f32[2,320,1024]{2,1,0:T(8,128)S(1)}, f32[4,1024]{1,0:T(4,128)S(1)}, bf16[2,320,128]{2,1,0:T(8,128)(2,1)S(1)}) custom-call(s32[3]{0:T(128)S(1)} %pad_add_fusion.place_ref, f32[1]{0:T(128)S(6)} %copy.17.freq_ref, f32[4,4]{1,0:T(4,128)S(1)} %copy-done.7, s32[6,1024]{1,0:T(8,128)S(1)} %bitcast.15, s32[2,64]{1,0:T(2,128)S(1)} %bitcast.17, ...), custom_call_target="tpu_custom_call" | custom-call | flops 3690987520 | bytes 6553600 | tf_op jit(solution)/shard_map/couple/couple/pallas_call | solution.py:228
  29.4 2.5 %collective-permute-done.6.rest_0_ = bf16[2,320,1024]{2,1,0:T(8,128)(2,1)S(1)} collective-permute-done((bf16[2,320,1024]{2,1,0:T(8,128)(2,1)}, bf16[2,320,1024]{2,1,0:T(8,128)(2,1)S(1)}, u32[]{:S(2)}, u32[]{:S(2)}) %collective-permute-start.6) | collective-permute-done | bytes 1310752 | tf_op jit(solution)/shard_map/instances/ppermute | solution.py:192
  31.9 1.6 %update.1 = bf16[2,320,1024]{2,1,0:T(8,128)(2,1)} custom-call(f32[2,320,1024]{2,1,0:T(8,128)S(1)} %get-tuple-element.14.ready_ref, f32[4,1024]{1,0:T(4,128)S(1)} %get-tuple-element.15.factor_ref, bf16[320,320]{1,0:T(8,128)(2,1)S(1)} %copy-done.1, bf16[2,320,128]{2,1,0:T(8,128)(2,1)S(1)} %get-tuple-element.16.spread_ref, ...), custom_call_target="tpu_custom_call" | custom-call | flops 419430400 | bytes 5242880 | tf_op jit(solution)/shard_map/update/update/pallas_call | solution.py:250
  (1 shorter events, 0.0 us)
Async XLA Ops:
  0.0 31.9 %collective-permute-start.6 = (bf16[2,320,1024]{2,1,0:T(8,128)(2,1)}, bf16[2,320,1024]{2,1,0:T(8,128)(2,1)S(1)}, u32[]{:S(2)}, u32[]{:S(2)}) collective-permute-start(bf16[2,320,1024]{2,1,0:T(8,128)(2,1)} %bitcast.10), channel_id=1, source_target_pairs={{0,2},{2,0},{1,3},{3,1},{4,6},{6,4},{5,7},{7,5},{8,10},{10,8},{9,1... | collective-permute-start | bytes 3932168 | tf_op jit(solution)/shard_map/instances/ppermute | solution.py:192
  4.2 1.3 %copy-start = (bf16[1,2,320,1024]{3,2,1,0:T(8,128)(2,1)S(1)}, bf16[1,2,320,1024]{3,2,1,0:T(8,128)(2,1)}, u32[]{:S(2)}) copy-start(bf16[1,2,320,1024]{3,2,1,0:T(8,128)(2,1)} %param.11) | copy-start | bytes 3932164
  5.6 11.8 %copy-start.8 = (s32[1,6,1024]{2,0,1:T(1,128)S(1)}, s32[1,6,1024]{2,0,1:T(1,128)}, u32[]{:S(2)}) copy-start(s32[1,6,1024]{2,0,1:T(1,128)} %param.15) | copy-start | bytes 73732
  5.6 13.4 %copy-start.1 = (bf16[320,320]{1,0:T(8,128)(2,1)S(1)}, bf16[320,320]{1,0:T(8,128)(2,1)}, u32[]{:S(2)}) copy-start(bf16[320,320]{1,0:T(8,128)(2,1)} %inverse_ref.3) | copy-start | bytes 614404
  5.6 13.4 %copy-start.2 = (bf16[1,2,320,1024]{3,2,1,0:T(8,128)(2,1)S(1)}, bf16[1,2,320,1024]{3,2,1,0:T(8,128)(2,1)}, u32[]{:S(2)}) copy-start(bf16[1,2,320,1024]{3,2,1,0:T(8,128)(2,1)} %param.12) | copy-start | bytes 3932164
  5.6 13.4 %copy-start.3 = (bf16[320,480]{1,0:T(8,128)(2,1)S(1)}, bf16[320,480]{1,0:T(8,128)(2,1)}, u32[]{:S(2)}) copy-start(bf16[320,480]{1,0:T(8,128)(2,1)} %lift_ref.1) | copy-start | bytes 921604
  5.6 13.4 %copy-start.4 = (bf16[320,320]{1,0:T(8,128)(2,1)S(1)}, bf16[320,320]{1,0:T(8,128)(2,1)}, u32[]{:S(2)}) copy-start(bf16[320,320]{1,0:T(8,128)(2,1)} %volume_ref.1) | copy-start | bytes 614404
  5.6 13.4 %copy-start.5 = (f32[1,1024]{1,0:T(1,128)S(1)}, f32[1,1024]{1,0:T(1,128)}, u32[]{:S(2)}) copy-start(f32[1,1024]{1,0:T(1,128)} %scale_ref.1) | copy-start | bytes 12292
  5.6 13.4 %copy-start.6 = (s32[1,2,64]{2,1,0:T(2,128)S(1)}, s32[1,2,64]{2,1,0:T(2,128)}, u32[]{:S(2)}) copy-start(s32[1,2,64]{2,1,0:T(2,128)} %param.16) | copy-start | bytes 1540
  5.6 13.4 %copy-start.7 = (f32[4,4]{1,0:T(4,128)S(1)}, f32[4,4]{1,0:T(4,128)}, u32[]{:S(2)}) copy-start(f32[4,4]{1,0:T(4,128)} %constant.13.clone.table_ref) | copy-start | bytes 196
  6.6 6.6 %collective-permute-start.5 = (bf16[2,80,64]{2,1,0:T(8,128)(2,1)S(1)}, bf16[2,80,64]{2,1,0:T(8,128)(2,1)S(1)}, u32[]{:S(2)}, u32[]{:S(2)}) collective-permute-start(bf16[2,80,64]{2,1,0:T(8,128)(2,1)S(1)} %get-tuple-element.13), channel_id=1, source_target_pairs={{0,13},{1,12},{4,1},{5,0},{8,5},{9,4},{12,9},{13,8},{2,15},{3,14},... | collective-permute-start | bytes 61448 | tf_op jit(solution)/shard_map/interface/ppermute | solution.py:219
  9.5 4.5 %collective-permute-start.4 = (bf16[2,80,64]{2,1,0:T(8,128)(2,1)S(1)}, bf16[2,80,64]{2,1,0:T(8,128)(2,1)S(1)}, u32[]{:S(2)}, u32[]{:S(2)}) collective-permute-start(bf16[2,80,64]{2,1,0:T(8,128)(2,1)S(1)} %get-tuple-element.13), channel_id=1, source_target_pairs={{0,9},{1,8},{4,13},{5,12},{8,1},{9,0},{12,5},{13,4},{2,11},{3,10},... | collective-permute-start | bytes 61448 | tf_op jit(solution)/shard_map/interface/ppermute | solution.py:219
  9.5 9.5 %collective-permute-start = (bf16[2,160,64]{2,1,0:T(8,128)(2,1)S(1)}, bf16[2,160,64]{2,1,0:T(8,128)(2,1)S(1)}, u32[]{:S(2)}, u32[]{:S(2)}) collective-permute-start(bf16[2,160,64]{2,1,0:T(8,128)(2,1)S(1)} %get-tuple-element.11), channel_id=1, source_target_pairs={{0,4},{4,8},{8,12},{12,0},{1,5},{5,9},{9,13},{13,1},{2,6},{6,10},{... | collective-permute-start | bytes 122888 | tf_op jit(solution)/shard_map/halo/ppermute | solution.py:216
  11.0 7.9 %collective-permute-start.1 = (bf16[2,160,64]{2,1,0:T(8,128)(2,1)S(1)}, bf16[2,160,64]{2,1,0:T(8,128)(2,1)S(1)}, u32[]{:S(2)}, u32[]{:S(2)}) collective-permute-start(bf16[2,160,64]{2,1,0:T(8,128)(2,1)S(1)} %get-tuple-element.12), channel_id=1, source_target_pairs={{0,12},{4,0},{8,4},{12,8},{1,13},{5,1},{9,5},{13,9},{2,14},{6,2},{... | collective-permute-start | bytes 122888 | tf_op jit(solution)/shard_map/halo/ppermute | solution.py:217
  13.3 5.6 %collective-permute-start.3 = (bf16[2,80,64]{2,1,0:T(8,128)(2,1)S(1)}, bf16[2,80,64]{2,1,0:T(8,128)(2,1)S(1)}, u32[]{:S(2)}, u32[]{:S(2)}) collective-permute-start(bf16[2,80,64]{2,1,0:T(8,128)(2,1)S(1)} %get-tuple-element.13), channel_id=1, source_target_pairs={{0,5},{1,4},{4,9},{5,8},{8,13},{9,12},{12,1},{13,0},{2,7},{3,6},{6... | collective-permute-start | bytes 61448 | tf_op jit(solution)/shard_map/interface/ppermute | solution.py:219
  13.9 5.0 %collective-permute-start.2 = (bf16[2,80,64]{2,1,0:T(8,128)(2,1)S(1)}, bf16[2,80,64]{2,1,0:T(8,128)(2,1)S(1)}, u32[]{:S(2)}, u32[]{:S(2)}) collective-permute-start(bf16[2,80,64]{2,1,0:T(8,128)(2,1)S(1)} %get-tuple-element.13), channel_id=1, source_target_pairs={{0,1},{1,0},{4,5},{5,4},{8,9},{9,8},{12,13},{13,12},{2,3},{3,2},{6... | collective-permute-start | bytes 61448 | tf_op jit(solution)/shard_map/interface/ppermute | solution.py:219

commit v24 on v23

--- a/solution.py
+++ b/solution.py
@@ -159,10 +159,12 @@
             for k in range(products):
                 at = n * products + k
                 value -= factor_ref[at : at + 1, cols] * moved[t % 2, k]
-            made[t, n] = value.astype(jnp.bfloat16)
-        copy = pltpu.make_async_copy(made.at[t], out_ref.at[:, :, cols], sems.at[t])
-        copy.start()
-        copies.append(copy)
+            made[n, :, cols] = value.astype(jnp.bfloat16)
+        if t > 0 or steps == 1:
+            sent = slice(0 if t == 1 else t * tile, (t + 1) * tile)
+            copy = pltpu.make_async_copy(made.at[:, :, sent], out_ref.at[:, :, sent], sems.at[t])
+            copy.start()
+            copies.append(copy)
     for copy in copies:
         copy.wait()
 
@@ -252,7 +254,7 @@
             out_shape=jax.ShapeDtypeStruct((count, dof, total), bf16),
             in_specs=[vmem] * (3 + peers),
             out_specs=pl.BlockSpec(memory_space=pl.ANY),
-            scratch_shapes=[pltpu.VMEM((steps, count, dof, tile), bf16),
+            scratch_shapes=[pltpu.VMEM((count, dof, total), bf16),
                             pltpu.VMEM((2, (peers - 1) * count, dof, tile), jnp.float32),
                             pltpu.SemaphoreType.DMA((steps,))],
             compiler_params=pltpu.CompilerParams(vmem_limit_bytes=VMEM_LIMIT),

time: 33.7 us -> 33.7 us (level)
  no operation moved by 1% of the time
where the time goes in v24:
time: 33.7 us; the launch traced here: 33.5 us
  Pallas kernels  13 us (39%)
  starting transfers between devices  12.4 us (37%)
  waiting for transfers between devices  4.67 us (14%)
  local copies, waits for them, and re-layouts  2.58 us (8%)
  between operations  0.79 us (2%)
    pallas_call x1, Pallas kernels, body(): pl.pallas_call(functools.partial(couple_kernel, shards, peers, deep), gri...  10.4 us
    ppermute x4, starting transfers between devices, body(): lax.ppermute(cross, ('space', 'row'), [(i * 2 + r, (i + d) % shards * 2 +...  5.62 us
    ppermute x1, starting transfers between devices, body(): lax.ppermute(current, 'inst', [(i, (i + d) % peers) for i in range(peers)])  2.94 us
    unnamed x20, local copies, waits for them, and re-layouts  2.58 us
    ppermute x1, waiting for transfers between devices, body(): lax.ppermute(current, 'inst', [(i, (i + d) % peers) for i in range(peers)])  2.5 us
    ppermute x1, starting transfers between devices, body(): lax.ppermute(down, 'space', [(i, (i - 1) % shards) for i in range(shards)])  2.25 us
    ppermute x4, waiting for transfers between devices, body(): lax.ppermute(cross, ('space', 'row'), [(i * 2 + r, (i + d) % shards * 2 +...  2.16 us
    pallas_call x1, Pallas kernels, body(): pl.pallas_call(functools.partial(update_kernel, tile, deep), out_shape=ja...  1.63 us
  transfers between devices with their start and end apart: 7, of which 3 were waited for; matrix products, arithmetic and copies ran while one was open for 4% of the time, Pallas kernels for 34%

profile of v24, /device:TPU:0, one launch (start us, length us, event | category | flops | bytes accessed | tf_op | source)
XLA Modules:
  0.0 33.5 jit_solution(11773906239779275917)
XLA Ops:
  0.0 2.9 %collective-permute-start.6 = (bf16[2,320,1024]{2,1,0:T(8,128)(2,1)}, bf16[2,320,1024]{2,1,0:T(8,128)(2,1)S(1)}, u32[]{:S(2)}, u32[]{:S(2)}) collective-permute-start(bf16[2,320,1024]{2,1,0:T(8,128)(2,1)} %bitcast.10), channel_id=1, source_target_pairs={{0,2},{2,0},{1,3},{3,1},{4,6},{6,4},{5,7},{7,5},{8,10},{10,8},{9,1... | collective-permute-start | bytes 3932168 | tf_op jit(solution)/shard_map/instances/ppermute | solution.py:194
  2.9 1.2 %copy.13.trace_ref = bf16[480,320]{1,0:T(8,128)(2,1)S(1)} copy(bf16[480,320]{0,1:T(8,128)(2,1)} %param.18) | data formatting | bytes 614400 | tf_op args[7]
  4.2 0.1 pad_add_fusion.place_ref
  4.2 0.0 copy-start
  4.2 1.3 %copy-done = bf16[1,2,320,1024]{3,2,1,0:T(8,128)(2,1)S(1)} copy-done((bf16[1,2,320,1024]{3,2,1,0:T(8,128)(2,1)S(1)}, bf16[1,2,320,1024]{3,2,1,0:T(8,128)(2,1)}, u32[]{:S(2)}) %copy-start) | copy-done | bytes 1310744
  5.6 0.0 copy-start.8
  5.6 0.0 copy-start.1
  5.6 0.0 copy-start.2
  5.6 0.0 copy-start.3
  5.6 0.0 copy-start.4
  5.6 0.0 copy-start.5
  5.6 0.0 copy-start.6
  5.6 0.0 copy-start.7
  5.6 1.0 %ends.1 = (bf16[2,160,64]{2,1,0:T(8,128)(2,1)S(1)}, bf16[2,160,64]{2,1,0:T(8,128)(2,1)S(1)}, bf16[2,80,64]{2,1,0:T(8,128)(2,1)S(1)}) custom-call(s32[3]{0:T(128)S(1)} %pad_add_fusion.place_ref, bf16[2,320,1024]{2,1,0:T(8,128)(2,1)S(1)} %bitcast.11, bf16[2,320,1024]{2,1,0:T(8,128)(2,1)S(1)} %bitcast.12, bf16[480,320]{1,0:T(8,128)(2,1)S(1)} %copy.13.trace_ref), custom_call_target="tpu_custom_call" | custom-call | flops 104857600 | bytes 1000000 | tf_op jit(solution)/shard_map/ends/ends/pallas_call | solution.py:198
  6.6 2.8 %collective-permute-start.5 = (bf16[2,80,64]{2,1,0:T(8,128)(2,1)S(1)}, bf16[2,80,64]{2,1,0:T(8,128)(2,1)S(1)}, u32[]{:S(2)}, u32[]{:S(2)}) collective-permute-start(bf16[2,80,64]{2,1,0:T(8,128)(2,1)S(1)} %get-tuple-element.13), channel_id=1, source_target_pairs={{0,13},{1,12},{4,1},{5,0},{8,5},{9,4},{12,9},{13,8},{2,15},{3,14},... | collective-permute-start | bytes 61448 | tf_op jit(solution)/shard_map/interface/ppermute | solution.py:221
  9.5 0.0 collective-permute-start.4
  9.5 1.6 %collective-permute-start = (bf16[2,160,64]{2,1,0:T(8,128)(2,1)S(1)}, bf16[2,160,64]{2,1,0:T(8,128)(2,1)S(1)}, u32[]{:S(2)}, u32[]{:S(2)}) collective-permute-start(bf16[2,160,64]{2,1,0:T(8,128)(2,1)S(1)} %get-tuple-element.11), channel_id=1, source_target_pairs={{0,4},{4,8},{8,12},{12,0},{1,5},{5,9},{9,13},{13,1},{2,6},{6,10},{... | collective-permute-start | bytes 122888 | tf_op jit(solution)/shard_map/halo/ppermute | solution.py:218
  11.0 2.2 %collective-permute-start.1 = (bf16[2,160,64]{2,1,0:T(8,128)(2,1)S(1)}, bf16[2,160,64]{2,1,0:T(8,128)(2,1)S(1)}, u32[]{:S(2)}, u32[]{:S(2)}) collective-permute-start(bf16[2,160,64]{2,1,0:T(8,128)(2,1)S(1)} %get-tuple-element.12), channel_id=1, source_target_pairs={{0,12},{4,0},{8,4},{12,8},{1,13},{5,1},{9,5},{13,9},{2,14},{6,2},{... | collective-permute-start | bytes 122888 | tf_op jit(solution)/shard_map/halo/ppermute | solution.py:219
  13.3 0.0 collective-permute-done.5.rest_3_
  13.3 0.0 collective-permute-start.3
  13.3 0.6 %collective-permute-done.4.rest_2_ = bf16[2,80,64]{2,1,0:T(8,128)(2,1)S(1)} collective-permute-done((bf16[2,80,64]{2,1,0:T(8,128)(2,1)S(1)}, bf16[2,80,64]{2,1,0:T(8,128)(2,1)S(1)}, u32[]{:S(2)}, u32[]{:S(2)}) %collective-permute-start.4) | collective-permute-done | bytes 20512 | tf_op jit(solution)/shard_map/interface/ppermute | solution.py:221
  13.9 2.8 %collective-permute-start.2 = (bf16[2,80,64]{2,1,0:T(8,128)(2,1)S(1)}, bf16[2,80,64]{2,1,0:T(8,128)(2,1)S(1)}, u32[]{:S(2)}, u32[]{:S(2)}) collective-permute-start(bf16[2,80,64]{2,1,0:T(8,128)(2,1)S(1)} %get-tuple-element.13), channel_id=1, source_target_pairs={{0,1},{1,0},{4,5},{5,4},{8,9},{9,8},{12,13},{13,12},{2,3},{3,2},{6... | collective-permute-start | bytes 61448 | tf_op jit(solution)/shard_map/interface/ppermute | solution.py:221
  17.4 0.0 copy-done.8
  17.4 1.5 %collective-permute-done.3.rest_1_ = bf16[2,80,64]{2,1,0:T(8,128)(2,1)S(1)} collective-permute-done((bf16[2,80,64]{2,1,0:T(8,128)(2,1)S(1)}, bf16[2,80,64]{2,1,0:T(8,128)(2,1)S(1)}, u32[]{:S(2)}, u32[]{:S(2)}) %collective-permute-start.3) | collective-permute-done | bytes 20512 | tf_op jit(solution)/shard_map/interface/ppermute | solution.py:221
  18.9 0.0 collective-permute-done.2.rest_0_
  18.9 0.0 collective-permute-done.low_ref
  18.9 0.0 collective-permute-done.1.high_ref
  18.9 0.0 copy-done.1
  18.9 0.0 copy-done.2
  19.0 0.0 copy-done.3
  19.0 0.0 copy-done.4
  19.0 0.0 copy-done.5
  19.0 0.0 copy-done.6
  19.0 0.0 copy-done.7
  19.0 10.4 %couple.1 = (f32[2,320,1024]{2,1,0:T(8,128)S(1)}, f32[4,1024]{1,0:T(4,128)S(1)}, bf16[2,320,128]{2,1,0:T(8,128)(2,1)S(1)}) custom-call(s32[3]{0:T(128)S(1)} %pad_add_fusion.place_ref, f32[1]{0:T(128)S(6)} %copy.17.freq_ref, f32[4,4]{1,0:T(4,128)S(1)} %copy-done.7, s32[6,1024]{1,0:T(8,128)S(1)} %bitcast.15, s32[2,64]{1,0:T(2,128)S(1)} %bitcast.17, ...), custom_call_target="tpu_custom_call" | custom-call | flops 3690987520 | bytes 6553600 | tf_op jit(solution)/shard_map/couple/couple/pallas_call | solution.py:230
  29.4 2.5 %collective-permute-done.6.rest_0_ = bf16[2,320,1024]{2,1,0:T(8,128)(2,1)S(1)} collective-permute-done((bf16[2,320,1024]{2,1,0:T(8,128)(2,1)}, bf16[2,320,1024]{2,1,0:T(8,128)(2,1)S(1)}, u32[]{:S(2)}, u32[]{:S(2)}) %collective-permute-start.6) | collective-permute-done | bytes 1310752 | tf_op jit(solution)/shard_map/instances/ppermute | solution.py:194
  31.9 1.6 %update.1 = bf16[2,320,1024]{2,1,0:T(8,128)(2,1)} custom-call(f32[2,320,1024]{2,1,0:T(8,128)S(1)} %get-tuple-element.14.ready_ref, f32[4,1024]{1,0:T(4,128)S(1)} %get-tuple-element.15.factor_ref, bf16[320,320]{1,0:T(8,128)(2,1)S(1)} %copy-done.1, bf16[2,320,128]{2,1,0:T(8,128)(2,1)S(1)} %get-tuple-element.16.spread_ref, ...), custom_call_target="tpu_custom_call" | custom-call | flops 419430400 | bytes 5242880 | tf_op jit(solution)/shard_map/update/update/pallas_call | solution.py:252
  (1 shorter events, 0.0 us)
Async XLA Ops:
  0.0 31.9 %collective-permute-start.6 = (bf16[2,320,1024]{2,1,0:T(8,128)(2,1)}, bf16[2,320,1024]{2,1,0:T(8,128)(2,1)S(1)}, u32[]{:S(2)}, u32[]{:S(2)}) collective-permute-start(bf16[2,320,1024]{2,1,0:T(8,128)(2,1)} %bitcast.10), channel_id=1, source_target_pairs={{0,2},{2,0},{1,3},{3,1},{4,6},{6,4},{5,7},{7,5},{8,10},{10,8},{9,1... | collective-permute-start | bytes 3932168 | tf_op jit(solution)/shard_map/instances/ppermute | solution.py:194
  4.2 1.3 %copy-start = (bf16[1,2,320,1024]{3,2,1,0:T(8,128)(2,1)S(1)}, bf16[1,2,320,1024]{3,2,1,0:T(8,128)(2,1)}, u32[]{:S(2)}) copy-start(bf16[1,2,320,1024]{3,2,1,0:T(8,128)(2,1)} %param.11) | copy-start | bytes 3932164
  5.6 11.8 %copy-start.8 = (s32[1,6,1024]{2,0,1:T(1,128)S(1)}, s32[1,6,1024]{2,0,1:T(1,128)}, u32[]{:S(2)}) copy-start(s32[1,6,1024]{2,0,1:T(1,128)} %param.15) | copy-start | bytes 73732
  5.6 13.4 %copy-start.1 = (bf16[320,320]{1,0:T(8,128)(2,1)S(1)}, bf16[320,320]{1,0:T(8,128)(2,1)}, u32[]{:S(2)}) copy-start(bf16[320,320]{1,0:T(8,128)(2,1)} %inverse_ref.3) | copy-start | bytes 614404
  5.6 13.4 %copy-start.2 = (bf16[1,2,320,1024]{3,2,1,0:T(8,128)(2,1)S(1)}, bf16[1,2,320,1024]{3,2,1,0:T(8,128)(2,1)}, u32[]{:S(2)}) copy-start(bf16[1,2,320,1024]{3,2,1,0:T(8,128)(2,1)} %param.12) | copy-start | bytes 3932164
  5.6 13.4 %copy-start.3 = (bf16[320,480]{1,0:T(8,128)(2,1)S(1)}, bf16[320,480]{1,0:T(8,128)(2,1)}, u32[]{:S(2)}) copy-start(bf16[320,480]{1,0:T(8,128)(2,1)} %lift_ref.1) | copy-start | bytes 921604
  5.6 13.4 %copy-start.4 = (bf16[320,320]{1,0:T(8,128)(2,1)S(1)}, bf16[320,320]{1,0:T(8,128)(2,1)}, u32[]{:S(2)}) copy-start(bf16[320,320]{1,0:T(8,128)(2,1)} %volume_ref.1) | copy-start | bytes 614404
  5.6 13.4 %copy-start.5 = (f32[1,1024]{1,0:T(1,128)S(1)}, f32[1,1024]{1,0:T(1,128)}, u32[]{:S(2)}) copy-start(f32[1,1024]{1,0:T(1,128)} %scale_ref.1) | copy-start | bytes 12292
  5.6 13.4 %copy-start.6 = (s32[1,2,64]{2,1,0:T(2,128)S(1)}, s32[1,2,64]{2,1,0:T(2,128)}, u32[]{:S(2)}) copy-start(s32[1,2,64]{2,1,0:T(2,128)} %param.16) | copy-start | bytes 1540
  5.6 13.4 %copy-start.7 = (f32[4,4]{1,0:T(4,128)S(1)}, f32[4,4]{1,0:T(4,128)}, u32[]{:S(2)}) copy-start(f32[4,4]{1,0:T(4,128)} %constant.13.clone.table_ref) | copy-start | bytes 196
  6.6 6.6 %collective-permute-start.5 = (bf16[2,80,64]{2,1,0:T(8,128)(2,1)S(1)}, bf16[2,80,64]{2,1,0:T(8,128)(2,1)S(1)}, u32[]{:S(2)}, u32[]{:S(2)}) collective-permute-start(bf16[2,80,64]{2,1,0:T(8,128)(2,1)S(1)} %get-tuple-element.13), channel_id=1, source_target_pairs={{0,13},{1,12},{4,1},{5,0},{8,5},{9,4},{12,9},{13,8},{2,15},{3,14},... | collective-permute-start | bytes 61448 | tf_op jit(solution)/shard_map/interface/ppermute | solution.py:221
  9.5 4.5 %collective-permute-start.4 = (bf16[2,80,64]{2,1,0:T(8,128)(2,1)S(1)}, bf16[2,80,64]{2,1,0:T(8,128)(2,1)S(1)}, u32[]{:S(2)}, u32[]{:S(2)}) collective-permute-start(bf16[2,80,64]{2,1,0:T(8,128)(2,1)S(1)} %get-tuple-element.13), channel_id=1, source_target_pairs={{0,9},{1,8},{4,13},{5,12},{8,1},{9,0},{12,5},{13,4},{2,11},{3,10},... | collective-permute-start | bytes 61448 | tf_op jit(solution)/shard_map/interface/ppermute | solution.py:221
  9.5 9.5 %collective-permute-start = (bf16[2,160,64]{2,1,0:T(8,128)(2,1)S(1)}, bf16[2,160,64]{2,1,0:T(8,128)(2,1)S(1)}, u32[]{:S(2)}, u32[]{:S(2)}) collective-permute-start(bf16[2,160,64]{2,1,0:T(8,128)(2,1)S(1)} %get-tuple-element.11), channel_id=1, source_target_pairs={{0,4},{4,8},{8,12},{12,0},{1,5},{5,9},{9,13},{13,1},{2,6},{6,10},{... | collective-permute-start | bytes 122888 | tf_op jit(solution)/shard_map/halo/ppermute | solution.py:218
  11.0 7.9 %collective-permute-start.1 = (bf16[2,160,64]{2,1,0:T(8,128)(2,1)S(1)}, bf16[2,160,64]{2,1,0:T(8,128)(2,1)S(1)}, u32[]{:S(2)}, u32[]{:S(2)}) collective-permute-start(bf16[2,160,64]{2,1,0:T(8,128)(2,1)S(1)} %get-tuple-element.12), channel_id=1, source_target_pairs={{0,12},{4,0},{8,4},{12,8},{1,13},{5,1},{9,5},{13,9},{2,14},{6,2},{... | collective-permute-start | bytes 122888 | tf_op jit(solution)/shard_map/halo/ppermute | solution.py:219
  13.3 5.6 %collective-permute-start.3 = (bf16[2,80,64]{2,1,0:T(8,128)(2,1)S(1)}, bf16[2,80,64]{2,1,0:T(8,128)(2,1)S(1)}, u32[]{:S(2)}, u32[]{:S(2)}) collective-permute-start(bf16[2,80,64]{2,1,0:T(8,128)(2,1)S(1)} %get-tuple-element.13), channel_id=1, source_target_pairs={{0,5},{1,4},{4,9},{5,8},{8,13},{9,12},{12,1},{13,0},{2,7},{3,6},{6... | collective-permute-start | bytes 61448 | tf_op jit(solution)/shard_map/interface/ppermute | solution.py:221
  13.9 5.0 %collective-permute-start.2 = (bf16[2,80,64]{2,1,0:T(8,128)(2,1)S(1)}, bf16[2,80,64]{2,1,0:T(8,128)(2,1)S(1)}, u32[]{:S(2)}, u32[]{:S(2)}) collective-permute-start(bf16[2,80,64]{2,1,0:T(8,128)(2,1)S(1)} %get-tuple-element.13), channel_id=1, source_target_pairs={{0,1},{1,0},{4,5},{5,4},{8,9},{9,8},{12,13},{13,12},{2,3},{3,2},{6... | collective-permute-start | bytes 61448 | tf_op jit(solution)/shard_map/interface/ppermute | solution.py:221

commit v25 on v4

--- a/solution.py
+++ b/solution.py
@@ -132,17 +132,24 @@
 def update_kernel(tile, ready_ref, factor_ref, inverse_ref, *rest):
     others, (out_ref, made, sems) = rest[:-3], rest[-3:]
     count, dof, total = ready_ref.shape
+    narrow = max(tile // count, LANES)
+    cuts = list(range(0, total - tile + 1, tile)) + list(range(total - tile + narrow, total + 1, narrow))
     copies = []
-    for t in range(total // tile):
-        cols = slice(t * tile, (t + 1) * tile)
-        moved = [dot(inverse_ref[...], other[m, :, cols]) for other in others for m in range(count)]
+    for p, (first, last) in enumerate(zip(cuts[:-1], cuts[1:])):
+        cols, size = slice(first, last), last - first
+        if size < tile:
+            wide = [dot(inverse_ref[...], jnp.concatenate([other[m, :, cols] for m in range(count)], axis=1))
+                    for other in others]
+            moved = [w[:, m * size : (m + 1) * size] for w in wide for m in range(count)]
+        else:
+            moved = [dot(inverse_ref[...], other[m, :, cols]) for other in others for m in range(count)]
         for n in range(count):
             value = ready_ref[n, :, cols]
             for k, part in enumerate(moved):
                 at = n * len(moved) + k
                 value -= factor_ref[at : at + 1, cols] * part
-            made[t, n] = value.astype(jnp.bfloat16)
-        copy = pltpu.make_async_copy(made.at[t], out_ref.at[:, :, cols], sems.at[t])
+            made[n, :, cols] = value.astype(jnp.bfloat16)
+        copy = pltpu.make_async_copy(made.at[:, :, cols], out_ref.at[:, :, cols], sems.at[p])
         copy.start()
         copies.append(copy)
     for copy in copies:
@@ -231,7 +238,7 @@
             out_shape=jax.ShapeDtypeStruct((count, dof, total), bf16),
             in_specs=[vmem] * (2 + peers),
             out_specs=pl.BlockSpec(memory_space=pl.ANY),
-            scratch_shapes=[pltpu.VMEM((steps, count, dof, tile), bf16), pltpu.SemaphoreType.DMA((steps,))],
+            scratch_shapes=[pltpu.VMEM((count, dof, total), bf16), pltpu.SemaphoreType.DMA((steps + count,))],
             compiler_params=pltpu.CompilerParams(vmem_limit_bytes=VMEM_LIMIT),
             cost_estimate=pl.CostEstimate(flops=2 * count * total * dof * dof * (peers - 1),
                                           bytes_accessed=count * dof * total * 8, transcendentals=0),

time: 33.8 us -> 33.8 us (level)
  no operation moved by 1% of the time
where the time goes in v25:
time: 33.8 us; the launch traced here: 33.6 us
  Pallas kernels  13.1 us (39%)
  starting transfers between devices  12.4 us (37%)
  waiting for transfers between devices  4.67 us (14%)
  local copies, waits for them, and re-layouts  2.58 us (8%)
  between operations  0.79 us (2%)
    pallas_call x1, Pallas kernels, body(): pl.pallas_call(functools.partial(couple_kernel, shards, peers), grid=(ste...  10.4 us
    ppermute x4, starting transfers between devices, body(): lax.ppermute(cross, ('space', 'row'), [(i * 2 + r, (i + d) % shards * 2 +...  5.62 us
    ppermute x1, starting transfers between devices, body(): lax.ppermute(current, 'inst', [(i, (i + d) % peers) for i in range(peers)])  2.94 us
    unnamed x20, local copies, waits for them, and re-layouts  2.58 us
    ppermute x1, waiting for transfers between devices, body(): lax.ppermute(current, 'inst', [(i, (i + d) % peers) for i in range(peers)])  2.5 us
    ppermute x1, starting transfers between devices, body(): lax.ppermute(down, 'space', [(i, (i - 1) % shards) for i in range(shards)])  2.25 us
    ppermute x4, waiting for transfers between devices, body(): lax.ppermute(cross, ('space', 'row'), [(i * 2 + r, (i + d) % shards * 2 +...  2.16 us
    pallas_call x1, Pallas kernels, body(): pl.pallas_call(functools.partial(update_kernel, tile), out_shape=jax.Shap...  1.66 us
  transfers between devices with their start and end apart: 7, of which 3 were waited for; matrix products, arithmetic and copies ran while one was open for 4% of the time, Pallas kernels for 34%

profile of v25, /device:TPU:0, one launch (start us, length us, event | category | flops | bytes accessed | tf_op | source)
XLA Modules:
  0.0 33.6 jit_solution(9996977972105175441)
XLA Ops:
  0.0 2.9 %collective-permute-start.6 = (bf16[2,320,1024]{2,1,0:T(8,128)(2,1)}, bf16[2,320,1024]{2,1,0:T(8,128)(2,1)S(1)}, u32[]{:S(2)}, u32[]{:S(2)}) collective-permute-start(bf16[2,320,1024]{2,1,0:T(8,128)(2,1)} %bitcast.10), channel_id=1, source_target_pairs={{0,2},{2,0},{1,3},{3,1},{4,6},{6,4},{5,7},{7,5},{8,10},{10,8},{9,1... | collective-permute-start | bytes 3932168 | tf_op jit(solution)/shard_map/instances/ppermute | solution.py:181
  2.9 1.2 %copy.13.trace_ref = bf16[480,320]{1,0:T(8,128)(2,1)S(1)} copy(bf16[480,320]{0,1:T(8,128)(2,1)} %param.18) | data formatting | bytes 614400 | tf_op args[7]
  4.2 0.1 pad_add_fusion.place_ref
  4.2 0.0 copy-start
  4.2 1.3 %copy-done = bf16[1,2,320,1024]{3,2,1,0:T(8,128)(2,1)S(1)} copy-done((bf16[1,2,320,1024]{3,2,1,0:T(8,128)(2,1)S(1)}, bf16[1,2,320,1024]{3,2,1,0:T(8,128)(2,1)}, u32[]{:S(2)}) %copy-start) | copy-done | bytes 1310744
  5.6 0.0 copy-start.8
  5.6 0.0 copy-start.1
  5.6 0.0 copy-start.2
  5.6 0.0 copy-start.3
  5.6 0.0 copy-start.4
  5.6 0.0 copy-start.5
  5.6 0.0 copy-start.6
  5.6 0.0 copy-start.7
  5.6 1.0 %ends.1 = (bf16[2,160,64]{2,1,0:T(8,128)(2,1)S(1)}, bf16[2,160,64]{2,1,0:T(8,128)(2,1)S(1)}, bf16[2,80,64]{2,1,0:T(8,128)(2,1)S(1)}) custom-call(s32[3]{0:T(128)S(1)} %pad_add_fusion.place_ref, bf16[2,320,1024]{2,1,0:T(8,128)(2,1)S(1)} %bitcast.11, bf16[2,320,1024]{2,1,0:T(8,128)(2,1)S(1)} %bitcast.12, bf16[480,320]{1,0:T(8,128)(2,1)S(1)} %copy.13.trace_ref), custom_call_target="tpu_custom_call" | custom-call | flops 104857600 | bytes 1000000 | tf_op jit(solution)/shard_map/ends/ends/pallas_call | solution.py:185
  6.6 2.8 %collective-permute-start.5 = (bf16[2,80,64]{2,1,0:T(8,128)(2,1)S(1)}, bf16[2,80,64]{2,1,0:T(8,128)(2,1)S(1)}, u32[]{:S(2)}, u32[]{:S(2)}) collective-permute-start(bf16[2,80,64]{2,1,0:T(8,128)(2,1)S(1)} %get-tuple-element.12), channel_id=1, source_target_pairs={{0,13},{1,12},{4,1},{5,0},{8,5},{9,4},{12,9},{13,8},{2,15},{3,14},... | collective-permute-start | bytes 61448 | tf_op jit(solution)/shard_map/interface/ppermute | solution.py:208
  9.5 0.0 collective-permute-start.4
  9.5 1.6 %collective-permute-start = (bf16[2,160,64]{2,1,0:T(8,128)(2,1)S(1)}, bf16[2,160,64]{2,1,0:T(8,128)(2,1)S(1)}, u32[]{:S(2)}, u32[]{:S(2)}) collective-permute-start(bf16[2,160,64]{2,1,0:T(8,128)(2,1)S(1)} %get-tuple-element.10), channel_id=1, source_target_pairs={{0,4},{4,8},{8,12},{12,0},{1,5},{5,9},{9,13},{13,1},{2,6},{6,10},{... | collective-permute-start | bytes 122888 | tf_op jit(solution)/shard_map/halo/ppermute | solution.py:205
  11.0 2.2 %collective-permute-start.1 = (bf16[2,160,64]{2,1,0:T(8,128)(2,1)S(1)}, bf16[2,160,64]{2,1,0:T(8,128)(2,1)S(1)}, u32[]{:S(2)}, u32[]{:S(2)}) collective-permute-start(bf16[2,160,64]{2,1,0:T(8,128)(2,1)S(1)} %get-tuple-element.11), channel_id=1, source_target_pairs={{0,12},{4,0},{8,4},{12,8},{1,13},{5,1},{9,5},{13,9},{2,14},{6,2},{... | collective-permute-start | bytes 122888 | tf_op jit(solution)/shard_map/halo/ppermute | solution.py:206
  13.3 0.0 collective-permute-done.5.rest_3_
  13.3 0.0 collective-permute-start.3
  13.3 0.6 %collective-permute-done.4.rest_2_ = bf16[2,80,64]{2,1,0:T(8,128)(2,1)S(1)} collective-permute-done((bf16[2,80,64]{2,1,0:T(8,128)(2,1)S(1)}, bf16[2,80,64]{2,1,0:T(8,128)(2,1)S(1)}, u32[]{:S(2)}, u32[]{:S(2)}) %collective-permute-start.4) | collective-permute-done | bytes 20512 | tf_op jit(solution)/shard_map/interface/ppermute | solution.py:208
  13.9 2.8 %collective-permute-start.2 = (bf16[2,80,64]{2,1,0:T(8,128)(2,1)S(1)}, bf16[2,80,64]{2,1,0:T(8,128)(2,1)S(1)}, u32[]{:S(2)}, u32[]{:S(2)}) collective-permute-start(bf16[2,80,64]{2,1,0:T(8,128)(2,1)S(1)} %get-tuple-element.12), channel_id=1, source_target_pairs={{0,1},{1,0},{4,5},{5,4},{8,9},{9,8},{12,13},{13,12},{2,3},{3,2},{6... | collective-permute-start | bytes 61448 | tf_op jit(solution)/shard_map/interface/ppermute | solution.py:208
  17.4 0.0 copy-done.8
  17.4 1.5 %collective-permute-done.3.rest_1_ = bf16[2,80,64]{2,1,0:T(8,128)(2,1)S(1)} collective-permute-done((bf16[2,80,64]{2,1,0:T(8,128)(2,1)S(1)}, bf16[2,80,64]{2,1,0:T(8,128)(2,1)S(1)}, u32[]{:S(2)}, u32[]{:S(2)}) %collective-permute-start.3) | collective-permute-done | bytes 20512 | tf_op jit(solution)/shard_map/interface/ppermute | solution.py:208
  18.9 0.0 collective-permute-done.2.rest_0_
  18.9 0.0 collective-permute-done.low_ref
  18.9 0.0 collective-permute-done.1.high_ref
  18.9 0.0 copy-done.1
  18.9 0.0 copy-done.2
  19.0 0.0 copy-done.3
  19.0 0.0 copy-done.4
  19.0 0.0 copy-done.5
  19.0 0.0 copy-done.6
  19.0 0.0 copy-done.7
  19.0 10.4 %couple.1 = (f32[2,320,1024]{2,1,0:T(8,128)S(1)}, f32[4,1024]{1,0:T(4,128)S(1)}) custom-call(s32[3]{0:T(128)S(1)} %pad_add_fusion.place_ref, f32[1]{0:T(128)S(6)} %copy.17.freq_ref, f32[4,4]{1,0:T(4,128)S(1)} %copy-done.7, s32[6,1024]{1,0:T(8,128)S(1)} %bitcast.15, s32[2,64]{1,0:T(2,128)S(1)} %bitcast.17, bf16[2,320,1024]{2,1,0:T(8,128)(2,1)S(1)} %bitcast.13, ...), custom_call_target="tpu_custom_call" | custom-call | flops 3690987520 | bytes 6553600 | tf_op jit(solution)/shard_map/couple/couple/pallas_call | solution.py:216
  29.4 2.5 %collective-permute-done.6.rest_0_ = bf16[2,320,1024]{2,1,0:T(8,128)(2,1)S(1)} collective-permute-done((bf16[2,320,1024]{2,1,0:T(8,128)(2,1)}, bf16[2,320,1024]{2,1,0:T(8,128)(2,1)S(1)}, u32[]{:S(2)}, u32[]{:S(2)}) %collective-permute-start.6) | collective-permute-done | bytes 1310752 | tf_op jit(solution)/shard_map/instances/ppermute | solution.py:181
  31.9 1.7 %update.1 = bf16[2,320,1024]{2,1,0:T(8,128)(2,1)} custom-call(f32[2,320,1024]{2,1,0:T(8,128)S(1)} %get-tuple-element.13.ready_ref, f32[4,1024]{1,0:T(4,128)S(1)} %get-tuple-element.14.factor_ref, bf16[320,320]{1,0:T(8,128)(2,1)S(1)} %copy-done.1, bf16[2,320,1024]{2,1,0:T(8,128)(2,1)S(1)} %collective-permute-done.6.rest_0_), custom_call_target="tpu_custom_call" | custom-call | flops 419430400 | bytes 5242880 | tf_op jit(solution)/shard_map/update/update/pallas_call | solution.py:236
  (1 shorter events, 0.0 us)
Async XLA Ops:
  0.0 31.9 %collective-permute-start.6 = (bf16[2,320,1024]{2,1,0:T(8,128)(2,1)}, bf16[2,320,1024]{2,1,0:T(8,128)(2,1)S(1)}, u32[]{:S(2)}, u32[]{:S(2)}) collective-permute-start(bf16[2,320,1024]{2,1,0:T(8,128)(2,1)} %bitcast.10), channel_id=1, source_target_pairs={{0,2},{2,0},{1,3},{3,1},{4,6},{6,4},{5,7},{7,5},{8,10},{10,8},{9,1... | collective-permute-start | bytes 3932168 | tf_op jit(solution)/shard_map/instances/ppermute | solution.py:181
  4.2 1.3 %copy-start = (bf16[1,2,320,1024]{3,2,1,0:T(8,128)(2,1)S(1)}, bf16[1,2,320,1024]{3,2,1,0:T(8,128)(2,1)}, u32[]{:S(2)}) copy-start(bf16[1,2,320,1024]{3,2,1,0:T(8,128)(2,1)} %param.11) | copy-start | bytes 3932164
  5.6 11.8 %copy-start.8 = (s32[1,6,1024]{2,0,1:T(1,128)S(1)}, s32[1,6,1024]{2,0,1:T(1,128)}, u32[]{:S(2)}) copy-start(s32[1,6,1024]{2,0,1:T(1,128)} %param.15) | copy-start | bytes 73732
  5.6 13.4 %copy-start.1 = (bf16[320,320]{1,0:T(8,128)(2,1)S(1)}, bf16[320,320]{1,0:T(8,128)(2,1)}, u32[]{:S(2)}) copy-start(bf16[320,320]{1,0:T(8,128)(2,1)} %inverse_ref.3) | copy-start | bytes 614404
  5.6 13.4 %copy-start.2 = (bf16[1,2,320,1024]{3,2,1,0:T(8,128)(2,1)S(1)}, bf16[1,2,320,1024]{3,2,1,0:T(8,128)(2,1)}, u32[]{:S(2)}) copy-start(bf16[1,2,320,1024]{3,2,1,0:T(8,128)(2,1)} %param.12) | copy-start | bytes 3932164
  5.6 13.4 %copy-start.3 = (bf16[320,480]{1,0:T(8,128)(2,1)S(1)}, bf16[320,480]{1,0:T(8,128)(2,1)}, u32[]{:S(2)}) copy-start(bf16[320,480]{1,0:T(8,128)(2,1)} %lift_ref.1) | copy-start | bytes 921604
  5.6 13.4 %copy-start.4 = (bf16[320,320]{1,0:T(8,128)(2,1)S(1)}, bf16[320,320]{1,0:T(8,128)(2,1)}, u32[]{:S(2)}) copy-start(bf16[320,320]{1,0:T(8,128)(2,1)} %volume_ref.1) | copy-start | bytes 614404
  5.6 13.4 %copy-start.5 = (f32[1,1024]{1,0:T(1,128)S(1)}, f32[1,1024]{1,0:T(1,128)}, u32[]{:S(2)}) copy-start(f32[1,1024]{1,0:T(1,128)} %scale_ref.1) | copy-start | bytes 12292
  5.6 13.4 %copy-start.6 = (s32[1,2,64]{2,1,0:T(2,128)S(1)}, s32[1,2,64]{2,1,0:T(2,128)}, u32[]{:S(2)}) copy-start(s32[1,2,64]{2,1,0:T(2,128)} %param.16) | copy-start | bytes 1540
  5.6 13.4 %copy-start.7 = (f32[4,4]{1,0:T(4,128)S(1)}, f32[4,4]{1,0:T(4,128)}, u32[]{:S(2)}) copy-start(f32[4,4]{1,0:T(4,128)} %constant.13.clone.table_ref) | copy-start | bytes 196
  6.6 6.6 %collective-permute-start.5 = (bf16[2,80,64]{2,1,0:T(8,128)(2,1)S(1)}, bf16[2,80,64]{2,1,0:T(8,128)(2,1)S(1)}, u32[]{:S(2)}, u32[]{:S(2)}) collective-permute-start(bf16[2,80,64]{2,1,0:T(8,128)(2,1)S(1)} %get-tuple-element.12), channel_id=1, source_target_pairs={{0,13},{1,12},{4,1},{5,0},{8,5},{9,4},{12,9},{13,8},{2,15},{3,14},... | collective-permute-start | bytes 61448 | tf_op jit(solution)/shard_map/interface/ppermute | solution.py:208
  9.5 4.5 %collective-permute-start.4 = (bf16[2,80,64]{2,1,0:T(8,128)(2,1)S(1)}, bf16[2,80,64]{2,1,0:T(8,128)(2,1)S(1)}, u32[]{:S(2)}, u32[]{:S(2)}) collective-permute-start(bf16[2,80,64]{2,1,0:T(8,128)(2,1)S(1)} %get-tuple-element.12), channel_id=1, source_target_pairs={{0,9},{1,8},{4,13},{5,12},{8,1},{9,0},{12,5},{13,4},{2,11},{3,10},... | collective-permute-start | bytes 61448 | tf_op jit(solution)/shard_map/interface/ppermute | solution.py:208
  9.5 9.5 %collective-permute-start = (bf16[2,160,64]{2,1,0:T(8,128)(2,1)S(1)}, bf16[2,160,64]{2,1,0:T(8,128)(2,1)S(1)}, u32[]{:S(2)}, u32[]{:S(2)}) collective-permute-start(bf16[2,160,64]{2,1,0:T(8,128)(2,1)S(1)} %get-tuple-element.10), channel_id=1, source_target_pairs={{0,4},{4,8},{8,12},{12,0},{1,5},{5,9},{9,13},{13,1},{2,6},{6,10},{... | collective-permute-start | bytes 122888 | tf_op jit(solution)/shard_map/halo/ppermute | solution.py:205
  11.0 7.9 %collective-permute-start.1 = (bf16[2,160,64]{2,1,0:T(8,128)(2,1)S(1)}, bf16[2,160,64]{2,1,0:T(8,128)(2,1)S(1)}, u32[]{:S(2)}, u32[]{:S(2)}) collective-permute-start(bf16[2,160,64]{2,1,0:T(8,128)(2,1)S(1)} %get-tuple-element.11), channel_id=1, source_target_pairs={{0,12},{4,0},{8,4},{12,8},{1,13},{5,1},{9,5},{13,9},{2,14},{6,2},{... | collective-permute-start | bytes 122888 | tf_op jit(solution)/shard_map/halo/ppermute | solution.py:206
  13.3 5.6 %collective-permute-start.3 = (bf16[2,80,64]{2,1,0:T(8,128)(2,1)S(1)}, bf16[2,80,64]{2,1,0:T(8,128)(2,1)S(1)}, u32[]{:S(2)}, u32[]{:S(2)}) collective-permute-start(bf16[2,80,64]{2,1,0:T(8,128)(2,1)S(1)} %get-tuple-element.12), channel_id=1, source_target_pairs={{0,5},{1,4},{4,9},{5,8},{8,13},{9,12},{12,1},{13,0},{2,7},{3,6},{6... | collective-permute-start | bytes 61448 | tf_op jit(solution)/shard_map/interface/ppermute | solution.py:208
  13.9 5.0 %collective-permute-start.2 = (bf16[2,80,64]{2,1,0:T(8,128)(2,1)S(1)}, bf16[2,80,64]{2,1,0:T(8,128)(2,1)S(1)}, u32[]{:S(2)}, u32[]{:S(2)}) collective-permute-start(bf16[2,80,64]{2,1,0:T(8,128)(2,1)S(1)} %get-tuple-element.12), channel_id=1, source_target_pairs={{0,1},{1,0},{4,5},{5,4},{8,9},{9,8},{12,13},{13,12},{2,3},{3,2},{6... | collective-permute-start | bytes 61448 | tf_op jit(solution)/shard_map/interface/ppermute | solution.py:208

commit v26 on v4

--- a/solution.py
+++ b/solution.py
@@ -39,10 +39,11 @@
     for n in range(first_ref.shape[0]):
         first = dot(trace_ref[...], first_ref[n]).astype(jnp.bfloat16)
         last = dot(trace_ref[4 * width :, :], last_ref[n]).astype(jnp.bfloat16)
-        down_ref[n] = first[4 * width :, :LAYER]
-        up_ref[n] = last[:, last.shape[1] - LAYER :]
-        rows = cross_ref.shape[2]
-        cross_ref[n] = jnp.where(section == 0, first[width : 2 * width, :rows], first[:width, :rows])
+        down_ref[:, n * LAYER : (n + 1) * LAYER] = first[4 * width :, :LAYER]
+        up_ref[:, n * LAYER : (n + 1) * LAYER] = last[:, last.shape[1] - LAYER :]
+        rows = cross_ref.shape[1] // first_ref.shape[0]
+        cross_ref[:, n * rows : (n + 1) * rows] = jnp.where(
+            section == 0, first[width : 2 * width, :rows], first[:width, :rows])
 
 
 def couple_kernel(shards, peers, place_ref, freq_ref, table_ref, adj_ref, partner_ref, all_ref, tile_ref, forcing_ref,
@@ -74,8 +75,8 @@
             values = dot(traces[OPPOSITE[f]], one_hot(adj - LAYER, total))
             if edge and f >= 4:
                 part = slice((5 - f) * width, (6 - f) * width)
-                below = jnp.concatenate([low_ref[n, part, :] for n in range(count)], axis=0)
-                above = jnp.concatenate([high_ref[n, part, :] for n in range(count)], axis=0)
+                below = jnp.concatenate([low_ref[part, n * LAYER : (n + 1) * LAYER] for n in range(count)], axis=0)
+                above = jnp.concatenate([high_ref[part, n * LAYER : (n + 1) * LAYER] for n in range(count)], axis=0)
                 values += dot(below, one_hot(adj, LAYER))
                 values += dot(above, one_hot(adj - (LAYER + total), LAYER))
             values = values.astype(jnp.bfloat16)
@@ -88,7 +89,7 @@
                     arrived = jnp.zeros((width, rows), jnp.float32)
                     for d in range(shards):
                         source = lax.rem(space - d + shards, shards)
-                        arrived += dot(pieces[d][n], one_hot(wanted - source * rows, rows))
+                        arrived += dot(pieces[d][:, n * rows : (n + 1) * rows], one_hot(wanted - source * rows, rows))
                     crossed.append(arrived)
                 crossed = jnp.concatenate(crossed, axis=0).astype(jnp.bfloat16)
                 crossed = jnp.concatenate(
@@ -178,16 +179,16 @@
         up, down, cross = pl.pallas_call(
             ends_kernel,
             grid=(1,),
-            out_shape=(jax.ShapeDtypeStruct((count, 2 * width, LAYER), bf16),
-                       jax.ShapeDtypeStruct((count, 2 * width, LAYER), bf16),
-                       jax.ShapeDtypeStruct((count, width, iface_rows), bf16)),
+            out_shape=(jax.ShapeDtypeStruct((2 * width, count * LAYER), bf16),
+                       jax.ShapeDtypeStruct((2 * width, count * LAYER), bf16),
+                       jax.ShapeDtypeStruct((width, count * iface_rows), bf16)),
             in_specs=[smem,
                       pl.BlockSpec((count, dof, LANES), lambda j: (0, 0, 0)),
                       pl.BlockSpec((count, dof, LANES), lambda j: (0, 0, total // LANES - 1)),
                       whole(trace_matrix)],
-            out_specs=(pl.BlockSpec((count, 2 * width, LAYER), lambda j: (0, 0, 0)),
-                       pl.BlockSpec((count, 2 * width, LAYER), lambda j: (0, 0, 0)),
-                       pl.BlockSpec((count, width, iface_rows), lambda j: (0, 0, 0))),
+            out_specs=(pl.BlockSpec((2 * width, count * LAYER), lambda j: (0, 0)),
+                       pl.BlockSpec((2 * width, count * LAYER), lambda j: (0, 0)),
+                       pl.BlockSpec((width, count * iface_rows), lambda j: (0, 0))),
             compiler_params=pltpu.CompilerParams(vmem_limit_bytes=VMEM_LIMIT),
             cost_estimate=pl.CostEstimate(flops=8 * width * dof * LANES * 2 * count,
                                           bytes_accessed=1_000_000, transcendentals=0),

time: 33.8 us -> 33.8 us (level)
  starting transfers between devices: 12.4 us -> 10.5 us
  waiting for transfers between devices: 4.67 us -> 6.48 us
    ppermute x4, starting transfers between devices: 5.62 us -> 3.78 us  [body(): lax.ppermute(cross, ('space', 'row'), [(i * 2 + r, (i + d) % shards * 2 +...]
    ppermute x4, waiting for transfers between devices: 2.16 us -> 3.37 us  [body(): lax.ppermute(cross, ('space', 'row'), [(i * 2 + r, (i + d) % shards * 2 +...]
    ppermute x1, waiting for transfers between devices: 2.5 us -> 3.1 us  [body(): lax.ppermute(current, 'inst', [(i, (i + d) % peers) for i in range(peers)])]
where the time goes in v26:
time: 33.8 us; the launch traced here: 33.6 us
  Pallas kernels  13.1 us (39%)
  starting transfers between devices  10.5 us (31%)
  waiting for transfers between devices  6.48 us (19%)
  local copies, waits for them, and re-layouts  2.58 us (8%)
  between operations  0.79 us (2%)
    pallas_call x1, Pallas kernels, body(): pl.pallas_call(functools.partial(couple_kernel, shards, peers), grid=(ste...  10.5 us
    ppermute x4, starting transfers between devices, body(): lax.ppermute(cross, ('space', 'row'), [(i * 2 + r, (i + d) % shards * 2 +...  3.78 us
    ppermute x4, waiting for transfers between devices, body(): lax.ppermute(cross, ('space', 'row'), [(i * 2 + r, (i + d) % shards * 2 +...  3.37 us
    ppermute x1, waiting for transfers between devices, body(): lax.ppermute(current, 'inst', [(i, (i + d) % peers) for i in range(peers)])  3.1 us
    ppermute x1, starting transfers between devices, body(): lax.ppermute(current, 'inst', [(i, (i + d) % peers) for i in range(peers)])  2.94 us
    unnamed x20, local copies, waits for them, and re-layouts  2.58 us
    ppermute x1, starting transfers between devices, body(): lax.ppermute(down, 'space', [(i, (i - 1) % shards) for i in range(shards)])  2.25 us
    pallas_call x1, Pallas kernels, body(): pl.pallas_call(functools.partial(update_kernel, tile), out_shape=jax.Shap...  1.64 us
  transfers between devices with their start and end apart: 7, of which 3 were waited for; matrix products, arithmetic and copies ran while one was open for 4% of the time, Pallas kernels for 34%

profile of v26, /device:TPU:0, one launch (start us, length us, event | category | flops | bytes accessed | tf_op | source)
XLA Modules:
  0.0 33.6 jit_solution(1224837313255545181)
XLA Ops:
  0.0 2.9 %collective-permute-start.6 = (bf16[2,320,1024]{2,1,0:T(8,128)(2,1)}, bf16[2,320,1024]{2,1,0:T(8,128)(2,1)S(1)}, u32[]{:S(2)}, u32[]{:S(2)}) collective-permute-start(bf16[2,320,1024]{2,1,0:T(8,128)(2,1)} %bitcast.10), channel_id=1, source_target_pairs={{0,2},{2,0},{1,3},{3,1},{4,6},{6,4},{5,7},{7,5},{8,10},{10,8},{9,1... | collective-permute-start | bytes 3932168 | tf_op jit(solution)/shard_map/instances/ppermute | solution.py:175
  2.9 1.2 %copy.13.trace_ref = bf16[480,320]{1,0:T(8,128)(2,1)S(1)} copy(bf16[480,320]{0,1:T(8,128)(2,1)} %param.18) | data formatting | bytes 614400 | tf_op args[7]
  4.2 0.1 pad_add_fusion.place_ref
  4.2 0.0 copy-start
  4.2 1.3 %copy-done = bf16[1,2,320,1024]{3,2,1,0:T(8,128)(2,1)S(1)} copy-done((bf16[1,2,320,1024]{3,2,1,0:T(8,128)(2,1)S(1)}, bf16[1,2,320,1024]{3,2,1,0:T(8,128)(2,1)}, u32[]{:S(2)}) %copy-start) | copy-done | bytes 1310744
  5.6 0.0 copy-start.8
  5.6 0.0 copy-start.1
  5.6 0.0 copy-start.2
  5.6 0.0 copy-start.3
  5.6 0.0 copy-start.4
  5.6 0.0 copy-start.5
  5.6 0.0 copy-start.6
  5.6 0.0 copy-start.7
  5.6 1.0 %ends.1 = (bf16[160,128]{1,0:T(8,128)(2,1)S(1)}, bf16[160,128]{1,0:T(8,128)(2,1)S(1)}, bf16[80,128]{1,0:T(8,128)(2,1)S(1)}) custom-call(s32[3]{0:T(128)S(1)} %pad_add_fusion.place_ref, bf16[2,320,1024]{2,1,0:T(8,128)(2,1)S(1)} %bitcast.11, bf16[2,320,1024]{2,1,0:T(8,128)(2,1)S(1)} %bitcast.12, bf16[480,320]{1,0:T(8,128)(2,1)S(1)} %copy.13.trace_ref), custom_call_target="tpu_custom_call" | custom-call | flops 104857600 | bytes 1000000 | tf_op jit(solution)/shard_map/ends/ends/pallas_call | solution.py:179
  6.6 2.8 %collective-permute-start.5 = (bf16[80,128]{1,0:T(8,128)(2,1)S(1)}, bf16[80,128]{1,0:T(8,128)(2,1)S(1)}, u32[]{:S(2)}, u32[]{:S(2)}) collective-permute-start(bf16[80,128]{1,0:T(8,128)(2,1)S(1)} %get-tuple-element.12), channel_id=1, source_target_pairs={{0,13},{1,12},{4,1},{5,0},{8,5},{9,4},{12,9},{13,8},{2,15},{3,14},... | collective-permute-start | bytes 61448 | tf_op jit(solution)/shard_map/interface/ppermute | solution.py:202
  9.4 0.0 collective-permute-start.4
  9.4 1.6 %collective-permute-start = (bf16[160,128]{1,0:T(8,128)(2,1)S(1)}, bf16[160,128]{1,0:T(8,128)(2,1)S(1)}, u32[]{:S(2)}, u32[]{:S(2)}) collective-permute-start(bf16[160,128]{1,0:T(8,128)(2,1)S(1)} %get-tuple-element.10), channel_id=1, source_target_pairs={{0,4},{4,8},{8,12},{12,0},{1,5},{5,9},{9,13},{13,1},{2,6},{6,10},{... | collective-permute-start | bytes 122888 | tf_op jit(solution)/shard_map/halo/ppermute | solution.py:199
  11.0 2.2 %collective-permute-start.1 = (bf16[160,128]{1,0:T(8,128)(2,1)S(1)}, bf16[160,128]{1,0:T(8,128)(2,1)S(1)}, u32[]{:S(2)}, u32[]{:S(2)}) collective-permute-start(bf16[160,128]{1,0:T(8,128)(2,1)S(1)} %get-tuple-element.11), channel_id=1, source_target_pairs={{0,12},{4,0},{8,4},{12,8},{1,13},{5,1},{9,5},{13,9},{2,14},{6,2},{... | collective-permute-start | bytes 122888 | tf_op jit(solution)/shard_map/halo/ppermute | solution.py:200
  13.3 0.0 collective-permute-done.5.rest_3_
  13.3 0.0 collective-permute-start.3
  13.3 0.3 collective-permute-done.4.rest_2_
  13.5 1.0 %collective-permute-start.2 = (bf16[80,128]{1,0:T(8,128)(2,1)S(1)}, bf16[80,128]{1,0:T(8,128)(2,1)S(1)}, u32[]{:S(2)}, u32[]{:S(2)}) collective-permute-start(bf16[80,128]{1,0:T(8,128)(2,1)S(1)} %get-tuple-element.12), channel_id=1, source_target_pairs={{0,1},{1,0},{4,5},{5,4},{8,9},{9,8},{12,13},{13,12},{2,3},{3,2},{6... | collective-permute-start | bytes 61448 | tf_op jit(solution)/shard_map/interface/ppermute | solution.py:202
  15.2 0.0 copy-done.8
  15.2 3.1 %collective-permute-done.3.rest_1_ = bf16[80,128]{1,0:T(8,128)(2,1)S(1)} collective-permute-done((bf16[80,128]{1,0:T(8,128)(2,1)S(1)}, bf16[80,128]{1,0:T(8,128)(2,1)S(1)}, u32[]{:S(2)}, u32[]{:S(2)}) %collective-permute-start.3) | collective-permute-done | bytes 20512 | tf_op jit(solution)/shard_map/interface/ppermute | solution.py:202
  18.3 0.0 collective-permute-done.2.rest_0_
  18.3 0.0 collective-permute-done.low_ref
  18.3 0.0 collective-permute-done.1.high_ref
  18.3 0.0 copy-done.1
  18.3 0.0 copy-done.2
  18.3 0.0 copy-done.3
  18.3 0.0 copy-done.4
  18.3 0.0 copy-done.5
  18.3 0.0 copy-done.6
  18.3 0.0 copy-done.7
  18.4 10.5 %couple.1 = (f32[2,320,1024]{2,1,0:T(8,128)S(1)}, f32[4,1024]{1,0:T(4,128)S(1)}) custom-call(s32[3]{0:T(128)S(1)} %pad_add_fusion.place_ref, f32[1]{0:T(128)S(6)} %copy.17.freq_ref, f32[4,4]{1,0:T(4,128)S(1)} %copy-done.7, s32[6,1024]{1,0:T(8,128)S(1)} %bitcast.15, s32[2,64]{1,0:T(2,128)S(1)} %bitcast.17, bf16[2,320,1024]{2,1,0:T(8,128)(2,1)S(1)} %bitcast.13, ...), custom_call_target="tpu_custom_call" | custom-call | flops 3690987520 | bytes 6553600 | tf_op jit(solution)/shard_map/couple/couple/pallas_call | solution.py:210
  28.8 3.1 %collective-permute-done.6.rest_0_ = bf16[2,320,1024]{2,1,0:T(8,128)(2,1)S(1)} collective-permute-done((bf16[2,320,1024]{2,1,0:T(8,128)(2,1)}, bf16[2,320,1024]{2,1,0:T(8,128)(2,1)S(1)}, u32[]{:S(2)}, u32[]{:S(2)}) %collective-permute-start.6) | collective-permute-done | bytes 1310752 | tf_op jit(solution)/shard_map/instances/ppermute | solution.py:175
  31.9 1.6 %update.1 = bf16[2,320,1024]{2,1,0:T(8,128)(2,1)} custom-call(f32[2,320,1024]{2,1,0:T(8,128)S(1)} %get-tuple-element.13.ready_ref, f32[4,1024]{1,0:T(4,128)S(1)} %get-tuple-element.14.factor_ref, bf16[320,320]{1,0:T(8,128)(2,1)S(1)} %copy-done.1, bf16[2,320,1024]{2,1,0:T(8,128)(2,1)S(1)} %collective-permute-done.6.rest_0_), custom_call_target="tpu_custom_call" | custom-call | flops 419430400 | bytes 5242880 | tf_op jit(solution)/shard_map/update/update/pallas_call | solution.py:230
  (1 shorter events, 0.0 us)
Async XLA Ops:
  0.0 31.9 %collective-permute-start.6 = (bf16[2,320,1024]{2,1,0:T(8,128)(2,1)}, bf16[2,320,1024]{2,1,0:T(8,128)(2,1)S(1)}, u32[]{:S(2)}, u32[]{:S(2)}) collective-permute-start(bf16[2,320,1024]{2,1,0:T(8,128)(2,1)} %bitcast.10), channel_id=1, source_target_pairs={{0,2},{2,0},{1,3},{3,1},{4,6},{6,4},{5,7},{7,5},{8,10},{10,8},{9,1... | collective-permute-start | bytes 3932168 | tf_op jit(solution)/shard_map/instances/ppermute | solution.py:175
  4.2 1.3 %copy-start = (bf16[1,2,320,1024]{3,2,1,0:T(8,128)(2,1)S(1)}, bf16[1,2,320,1024]{3,2,1,0:T(8,128)(2,1)}, u32[]{:S(2)}) copy-start(bf16[1,2,320,1024]{3,2,1,0:T(8,128)(2,1)} %param.11) | copy-start | bytes 3932164
  5.6 9.6 %copy-start.8 = (s32[1,6,1024]{2,0,1:T(1,128)S(1)}, s32[1,6,1024]{2,0,1:T(1,128)}, u32[]{:S(2)}) copy-start(s32[1,6,1024]{2,0,1:T(1,128)} %param.15) | copy-start | bytes 73732
  5.6 12.7 %copy-start.1 = (bf16[320,320]{1,0:T(8,128)(2,1)S(1)}, bf16[320,320]{1,0:T(8,128)(2,1)}, u32[]{:S(2)}) copy-start(bf16[320,320]{1,0:T(8,128)(2,1)} %inverse_ref.3) | copy-start | bytes 614404
  5.6 12.7 %copy-start.2 = (bf16[1,2,320,1024]{3,2,1,0:T(8,128)(2,1)S(1)}, bf16[1,2,320,1024]{3,2,1,0:T(8,128)(2,1)}, u32[]{:S(2)}) copy-start(bf16[1,2,320,1024]{3,2,1,0:T(8,128)(2,1)} %param.12) | copy-start | bytes 3932164
  5.6 12.7 %copy-start.3 = (bf16[320,480]{1,0:T(8,128)(2,1)S(1)}, bf16[320,480]{1,0:T(8,128)(2,1)}, u32[]{:S(2)}) copy-start(bf16[320,480]{1,0:T(8,128)(2,1)} %lift_ref.1) | copy-start | bytes 921604
  5.6 12.8 %copy-start.4 = (bf16[320,320]{1,0:T(8,128)(2,1)S(1)}, bf16[320,320]{1,0:T(8,128)(2,1)}, u32[]{:S(2)}) copy-start(bf16[320,320]{1,0:T(8,128)(2,1)} %volume_ref.1) | copy-start | bytes 614404
  5.6 12.7 %copy-start.5 = (f32[1,1024]{1,0:T(1,128)S(1)}, f32[1,1024]{1,0:T(1,128)}, u32[]{:S(2)}) copy-start(f32[1,1024]{1,0:T(1,128)} %scale_ref.1) | copy-start | bytes 12292
  5.6 12.7 %copy-start.6 = (s32[1,2,64]{2,1,0:T(2,128)S(1)}, s32[1,2,64]{2,1,0:T(2,128)}, u32[]{:S(2)}) copy-start(s32[1,2,64]{2,1,0:T(2,128)} %param.16) | copy-start | bytes 1540
  5.6 12.7 %copy-start.7 = (f32[4,4]{1,0:T(4,128)S(1)}, f32[4,4]{1,0:T(4,128)}, u32[]{:S(2)}) copy-start(f32[4,4]{1,0:T(4,128)} %constant.13.clone.table_ref) | copy-start | bytes 196
  6.6 6.6 %collective-permute-start.5 = (bf16[80,128]{1,0:T(8,128)(2,1)S(1)}, bf16[80,128]{1,0:T(8,128)(2,1)S(1)}, u32[]{:S(2)}, u32[]{:S(2)}) collective-permute-start(bf16[80,128]{1,0:T(8,128)(2,1)S(1)} %get-tuple-element.12), channel_id=1, source_target_pairs={{0,13},{1,12},{4,1},{5,0},{8,5},{9,4},{12,9},{13,8},{2,15},{3,14},... | collective-permute-start | bytes 61448 | tf_op jit(solution)/shard_map/interface/ppermute | solution.py:202
  9.4 4.1 %collective-permute-start.4 = (bf16[80,128]{1,0:T(8,128)(2,1)S(1)}, bf16[80,128]{1,0:T(8,128)(2,1)S(1)}, u32[]{:S(2)}, u32[]{:S(2)}) collective-permute-start(bf16[80,128]{1,0:T(8,128)(2,1)S(1)} %get-tuple-element.12), channel_id=1, source_target_pairs={{0,9},{1,8},{4,13},{5,12},{8,1},{9,0},{12,5},{13,4},{2,11},{3,10},... | collective-permute-start | bytes 61448 | tf_op jit(solution)/shard_map/interface/ppermute | solution.py:202
  9.4 8.8 %collective-permute-start = (bf16[160,128]{1,0:T(8,128)(2,1)S(1)}, bf16[160,128]{1,0:T(8,128)(2,1)S(1)}, u32[]{:S(2)}, u32[]{:S(2)}) collective-permute-start(bf16[160,128]{1,0:T(8,128)(2,1)S(1)} %get-tuple-element.10), channel_id=1, source_target_pairs={{0,4},{4,8},{8,12},{12,0},{1,5},{5,9},{9,13},{13,1},{2,6},{6,10},{... | collective-permute-start | bytes 122888 | tf_op jit(solution)/shard_map/halo/ppermute | solution.py:199
  11.0 7.3 %collective-permute-start.1 = (bf16[160,128]{1,0:T(8,128)(2,1)S(1)}, bf16[160,128]{1,0:T(8,128)(2,1)S(1)}, u32[]{:S(2)}, u32[]{:S(2)}) collective-permute-start(bf16[160,128]{1,0:T(8,128)(2,1)S(1)} %get-tuple-element.11), channel_id=1, source_target_pairs={{0,12},{4,0},{8,4},{12,8},{1,13},{5,1},{9,5},{13,9},{2,14},{6,2},{... | collective-permute-start | bytes 122888 | tf_op jit(solution)/shard_map/halo/ppermute | solution.py:200
  13.3 5.0 %collective-permute-start.3 = (bf16[80,128]{1,0:T(8,128)(2,1)S(1)}, bf16[80,128]{1,0:T(8,128)(2,1)S(1)}, u32[]{:S(2)}, u32[]{:S(2)}) collective-permute-start(bf16[80,128]{1,0:T(8,128)(2,1)S(1)} %get-tuple-element.12), channel_id=1, source_target_pairs={{0,5},{1,4},{4,9},{5,8},{8,13},{9,12},{12,1},{13,0},{2,7},{3,6},{6... | collective-permute-start | bytes 61448 | tf_op jit(solution)/shard_map/interface/ppermute | solution.py:202
  13.5 4.7 %collective-permute-start.2 = (bf16[80,128]{1,0:T(8,128)(2,1)S(1)}, bf16[80,128]{1,0:T(8,128)(2,1)S(1)}, u32[]{:S(2)}, u32[]{:S(2)}) collective-permute-start(bf16[80,128]{1,0:T(8,128)(2,1)S(1)} %get-tuple-element.12), channel_id=1, source_target_pairs={{0,1},{1,0},{4,5},{5,4},{8,9},{9,8},{12,13},{13,12},{2,3},{3,2},{6... | collective-permute-start | bytes 61448 | tf_op jit(solution)/shard_map/interface/ppermute | solution.py:202

commit v27 on v23

--- a/solution.py
+++ b/solution.py
@@ -39,10 +39,11 @@
     for n in range(first_ref.shape[0]):
         first = dot(trace_ref[...], first_ref[n]).astype(jnp.bfloat16)
         last = dot(trace_ref[4 * width :, :], last_ref[n]).astype(jnp.bfloat16)
-        down_ref[n] = first[4 * width :, :LAYER]
-        up_ref[n] = last[:, last.shape[1] - LAYER :]
-        rows = cross_ref.shape[2]
-        cross_ref[n] = jnp.where(section == 0, first[width : 2 * width, :rows], first[:width, :rows])
+        down_ref[:, n * LAYER : (n + 1) * LAYER] = first[4 * width :, :LAYER]
+        up_ref[:, n * LAYER : (n + 1) * LAYER] = last[:, last.shape[1] - LAYER :]
+        rows = cross_ref.shape[1] // first_ref.shape[0]
+        cross_ref[:, n * rows : (n + 1) * rows] = jnp.where(
+            section == 0, first[width : 2 * width, :rows], first[:width, :rows])
 
 
 def couple_kernel(shards, peers, deep, place_ref, freq_ref, table_ref, adj_ref, partner_ref, all_ref, tile_ref, forcing_ref,
@@ -79,8 +80,8 @@
             values = dot(traces[OPPOSITE[f]], one_hot(adj - LAYER, total))
             if edge and f >= 4:
                 part = slice((5 - f) * width, (6 - f) * width)
-                below = jnp.concatenate([low_ref[n, part, :] for n in range(count)], axis=0)
-                above = jnp.concatenate([high_ref[n, part, :] for n in range(count)], axis=0)
+                below = jnp.concatenate([low_ref[part, n * LAYER : (n + 1) * LAYER] for n in range(count)], axis=0)
+                above = jnp.concatenate([high_ref[part, n * LAYER : (n + 1) * LAYER] for n in range(count)], axis=0)
                 values += dot(below, one_hot(adj, LAYER))
                 values += dot(above, one_hot(adj - (LAYER + total), LAYER))
             values = values.astype(jnp.bfloat16)
@@ -93,7 +94,7 @@
                     arrived = jnp.zeros((width, rows), jnp.float32)
                     for d in range(shards):
                         source = lax.rem(space - d + shards, shards)
-                        arrived += dot(pieces[d][n], one_hot(wanted - source * rows, rows))
+                        arrived += dot(pieces[d][:, n * rows : (n + 1) * rows], one_hot(wanted - source * rows, rows))
                     crossed.append(arrived)
                 crossed = jnp.concatenate(crossed, axis=0).astype(jnp.bfloat16)
                 crossed = jnp.concatenate(
@@ -196,16 +197,16 @@
         up, down, cross = pl.pallas_call(
             ends_kernel,
             grid=(1,),
-            out_shape=(jax.ShapeDtypeStruct((count, 2 * width, LAYER), bf16),
-                       jax.ShapeDtypeStruct((count, 2 * width, LAYER), bf16),
-                       jax.ShapeDtypeStruct((count, width, iface_rows), bf16)),
+            out_shape=(jax.ShapeDtypeStruct((2 * width, count * LAYER), bf16),
+                       jax.ShapeDtypeStruct((2 * width, count * LAYER), bf16),
+                       jax.ShapeDtypeStruct((width, count * iface_rows), bf16)),
             in_specs=[smem,
                       pl.BlockSpec((count, dof, LANES), lambda j: (0, 0, 0)),
                       pl.BlockSpec((count, dof, LANES), lambda j: (0, 0, total // LANES - 1)),
                       whole(trace_matrix)],
-            out_specs=(pl.BlockSpec((count, 2 * width, LAYER), lambda j: (0, 0, 0)),
-                       pl.BlockSpec((count, 2 * width, LAYER), lambda j: (0, 0, 0)),
-                       pl.BlockSpec((count, width, iface_rows), lambda j: (0, 0, 0))),
+            out_specs=(pl.BlockSpec((2 * width, count * LAYER), lambda j: (0, 0)),
+                       pl.BlockSpec((2 * width, count * LAYER), lambda j: (0, 0)),
+                       pl.BlockSpec((width, count * iface_rows), lambda j: (0, 0))),
             compiler_params=pltpu.CompilerParams(vmem_limit_bytes=VMEM_LIMIT),
             cost_estimate=pl.CostEstimate(flops=8 * width * dof * LANES * 2 * count,
                                           bytes_accessed=1_000_000, transcendentals=0),

time: 33.7 us -> 33.7 us (level)
  starting transfers between devices: 12.4 us -> 10.5 us
  waiting for transfers between devices: 4.67 us -> 6.47 us
    ppermute x4, starting transfers between devices: 5.62 us -> 3.78 us  [body(): lax.ppermute(cross, ('space', 'row'), [(i * 2 + r, (i + d) % shards * 2 +...]
    ppermute x4, waiting for transfers between devices: 2.16 us -> 3.37 us  [body(): lax.ppermute(cross, ('space', 'row'), [(i * 2 + r, (i + d) % shards * 2 +...]
    ppermute x1, waiting for transfers between devices: 2.5 us -> 3.1 us  [body(): lax.ppermute(current, 'inst', [(i, (i + d) % peers) for i in range(peers)])]
where the time goes in v27:
time: 33.7 us; the launch traced here: 33.5 us
  Pallas kernels  13.1 us (39%)
  starting transfers between devices  10.5 us (31%)
  waiting for transfers between devices  6.47 us (19%)
  local copies, waits for them, and re-layouts  2.58 us (8%)
  between operations  0.79 us (2%)
    pallas_call x1, Pallas kernels, body(): pl.pallas_call(functools.partial(couple_kernel, shards, peers, deep), gri...  10.5 us
    ppermute x4, starting transfers between devices, body(): lax.ppermute(cross, ('space', 'row'), [(i * 2 + r, (i + d) % shards * 2 +...  3.78 us
    ppermute x4, waiting for transfers between devices, body(): lax.ppermute(cross, ('space', 'row'), [(i * 2 + r, (i + d) % shards * 2 +...  3.37 us
    ppermute x1, waiting for transfers between devices, body(): lax.ppermute(current, 'inst', [(i, (i + d) % peers) for i in range(peers)])  3.1 us
    ppermute x1, starting transfers between devices, body(): lax.ppermute(current, 'inst', [(i, (i + d) % peers) for i in range(peers)])  2.94 us
    unnamed x20, local copies, waits for them, and re-layouts  2.58 us
    ppermute x1, starting transfers between devices, body(): lax.ppermute(down, 'space', [(i, (i - 1) % shards) for i in range(shards)])  2.25 us
    pallas_call x1, Pallas kernels, body(): pl.pallas_call(functools.partial(update_kernel, tile, deep), out_shape=ja...  1.62 us
  transfers between devices with their start and end apart: 7, of which 3 were waited for; matrix products, arithmetic and copies ran while one was open for 4% of the time, Pallas kernels for 34%

profile of v27, /device:TPU:0, one launch (start us, length us, event | category | flops | bytes accessed | tf_op | source)
XLA Modules:
  0.0 33.5 jit_solution(5539595215579060124)
XLA Ops:
  0.0 2.9 %collective-permute-start.6 = (bf16[2,320,1024]{2,1,0:T(8,128)(2,1)}, bf16[2,320,1024]{2,1,0:T(8,128)(2,1)S(1)}, u32[]{:S(2)}, u32[]{:S(2)}) collective-permute-start(bf16[2,320,1024]{2,1,0:T(8,128)(2,1)} %bitcast.10), channel_id=1, source_target_pairs={{0,2},{2,0},{1,3},{3,1},{4,6},{6,4},{5,7},{7,5},{8,10},{10,8},{9,1... | collective-permute-start | bytes 3932168 | tf_op jit(solution)/shard_map/instances/ppermute | solution.py:193
  2.9 1.2 %copy.13.trace_ref = bf16[480,320]{1,0:T(8,128)(2,1)S(1)} copy(bf16[480,320]{0,1:T(8,128)(2,1)} %param.18) | data formatting | bytes 614400 | tf_op args[7]
  4.2 0.1 pad_add_fusion.place_ref
  4.2 0.0 copy-start
  4.2 1.3 %copy-done = bf16[1,2,320,1024]{3,2,1,0:T(8,128)(2,1)S(1)} copy-done((bf16[1,2,320,1024]{3,2,1,0:T(8,128)(2,1)S(1)}, bf16[1,2,320,1024]{3,2,1,0:T(8,128)(2,1)}, u32[]{:S(2)}) %copy-start) | copy-done | bytes 1310744
  5.6 0.0 copy-start.8
  5.6 0.0 copy-start.1
  5.6 0.0 copy-start.2
  5.6 0.0 copy-start.3
  5.6 0.0 copy-start.4
  5.6 0.0 copy-start.5
  5.6 0.0 copy-start.6
  5.6 0.0 copy-start.7
  5.6 1.0 %ends.1 = (bf16[160,128]{1,0:T(8,128)(2,1)S(1)}, bf16[160,128]{1,0:T(8,128)(2,1)S(1)}, bf16[80,128]{1,0:T(8,128)(2,1)S(1)}) custom-call(s32[3]{0:T(128)S(1)} %pad_add_fusion.place_ref, bf16[2,320,1024]{2,1,0:T(8,128)(2,1)S(1)} %bitcast.11, bf16[2,320,1024]{2,1,0:T(8,128)(2,1)S(1)} %bitcast.12, bf16[480,320]{1,0:T(8,128)(2,1)S(1)} %copy.13.trace_ref), custom_call_target="tpu_custom_call" | custom-call | flops 104857600 | bytes 1000000 | tf_op jit(solution)/shard_map/ends/ends/pallas_call | solution.py:197
  6.6 2.8 %collective-permute-start.5 = (bf16[80,128]{1,0:T(8,128)(2,1)S(1)}, bf16[80,128]{1,0:T(8,128)(2,1)S(1)}, u32[]{:S(2)}, u32[]{:S(2)}) collective-permute-start(bf16[80,128]{1,0:T(8,128)(2,1)S(1)} %get-tuple-element.13), channel_id=1, source_target_pairs={{0,13},{1,12},{4,1},{5,0},{8,5},{9,4},{12,9},{13,8},{2,15},{3,14},... | collective-permute-start | bytes 61448 | tf_op jit(solution)/shard_map/interface/ppermute | solution.py:220
  9.4 0.0 collective-permute-start.4
  9.4 1.6 %collective-permute-start = (bf16[160,128]{1,0:T(8,128)(2,1)S(1)}, bf16[160,128]{1,0:T(8,128)(2,1)S(1)}, u32[]{:S(2)}, u32[]{:S(2)}) collective-permute-start(bf16[160,128]{1,0:T(8,128)(2,1)S(1)} %get-tuple-element.11), channel_id=1, source_target_pairs={{0,4},{4,8},{8,12},{12,0},{1,5},{5,9},{9,13},{13,1},{2,6},{6,10},{... | collective-permute-start | bytes 122888 | tf_op jit(solution)/shard_map/halo/ppermute | solution.py:217
  11.0 2.2 %collective-permute-start.1 = (bf16[160,128]{1,0:T(8,128)(2,1)S(1)}, bf16[160,128]{1,0:T(8,128)(2,1)S(1)}, u32[]{:S(2)}, u32[]{:S(2)}) collective-permute-start(bf16[160,128]{1,0:T(8,128)(2,1)S(1)} %get-tuple-element.12), channel_id=1, source_target_pairs={{0,12},{4,0},{8,4},{12,8},{1,13},{5,1},{9,5},{13,9},{2,14},{6,2},{... | collective-permute-start | bytes 122888 | tf_op jit(solution)/shard_map/halo/ppermute | solution.py:218
  13.3 0.0 collective-permute-done.5.rest_3_
  13.3 0.0 collective-permute-start.3
  13.3 0.3 collective-permute-done.4.rest_2_
  13.5 1.0 %collective-permute-start.2 = (bf16[80,128]{1,0:T(8,128)(2,1)S(1)}, bf16[80,128]{1,0:T(8,128)(2,1)S(1)}, u32[]{:S(2)}, u32[]{:S(2)}) collective-permute-start(bf16[80,128]{1,0:T(8,128)(2,1)S(1)} %get-tuple-element.13), channel_id=1, source_target_pairs={{0,1},{1,0},{4,5},{5,4},{8,9},{9,8},{12,13},{13,12},{2,3},{3,2},{6... | collective-permute-start | bytes 61448 | tf_op jit(solution)/shard_map/interface/ppermute | solution.py:220
  15.2 0.0 copy-done.8
  15.2 3.1 %collective-permute-done.3.rest_1_ = bf16[80,128]{1,0:T(8,128)(2,1)S(1)} collective-permute-done((bf16[80,128]{1,0:T(8,128)(2,1)S(1)}, bf16[80,128]{1,0:T(8,128)(2,1)S(1)}, u32[]{:S(2)}, u32[]{:S(2)}) %collective-permute-start.3) | collective-permute-done | bytes 20512 | tf_op jit(solution)/shard_map/interface/ppermute | solution.py:220
  18.3 0.0 collective-permute-done.2.rest_0_
  18.3 0.0 collective-permute-done.low_ref
  18.3 0.0 collective-permute-done.1.high_ref
  18.3 0.0 copy-done.1
  18.3 0.0 copy-done.2
  18.3 0.0 copy-done.3
  18.3 0.0 copy-done.4
  18.3 0.0 copy-done.5
  18.3 0.0 copy-done.6
  18.3 0.0 copy-done.7
  18.4 10.5 %couple.1 = (f32[2,320,1024]{2,1,0:T(8,128)S(1)}, f32[4,1024]{1,0:T(4,128)S(1)}, bf16[2,320,128]{2,1,0:T(8,128)(2,1)S(1)}) custom-call(s32[3]{0:T(128)S(1)} %pad_add_fusion.place_ref, f32[1]{0:T(128)S(6)} %copy.17.freq_ref, f32[4,4]{1,0:T(4,128)S(1)} %copy-done.7, s32[6,1024]{1,0:T(8,128)S(1)} %bitcast.15, s32[2,64]{1,0:T(2,128)S(1)} %bitcast.17, ...), custom_call_target="tpu_custom_call" | custom-call | flops 3690987520 | bytes 6553600 | tf_op jit(solution)/shard_map/couple/couple/pallas_call | solution.py:229
  28.8 3.1 %collective-permute-done.6.rest_0_ = bf16[2,320,1024]{2,1,0:T(8,128)(2,1)S(1)} collective-permute-done((bf16[2,320,1024]{2,1,0:T(8,128)(2,1)}, bf16[2,320,1024]{2,1,0:T(8,128)(2,1)S(1)}, u32[]{:S(2)}, u32[]{:S(2)}) %collective-permute-start.6) | collective-permute-done | bytes 1310752 | tf_op jit(solution)/shard_map/instances/ppermute | solution.py:193
  31.9 1.6 %update.1 = bf16[2,320,1024]{2,1,0:T(8,128)(2,1)} custom-call(f32[2,320,1024]{2,1,0:T(8,128)S(1)} %get-tuple-element.14.ready_ref, f32[4,1024]{1,0:T(4,128)S(1)} %get-tuple-element.15.factor_ref, bf16[320,320]{1,0:T(8,128)(2,1)S(1)} %copy-done.1, bf16[2,320,128]{2,1,0:T(8,128)(2,1)S(1)} %get-tuple-element.16.spread_ref, ...), custom_call_target="tpu_custom_call" | custom-call | flops 419430400 | bytes 5242880 | tf_op jit(solution)/shard_map/update/update/pallas_call | solution.py:251
  (1 shorter events, 0.0 us)
Async XLA Ops:
  0.0 31.9 %collective-permute-start.6 = (bf16[2,320,1024]{2,1,0:T(8,128)(2,1)}, bf16[2,320,1024]{2,1,0:T(8,128)(2,1)S(1)}, u32[]{:S(2)}, u32[]{:S(2)}) collective-permute-start(bf16[2,320,1024]{2,1,0:T(8,128)(2,1)} %bitcast.10), channel_id=1, source_target_pairs={{0,2},{2,0},{1,3},{3,1},{4,6},{6,4},{5,7},{7,5},{8,10},{10,8},{9,1... | collective-permute-start | bytes 3932168 | tf_op jit(solution)/shard_map/instances/ppermute | solution.py:193
  4.2 1.3 %copy-start = (bf16[1,2,320,1024]{3,2,1,0:T(8,128)(2,1)S(1)}, bf16[1,2,320,1024]{3,2,1,0:T(8,128)(2,1)}, u32[]{:S(2)}) copy-start(bf16[1,2,320,1024]{3,2,1,0:T(8,128)(2,1)} %param.11) | copy-start | bytes 3932164
  5.6 9.6 %copy-start.8 = (s32[1,6,1024]{2,0,1:T(1,128)S(1)}, s32[1,6,1024]{2,0,1:T(1,128)}, u32[]{:S(2)}) copy-start(s32[1,6,1024]{2,0,1:T(1,128)} %param.15) | copy-start | bytes 73732
  5.6 12.7 %copy-start.1 = (bf16[320,320]{1,0:T(8,128)(2,1)S(1)}, bf16[320,320]{1,0:T(8,128)(2,1)}, u32[]{:S(2)}) copy-start(bf16[320,320]{1,0:T(8,128)(2,1)} %inverse_ref.3) | copy-start | bytes 614404
  5.6 12.7 %copy-start.2 = (bf16[1,2,320,1024]{3,2,1,0:T(8,128)(2,1)S(1)}, bf16[1,2,320,1024]{3,2,1,0:T(8,128)(2,1)}, u32[]{:S(2)}) copy-start(bf16[1,2,320,1024]{3,2,1,0:T(8,128)(2,1)} %param.12) | copy-start | bytes 3932164
  5.6 12.7 %copy-start.3 = (bf16[320,480]{1,0:T(8,128)(2,1)S(1)}, bf16[320,480]{1,0:T(8,128)(2,1)}, u32[]{:S(2)}) copy-start(bf16[320,480]{1,0:T(8,128)(2,1)} %lift_ref.1) | copy-start | bytes 921604
  5.6 12.8 %copy-start.4 = (bf16[320,320]{1,0:T(8,128)(2,1)S(1)}, bf16[320,320]{1,0:T(8,128)(2,1)}, u32[]{:S(2)}) copy-start(bf16[320,320]{1,0:T(8,128)(2,1)} %volume_ref.1) | copy-start | bytes 614404
  5.6 12.7 %copy-start.5 = (f32[1,1024]{1,0:T(1,128)S(1)}, f32[1,1024]{1,0:T(1,128)}, u32[]{:S(2)}) copy-start(f32[1,1024]{1,0:T(1,128)} %scale_ref.1) | copy-start | bytes 12292
  5.6 12.7 %copy-start.6 = (s32[1,2,64]{2,1,0:T(2,128)S(1)}, s32[1,2,64]{2,1,0:T(2,128)}, u32[]{:S(2)}) copy-start(s32[1,2,64]{2,1,0:T(2,128)} %param.16) | copy-start | bytes 1540
  5.6 12.7 %copy-start.7 = (f32[4,4]{1,0:T(4,128)S(1)}, f32[4,4]{1,0:T(4,128)}, u32[]{:S(2)}) copy-start(f32[4,4]{1,0:T(4,128)} %constant.13.clone.table_ref) | copy-start | bytes 196
  6.6 6.6 %collective-permute-start.5 = (bf16[80,128]{1,0:T(8,128)(2,1)S(1)}, bf16[80,128]{1,0:T(8,128)(2,1)S(1)}, u32[]{:S(2)}, u32[]{:S(2)}) collective-permute-start(bf16[80,128]{1,0:T(8,128)(2,1)S(1)} %get-tuple-element.13), channel_id=1, source_target_pairs={{0,13},{1,12},{4,1},{5,0},{8,5},{9,4},{12,9},{13,8},{2,15},{3,14},... | collective-permute-start | bytes 61448 | tf_op jit(solution)/shard_map/interface/ppermute | solution.py:220
  9.4 4.1 %collective-permute-start.4 = (bf16[80,128]{1,0:T(8,128)(2,1)S(1)}, bf16[80,128]{1,0:T(8,128)(2,1)S(1)}, u32[]{:S(2)}, u32[]{:S(2)}) collective-permute-start(bf16[80,128]{1,0:T(8,128)(2,1)S(1)} %get-tuple-element.13), channel_id=1, source_target_pairs={{0,9},{1,8},{4,13},{5,12},{8,1},{9,0},{12,5},{13,4},{2,11},{3,10},... | collective-permute-start | bytes 61448 | tf_op jit(solution)/shard_map/interface/ppermute | solution.py:220
  9.4 8.8 %collective-permute-start = (bf16[160,128]{1,0:T(8,128)(2,1)S(1)}, bf16[160,128]{1,0:T(8,128)(2,1)S(1)}, u32[]{:S(2)}, u32[]{:S(2)}) collective-permute-start(bf16[160,128]{1,0:T(8,128)(2,1)S(1)} %get-tuple-element.11), channel_id=1, source_target_pairs={{0,4},{4,8},{8,12},{12,0},{1,5},{5,9},{9,13},{13,1},{2,6},{6,10},{... | collective-permute-start | bytes 122888 | tf_op jit(solution)/shard_map/halo/ppermute | solution.py:217
  11.0 7.3 %collective-permute-start.1 = (bf16[160,128]{1,0:T(8,128)(2,1)S(1)}, bf16[160,128]{1,0:T(8,128)(2,1)S(1)}, u32[]{:S(2)}, u32[]{:S(2)}) collective-permute-start(bf16[160,128]{1,0:T(8,128)(2,1)S(1)} %get-tuple-element.12), channel_id=1, source_target_pairs={{0,12},{4,0},{8,4},{12,8},{1,13},{5,1},{9,5},{13,9},{2,14},{6,2},{... | collective-permute-start | bytes 122888 | tf_op jit(solution)/shard_map/halo/ppermute | solution.py:218
  13.3 5.0 %collective-permute-start.3 = (bf16[80,128]{1,0:T(8,128)(2,1)S(1)}, bf16[80,128]{1,0:T(8,128)(2,1)S(1)}, u32[]{:S(2)}, u32[]{:S(2)}) collective-permute-start(bf16[80,128]{1,0:T(8,128)(2,1)S(1)} %get-tuple-element.13), channel_id=1, source_target_pairs={{0,5},{1,4},{4,9},{5,8},{8,13},{9,12},{12,1},{13,0},{2,7},{3,6},{6... | collective-permute-start | bytes 61448 | tf_op jit(solution)/shard_map/interface/ppermute | solution.py:220
  13.5 4.7 %collective-permute-start.2 = (bf16[80,128]{1,0:T(8,128)(2,1)S(1)}, bf16[80,128]{1,0:T(8,128)(2,1)S(1)}, u32[]{:S(2)}, u32[]{:S(2)}) collective-permute-start(bf16[80,128]{1,0:T(8,128)(2,1)S(1)} %get-tuple-element.13), channel_id=1, source_target_pairs={{0,1},{1,0},{4,5},{5,4},{8,9},{9,8},{12,13},{13,12},{2,3},{3,2},{6... | collective-permute-start | bytes 61448 | tf_op jit(solution)/shard_map/interface/ppermute | solution.py:220

commit v28 on v26

--- a/solution.py
+++ b/solution.py
@@ -143,9 +143,14 @@
                 at = n * len(moved) + k
                 value -= factor_ref[at : at + 1, cols] * part
             made[t, n] = value.astype(jnp.bfloat16)
-        copy = pltpu.make_async_copy(made.at[t], out_ref.at[:, :, cols], sems.at[t])
-        copy.start()
-        copies.append(copy)
+            if t == total // tile - 1:
+                copy = pltpu.make_async_copy(made.at[t, n], out_ref.at[n, :, cols], sems.at[t + n])
+                copy.start()
+                copies.append(copy)
+        if t < total // tile - 1:
+            copy = pltpu.make_async_copy(made.at[t], out_ref.at[:, :, cols], sems.at[t])
+            copy.start()
+            copies.append(copy)
     for copy in copies:
         copy.wait()
 
@@ -232,7 +237,7 @@
             out_shape=jax.ShapeDtypeStruct((count, dof, total), bf16),
             in_specs=[vmem] * (2 + peers),
             out_specs=pl.BlockSpec(memory_space=pl.ANY),
-            scratch_shapes=[pltpu.VMEM((steps, count, dof, tile), bf16), pltpu.SemaphoreType.DMA((steps,))],
+            scratch_shapes=[pltpu.VMEM((steps, count, dof, tile), bf16), pltpu.SemaphoreType.DMA((steps + count - 1,))],
             compiler_params=pltpu.CompilerParams(vmem_limit_bytes=VMEM_LIMIT),
             cost_estimate=pl.CostEstimate(flops=2 * count * total * dof * dof * (peers - 1),
                                           bytes_accessed=count * dof * total * 8, transcendentals=0),

time: 33.8 us -> 33.7 us (level)
  no operation moved by 1% of the time
where the time goes in v28:
time: 33.7 us; the launch traced here: 33.6 us
  Pallas kernels  13.1 us (39%)
  starting transfers between devices  10.5 us (31%)
  waiting for transfers between devices  6.48 us (19%)
  local copies, waits for them, and re-layouts  2.58 us (8%)
  between operations  0.79 us (2%)
    pallas_call x1, Pallas kernels, body(): pl.pallas_call(functools.partial(couple_kernel, shards, peers), grid=(ste...  10.5 us
    ppermute x4, starting transfers between devices, body(): lax.ppermute(cross, ('space', 'row'), [(i * 2 + r, (i + d) % shards * 2 +...  3.78 us
    ppermute x4, waiting for transfers between devices, body(): lax.ppermute(cross, ('space', 'row'), [(i * 2 + r, (i + d) % shards * 2 +...  3.37 us
    ppermute x1, waiting for transfers between devices, body(): lax.ppermute(current, 'inst', [(i, (i + d) % peers) for i in range(peers)])  3.1 us
    ppermute x1, starting transfers between devices, body(): lax.ppermute(current, 'inst', [(i, (i + d) % peers) for i in range(peers)])  2.94 us
    unnamed x20, local copies, waits for them, and re-layouts  2.58 us
    ppermute x1, starting transfers between devices, body(): lax.ppermute(down, 'space', [(i, (i - 1) % shards) for i in range(shards)])  2.25 us
    pallas_call x1, Pallas kernels, body(): pl.pallas_call(functools.partial(update_kernel, tile), out_shape=jax.Shap...  1.64 us
  transfers between devices with their start and end apart: 7, of which 3 were waited for; matrix products, arithmetic and copies ran while one was open for 4% of the time, Pallas kernels for 34%

profile of v28, /device:TPU:0, one launch (start us, length us, event | category | flops | bytes accessed | tf_op | source)
XLA Modules:
  0.0 33.6 jit_solution(2434415164866440788)
XLA Ops:
  0.0 2.9 %collective-permute-start.6 = (bf16[2,320,1024]{2,1,0:T(8,128)(2,1)}, bf16[2,320,1024]{2,1,0:T(8,128)(2,1)S(1)}, u32[]{:S(2)}, u32[]{:S(2)}) collective-permute-start(bf16[2,320,1024]{2,1,0:T(8,128)(2,1)} %bitcast.10), channel_id=1, source_target_pairs={{0,2},{2,0},{1,3},{3,1},{4,6},{6,4},{5,7},{7,5},{8,10},{10,8},{9,1... | collective-permute-start | bytes 3932168 | tf_op jit(solution)/shard_map/instances/ppermute | solution.py:180
  2.9 1.2 %copy.13.trace_ref = bf16[480,320]{1,0:T(8,128)(2,1)S(1)} copy(bf16[480,320]{0,1:T(8,128)(2,1)} %param.18) | data formatting | bytes 614400 | tf_op args[7]
  4.2 0.1 pad_add_fusion.place_ref
  4.2 0.0 copy-start
  4.2 1.3 %copy-done = bf16[1,2,320,1024]{3,2,1,0:T(8,128)(2,1)S(1)} copy-done((bf16[1,2,320,1024]{3,2,1,0:T(8,128)(2,1)S(1)}, bf16[1,2,320,1024]{3,2,1,0:T(8,128)(2,1)}, u32[]{:S(2)}) %copy-start) | copy-done | bytes 1310744
  5.6 0.0 copy-start.8
  5.6 0.0 copy-start.1
  5.6 0.0 copy-start.2
  5.6 0.0 copy-start.3
  5.6 0.0 copy-start.4
  5.6 0.0 copy-start.5
  5.6 0.0 copy-start.6
  5.6 0.0 copy-start.7
  5.6 1.0 %ends.1 = (bf16[160,128]{1,0:T(8,128)(2,1)S(1)}, bf16[160,128]{1,0:T(8,128)(2,1)S(1)}, bf16[80,128]{1,0:T(8,128)(2,1)S(1)}) custom-call(s32[3]{0:T(128)S(1)} %pad_add_fusion.place_ref, bf16[2,320,1024]{2,1,0:T(8,128)(2,1)S(1)} %bitcast.11, bf16[2,320,1024]{2,1,0:T(8,128)(2,1)S(1)} %bitcast.12, bf16[480,320]{1,0:T(8,128)(2,1)S(1)} %copy.13.trace_ref), custom_call_target="tpu_custom_call" | custom-call | flops 104857600 | bytes 1000000 | tf_op jit(solution)/shard_map/ends/ends/pallas_call | solution.py:184
  6.6 2.8 %collective-permute-start.5 = (bf16[80,128]{1,0:T(8,128)(2,1)S(1)}, bf16[80,128]{1,0:T(8,128)(2,1)S(1)}, u32[]{:S(2)}, u32[]{:S(2)}) collective-permute-start(bf16[80,128]{1,0:T(8,128)(2,1)S(1)} %get-tuple-element.12), channel_id=1, source_target_pairs={{0,13},{1,12},{4,1},{5,0},{8,5},{9,4},{12,9},{13,8},{2,15},{3,14},... | collective-permute-start | bytes 61448 | tf_op jit(solution)/shard_map/interface/ppermute | solution.py:207
  9.4 0.0 collective-permute-start.4
  9.4 1.6 %collective-permute-start = (bf16[160,128]{1,0:T(8,128)(2,1)S(1)}, bf16[160,128]{1,0:T(8,128)(2,1)S(1)}, u32[]{:S(2)}, u32[]{:S(2)}) collective-permute-start(bf16[160,128]{1,0:T(8,128)(2,1)S(1)} %get-tuple-element.10), channel_id=1, source_target_pairs={{0,4},{4,8},{8,12},{12,0},{1,5},{5,9},{9,13},{13,1},{2,6},{6,10},{... | collective-permute-start | bytes 122888 | tf_op jit(solution)/shard_map/halo/ppermute | solution.py:204
  11.0 2.2 %collective-permute-start.1 = (bf16[160,128]{1,0:T(8,128)(2,1)S(1)}, bf16[160,128]{1,0:T(8,128)(2,1)S(1)}, u32[]{:S(2)}, u32[]{:S(2)}) collective-permute-start(bf16[160,128]{1,0:T(8,128)(2,1)S(1)} %get-tuple-element.11), channel_id=1, source_target_pairs={{0,12},{4,0},{8,4},{12,8},{1,13},{5,1},{9,5},{13,9},{2,14},{6,2},{... | collective-permute-start | bytes 122888 | tf_op jit(solution)/shard_map/halo/ppermute | solution.py:205
  13.3 0.0 collective-permute-done.5.rest_3_
  13.3 0.0 collective-permute-start.3
  13.3 0.3 collective-permute-done.4.rest_2_
  13.5 1.0 %collective-permute-start.2 = (bf16[80,128]{1,0:T(8,128)(2,1)S(1)}, bf16[80,128]{1,0:T(8,128)(2,1)S(1)}, u32[]{:S(2)}, u32[]{:S(2)}) collective-permute-start(bf16[80,128]{1,0:T(8,128)(2,1)S(1)} %get-tuple-element.12), channel_id=1, source_target_pairs={{0,1},{1,0},{4,5},{5,4},{8,9},{9,8},{12,13},{13,12},{2,3},{3,2},{6... | collective-permute-start | bytes 61448 | tf_op jit(solution)/shard_map/interface/ppermute | solution.py:207
  15.2 0.0 copy-done.8
  15.2 3.1 %collective-permute-done.3.rest_1_ = bf16[80,128]{1,0:T(8,128)(2,1)S(1)} collective-permute-done((bf16[80,128]{1,0:T(8,128)(2,1)S(1)}, bf16[80,128]{1,0:T(8,128)(2,1)S(1)}, u32[]{:S(2)}, u32[]{:S(2)}) %collective-permute-start.3) | collective-permute-done | bytes 20512 | tf_op jit(solution)/shard_map/interface/ppermute | solution.py:207
  18.3 0.0 collective-permute-done.2.rest_0_
  18.3 0.0 collective-permute-done.low_ref
  18.3 0.0 collective-permute-done.1.high_ref
  18.3 0.0 copy-done.1
  18.3 0.0 copy-done.2
  18.3 0.0 copy-done.3
  18.3 0.0 copy-done.4
  18.3 0.0 copy-done.5
  18.3 0.0 copy-done.6
  18.3 0.0 copy-done.7
  18.4 10.5 %couple.1 = (f32[2,320,1024]{2,1,0:T(8,128)S(1)}, f32[4,1024]{1,0:T(4,128)S(1)}) custom-call(s32[3]{0:T(128)S(1)} %pad_add_fusion.place_ref, f32[1]{0:T(128)S(6)} %copy.17.freq_ref, f32[4,4]{1,0:T(4,128)S(1)} %copy-done.7, s32[6,1024]{1,0:T(8,128)S(1)} %bitcast.15, s32[2,64]{1,0:T(2,128)S(1)} %bitcast.17, bf16[2,320,1024]{2,1,0:T(8,128)(2,1)S(1)} %bitcast.13, ...), custom_call_target="tpu_custom_call" | custom-call | flops 3690987520 | bytes 6553600 | tf_op jit(solution)/shard_map/couple/couple/pallas_call | solution.py:215
  28.8 3.1 %collective-permute-done.6.rest_0_ = bf16[2,320,1024]{2,1,0:T(8,128)(2,1)S(1)} collective-permute-done((bf16[2,320,1024]{2,1,0:T(8,128)(2,1)}, bf16[2,320,1024]{2,1,0:T(8,128)(2,1)S(1)}, u32[]{:S(2)}, u32[]{:S(2)}) %collective-permute-start.6) | collective-permute-done | bytes 1310752 | tf_op jit(solution)/shard_map/instances/ppermute | solution.py:180
  31.9 1.6 %update.1 = bf16[2,320,1024]{2,1,0:T(8,128)(2,1)} custom-call(f32[2,320,1024]{2,1,0:T(8,128)S(1)} %get-tuple-element.13.ready_ref, f32[4,1024]{1,0:T(4,128)S(1)} %get-tuple-element.14.factor_ref, bf16[320,320]{1,0:T(8,128)(2,1)S(1)} %copy-done.1, bf16[2,320,1024]{2,1,0:T(8,128)(2,1)S(1)} %collective-permute-done.6.rest_0_), custom_call_target="tpu_custom_call" | custom-call | flops 419430400 | bytes 5242880 | tf_op jit(solution)/shard_map/update/update/pallas_call | solution.py:235
  (1 shorter events, 0.0 us)
Async XLA Ops:
  0.0 31.9 %collective-permute-start.6 = (bf16[2,320,1024]{2,1,0:T(8,128)(2,1)}, bf16[2,320,1024]{2,1,0:T(8,128)(2,1)S(1)}, u32[]{:S(2)}, u32[]{:S(2)}) collective-permute-start(bf16[2,320,1024]{2,1,0:T(8,128)(2,1)} %bitcast.10), channel_id=1, source_target_pairs={{0,2},{2,0},{1,3},{3,1},{4,6},{6,4},{5,7},{7,5},{8,10},{10,8},{9,1... | collective-permute-start | bytes 3932168 | tf_op jit(solution)/shard_map/instances/ppermute | solution.py:180
  4.2 1.3 %copy-start = (bf16[1,2,320,1024]{3,2,1,0:T(8,128)(2,1)S(1)}, bf16[1,2,320,1024]{3,2,1,0:T(8,128)(2,1)}, u32[]{:S(2)}) copy-start(bf16[1,2,320,1024]{3,2,1,0:T(8,128)(2,1)} %param.11) | copy-start | bytes 3932164
  5.6 9.6 %copy-start.8 = (s32[1,6,1024]{2,0,1:T(1,128)S(1)}, s32[1,6,1024]{2,0,1:T(1,128)}, u32[]{:S(2)}) copy-start(s32[1,6,1024]{2,0,1:T(1,128)} %param.15) | copy-start | bytes 73732
  5.6 12.7 %copy-start.1 = (bf16[320,320]{1,0:T(8,128)(2,1)S(1)}, bf16[320,320]{1,0:T(8,128)(2,1)}, u32[]{:S(2)}) copy-start(bf16[320,320]{1,0:T(8,128)(2,1)} %inverse_ref.3) | copy-start | bytes 614404
  5.6 12.7 %copy-start.2 = (bf16[1,2,320,1024]{3,2,1,0:T(8,128)(2,1)S(1)}, bf16[1,2,320,1024]{3,2,1,0:T(8,128)(2,1)}, u32[]{:S(2)}) copy-start(bf16[1,2,320,1024]{3,2,1,0:T(8,128)(2,1)} %param.12) | copy-start | bytes 3932164
  5.6 12.7 %copy-start.3 = (bf16[320,480]{1,0:T(8,128)(2,1)S(1)}, bf16[320,480]{1,0:T(8,128)(2,1)}, u32[]{:S(2)}) copy-start(bf16[320,480]{1,0:T(8,128)(2,1)} %lift_ref.1) | copy-start | bytes 921604
  5.6 12.8 %copy-start.4 = (bf16[320,320]{1,0:T(8,128)(2,1)S(1)}, bf16[320,320]{1,0:T(8,128)(2,1)}, u32[]{:S(2)}) copy-start(bf16[320,320]{1,0:T(8,128)(2,1)} %volume_ref.1) | copy-start | bytes 614404
  5.6 12.7 %copy-start.5 = (f32[1,1024]{1,0:T(1,128)S(1)}, f32[1,1024]{1,0:T(1,128)}, u32[]{:S(2)}) copy-start(f32[1,1024]{1,0:T(1,128)} %scale_ref.1) | copy-start | bytes 12292
  5.6 12.7 %copy-start.6 = (s32[1,2,64]{2,1,0:T(2,128)S(1)}, s32[1,2,64]{2,1,0:T(2,128)}, u32[]{:S(2)}) copy-start(s32[1,2,64]{2,1,0:T(2,128)} %param.16) | copy-start | bytes 1540
  5.6 12.7 %copy-start.7 = (f32[4,4]{1,0:T(4,128)S(1)}, f32[4,4]{1,0:T(4,128)}, u32[]{:S(2)}) copy-start(f32[4,4]{1,0:T(4,128)} %constant.13.clone.table_ref) | copy-start | bytes 196
  6.6 6.6 %collective-permute-start.5 = (bf16[80,128]{1,0:T(8,128)(2,1)S(1)}, bf16[80,128]{1,0:T(8,128)(2,1)S(1)}, u32[]{:S(2)}, u32[]{:S(2)}) collective-permute-start(bf16[80,128]{1,0:T(8,128)(2,1)S(1)} %get-tuple-element.12), channel_id=1, source_target_pairs={{0,13},{1,12},{4,1},{5,0},{8,5},{9,4},{12,9},{13,8},{2,15},{3,14},... | collective-permute-start | bytes 61448 | tf_op jit(solution)/shard_map/interface/ppermute | solution.py:207
  9.4 4.1 %collective-permute-start.4 = (bf16[80,128]{1,0:T(8,128)(2,1)S(1)}, bf16[80,128]{1,0:T(8,128)(2,1)S(1)}, u32[]{:S(2)}, u32[]{:S(2)}) collective-permute-start(bf16[80,128]{1,0:T(8,128)(2,1)S(1)} %get-tuple-element.12), channel_id=1, source_target_pairs={{0,9},{1,8},{4,13},{5,12},{8,1},{9,0},{12,5},{13,4},{2,11},{3,10},... | collective-permute-start | bytes 61448 | tf_op jit(solution)/shard_map/interface/ppermute | solution.py:207
  9.4 8.8 %collective-permute-start = (bf16[160,128]{1,0:T(8,128)(2,1)S(1)}, bf16[160,128]{1,0:T(8,128)(2,1)S(1)}, u32[]{:S(2)}, u32[]{:S(2)}) collective-permute-start(bf16[160,128]{1,0:T(8,128)(2,1)S(1)} %get-tuple-element.10), channel_id=1, source_target_pairs={{0,4},{4,8},{8,12},{12,0},{1,5},{5,9},{9,13},{13,1},{2,6},{6,10},{... | collective-permute-start | bytes 122888 | tf_op jit(solution)/shard_map/halo/ppermute | solution.py:204
  11.0 7.3 %collective-permute-start.1 = (bf16[160,128]{1,0:T(8,128)(2,1)S(1)}, bf16[160,128]{1,0:T(8,128)(2,1)S(1)}, u32[]{:S(2)}, u32[]{:S(2)}) collective-permute-start(bf16[160,128]{1,0:T(8,128)(2,1)S(1)} %get-tuple-element.11), channel_id=1, source_target_pairs={{0,12},{4,0},{8,4},{12,8},{1,13},{5,1},{9,5},{13,9},{2,14},{6,2},{... | collective-permute-start | bytes 122888 | tf_op jit(solution)/shard_map/halo/ppermute | solution.py:205
  13.3 5.0 %collective-permute-start.3 = (bf16[80,128]{1,0:T(8,128)(2,1)S(1)}, bf16[80,128]{1,0:T(8,128)(2,1)S(1)}, u32[]{:S(2)}, u32[]{:S(2)}) collective-permute-start(bf16[80,128]{1,0:T(8,128)(2,1)S(1)} %get-tuple-element.12), channel_id=1, source_target_pairs={{0,5},{1,4},{4,9},{5,8},{8,13},{9,12},{12,1},{13,0},{2,7},{3,6},{6... | collective-permute-start | bytes 61448 | tf_op jit(solution)/shard_map/interface/ppermute | solution.py:207
  13.5 4.7 %collective-permute-start.2 = (bf16[80,128]{1,0:T(8,128)(2,1)S(1)}, bf16[80,128]{1,0:T(8,128)(2,1)S(1)}, u32[]{:S(2)}, u32[]{:S(2)}) collective-permute-start(bf16[80,128]{1,0:T(8,128)(2,1)S(1)} %get-tuple-element.12), channel_id=1, source_target_pairs={{0,1},{1,0},{4,5},{5,4},{8,9},{9,8},{12,13},{13,12},{2,3},{3,2},{6... | collective-permute-start | bytes 61448 | tf_op jit(solution)/shard_map/interface/ppermute | solution.py:207

commit v29 on v28

--- a/solution.py
+++ b/solution.py
@@ -133,10 +133,13 @@
 def update_kernel(tile, ready_ref, factor_ref, inverse_ref, *rest):
     others, (out_ref, made, sems) = rest[:-3], rest[-3:]
     count, dof, total = ready_ref.shape
+    depths = [(low, min(low + tile, dof)) for low in range(0, dof, tile)]
     copies = []
     for t in range(total // tile):
         cols = slice(t * tile, (t + 1) * tile)
-        moved = [dot(inverse_ref[...], other[m, :, cols]) for other in others for m in range(count)]
+        moved = [[dot(inverse_ref[:, low:high], other[m, low:high, cols]) for low, high in depths]
+                 for other in others for m in range(count)]
+        moved = [functools.reduce(jnp.add, parts) for parts in moved]
         for n in range(count):
             value = ready_ref[n, :, cols]
             for k, part in enumerate(moved):

time: 33.7 us -> 33.7 us (level)
  no operation moved by 1% of the time
where the time goes in v29:
time: 33.7 us; the launch traced here: 33.5 us
  Pallas kernels  13.1 us (39%)
  starting transfers between devices  10.5 us (31%)
  waiting for transfers between devices  6.48 us (19%)
  local copies, waits for them, and re-layouts  2.58 us (8%)
  between operations  0.79 us (2%)
    pallas_call x1, Pallas kernels, body(): pl.pallas_call(functools.partial(couple_kernel, shards, peers), grid=(ste...  10.5 us
    ppermute x4, starting transfers between devices, body(): lax.ppermute(cross, ('space', 'row'), [(i * 2 + r, (i + d) % shards * 2 +...  3.78 us
    ppermute x4, waiting for transfers between devices, body(): lax.ppermute(cross, ('space', 'row'), [(i * 2 + r, (i + d) % shards * 2 +...  3.37 us
    ppermute x1, waiting for transfers between devices, body(): lax.ppermute(current, 'inst', [(i, (i + d) % peers) for i in range(peers)])  3.1 us
    ppermute x1, starting transfers between devices, body(): lax.ppermute(current, 'inst', [(i, (i + d) % peers) for i in range(peers)])  2.94 us
    unnamed x20, local copies, waits for them, and re-layouts  2.58 us
    ppermute x1, starting transfers between devices, body(): lax.ppermute(down, 'space', [(i, (i - 1) % shards) for i in range(shards)])  2.25 us
    pallas_call x1, Pallas kernels, body(): pl.pallas_call(functools.partial(update_kernel, tile), out_shape=jax.Shap...  1.61 us
  transfers between devices with their start and end apart: 7, of which 3 were waited for; matrix products, arithmetic and copies ran while one was open for 4% of the time, Pallas kernels for 34%

profile of v29, /device:TPU:0, one launch (start us, length us, event | category | flops | bytes accessed | tf_op | source)
XLA Modules:
  0.0 33.5 jit_solution(12836873174539793927)
XLA Ops:
  0.0 2.9 %collective-permute-start.6 = (bf16[2,320,1024]{2,1,0:T(8,128)(2,1)}, bf16[2,320,1024]{2,1,0:T(8,128)(2,1)S(1)}, u32[]{:S(2)}, u32[]{:S(2)}) collective-permute-start(bf16[2,320,1024]{2,1,0:T(8,128)(2,1)} %bitcast.10), channel_id=1, source_target_pairs={{0,2},{2,0},{1,3},{3,1},{4,6},{6,4},{5,7},{7,5},{8,10},{10,8},{9,1... | collective-permute-start | bytes 3932168 | tf_op jit(solution)/shard_map/instances/ppermute | solution.py:183
  2.9 1.2 %copy.13.trace_ref = bf16[480,320]{1,0:T(8,128)(2,1)S(1)} copy(bf16[480,320]{0,1:T(8,128)(2,1)} %param.18) | data formatting | bytes 614400 | tf_op args[7]
  4.2 0.1 pad_add_fusion.place_ref
  4.2 0.0 copy-start
  4.2 1.3 %copy-done = bf16[1,2,320,1024]{3,2,1,0:T(8,128)(2,1)S(1)} copy-done((bf16[1,2,320,1024]{3,2,1,0:T(8,128)(2,1)S(1)}, bf16[1,2,320,1024]{3,2,1,0:T(8,128)(2,1)}, u32[]{:S(2)}) %copy-start) | copy-done | bytes 1310744
  5.6 0.0 copy-start.8
  5.6 0.0 copy-start.1
  5.6 0.0 copy-start.2
  5.6 0.0 copy-start.3
  5.6 0.0 copy-start.4
  5.6 0.0 copy-start.5
  5.6 0.0 copy-start.6
  5.6 0.0 copy-start.7
  5.6 1.0 %ends.1 = (bf16[160,128]{1,0:T(8,128)(2,1)S(1)}, bf16[160,128]{1,0:T(8,128)(2,1)S(1)}, bf16[80,128]{1,0:T(8,128)(2,1)S(1)}) custom-call(s32[3]{0:T(128)S(1)} %pad_add_fusion.place_ref, bf16[2,320,1024]{2,1,0:T(8,128)(2,1)S(1)} %bitcast.11, bf16[2,320,1024]{2,1,0:T(8,128)(2,1)S(1)} %bitcast.12, bf16[480,320]{1,0:T(8,128)(2,1)S(1)} %copy.13.trace_ref), custom_call_target="tpu_custom_call" | custom-call | flops 104857600 | bytes 1000000 | tf_op jit(solution)/shard_map/ends/ends/pallas_call | solution.py:187
  6.6 2.8 %collective-permute-start.5 = (bf16[80,128]{1,0:T(8,128)(2,1)S(1)}, bf16[80,128]{1,0:T(8,128)(2,1)S(1)}, u32[]{:S(2)}, u32[]{:S(2)}) collective-permute-start(bf16[80,128]{1,0:T(8,128)(2,1)S(1)} %get-tuple-element.12), channel_id=1, source_target_pairs={{0,13},{1,12},{4,1},{5,0},{8,5},{9,4},{12,9},{13,8},{2,15},{3,14},... | collective-permute-start | bytes 61448 | tf_op jit(solution)/shard_map/interface/ppermute | solution.py:210
  9.4 0.0 collective-permute-start.4
  9.4 1.6 %collective-permute-start = (bf16[160,128]{1,0:T(8,128)(2,1)S(1)}, bf16[160,128]{1,0:T(8,128)(2,1)S(1)}, u32[]{:S(2)}, u32[]{:S(2)}) collective-permute-start(bf16[160,128]{1,0:T(8,128)(2,1)S(1)} %get-tuple-element.10), channel_id=1, source_target_pairs={{0,4},{4,8},{8,12},{12,0},{1,5},{5,9},{9,13},{13,1},{2,6},{6,10},{... | collective-permute-start | bytes 122888 | tf_op jit(solution)/shard_map/halo/ppermute | solution.py:207
  11.0 2.2 %collective-permute-start.1 = (bf16[160,128]{1,0:T(8,128)(2,1)S(1)}, bf16[160,128]{1,0:T(8,128)(2,1)S(1)}, u32[]{:S(2)}, u32[]{:S(2)}) collective-permute-start(bf16[160,128]{1,0:T(8,128)(2,1)S(1)} %get-tuple-element.11), channel_id=1, source_target_pairs={{0,12},{4,0},{8,4},{12,8},{1,13},{5,1},{9,5},{13,9},{2,14},{6,2},{... | collective-permute-start | bytes 122888 | tf_op jit(solution)/shard_map/halo/ppermute | solution.py:208
  13.3 0.0 collective-permute-done.5.rest_3_
  13.3 0.0 collective-permute-start.3
  13.3 0.3 collective-permute-done.4.rest_2_
  13.5 1.0 %collective-permute-start.2 = (bf16[80,128]{1,0:T(8,128)(2,1)S(1)}, bf16[80,128]{1,0:T(8,128)(2,1)S(1)}, u32[]{:S(2)}, u32[]{:S(2)}) collective-permute-start(bf16[80,128]{1,0:T(8,128)(2,1)S(1)} %get-tuple-element.12), channel_id=1, source_target_pairs={{0,1},{1,0},{4,5},{5,4},{8,9},{9,8},{12,13},{13,12},{2,3},{3,2},{6... | collective-permute-start | bytes 61448 | tf_op jit(solution)/shard_map/interface/ppermute | solution.py:210
  15.2 0.0 copy-done.8
  15.2 3.1 %collective-permute-done.3.rest_1_ = bf16[80,128]{1,0:T(8,128)(2,1)S(1)} collective-permute-done((bf16[80,128]{1,0:T(8,128)(2,1)S(1)}, bf16[80,128]{1,0:T(8,128)(2,1)S(1)}, u32[]{:S(2)}, u32[]{:S(2)}) %collective-permute-start.3) | collective-permute-done | bytes 20512 | tf_op jit(solution)/shard_map/interface/ppermute | solution.py:210
  18.3 0.0 collective-permute-done.2.rest_0_
  18.3 0.0 collective-permute-done.low_ref
  18.3 0.0 collective-permute-done.1.high_ref
  18.3 0.0 copy-done.1
  18.3 0.0 copy-done.2
  18.3 0.0 copy-done.3
  18.3 0.0 copy-done.4
  18.3 0.0 copy-done.5
  18.3 0.0 copy-done.6
  18.3 0.0 copy-done.7
  18.4 10.5 %couple.1 = (f32[2,320,1024]{2,1,0:T(8,128)S(1)}, f32[4,1024]{1,0:T(4,128)S(1)}) custom-call(s32[3]{0:T(128)S(1)} %pad_add_fusion.place_ref, f32[1]{0:T(128)S(6)} %copy.17.freq_ref, f32[4,4]{1,0:T(4,128)S(1)} %copy-done.7, s32[6,1024]{1,0:T(8,128)S(1)} %bitcast.15, s32[2,64]{1,0:T(2,128)S(1)} %bitcast.17, bf16[2,320,1024]{2,1,0:T(8,128)(2,1)S(1)} %bitcast.13, ...), custom_call_target="tpu_custom_call" | custom-call | flops 3690987520 | bytes 6553600 | tf_op jit(solution)/shard_map/couple/couple/pallas_call | solution.py:218
  28.8 3.1 %collective-permute-done.6.rest_0_ = bf16[2,320,1024]{2,1,0:T(8,128)(2,1)S(1)} collective-permute-done((bf16[2,320,1024]{2,1,0:T(8,128)(2,1)}, bf16[2,320,1024]{2,1,0:T(8,128)(2,1)S(1)}, u32[]{:S(2)}, u32[]{:S(2)}) %collective-permute-start.6) | collective-permute-done | bytes 1310752 | tf_op jit(solution)/shard_map/instances/ppermute | solution.py:183
  31.9 1.6 %update.1 = bf16[2,320,1024]{2,1,0:T(8,128)(2,1)} custom-call(f32[2,320,1024]{2,1,0:T(8,128)S(1)} %get-tuple-element.13.ready_ref, f32[4,1024]{1,0:T(4,128)S(1)} %get-tuple-element.14.factor_ref, bf16[320,320]{1,0:T(8,128)(2,1)S(1)} %copy-done.1, bf16[2,320,1024]{2,1,0:T(8,128)(2,1)S(1)} %collective-permute-done.6.rest_0_), custom_call_target="tpu_custom_call" | custom-call | flops 419430400 | bytes 5242880 | tf_op jit(solution)/shard_map/update/update/pallas_call | solution.py:238
  (1 shorter events, 0.0 us)
Async XLA Ops:
  0.0 31.9 %collective-permute-start.6 = (bf16[2,320,1024]{2,1,0:T(8,128)(2,1)}, bf16[2,320,1024]{2,1,0:T(8,128)(2,1)S(1)}, u32[]{:S(2)}, u32[]{:S(2)}) collective-permute-start(bf16[2,320,1024]{2,1,0:T(8,128)(2,1)} %bitcast.10), channel_id=1, source_target_pairs={{0,2},{2,0},{1,3},{3,1},{4,6},{6,4},{5,7},{7,5},{8,10},{10,8},{9,1... | collective-permute-start | bytes 3932168 | tf_op jit(solution)/shard_map/instances/ppermute | solution.py:183
  4.2 1.3 %copy-start = (bf16[1,2,320,1024]{3,2,1,0:T(8,128)(2,1)S(1)}, bf16[1,2,320,1024]{3,2,1,0:T(8,128)(2,1)}, u32[]{:S(2)}) copy-start(bf16[1,2,320,1024]{3,2,1,0:T(8,128)(2,1)} %param.11) | copy-start | bytes 3932164
  5.6 9.6 %copy-start.8 = (s32[1,6,1024]{2,0,1:T(1,128)S(1)}, s32[1,6,1024]{2,0,1:T(1,128)}, u32[]{:S(2)}) copy-start(s32[1,6,1024]{2,0,1:T(1,128)} %param.15) | copy-start | bytes 73732
  5.6 12.7 %copy-start.1 = (bf16[320,320]{1,0:T(8,128)(2,1)S(1)}, bf16[320,320]{1,0:T(8,128)(2,1)}, u32[]{:S(2)}) copy-start(bf16[320,320]{1,0:T(8,128)(2,1)} %inverse_ref.3) | copy-start | bytes 614404
  5.6 12.7 %copy-start.2 = (bf16[1,2,320,1024]{3,2,1,0:T(8,128)(2,1)S(1)}, bf16[1,2,320,1024]{3,2,1,0:T(8,128)(2,1)}, u32[]{:S(2)}) copy-start(bf16[1,2,320,1024]{3,2,1,0:T(8,128)(2,1)} %param.12) | copy-start | bytes 3932164
  5.6 12.7 %copy-start.3 = (bf16[320,480]{1,0:T(8,128)(2,1)S(1)}, bf16[320,480]{1,0:T(8,128)(2,1)}, u32[]{:S(2)}) copy-start(bf16[320,480]{1,0:T(8,128)(2,1)} %lift_ref.1) | copy-start | bytes 921604
  5.6 12.8 %copy-start.4 = (bf16[320,320]{1,0:T(8,128)(2,1)S(1)}, bf16[320,320]{1,0:T(8,128)(2,1)}, u32[]{:S(2)}) copy-start(bf16[320,320]{1,0:T(8,128)(2,1)} %volume_ref.1) | copy-start | bytes 614404
  5.6 12.7 %copy-start.5 = (f32[1,1024]{1,0:T(1,128)S(1)}, f32[1,1024]{1,0:T(1,128)}, u32[]{:S(2)}) copy-start(f32[1,1024]{1,0:T(1,128)} %scale_ref.1) | copy-start | bytes 12292
  5.6 12.7 %copy-start.6 = (s32[1,2,64]{2,1,0:T(2,128)S(1)}, s32[1,2,64]{2,1,0:T(2,128)}, u32[]{:S(2)}) copy-start(s32[1,2,64]{2,1,0:T(2,128)} %param.16) | copy-start | bytes 1540
  5.6 12.7 %copy-start.7 = (f32[4,4]{1,0:T(4,128)S(1)}, f32[4,4]{1,0:T(4,128)}, u32[]{:S(2)}) copy-start(f32[4,4]{1,0:T(4,128)} %constant.13.clone.table_ref) | copy-start | bytes 196
  6.6 6.6 %collective-permute-start.5 = (bf16[80,128]{1,0:T(8,128)(2,1)S(1)}, bf16[80,128]{1,0:T(8,128)(2,1)S(1)}, u32[]{:S(2)}, u32[]{:S(2)}) collective-permute-start(bf16[80,128]{1,0:T(8,128)(2,1)S(1)} %get-tuple-element.12), channel_id=1, source_target_pairs={{0,13},{1,12},{4,1},{5,0},{8,5},{9,4},{12,9},{13,8},{2,15},{3,14},... | collective-permute-start | bytes 61448 | tf_op jit(solution)/shard_map/interface/ppermute | solution.py:210
  9.4 4.1 %collective-permute-start.4 = (bf16[80,128]{1,0:T(8,128)(2,1)S(1)}, bf16[80,128]{1,0:T(8,128)(2,1)S(1)}, u32[]{:S(2)}, u32[]{:S(2)}) collective-permute-start(bf16[80,128]{1,0:T(8,128)(2,1)S(1)} %get-tuple-element.12), channel_id=1, source_target_pairs={{0,9},{1,8},{4,13},{5,12},{8,1},{9,0},{12,5},{13,4},{2,11},{3,10},... | collective-permute-start | bytes 61448 | tf_op jit(solution)/shard_map/interface/ppermute | solution.py:210
  9.4 8.8 %collective-permute-start = (bf16[160,128]{1,0:T(8,128)(2,1)S(1)}, bf16[160,128]{1,0:T(8,128)(2,1)S(1)}, u32[]{:S(2)}, u32[]{:S(2)}) collective-permute-start(bf16[160,128]{1,0:T(8,128)(2,1)S(1)} %get-tuple-element.10), channel_id=1, source_target_pairs={{0,4},{4,8},{8,12},{12,0},{1,5},{5,9},{9,13},{13,1},{2,6},{6,10},{... | collective-permute-start | bytes 122888 | tf_op jit(solution)/shard_map/halo/ppermute | solution.py:207
  11.0 7.3 %collective-permute-start.1 = (bf16[160,128]{1,0:T(8,128)(2,1)S(1)}, bf16[160,128]{1,0:T(8,128)(2,1)S(1)}, u32[]{:S(2)}, u32[]{:S(2)}) collective-permute-start(bf16[160,128]{1,0:T(8,128)(2,1)S(1)} %get-tuple-element.11), channel_id=1, source_target_pairs={{0,12},{4,0},{8,4},{12,8},{1,13},{5,1},{9,5},{13,9},{2,14},{6,2},{... | collective-permute-start | bytes 122888 | tf_op jit(solution)/shard_map/halo/ppermute | solution.py:208
  13.3 5.0 %collective-permute-start.3 = (bf16[80,128]{1,0:T(8,128)(2,1)S(1)}, bf16[80,128]{1,0:T(8,128)(2,1)S(1)}, u32[]{:S(2)}, u32[]{:S(2)}) collective-permute-start(bf16[80,128]{1,0:T(8,128)(2,1)S(1)} %get-tuple-element.12), channel_id=1, source_target_pairs={{0,5},{1,4},{4,9},{5,8},{8,13},{9,12},{12,1},{13,0},{2,7},{3,6},{6... | collective-permute-start | bytes 61448 | tf_op jit(solution)/shard_map/interface/ppermute | solution.py:210
  13.5 4.7 %collective-permute-start.2 = (bf16[80,128]{1,0:T(8,128)(2,1)S(1)}, bf16[80,128]{1,0:T(8,128)(2,1)S(1)}, u32[]{:S(2)}, u32[]{:S(2)}) collective-permute-start(bf16[80,128]{1,0:T(8,128)(2,1)S(1)} %get-tuple-element.12), channel_id=1, source_target_pairs={{0,1},{1,0},{4,5},{5,4},{8,9},{9,8},{12,13},{13,12},{2,3},{3,2},{6... | collective-permute-start | bytes 61448 | tf_op jit(solution)/shard_map/interface/ppermute | solution.py:210
